TPU v7x, 32 devices: a whole 2x2x4 slice. The times are simulated.
32 devices in a mesh: seq: 4 (over y, core), kv: 2 (over x), dp: 4 (over z).
Axes of the slice: x: 2, y: 2, z: 4, core: 2. Of those that a mesh axis runs over, the one named last changes fastest.
Arguments:
- queries: bfloat16 [4096, 2048], P(('dp', 'seq', 'kv')), parts along dimension 0, may hold values from -9 to 9
- keys: bfloat16 [4096, 512], P(('dp', 'seq', 'kv')), parts along dimension 0, may hold values from -4 to 4
- values: bfloat16 [4096, 512], P(('dp', 'seq', 'kv')), parts along dimension 0, may hold values from -6 to 6
- doc_ids: int32 [4096], P(('dp', 'seq', 'kv')), parts along dimension 0, may hold values from 0 to 7, never falling along the last dimension, each value on 1 to 256 neighbouring positions
- beta: float32 [16], replicated, may hold values from -2 to 2
- lin_gain: float32 [2048], replicated, may hold values from 0.1 to 1.9
Outputs:
- mixed: float32 [4096, 2048], P(('dp', 'seq', 'kv')), parts along dimension 0
There are 4 independent parts, one for each index of `dp`. A program takes and returns all parts, laid end to end along the dimension named above; an argument that names none is the same for every part. Nothing has to cross between parts.
Inputs may be any that keep to these rules, and one draw needn't show every extreme that they name: `doc_ids`: document ids never fall along a packed sequence; each document holds 1 to 256 tokens.
All inputs are finite; a program needn't handle non-finite values.
Results may differ from a plain program's by a relative error of at most 0.0012.
Values may be sent and summed in bfloat16 or wider, within the bound.
No kernel may reach another device: no remote copies, remote signals or barrier semaphores. Data moves between devices by JAX's collectives and lax.ppermute only.
A program may use at most 64 MiB of HBM per device.

v0:
```python
import jax
import jax.numpy as jnp
from jax import lax
from jax.sharding import PartitionSpec as P

HEADS = 16
KV_HEADS = 4
HEAD_DIM = 128


def carried_in(part, axis, combine, identity):
    place = lax.axis_index(axis)
    gathered = jax.tree.map(lambda a: lax.all_gather(a, axis), part)
    state = jax.tree.map(lambda a, e: jnp.zeros_like(a) + jnp.asarray(e, a.dtype), part, identity)

    def one(step, state):
        return combine(
            state, jax.tree.map(lambda a: lax.dynamic_index_in_dim(a, step, 0, False), gathered)
        )

    return lax.fori_loop(0, place, one, state)


def join_states(earlier, later):
    state_early, first_early, last_early = earlier
    state_late, first_late, last_late = later
    empty_late = first_late < 0
    joined = (first_late == last_late) & (last_early == first_late)
    merged = state_late + jnp.where(joined, state_early, jnp.zeros_like(state_early))
    combined = jnp.where(empty_late, state_early, merged)
    first_doc = jnp.where(first_early < 0, first_late, first_early)
    last_doc = jnp.where(empty_late, last_early, last_late)
    return (combined, first_doc, last_doc)


def tail_merge(one_side, other_side):
    state_one, first_one, last_one = one_side
    state_other, first_other, last_other = other_side
    top_doc = jnp.maximum(last_one, last_other)
    state_sum = jnp.where(last_one == top_doc, state_one, jnp.zeros_like(state_one))
    state_sum = state_sum + jnp.where(
        last_other == top_doc, state_other, jnp.zeros_like(state_other)
    )
    return (state_sum, jnp.minimum(first_one, first_other), top_doc)


def tail_state(key_rows, value_rows, doc_rows, target_doc):
    count = key_rows.shape[0]
    key_heads = key_rows.reshape(count, KV_HEADS, HEAD_DIM)
    value_heads = value_rows.reshape(count, KV_HEADS, HEAD_DIM)
    live = doc_rows == target_doc
    masked = jnp.where(live[:, None, None], key_heads, jnp.zeros_like(key_heads))
    return jnp.einsum("rgd,rge->gde", masked, value_heads, preferred_element_type=jnp.float32)


def attend_block(
    carry, query_heads, query_pos, query_doc, key_rows, value_rows, key_doc, key_start
):
    running_max, running_sum, accumulated = carry
    key_count = key_rows.shape[0]
    key_heads = key_rows.reshape(key_count, KV_HEADS, HEAD_DIM)
    value_heads = value_rows.reshape(key_count, KV_HEADS, HEAD_DIM)
    scores = jnp.einsum(
        "rgqd,kgd->gqrk", query_heads, key_heads, preferred_element_type=jnp.float32
    )
    scores = scores / jnp.sqrt(jnp.float32(HEAD_DIM))
    key_pos = key_start + jnp.arange(key_count, dtype=jnp.int32)
    allowed = (key_pos[None, :] <= query_pos[:, None]) & (key_doc[None, :] == query_doc[:, None])
    masked = jnp.where(allowed, scores, jnp.float32(-1e30))
    new_max = jnp.maximum(running_max, jnp.max(masked, axis=-1))
    factor = jnp.exp(running_max - new_max)
    weights = jnp.where(allowed, jnp.exp(masked - new_max[..., None]), jnp.float32(0.0))
    new_sum = running_sum * factor + jnp.sum(weights, axis=-1)
    product = jnp.einsum(
        "gqrk,kge->gqre",
        weights.astype(jnp.bfloat16),
        value_heads,
        preferred_element_type=jnp.float32,
    )
    new_accum = accumulated * factor[..., None] + product
    return (new_max, new_sum, new_accum)


def on_device(queries, keys, values, doc_ids, beta, lin_gain):
    row_count = queries.shape[0]
    groups = HEADS // KV_HEADS
    query_heads = queries.reshape(row_count, KV_HEADS, groups, HEAD_DIM)
    position = lax.axis_index("kv") * row_count
    query_pos = position + jnp.arange(row_count, dtype=jnp.int32)
    last_query = position + row_count - 1
    initial = (
        jnp.full((KV_HEADS, groups, row_count), -1e30, jnp.float32),
        jnp.zeros((KV_HEADS, groups, row_count), jnp.float32),
        jnp.zeros((KV_HEADS, groups, row_count, HEAD_DIM), jnp.float32),
    )
    empty_tail = (
        jnp.zeros((KV_HEADS, HEAD_DIM, HEAD_DIM), jnp.float32),
        jnp.array(2**30, jnp.int32),
        jnp.array(-1, jnp.int32),
    )
    key_piece = lax.all_gather(keys, "kv", axis=0, tiled=True)
    value_piece = lax.all_gather(values, "kv", axis=0, tiled=True)
    doc_piece = lax.all_gather(doc_ids, "kv", axis=0, tiled=True)
    blocks = key_piece.shape[0] // row_count

    def one_block(state, item):
        soft_state, tail_now = state
        key_block, value_block, doc_block, number = item
        block_start = number * row_count
        soft_next = lax.cond(
            block_start <= last_query,
            lambda inner: attend_block(
                inner,
                query_heads,
                query_pos,
                doc_ids,
                key_block,
                value_block,
                doc_block,
                block_start,
            ),
            lambda inner: inner,
            soft_state,
        )
        block_tail = (
            tail_state(key_block, value_block, doc_block, doc_block[-1]),
            doc_block[0],
            doc_block[-1],
        )
        tail_now = tail_merge(tail_now, block_tail)
        return ((soft_next, tail_now), None)

    stacked = (
        key_piece.reshape(blocks, row_count, -1),
        value_piece.reshape(blocks, row_count, -1),
        doc_piece.reshape(blocks, row_count),
        jnp.arange(blocks, dtype=jnp.int32),
    )
    result, _ = lax.scan(one_block, (initial, empty_tail), stacked)
    running, segment_tail = result
    running_max, running_sum, accumulated = running
    soft_out = jnp.transpose(accumulated / running_sum[..., None], (2, 0, 1, 3))
    identity = (
        jnp.zeros((KV_HEADS, HEAD_DIM, HEAD_DIM), jnp.float32),
        jnp.array(-1, jnp.int32),
        jnp.array(-1, jnp.int32),
    )
    memory = carried_in(segment_tail, "seq", join_states, identity)
    memory_state, memory_first, memory_last = memory
    query_float = query_heads.astype(jnp.float32)
    recalled = jnp.einsum(
        "rgqd,gde->rgqe", query_float, memory_state, precision=lax.Precision.HIGHEST
    )
    recalled = jnp.where((doc_ids == memory_last)[:, None, None, None], recalled, jnp.float32(0.0))
    mean_square = jnp.mean(recalled * recalled, axis=-1, keepdims=True)
    normed = (
        recalled * lax.rsqrt(mean_square + 1e-06) * lin_gain.reshape(KV_HEADS, groups, HEAD_DIM)
    )
    mixing = jax.nn.sigmoid(beta).reshape(KV_HEADS, groups)[None, :, :, None]
    mixed = mixing * normed + (1.0 - mixing) * soft_out
    return mixed.reshape(row_count, HEADS * HEAD_DIM).astype(jnp.float32)


def solution(mesh):
    in_specs = (
        P(("dp", "seq", "kv"), None),
        P(("dp", "seq", "kv"), None),
        P(("dp", "seq", "kv"), None),
        P(("dp", "seq", "kv")),
        P(),
        P(),
    )
    out_specs = P(("dp", "seq", "kv"), None)
    return jax.shard_map(
        on_device, mesh=mesh, in_specs=in_specs, out_specs=out_specs, check_vma=False
    )
```

profile of v0, /device:TPU:7, one launch (start us, length us, event | category | flops | bytes accessed | tf_op | source)
XLA Modules:
  0.0 81.4 jit_solution(18401438892241153620)
XLA Ops:
  6.5 5.4 %all_gather.27 = bf16[256,512]{1,0:T(8,128)(2,1)S(1)} all-gather(bf16[128,512]{1,0:T(8,128)(2,1)} %param.13), channel_id=1, replica_groups=mesh['seq'=4,'kv'=2,'dp'=4] {'kv'}, dimensions={0}, use_global_device_ids=true | all-gather | bytes 393216 | tf_op jit(solution)/shard_map/all_gather | solution.py:101
  11.9 4.7 %all_gather.28 = bf16[256,512]{1,0:T(8,128)(2,1)S(1)} all-gather(bf16[128,512]{1,0:T(8,128)(2,1)} %param.14), channel_id=1, replica_groups=mesh['seq'=4,'kv'=2,'dp'=4] {'kv'}, dimensions={0}, use_global_device_ids=true | all-gather | bytes 393216 | tf_op jit(solution)/shard_map/all_gather | solution.py:102
  16.6 0.7 copy-done.2
  17.3 3.1 %all-gather.1 = s32[2,1,128]{2,1,0:T(1,128)S(1)} all-gather(s32[1,1,128]{2,1,0:T(1,128)S(1)} %bitcast.98), channel_id=1, replica_groups=mesh['seq'=4,'kv'=2,'dp'=4] {'kv'}, dimensions={0}, use_global_device_ids=true | all-gather | bytes 1536 | tf_op jit(solution)/shard_map/all_gather | solution.py:103
  21.0 12.9 %while.36 = (s32[]{:T(128)}, f32[4,4,128]{2,1,0:T(4,128)S(1)}, f32[4,4,128]{2,1,0:T(4,128)S(1)}, f32[4,4,128,128]{3,2,1,0:T(8,128)S(1)}, f32[4,128,128]{2,1,0:T(...) while((s32[]{:T(128)}, f32[4,4,128]{2,1,0:T(4,128)S(1)}, ...), condition=%wide.region_5.6_spmd.clone, body=%wide.region_0.5_spmd.clone.sunk | while | flops 154259840 | bytes 8067273 | solution.py:139
  21.0 0.6 dynamic_slice.52
  22.6 1.5 %conditional.3 = ((f32[4,4,128]{2,1,0:T(4,128)S(1)}, f32[4,4,128]{2,1,0:T(4,128)S(1)}, f32[4,4,128,128]{3,2,1,0:T(8,128)S(1)})) conditional(s32[]{:T(128)} %convert_element_type.11, (f32[4,4,128]{2,1,0:T(4,128)S(1)}, f32[4,4,128]{2,1,0:T(4,128)S(1)}, f32[4,4,128,128]{3,2,1,0:T(8,128)S(1)}) %tuple.66, (s32[]{:T(128)}, s32[]{:T(128)}, ...), branch_computations={%region_1.1_spmd, %region_2.4_spmd} | conditional | flops 137154816 | bytes 6229544 | solution.py:110
  23.4 0.7 convolution_add_fusion
  24.1 0.6 fusion.34
  24.7 0.6 compare_bitcast_fusion.2
  27.5 0.6 dynamic_slice.52
  29.1 1.5 %conditional.3 = ((f32[4,4,128]{2,1,0:T(4,128)S(1)}, f32[4,4,128]{2,1,0:T(4,128)S(1)}, f32[4,4,128,128]{3,2,1,0:T(8,128)S(1)})) conditional(s32[]{:T(128)} %convert_element_type.11, (f32[4,4,128]{2,1,0:T(4,128)S(1)}, f32[4,4,128]{2,1,0:T(4,128)S(1)}, f32[4,4,128,128]{3,2,1,0:T(8,128)S(1)}) %tuple.66, (s32[]{:T(128)}, s32[]{:T(128)}, ...), branch_computations={%region_1.1_spmd, %region_2.4_spmd} | conditional | flops 137154816 | bytes 6229544 | solution.py:110
  29.8 0.7 convolution_add_fusion
  30.5 0.6 fusion.34
  31.1 0.6 compare_bitcast_fusion.2
  33.9 0.7 copy-done
  34.7 0.6 copy-done.5
  35.9 0.7 dynamic-update-slice
  36.6 0.7 dynamic-update-slice.1
  37.3 6.4 %all-reduce.2 = (s32[4]{0:T(128)S(1)}, s32[4]{0:T(128)S(1)}) all-reduce(s32[4]{0:T(128)S(1)} %dynamic-update-slice, s32[4]{0:T(128)S(1)} %dynamic-update-slice.1), channel_id=1, replica_groups=mesh['seq'=4,'kv'=2,'dp'=4] {'seq'}, use_global_device_ids=true, to_apply=%add | all-reduce | flops 8 | bytes 64
  44.0 0.6 copy-done.4
  44.8 10.6 %all-gather.4.cloned.1.call-done = f32[16,128,128]{2,1,0:T(8,128)} async-done(((f32[4,128,128]{2,1,0:T(8,128)}), f32[16,128,128]{2,1,0:T(8,128)}) %all-gather.4.cloned.1.call-update) | async-done | bytes 1048592 | tf_op jit(solution)/shard_map/all_gather | solution.py:13
  55.4 15.9 %while.35 = (s32[]{:T(128)}, f32[4,128,128]{2,1,0:T(8,128)S(1)}, s32[]{:T(128)}, s32[]{:T(128)}, s32[4]{0:T(128)S(1)}, /*index=5*/f32[4,4,128,128]{3,2,1,0:T(8,1...) while((s32[]{:T(128)}, f32[4,128,128]{2,1,0:T(8,128)S(1)}, s32[]{:T(128)}, s32[]{:T(128)}, s32[4]{0:T(128)S(1)}, ...), condition=%wide.region_7.8_spmd, body=%wide.region_6.7_spmd.sunk | while | flops 196618 | bytes 786648 | solution.py:21
  55.4 0.6 dynamic_slice.47
  59.1 1.0 %fusion.31 = f32[4,128,128]{2,1,0:T(8,128)S(1)} fusion(f32[4,128,128]{2,1,0:T(8,128)S(1)} %get-tuple-element.606, f32[4,4,128,128]{3,2,1,0:T(8,128)} %get-tuple-element.620, s32[]{:T(128)S(6)} %select_n.110, pred[]{:T(512)S(6)} %and.11, pred[]{:T(512)S(6)} %lt.26), kind=kLoop, calls=%fused_computation.18.clone.1 | loop fusion | flops 196608 | bytes 786438 | tf_op jit(solution)/shard_map/while/body/jit(_where)/select_n | solution.py:30
  60.7 0.6 dynamic_slice.47
  64.4 1.0 %fusion.31 = f32[4,128,128]{2,1,0:T(8,128)S(1)} fusion(f32[4,128,128]{2,1,0:T(8,128)S(1)} %get-tuple-element.606, f32[4,4,128,128]{3,2,1,0:T(8,128)} %get-tuple-element.620, s32[]{:T(128)S(6)} %select_n.110, pred[]{:T(512)S(6)} %and.11, pred[]{:T(512)S(6)} %lt.26), kind=kLoop, calls=%fused_computation.18.clone.1 | loop fusion | flops 196608 | bytes 786438 | tf_op jit(solution)/shard_map/while/body/jit(_where)/select_n | solution.py:30
  66.0 0.6 dynamic_slice.47
  69.7 1.0 %fusion.31 = f32[4,128,128]{2,1,0:T(8,128)S(1)} fusion(f32[4,128,128]{2,1,0:T(8,128)S(1)} %get-tuple-element.606, f32[4,4,128,128]{3,2,1,0:T(8,128)} %get-tuple-element.620, s32[]{:T(128)S(6)} %select_n.110, pred[]{:T(512)S(6)} %and.11, pred[]{:T(512)S(6)} %lt.26), kind=kLoop, calls=%fused_computation.18.clone.1 | loop fusion | flops 196608 | bytes 786438 | tf_op jit(solution)/shard_map/while/body/jit(_where)/select_n | solution.py:30
  71.4 0.7 multiply_reduce_fusion
  72.1 0.7 copy-done.3
  73.2 1.3 %copy.52 = f32[128,2048]{1,0:T(8,128)} copy(f32[128,2048]{0,1:T(8,128)S(1)} %bitcast.88) | data formatting | bytes 2097152 | tf_op jit(solution)/shard_map/reshape | solution.py:161
  (56 shorter events, 6.4 us)
Async XLA Ops:
  6.5 13.8 %copy-start.1 = (bf16[128,2048]{1,0:T(8,128)(2,1)S(1)}, bf16[128,2048]{1,0:T(8,128)(2,1)}, u32[]{:S(2)}) copy-start(bf16[128,2048]{1,0:T(8,128)(2,1)} %param.12) | copy-start | bytes 1572868
  6.5 48.8 %all-gather.4.cloned.1.call-start = ((), (), s32[]{:S(2)}) async-start(), calls=%async_computation | async-start | bytes 1310720 | tf_op jit(solution)/shard_map/all_gather | solution.py:13
  16.6 0.7 copy-start.2
  33.9 0.7 copy-start
  34.7 0.7 copy-start.5
  44.0 0.7 copy-start.4
  72.1 0.7 copy-start.3
Sparse Core Ops, SparseCore 0:
  34.8 20.5 all-gather.3
where the time goes:
time: 81.9 us; the launch traced here: 81.4 us
  blocking collectives  19.5 us (24%)
  loops' own time  14.7 us (18%)
  local copies, waits for them, and re-layouts  14.1 us (17%)
  between operations  13.5 us (16%)
  waiting for transfers between devices  10.6 us (13%)
  other arithmetic  5.59 us (7%)
  matrix products  3.26 us (4%)
    all_gather x1, waiting for transfers between devices, carried_in(): gathered = jax.tree.map(lambda a: lax.all_gather(a, axis), part)  10.6 us
    another operation x1, loops' own time, carried_in(): return lax.fori_loop(0, place, one, state)  9.34 us
    unnamed x1, blocking collectives  6.4 us
    unnamed x19, local copies, waits for them, and re-layouts  5.81 us
    all_gather x1, blocking collectives, on_device(): key_piece = lax.all_gather(keys, 'kv', axis=0, tiled=True)  5.37 us
    another operation x1, loops' own time, on_device(): result, _ = lax.scan(one_block, (initial, empty_tail), stacked)  5.26 us
    all_gather x1, blocking collectives, on_device(): value_piece = lax.all_gather(values, 'kv', axis=0, tiled=True)  4.69 us
    dynamic_slice x6, local copies, waits for them, and re-layouts, one(): lax.dynamic_index_in_dim(a, step, 0, False)  3.48 us
  transfers between devices with their start and end apart: 1, of which 1 were waited for; matrix products, arithmetic and copies ran while one was open for 3% of the time, Pallas kernels for 0%

commit v1 on v0

--- a/solution.py
+++ b/solution.py
@@ -1,11 +1,141 @@
+import functools
+
 import jax
 import jax.numpy as jnp
 from jax import lax
+from jax.experimental import pallas as pl
+from jax.experimental.pallas import tpu as pltpu
 from jax.sharding import PartitionSpec as P
 
 HEADS = 16
 KV_HEADS = 4
 HEAD_DIM = 128
+GROUPS = HEADS // KV_HEADS
+LONGEST = 4
+
+NT = (((1,), (1,)), ((), ()))
+TN = (((0,), (0,)), ((), ()))
+NN = (((1,), (0,)), ((), ()))
+
+
+def dot(a, b, dims):
+    return lax.dot_general(a, b, dims, preferred_element_type=jnp.float32)
+
+
+def column(row):
+    n = row.shape[1]
+    return jnp.transpose(jnp.broadcast_to(row, (HEAD_DIM, n)))
+
+
+def mix_kernel(blocks, n_kv, place_ref, beta_ref, *refs):
+    q_ref, gain_ref = refs[:2]
+    key_refs = refs[2 : 2 + blocks]
+    value_refs = refs[2 + blocks : 2 + 2 * blocks]
+    doc_refs = refs[2 + 2 * blocks : 2 + 3 * blocks]
+    out_ref = refs[2 + 3 * blocks]
+    rows = q_ref.shape[0]
+    segment, part = place_ref[0], place_ref[1]
+    docs = [ref[...].astype(jnp.float32) for ref in doc_refs]
+    own = docs[0]
+    first = own[:, 0:1]
+    for j in range(1, n_kv):
+        first = jnp.where(part == j, docs[j][:, 0:1], first)
+    first = jnp.broadcast_to(first, (1, rows))
+    reads = jnp.where((own == first) & (segment > 0), 1.0, 0.0)
+
+    place = lax.broadcasted_iota(jnp.int32, (rows, rows), 0)
+    row = lax.broadcasted_iota(jnp.int32, (rows, rows), 1)
+    allowed = [(place <= row) & (column(docs[0]) == own)]
+    for j in range(1, n_kv):
+        allowed.append((column(docs[j]) == own) & (j <= part))
+
+    live = []
+    for j in range(1, blocks):
+        other = jnp.where((docs[j] == first) & (j > part), 0.0, 1.0)
+        count = jnp.sum(other, axis=1, keepdims=True).astype(jnp.int32)
+        live.append(lax.broadcasted_iota(jnp.int32, (rows, HEAD_DIM), 0) >= count)
+
+    gain = gain_ref[...]
+    scale = 1.0 / (float(HEAD_DIM) ** 0.5)
+    for g in range(KV_HEADS):
+        cols = slice(g * HEAD_DIM, (g + 1) * HEAD_DIM)
+        heads = [
+            q_ref[:, (g * GROUPS + i) * HEAD_DIM : (g * GROUPS + i + 1) * HEAD_DIM]
+            for i in range(GROUPS)
+        ]
+        q = jnp.concatenate(heads, axis=0)
+        state = jnp.zeros((HEAD_DIM, HEAD_DIM), jnp.float32)
+        for j in range(1, blocks):
+            k = key_refs[j][:, cols]
+            k = jnp.where(live[j - 1], k.astype(jnp.float32), 0.0).astype(jnp.bfloat16)
+            state = state + dot(value_refs[j][:, cols], k, TN)
+        high = state.astype(jnp.bfloat16)
+        low = (state - high.astype(jnp.float32)).astype(jnp.bfloat16)
+        recalled = dot(high, q, NT) + dot(low, q, NT)
+        scores = [dot(key_refs[j][:, cols], q, NT) for j in range(n_kv)]
+        for i in range(GROUPS):
+            h = g * GROUPS + i
+            cut = slice(i * rows, (i + 1) * rows)
+            masked = [
+                jnp.where(allowed[j], scores[j][:, cut] * scale, -1e30) for j in range(n_kv)
+            ]
+            top = functools.reduce(
+                jnp.maximum, [jnp.max(m, axis=0, keepdims=True) for m in masked]
+            )
+            weights = [jnp.exp(m - top) for m in masked]
+            total = functools.reduce(
+                jnp.add, [jnp.sum(w, axis=0, keepdims=True) for w in weights]
+            )
+            summed = functools.reduce(
+                jnp.add,
+                [
+                    dot(value_refs[j][:, cols], weights[j].astype(jnp.bfloat16), TN)
+                    for j in range(n_kv)
+                ],
+            )
+            read = recalled[:, cut]
+            square = jnp.sum(read * read, axis=0, keepdims=True) * (1.0 / HEAD_DIM)
+            share = 1.0 / (1.0 + jnp.exp(-jnp.full((1, rows), beta_ref[h], jnp.float32)))
+            read_scale = share * lax.rsqrt(square + 1e-06) * reads
+            mixed = (
+                column(gain[h : h + 1, :]) * (read * read_scale)
+                + summed * ((1.0 - share) / total)
+            )
+            out_ref[:, h * HEAD_DIM : (h + 1) * HEAD_DIM] = jnp.transpose(mixed)
+
+
+def near_device(n_seq, n_kv, queries, keys, values, doc_ids, beta, lin_gain):
+    rows = queries.shape[0]
+    devices = n_seq * n_kv
+    blocks = 2 * n_kv
+    doc_row = doc_ids.reshape(1, rows)
+    key_list, value_list, doc_list = [keys], [values], [doc_row]
+    for j in range(1, blocks):
+        pairs = [
+            (b - j, b) for b in range(j, devices) if j <= b % n_kv + n_kv
+        ]
+        send = functools.partial(lax.ppermute, axis_name=("seq", "kv"), perm=pairs)
+        key_list.append(send(keys))
+        value_list.append(send(values))
+        doc_list.append(send(doc_row))
+    place = jnp.stack([lax.axis_index("seq"), lax.axis_index("kv")]).astype(jnp.int32)
+    vmem = pl.BlockSpec(memory_space=pltpu.VMEM)
+    smem = pl.BlockSpec(memory_space=pltpu.SMEM)
+    return pl.pallas_call(
+        functools.partial(mix_kernel, blocks, n_kv),
+        out_shape=jax.ShapeDtypeStruct((rows, HEADS * HEAD_DIM), jnp.float32),
+        in_specs=[smem, smem] + [vmem] * (2 + 3 * blocks),
+        out_specs=vmem,
+        compiler_params=pltpu.CompilerParams(vmem_limit_bytes=32 * 1024 * 1024),
+    )(
+        place,
+        beta,
+        queries,
+        lin_gain.reshape(HEADS, HEAD_DIM),
+        *key_list,
+        *value_list,
+        *doc_list,
+    )
 
 
 def carried_in(part, axis, combine, identity):
@@ -81,7 +211,7 @@
     return (new_max, new_sum, new_accum)
 
 
-def on_device(queries, keys, values, doc_ids, beta, lin_gain):
+def far_device(queries, keys, values, doc_ids, beta, lin_gain):
     row_count = queries.shape[0]
     groups = HEADS // KV_HEADS
     query_heads = queries.reshape(row_count, KV_HEADS, groups, HEAD_DIM)
@@ -162,6 +292,7 @@
 
 
 def solution(mesh):
+    n_seq, n_kv = mesh.shape["seq"], mesh.shape["kv"]
     in_specs = (
         P(("dp", "seq", "kv"), None),
         P(("dp", "seq", "kv"), None),
@@ -171,6 +302,10 @@
         P(),
     )
     out_specs = P(("dp", "seq", "kv"), None)
+    if n_seq <= LONGEST:
+        on_device = functools.partial(near_device, n_seq, n_kv)
+    else:
+        on_device = far_device
     return jax.shard_map(
         on_device, mesh=mesh, in_specs=in_specs, out_specs=out_specs, check_vma=False
     )

time: 81.9 us -> 34 us (0.42)
  the two profiles are of different devices: /device:TPU:7 before, /device:TPU:0 now
where the time goes in v1:
time: 34 us; the launch traced here: 33.6 us
  starting transfers between devices  21.8 us (64%)
  waiting for transfers between devices  4.37 us (13%)
  Pallas kernels  4.36 us (13%)
  local copies, waits for them, and re-layouts  2.86 us (8%)
    ppermute x3, starting transfers between devices, near_device(): doc_list.append(send(doc_row))  9.22 us
    ppermute x3, starting transfers between devices, near_device(): key_list.append(send(keys))  7.41 us
    ppermute x3, starting transfers between devices, near_device(): value_list.append(send(values))  5.14 us
    pallas_call x1, Pallas kernels, near_device(): pl.pallas_call(functools.partial(mix_kernel, blocks, n_kv), out_shape=jax...  4.36 us
    ppermute x3, waiting for transfers between devices, near_device(): value_list.append(send(values))  4.36 us
    unnamed x12, local copies, waits for them, and re-layouts  2.86 us
  transfers between devices with their start and end apart: 9, of which 2 were waited for; matrix products, arithmetic and copies ran while one was open for 0% of the time, Pallas kernels for 0%

profile of v1, /device:TPU:0, one launch (start us, length us, event | category | flops | bytes accessed | tf_op | source)
XLA Modules:
  0.0 33.6 jit_solution(9225963464232358082)
XLA Ops:
  0.0 0.0 copy-start.5
  0.0 2.5 %collective-permute-start.1 = (bf16[128,512]{1,0:T(8,128)(2,1)}, bf16[128,512]{1,0:T(8,128)(2,1)S(1)}, u32[]{:S(2)}, u32[]{:S(2)}) collective-permute-start(bf16[128,512]{1,0:T(8,128)(2,1)} %refs_2_.1), channel_id=1, source_target_pairs={{0,8},{4,12},{8,16},{12,20},{16,24},{20,28},{1,9},{5,13},{9,17},{1... | collective-permute-start | bytes 393224 | tf_op jit(solution)/shard_map/ppermute | solution.py:118
  2.5 0.0 copy-done.5
  2.5 5.6 %collective-permute-start.8 = (s32[1,128]{1,0:T(1,128)S(1)}, s32[1,128]{1,0:T(1,128)S(1)}, u32[]{:S(2)}, u32[]{:S(2)}) collective-permute-start(s32[1,128]{1,0:T(1,128)S(1)} %bitcast.5), channel_id=1, source_target_pairs={{0,12},{8,20},{16,28},{1,13},{9,21},{17,29},{2,14},{10,22},{18,30}... | collective-permute-start | bytes 1544 | tf_op jit(solution)/shard_map/ppermute | solution.py:120
  8.1 1.7 %collective-permute-start.7 = (s32[1,128]{1,0:T(1,128)S(1)}, s32[1,128]{1,0:T(1,128)S(1)}, u32[]{:S(2)}, u32[]{:S(2)}) collective-permute-start(s32[1,128]{1,0:T(1,128)S(1)} %bitcast.6), channel_id=1, source_target_pairs={{0,8},{4,12},{8,16},{12,20},{16,24},{20,28},{1,9},{5,13},{9,17},{1... | collective-permute-start | bytes 1544 | tf_op jit(solution)/shard_map/ppermute | solution.py:120
  9.9 1.8 %collective-permute-start.6 = (s32[1,128]{1,0:T(1,128)S(1)}, s32[1,128]{1,0:T(1,128)S(1)}, u32[]{:S(2)}, u32[]{:S(2)}) collective-permute-start(s32[1,128]{1,0:T(1,128)S(1)} %bitcast.7), channel_id=1, source_target_pairs={{0,4},{4,8},{8,12},{12,16},{16,20},{20,24},{24,28},{1,5},{5,9},{9,... | collective-permute-start | bytes 1544 | tf_op jit(solution)/shard_map/ppermute | solution.py:120
  11.7 3.6 %collective-permute-start = (bf16[128,512]{1,0:T(8,128)(2,1)}, bf16[128,512]{1,0:T(8,128)(2,1)S(1)}, u32[]{:S(2)}, u32[]{:S(2)}) collective-permute-start(bf16[128,512]{1,0:T(8,128)(2,1)} %refs_2_.1), channel_id=1, source_target_pairs={{0,4},{4,8},{8,12},{12,16},{16,20},{20,24},{24,28},{1,5},{5,9},{9,... | collective-permute-start | bytes 393224 | tf_op jit(solution)/shard_map/ppermute | solution.py:118
  15.4 0.0 collective-permute-done.8.refs_13_
  15.4 1.3 %collective-permute-start.2 = (bf16[128,512]{1,0:T(8,128)(2,1)}, bf16[128,512]{1,0:T(8,128)(2,1)S(1)}, u32[]{:S(2)}, u32[]{:S(2)}) collective-permute-start(bf16[128,512]{1,0:T(8,128)(2,1)} %refs_2_.1), channel_id=1, source_target_pairs={{0,12},{8,20},{16,28},{1,13},{9,21},{17,29},{2,14},{10,22},{18,30}... | collective-permute-start | bytes 393224 | tf_op jit(solution)/shard_map/ppermute | solution.py:118
  16.7 0.0 collective-permute-done.7.refs_12_
  16.7 1.3 %collective-permute-start.4 = (bf16[128,512]{1,0:T(8,128)(2,1)}, bf16[128,512]{1,0:T(8,128)(2,1)S(1)}, u32[]{:S(2)}, u32[]{:S(2)}) collective-permute-start(bf16[128,512]{1,0:T(8,128)(2,1)} %refs_6_.1), channel_id=1, source_target_pairs={{0,8},{4,12},{8,16},{12,20},{16,24},{20,28},{1,9},{5,13},{9,17},{1... | collective-permute-start | bytes 393224 | tf_op jit(solution)/shard_map/ppermute | solution.py:119
  18.0 0.0 collective-permute-done.6.refs_11_
  18.0 2.3 %collective-permute-start.3 = (bf16[128,512]{1,0:T(8,128)(2,1)}, bf16[128,512]{1,0:T(8,128)(2,1)S(1)}, u32[]{:S(2)}, u32[]{:S(2)}) collective-permute-start(bf16[128,512]{1,0:T(8,128)(2,1)} %refs_6_.1), channel_id=1, source_target_pairs={{0,4},{4,8},{8,12},{12,16},{16,20},{20,24},{24,28},{1,5},{5,9},{9,... | collective-permute-start | bytes 393224 | tf_op jit(solution)/shard_map/ppermute | solution.py:119
  20.3 0.0 collective-permute-done.1.refs_4_
  20.3 1.5 %collective-permute-start.5 = (bf16[128,512]{1,0:T(8,128)(2,1)}, bf16[128,512]{1,0:T(8,128)(2,1)S(1)}, u32[]{:S(2)}, u32[]{:S(2)}) collective-permute-start(bf16[128,512]{1,0:T(8,128)(2,1)} %refs_6_.1), channel_id=1, source_target_pairs={{0,12},{8,20},{16,28},{1,13},{9,21},{17,29},{2,14},{10,22},{18,30}... | collective-permute-start | bytes 393224 | tf_op jit(solution)/shard_map/ppermute | solution.py:119
  21.9 0.0 copy-start.3
  21.9 0.1 pad_add_fusion.place_ref
  22.0 0.0 copy-start.4
  22.0 0.0 collective-permute-done.refs_3_
  22.0 0.0 collective-permute-done.2.refs_5_
  22.0 0.0 collective-permute-done.4.refs_8_
  22.0 2.5 %collective-permute-done.3.refs_7_ = bf16[128,512]{1,0:T(8,128)(2,1)S(1)} collective-permute-done((bf16[128,512]{1,0:T(8,128)(2,1)}, bf16[128,512]{1,0:T(8,128)(2,1)S(1)}, u32[]{:S(2)}, u32[]{:S(2)}) %collective-permute-start.3) | collective-permute-done | bytes 131104 | tf_op jit(solution)/shard_map/ppermute | solution.py:119
  24.5 1.9 %collective-permute-done.5.refs_9_ = bf16[128,512]{1,0:T(8,128)(2,1)S(1)} collective-permute-done((bf16[128,512]{1,0:T(8,128)(2,1)}, bf16[128,512]{1,0:T(8,128)(2,1)S(1)}, u32[]{:S(2)}, u32[]{:S(2)}) %collective-permute-start.5) | collective-permute-done | bytes 131104 | tf_op jit(solution)/shard_map/ppermute | solution.py:119
  26.4 0.0 copy-done.3
  26.4 0.0 copy-done.4
  26.4 0.0 copy-start
  26.4 1.0 %copy-done = bf16[128,2048]{1,0:T(8,128)(2,1)S(1)} copy-done((bf16[128,2048]{1,0:T(8,128)(2,1)S(1)}, bf16[128,2048]{1,0:T(8,128)(2,1)}, u32[]{:S(2)}) %copy-start) | copy-done | bytes 524312
  27.4 0.0 copy-start.1
  27.4 0.9 %copy-done.1 = bf16[128,512]{1,0:T(8,128)(2,1)S(1)} copy-done((bf16[128,512]{1,0:T(8,128)(2,1)S(1)}, bf16[128,512]{1,0:T(8,128)(2,1)}, u32[]{:S(2)}) %copy-start.1) | copy-done | bytes 131096
  28.3 0.0 copy-start.2
  28.3 0.9 %copy-done.2 = bf16[128,512]{1,0:T(8,128)(2,1)S(1)} copy-done((bf16[128,512]{1,0:T(8,128)(2,1)S(1)}, bf16[128,512]{1,0:T(8,128)(2,1)}, u32[]{:S(2)}) %copy-start.2) | copy-done | bytes 131096
  29.2 4.4 %shard_map.64 = f32[128,2048]{1,0:T(8,128)} custom-call(s32[2]{0:T(128)S(1)} %pad_add_fusion.place_ref, f32[16]{0:T(128)S(1)} %copy-done.4, bf16[128,2048]{1,0:T(8,128)(2,1)S(1)} %copy-done, f32[16,128]{1,0:T(8,128)S(1)} %bitcast.4, bf16[128,512]{1,0:T(8,128)(2,1)S(1)} %copy-done.1, bf16[128,512]{1,0:T(8,128)(2,1)S(1)} %collective-permute-done.refs_3_, ...), custom_call_target="tpu_custom_call" | custom-call | tf_op jit(solution)/shard_map/pallas_call | solution.py:124
Async XLA Ops:
  0.0 2.5 %copy-start.5 = (s32[128]{0:T(128)S(1)}, s32[128]{0:T(128)}, u32[]{:S(2)}) copy-start(s32[128]{0:T(128)} %param.9) | copy-start | bytes 1540
  0.0 20.3 %collective-permute-start.1 = (bf16[128,512]{1,0:T(8,128)(2,1)}, bf16[128,512]{1,0:T(8,128)(2,1)S(1)}, u32[]{:S(2)}, u32[]{:S(2)}) collective-permute-start(bf16[128,512]{1,0:T(8,128)(2,1)} %refs_2_.1), channel_id=1, source_target_pairs={{0,8},{4,12},{8,16},{12,20},{16,24},{20,28},{1,9},{5,13},{9,17},{1... | collective-permute-start | bytes 393224 | tf_op jit(solution)/shard_map/ppermute | solution.py:118
  2.5 12.9 %collective-permute-start.8 = (s32[1,128]{1,0:T(1,128)S(1)}, s32[1,128]{1,0:T(1,128)S(1)}, u32[]{:S(2)}, u32[]{:S(2)}) collective-permute-start(s32[1,128]{1,0:T(1,128)S(1)} %bitcast.5), channel_id=1, source_target_pairs={{0,12},{8,20},{16,28},{1,13},{9,21},{17,29},{2,14},{10,22},{18,30}... | collective-permute-start | bytes 1544 | tf_op jit(solution)/shard_map/ppermute | solution.py:120
  8.1 8.6 %collective-permute-start.7 = (s32[1,128]{1,0:T(1,128)S(1)}, s32[1,128]{1,0:T(1,128)S(1)}, u32[]{:S(2)}, u32[]{:S(2)}) collective-permute-start(s32[1,128]{1,0:T(1,128)S(1)} %bitcast.6), channel_id=1, source_target_pairs={{0,8},{4,12},{8,16},{12,20},{16,24},{20,28},{1,9},{5,13},{9,17},{1... | collective-permute-start | bytes 1544 | tf_op jit(solution)/shard_map/ppermute | solution.py:120
  9.9 8.1 %collective-permute-start.6 = (s32[1,128]{1,0:T(1,128)S(1)}, s32[1,128]{1,0:T(1,128)S(1)}, u32[]{:S(2)}, u32[]{:S(2)}) collective-permute-start(s32[1,128]{1,0:T(1,128)S(1)} %bitcast.7), channel_id=1, source_target_pairs={{0,4},{4,8},{8,12},{12,16},{16,20},{20,24},{24,28},{1,5},{5,9},{9,... | collective-permute-start | bytes 1544 | tf_op jit(solution)/shard_map/ppermute | solution.py:120
  11.7 10.2 %collective-permute-start = (bf16[128,512]{1,0:T(8,128)(2,1)}, bf16[128,512]{1,0:T(8,128)(2,1)S(1)}, u32[]{:S(2)}, u32[]{:S(2)}) collective-permute-start(bf16[128,512]{1,0:T(8,128)(2,1)} %refs_2_.1), channel_id=1, source_target_pairs={{0,4},{4,8},{8,12},{12,16},{16,20},{20,24},{24,28},{1,5},{5,9},{9,... | collective-permute-start | bytes 393224 | tf_op jit(solution)/shard_map/ppermute | solution.py:118
  15.4 6.6 %collective-permute-start.2 = (bf16[128,512]{1,0:T(8,128)(2,1)}, bf16[128,512]{1,0:T(8,128)(2,1)S(1)}, u32[]{:S(2)}, u32[]{:S(2)}) collective-permute-start(bf16[128,512]{1,0:T(8,128)(2,1)} %refs_2_.1), channel_id=1, source_target_pairs={{0,12},{8,20},{16,28},{1,13},{9,21},{17,29},{2,14},{10,22},{18,30}... | collective-permute-start | bytes 393224 | tf_op jit(solution)/shard_map/ppermute | solution.py:118
  16.7 5.3 %collective-permute-start.4 = (bf16[128,512]{1,0:T(8,128)(2,1)}, bf16[128,512]{1,0:T(8,128)(2,1)S(1)}, u32[]{:S(2)}, u32[]{:S(2)}) collective-permute-start(bf16[128,512]{1,0:T(8,128)(2,1)} %refs_6_.1), channel_id=1, source_target_pairs={{0,8},{4,12},{8,16},{12,20},{16,24},{20,28},{1,9},{5,13},{9,17},{1... | collective-permute-start | bytes 393224 | tf_op jit(solution)/shard_map/ppermute | solution.py:119
  18.0 6.5 %collective-permute-start.3 = (bf16[128,512]{1,0:T(8,128)(2,1)}, bf16[128,512]{1,0:T(8,128)(2,1)S(1)}, u32[]{:S(2)}, u32[]{:S(2)}) collective-permute-start(bf16[128,512]{1,0:T(8,128)(2,1)} %refs_6_.1), channel_id=1, source_target_pairs={{0,4},{4,8},{8,12},{12,16},{16,20},{20,24},{24,28},{1,5},{5,9},{9,... | collective-permute-start | bytes 393224 | tf_op jit(solution)/shard_map/ppermute | solution.py:119
  20.3 6.0 %collective-permute-start.5 = (bf16[128,512]{1,0:T(8,128)(2,1)}, bf16[128,512]{1,0:T(8,128)(2,1)S(1)}, u32[]{:S(2)}, u32[]{:S(2)}) collective-permute-start(bf16[128,512]{1,0:T(8,128)(2,1)} %refs_6_.1), channel_id=1, source_target_pairs={{0,12},{8,20},{16,28},{1,13},{9,21},{17,29},{2,14},{10,22},{18,30}... | collective-permute-start | bytes 393224 | tf_op jit(solution)/shard_map/ppermute | solution.py:119
  21.9 4.5 %copy-start.3 = (f32[2048]{0:T(1024)S(1)}, f32[2048]{0:T(1024)}, u32[]{:S(2)}) copy-start(f32[2048]{0:T(1024)} %param.11) | copy-start | bytes 24580
  22.0 4.4 %copy-start.4 = (f32[16]{0:T(128)S(1)}, f32[16]{0:T(128)}, u32[]{:S(2)}) copy-start(f32[16]{0:T(128)} %beta_ref.1) | copy-start | bytes 196
  26.4 1.0 %copy-start = (bf16[128,2048]{1,0:T(8,128)(2,1)S(1)}, bf16[128,2048]{1,0:T(8,128)(2,1)}, u32[]{:S(2)}) copy-start(bf16[128,2048]{1,0:T(8,128)(2,1)} %refs_0_.1) | copy-start | bytes 1572868
  27.4 0.9 %copy-start.1 = (bf16[128,512]{1,0:T(8,128)(2,1)S(1)}, bf16[128,512]{1,0:T(8,128)(2,1)}, u32[]{:S(2)}) copy-start(bf16[128,512]{1,0:T(8,128)(2,1)} %refs_2_.1) | copy-start | bytes 393220
  28.3 0.9 %copy-start.2 = (bf16[128,512]{1,0:T(8,128)(2,1)S(1)}, bf16[128,512]{1,0:T(8,128)(2,1)}, u32[]{:S(2)}) copy-start(bf16[128,512]{1,0:T(8,128)(2,1)} %refs_6_.1) | copy-start | bytes 393220

commit v2 on v0

--- a/solution.py
+++ b/solution.py
@@ -1,11 +1,214 @@
+import functools
+import math
+
 import jax
 import jax.numpy as jnp
 from jax import lax
+from jax.experimental import pallas as pl
+from jax.experimental.pallas import tpu as pltpu
 from jax.sharding import PartitionSpec as P
 
 HEADS = 16
 KV_HEADS = 4
 HEAD_DIM = 128
+GROUPS = HEADS // KV_HEADS
+LONGEST = 4
+SCALE = math.log2(math.e) / math.sqrt(HEAD_DIM)
+LOWEST = -1e30
+DOC_ROWS = 16
+
+NT = (((1,), (1,)), ((), ()))
+TN = (((0,), (0,)), ((), ()))
+
+
+def dot(a, b, dims):
+    return lax.dot_general(a, b, dims, preferred_element_type=jnp.float32)
+
+
+def column(row):
+    return jnp.transpose(jnp.broadcast_to(row, (HEAD_DIM, row.shape[1])))
+
+
+def group_cols(g):
+    return slice(g * HEAD_DIM, (g + 1) * HEAD_DIM)
+
+
+def head_cols(h):
+    return slice(h * HEAD_DIM, (h + 1) * HEAD_DIM)
+
+
+def group_queries(q_ref, g):
+    return jnp.concatenate([q_ref[:, head_cols(g * GROUPS + i)] for i in range(GROUPS)], axis=0)
+
+
+def pack_kernel(key_ref, value_ref, doc_ref, out_ref, doc_scratch, sems):
+    rows = key_ref.shape[0]
+    doc_copy = pltpu.make_async_copy(doc_ref, doc_scratch, sems.at[0])
+    key_copy = pltpu.make_async_copy(key_ref, out_ref.at[0:rows], sems.at[1])
+    value_copy = pltpu.make_async_copy(value_ref, out_ref.at[rows : 2 * rows], sems.at[2])
+    doc_copy.start()
+    key_copy.start()
+    value_copy.start()
+    doc_copy.wait()
+    docs = jnp.broadcast_to(doc_scratch[...].astype(jnp.float32), (DOC_ROWS, rows))
+    out_ref[2 * rows : 2 * rows + DOC_ROWS, 0:rows] = docs.astype(jnp.bfloat16)
+    key_copy.wait()
+    value_copy.wait()
+
+
+def payload_docs(ref, rows):
+    return ref[2 * rows : 2 * rows + DOC_ROWS, 0:rows].astype(jnp.float32)[0:1, :]
+
+
+def own_kernel(beta_ref, q_ref, own_ref, gain_ref, summed_ref, stats_ref, gain_out_ref):
+    rows = q_ref.shape[0]
+    docs = payload_docs(own_ref, rows)
+    place = lax.broadcasted_iota(jnp.int32, (rows, rows), 0)
+    row = lax.broadcasted_iota(jnp.int32, (rows, rows), 1)
+    allowed = (place <= row) & (column(docs) == docs)
+    bias = jnp.where(allowed, 0.0, LOWEST)
+    for g in range(KV_HEADS):
+        scores = dot(own_ref[0:rows, group_cols(g)], group_queries(q_ref, g), NT)
+        tops, totals, weights, rest = [], [], [], []
+        for i in range(GROUPS):
+            h = g * GROUPS + i
+            masked = scores[:, i * rows : (i + 1) * rows] * SCALE + bias
+            top = jnp.max(masked, axis=0, keepdims=True)
+            weight = jnp.exp2(masked - top)
+            tops.append(top)
+            totals.append(jnp.sum(weight, axis=0, keepdims=True))
+            weights.append(weight.astype(jnp.bfloat16))
+            share = 1.0 / (1.0 + jnp.exp(-jnp.full((1, HEAD_DIM), beta_ref[h], jnp.float32)))
+            rest.append(jnp.broadcast_to((1.0 - share)[:, 0:1], (1, rows)))
+            gain_out_ref[head_cols(h), :] = column(gain_ref[h : h + 1, :] * share)
+        summed_ref[group_cols(g), :] = dot(
+            own_ref[rows : 2 * rows, group_cols(g)], jnp.concatenate(weights, axis=1), TN
+        )
+        stats_ref[g : g + 1, :] = jnp.concatenate(tops, axis=1)
+        stats_ref[KV_HEADS + g : KV_HEADS + g + 1, :] = jnp.concatenate(totals, axis=1)
+        stats_ref[2 * KV_HEADS + g : 2 * KV_HEADS + g + 1, :] = jnp.concatenate(rest, axis=1)
+
+
+def join_kernel(
+    q_ref, own_ref, one_ref, two_ref, summed_ref, stats_ref, gain_ref, out_ref, held, sems
+):
+    rows = q_ref.shape[0]
+    part = lax.axis_index("kv")
+    own = payload_docs(own_ref, rows)
+    first = jnp.broadcast_to(own[:, 0:1], (1, rows))
+    reads = jnp.where(own == first, 1.0, 0.0)
+
+    def tail(ref):
+        others = jnp.where(payload_docs(ref, rows) == first, 0.0, 1.0)
+        count = jnp.sum(others, axis=1, keepdims=True)
+        place = lax.broadcasted_iota(jnp.int32, (rows, HEAD_DIM), 0).astype(jnp.float32)
+        return place >= count
+
+    tail_one, tail_two = tail(one_ref), tail(two_ref)
+    in_memory = tail_one & (part == 0)
+    row_bias = jnp.where((own == first) & (part == 1), 0.0, LOWEST)
+    bias = jnp.where(tail_one, row_bias, LOWEST)
+
+    copies = []
+    for g in range(KV_HEADS):
+        cols = group_cols(g)
+        q = group_queries(q_ref, g)
+        key_one, value_one = one_ref[0:rows, cols], one_ref[rows : 2 * rows, cols]
+        key_two, value_two = two_ref[0:rows, cols], two_ref[rows : 2 * rows, cols]
+        memory_keys = jnp.concatenate(
+            [
+                jnp.where(in_memory, key_one.astype(jnp.float32), 0.0).astype(jnp.bfloat16),
+                jnp.where(tail_two, key_two.astype(jnp.float32), 0.0).astype(jnp.bfloat16),
+            ],
+            axis=0,
+        )
+        state = dot(jnp.concatenate([value_one, value_two], axis=0), memory_keys, TN)
+        high = state.astype(jnp.bfloat16)
+        low = (state - high.astype(jnp.float32)).astype(jnp.bfloat16)
+        recalled = dot(high, q, NT) + dot(low, q, NT)
+        scores = dot(key_one, q, NT)
+        weights, factors, totals = [], [], []
+        for i in range(GROUPS):
+            cut = slice(i * rows, (i + 1) * rows)
+            masked = scores[:, cut] * SCALE + bias
+            top_own = stats_ref[g : g + 1, cut]
+            top = jnp.maximum(jnp.max(masked, axis=0, keepdims=True), top_own)
+            weight = jnp.exp2(masked - top)
+            factor = jnp.exp2(top_own - top)
+            total = stats_ref[KV_HEADS + g : KV_HEADS + g + 1, cut] * factor
+            totals.append(total + jnp.sum(weight, axis=0, keepdims=True))
+            factors.append(factor)
+            weights.append(weight.astype(jnp.bfloat16))
+        added = dot(value_one, jnp.concatenate(weights, axis=1), TN)
+        for i in range(GROUPS):
+            h = g * GROUPS + i
+            cut = slice(i * rows, (i + 1) * rows)
+            read = recalled[:, cut]
+            square = jnp.sum(read * read, axis=0, keepdims=True) * (1.0 / HEAD_DIM)
+            read = read * (lax.rsqrt(square + 1e-06) * reads)
+            summed = summed_ref[cols, cut] * factors[i] + added[:, cut]
+            rest = stats_ref[2 * KV_HEADS + g : 2 * KV_HEADS + g + 1, cut]
+            mixed = read * gain_ref[head_cols(h), :] + summed * (rest / totals[i])
+            held[:, head_cols(h)] = jnp.transpose(mixed)
+        wide = slice(g * GROUPS * HEAD_DIM, (g + 1) * GROUPS * HEAD_DIM)
+        copy = pltpu.make_async_copy(held.at[:, wide], out_ref.at[:, wide], sems.at[g])
+        copy.start()
+        copies.append(copy)
+    for copy in copies:
+        copy.wait()
+
+
+def near_device(n_seq, n_kv, queries, keys, values, doc_ids, beta, lin_gain):
+    rows = queries.shape[0]
+    devices = n_seq * n_kv
+    vmem = pl.BlockSpec(memory_space=pltpu.VMEM)
+    smem = pl.BlockSpec(memory_space=pltpu.SMEM)
+    hbm = pl.BlockSpec(memory_space=pltpu.HBM)
+    params = pltpu.CompilerParams(vmem_limit_bytes=32 * 1024 * 1024)
+    width = KV_HEADS * HEAD_DIM
+    deep = 2 * rows + DOC_ROWS
+    own = pl.pallas_call(
+        pack_kernel,
+        out_shape=jax.ShapeDtypeStruct((deep, width), jnp.bfloat16),
+        in_specs=[hbm] * 3,
+        out_specs=vmem,
+        scratch_shapes=[pltpu.VMEM((1, rows), jnp.int32), pltpu.SemaphoreType.DMA((3,))],
+        compiler_params=params,
+        cost_estimate=pl.CostEstimate(flops=0, bytes_accessed=4 * rows * width, transcendentals=0),
+    )(keys, values, doc_ids.reshape(1, rows))
+
+    def before(j):
+        pairs = [(b - j, b) for b in range(j, devices)]
+        return lax.ppermute(own, ("seq", "kv"), pairs)
+
+    one, two = before(1), before(2)
+    summed, stats, gains = pl.pallas_call(
+        own_kernel,
+        out_shape=[
+            jax.ShapeDtypeStruct((KV_HEADS * HEAD_DIM, GROUPS * rows), jnp.float32),
+            jax.ShapeDtypeStruct((4 * KV_HEADS, GROUPS * rows), jnp.float32),
+            jax.ShapeDtypeStruct((HEADS * HEAD_DIM, rows), jnp.float32),
+        ],
+        in_specs=[smem, vmem, vmem, vmem],
+        out_specs=[vmem] * 3,
+        compiler_params=params,
+        cost_estimate=pl.CostEstimate(
+            flops=4 * HEADS * HEAD_DIM * rows * rows,
+            bytes_accessed=4 * 1024 * 1024,
+            transcendentals=HEADS * rows * rows,
+        ),
+    )(beta, queries, own, lin_gain.reshape(HEADS, HEAD_DIM))
+    return pl.pallas_call(
+        join_kernel,
+        out_shape=jax.ShapeDtypeStruct((rows, HEADS * HEAD_DIM), jnp.float32),
+        in_specs=[vmem] * 7,
+        out_specs=hbm,
+        scratch_shapes=[
+            pltpu.VMEM((rows, HEADS * HEAD_DIM), jnp.float32),
+            pltpu.SemaphoreType.DMA((KV_HEADS,)),
+        ],
+        compiler_params=params,
+    )(queries, own, one, two, summed, stats, gains)
 
 
 def carried_in(part, axis, combine, identity):
@@ -81,7 +284,7 @@
     return (new_max, new_sum, new_accum)
 
 
-def on_device(queries, keys, values, doc_ids, beta, lin_gain):
+def far_device(queries, keys, values, doc_ids, beta, lin_gain):
     row_count = queries.shape[0]
     groups = HEADS // KV_HEADS
     query_heads = queries.reshape(row_count, KV_HEADS, groups, HEAD_DIM)
@@ -162,6 +365,7 @@
 
 
 def solution(mesh):
+    n_seq, n_kv = mesh.shape["seq"], mesh.shape["kv"]
     in_specs = (
         P(("dp", "seq", "kv"), None),
         P(("dp", "seq", "kv"), None),
@@ -171,6 +375,10 @@
         P(),
     )
     out_specs = P(("dp", "seq", "kv"), None)
+    if n_kv == 2 and n_seq * n_kv <= 2 * LONGEST:
+        on_device = functools.partial(near_device, n_seq, n_kv)
+    else:
+        on_device = far_device
     return jax.shard_map(
         on_device, mesh=mesh, in_specs=in_specs, out_specs=out_specs, check_vma=False
     )

time: 81.9 us -> 20.7 us (0.25)
  the two profiles are of different devices: /device:TPU:7 before, /device:TPU:1 now
where the time goes in v2:
time: 20.7 us; the launch traced here: 20.5 us
  starting transfers between devices  7.66 us (37%)
  waiting for transfers between devices  5.14 us (25%)
  Pallas kernels  5.06 us (24%)
  local copies, waits for them, and re-layouts  2.53 us (12%)
    ppermute x2, starting transfers between devices, before(): return lax.ppermute(own, ('seq', 'kv'), pairs)  7.66 us
    ppermute x2, waiting for transfers between devices, before(): return lax.ppermute(own, ('seq', 'kv'), pairs)  5.14 us
    pallas_call x1, Pallas kernels, near_device(): pl.pallas_call(join_kernel, out_shape=jax.ShapeDtypeStruct((rows, HEADS *...  2.98 us
    unnamed x12, local copies, waits for them, and re-layouts  2.53 us
    pallas_call x1, Pallas kernels, near_device(): pl.pallas_call(own_kernel, out_shape=[jax.ShapeDtypeStruct((KV_HEADS * HE...  1.72 us
  transfers between devices with their start and end apart: 2, of which 1 were waited for; matrix products, arithmetic and copies ran while one was open for 0% of the time, Pallas kernels for 8%

profile of v2, /device:TPU:1, one launch (start us, length us, event | category | flops | bytes accessed | tf_op | source)
XLA Modules:
  0.0 20.5 jit_solution(12829031171649651554)
XLA Ops:
  0.0 0.0 copy-start
  0.0 0.0 copy-start.1
  0.0 1.0 %copy-done.1 = bf16[128,512]{1,0:T(8,128)(2,1)S(1)} copy-done((bf16[128,512]{1,0:T(8,128)(2,1)S(1)}, bf16[128,512]{1,0:T(8,128)(2,1)}, u32[]{:S(2)}) %copy-start.1) | copy-done | bytes 131096
  1.0 0.0 copy-start.2
  1.0 0.9 %copy-done.2 = bf16[128,512]{1,0:T(8,128)(2,1)S(1)} copy-done((bf16[128,512]{1,0:T(8,128)(2,1)S(1)}, bf16[128,512]{1,0:T(8,128)(2,1)}, u32[]{:S(2)}) %copy-start.2) | copy-done | bytes 131096
  1.9 0.0 copy-start.4
  1.9 0.7 %copy-done.4 = s32[128]{0:T(128)S(1)} copy-done((s32[128]{0:T(128)S(1)}, s32[128]{0:T(128)}, u32[]{:S(2)}) %copy-start.4) | copy-done | bytes 536
  2.5 0.0 copy-start.3
  2.5 0.4 %shard_map.64.own_ref = bf16[272,512]{1,0:T(8,128)(2,1)S(1)} custom-call(bf16[128,512]{1,0:T(8,128)(2,1)S(1)} %copy-done.1, bf16[128,512]{1,0:T(8,128)(2,1)S(1)} %copy-done.2, s32[1,128]{1,0:T(1,128)S(1)} %bitcast.3), custom_call_target="tpu_custom_call" | custom-call | bytes 262144 | tf_op jit(solution)/shard_map/pallas_call | solution.py:170
  2.9 0.0 copy-start.5
  2.9 4.5 %collective-permute-start.1 = (bf16[272,512]{1,0:T(8,128)(2,1)S(1)}, bf16[272,512]{1,0:T(8,128)(2,1)S(1)}, u32[]{:S(2)}, u32[]{:S(2)}) collective-permute-start(bf16[272,512]{1,0:T(8,128)(2,1)S(1)} %shard_map.64.own_ref), channel_id=1, source_target_pairs={{0,8},{4,12},{8,16},{12,20},{16,24},{20,28},{1,9},{5,13},{9,17},{1... | collective-permute-start | bytes 835592 | tf_op jit(solution)/shard_map/ppermute | solution.py:182
  7.5 3.1 %collective-permute-start = (bf16[272,512]{1,0:T(8,128)(2,1)S(1)}, bf16[272,512]{1,0:T(8,128)(2,1)S(1)}, u32[]{:S(2)}, u32[]{:S(2)}) collective-permute-start(bf16[272,512]{1,0:T(8,128)(2,1)S(1)} %shard_map.64.own_ref), channel_id=1, source_target_pairs={{0,4},{4,8},{8,12},{12,16},{16,20},{20,24},{24,28},{1,5},{5,9},{9,... | collective-permute-start | bytes 835592 | tf_op jit(solution)/shard_map/ppermute | solution.py:182
  10.6 0.0 copy-done
  10.6 0.0 copy-done.3
  10.6 0.0 copy-done.5
  10.6 1.7 %shard_map.65 = (f32[512,512]{1,0:T(8,128)S(1)}, f32[16,512]{1,0:T(8,128)S(1)}, f32[2048,128]{1,0:T(8,128)S(1)}) custom-call(f32[16]{0:T(128)S(1)} %copy-done.5, bf16[128,2048]{1,0:T(8,128)(2,1)S(1)} %copy-done, bf16[272,512]{1,0:T(8,128)(2,1)S(1)} %shard_map.64.own_ref, f32[16,128]{1,0:T(8,128)S(1)} %bitcast.2), custom_call_target="tpu_custom_call" | custom-call | flops 134217728 | bytes 4194304 | tf_op jit(solution)/shard_map/pallas_call | solution.py:185
  12.3 0.0 collective-permute-done.1.two_ref
  12.3 5.1 %collective-permute-done.one_ref = bf16[272,512]{1,0:T(8,128)(2,1)S(1)} collective-permute-done((bf16[272,512]{1,0:T(8,128)(2,1)S(1)}, bf16[272,512]{1,0:T(8,128)(2,1)S(1)}, u32[]{:S(2)}, u32[]{:S(2)}) %collective-permute-start) | collective-permute-done | bytes 278560 | tf_op jit(solution)/shard_map/ppermute | solution.py:182
  17.5 3.0 %shard_map.66 = f32[128,2048]{1,0:T(8,128)} custom-call(bf16[128,2048]{1,0:T(8,128)(2,1)S(1)} %copy-done, bf16[272,512]{1,0:T(8,128)(2,1)S(1)} %shard_map.64.own_ref, bf16[272,512]{1,0:T(8,128)(2,1)S(1)} %collective-permute-done.one_ref, bf16[272,512]{1,0:T(8,128)(2,1)S(1)} %collective-permute-done.1.two_ref, f32[512,512]{1,0:T(8,128)S(1)} %get-tuple-element.8.summed_ref, ...), custom_call_target="tpu_custom_call" | custom-call | tf_op jit(solution)/shard_map/pallas_call | solution.py:201
Async XLA Ops:
  0.0 10.6 %copy-start = (bf16[128,2048]{1,0:T(8,128)(2,1)S(1)}, bf16[128,2048]{1,0:T(8,128)(2,1)}, u32[]{:S(2)}) copy-start(bf16[128,2048]{1,0:T(8,128)(2,1)} %q_ref.3) | copy-start | bytes 1572868
  0.0 1.0 %copy-start.1 = (bf16[128,512]{1,0:T(8,128)(2,1)S(1)}, bf16[128,512]{1,0:T(8,128)(2,1)}, u32[]{:S(2)}) copy-start(bf16[128,512]{1,0:T(8,128)(2,1)} %key_ref.1) | copy-start | bytes 393220
  1.0 0.9 %copy-start.2 = (bf16[128,512]{1,0:T(8,128)(2,1)S(1)}, bf16[128,512]{1,0:T(8,128)(2,1)}, u32[]{:S(2)}) copy-start(bf16[128,512]{1,0:T(8,128)(2,1)} %value_ref.1) | copy-start | bytes 393220
  1.9 0.7 %copy-start.4 = (s32[128]{0:T(128)S(1)}, s32[128]{0:T(128)}, u32[]{:S(2)}) copy-start(s32[128]{0:T(128)} %param.9) | copy-start | bytes 1540
  2.5 8.1 %copy-start.3 = (f32[2048]{0:T(1024)S(1)}, f32[2048]{0:T(1024)}, u32[]{:S(2)}) copy-start(f32[2048]{0:T(1024)} %param.11) | copy-start | bytes 24580
  2.9 7.7 %copy-start.5 = (f32[16]{0:T(128)S(1)}, f32[16]{0:T(128)}, u32[]{:S(2)}) copy-start(f32[16]{0:T(128)} %beta_ref.1) | copy-start | bytes 196
  2.9 9.4 %collective-permute-start.1 = (bf16[272,512]{1,0:T(8,128)(2,1)S(1)}, bf16[272,512]{1,0:T(8,128)(2,1)S(1)}, u32[]{:S(2)}, u32[]{:S(2)}) collective-permute-start(bf16[272,512]{1,0:T(8,128)(2,1)S(1)} %shard_map.64.own_ref), channel_id=1, source_target_pairs={{0,8},{4,12},{8,16},{12,20},{16,24},{20,28},{1,9},{5,13},{9,17},{1... | collective-permute-start | bytes 835592 | tf_op jit(solution)/shard_map/ppermute | solution.py:182
  7.5 10.0 %collective-permute-start = (bf16[272,512]{1,0:T(8,128)(2,1)S(1)}, bf16[272,512]{1,0:T(8,128)(2,1)S(1)}, u32[]{:S(2)}, u32[]{:S(2)}) collective-permute-start(bf16[272,512]{1,0:T(8,128)(2,1)S(1)} %shard_map.64.own_ref), channel_id=1, source_target_pairs={{0,4},{4,8},{8,12},{12,16},{16,20},{20,24},{24,28},{1,5},{5,9},{9,... | collective-permute-start | bytes 835592 | tf_op jit(solution)/shard_map/ppermute | solution.py:182

commit v3 on v0

--- a/solution.py
+++ b/solution.py
@@ -1,11 +1,300 @@
+import functools
+import math
+
 import jax
 import jax.numpy as jnp
 from jax import lax
+from jax.experimental import pallas as pl
+from jax.experimental.pallas import tpu as pltpu
 from jax.sharding import PartitionSpec as P
 
 HEADS = 16
 KV_HEADS = 4
 HEAD_DIM = 128
+GROUPS = HEADS // KV_HEADS
+LONGEST = 4
+SCALE = math.log2(math.e) / math.sqrt(HEAD_DIM)
+LOWEST = -1e30
+DOC_ROWS = 16
+
+NT = (((1,), (1,)), ((), ()))
+TN = (((0,), (0,)), ((), ()))
+
+
+def dot(a, b, dims):
+    return lax.dot_general(a, b, dims, preferred_element_type=jnp.float32)
+
+
+def column(row):
+    return jnp.transpose(jnp.broadcast_to(row, (HEAD_DIM, row.shape[1])))
+
+
+def part_of(i, size):
+    return slice(i * size, (i + 1) * size)
+
+
+def group_queries(q_ref, g):
+    heads = [q_ref[:, part_of(g * GROUPS + i, HEAD_DIM)] for i in range(GROUPS)]
+    return jnp.concatenate(heads, axis=0)
+
+
+def payload_keys(ref, g, rows):
+    return ref[part_of(g, rows), :]
+
+
+def payload_values(ref, g, rows):
+    return ref[part_of(KV_HEADS + g, rows), :]
+
+
+def payload_docs(ref, rows):
+    start = 2 * KV_HEADS * rows
+    return ref[start : start + DOC_ROWS, :].astype(jnp.float32)[0:1, :]
+
+
+def pack_kernel(key_ref, value_ref, doc_ref, out_ref, doc_scratch, doc_rows, sems):
+    rows = key_ref.shape[0]
+    doc_copy = pltpu.make_async_copy(doc_ref, doc_scratch, sems.at[2 * KV_HEADS])
+    doc_copy.start()
+    copies = []
+    for g in range(2 * KV_HEADS):
+        source = key_ref if g < KV_HEADS else value_ref
+        copy = pltpu.make_async_copy(
+            source.at[:, part_of(g % KV_HEADS, HEAD_DIM)],
+            out_ref.at[part_of(g, rows), :],
+            sems.at[g],
+        )
+        copy.start()
+        copies.append(copy)
+    doc_copy.wait()
+    docs = jnp.broadcast_to(doc_scratch[...].astype(jnp.float32), (DOC_ROWS, rows))
+    doc_rows[...] = docs.astype(jnp.bfloat16)
+    start = 2 * KV_HEADS * rows
+    doc_copy = pltpu.make_async_copy(
+        doc_rows, out_ref.at[start : start + DOC_ROWS, :], sems.at[2 * KV_HEADS + 1]
+    )
+    doc_copy.start()
+    for copy in copies:
+        copy.wait()
+    doc_copy.wait()
+
+
+def own_kernel(beta_ref, q_ref, own_ref, gain_ref, summed_ref, stats_ref, gain_out_ref):
+    rows = q_ref.shape[0]
+    docs = payload_docs(own_ref, rows)
+    place = lax.broadcasted_iota(jnp.int32, (rows, rows), 0)
+    row = lax.broadcasted_iota(jnp.int32, (rows, rows), 1)
+    allowed = (place <= row) & (column(docs) == docs)
+    bias = jnp.where(allowed, 0.0, LOWEST)
+    for g in range(KV_HEADS):
+        scores = dot(payload_keys(own_ref, g, rows), group_queries(q_ref, g), NT)
+        tops, totals, weights, rest = [], [], [], []
+        for i in range(GROUPS):
+            h = g * GROUPS + i
+            masked = scores[:, part_of(i, rows)] * SCALE + bias
+            top = jnp.max(masked, axis=0, keepdims=True)
+            weight = jnp.exp2(masked - top)
+            tops.append(top)
+            totals.append(jnp.sum(weight, axis=0, keepdims=True))
+            weights.append(weight.astype(jnp.bfloat16))
+            share = 1.0 / (1.0 + jnp.exp(-jnp.full((1, HEAD_DIM), beta_ref[h], jnp.float32)))
+            rest.append(jnp.broadcast_to((1.0 - share)[:, 0:1], (1, rows)))
+            gain_out_ref[part_of(h, HEAD_DIM), :] = column(gain_ref[h : h + 1, :] * share)
+        summed_ref[part_of(g, HEAD_DIM), :] = dot(
+            payload_values(own_ref, g, rows), jnp.concatenate(weights, axis=1), TN
+        )
+        stats_ref[g : g + 1, :] = jnp.concatenate(tops, axis=1)
+        stats_ref[KV_HEADS + g : KV_HEADS + g + 1, :] = jnp.concatenate(totals, axis=1)
+        stats_ref[2 * KV_HEADS + g : 2 * KV_HEADS + g + 1, :] = jnp.concatenate(rest, axis=1)
+
+
+def first_document(own_ref, rows):
+    own = payload_docs(own_ref, rows)
+    first = jnp.broadcast_to(own[:, 0:1], (1, rows))
+    return first, own == first
+
+
+def tail(ref, first, rows):
+    others = jnp.where(payload_docs(ref, rows) == first, 0.0, 1.0)
+    count = jnp.sum(others, axis=1, keepdims=True)
+    place = lax.broadcasted_iota(jnp.int32, (rows, HEAD_DIM), 0).astype(jnp.float32)
+    return place >= count
+
+
+def block_state(ref, live, g, rows):
+    keys = payload_keys(ref, g, rows).astype(jnp.float32)
+    keys = jnp.where(live, keys, 0.0).astype(jnp.bfloat16)
+    return dot(payload_values(ref, g, rows), keys, TN)
+
+
+def memory_read(state, q_ref, g, gain_ref, reads):
+    rows = q_ref.shape[0]
+    q = group_queries(q_ref, g)
+    high = state.astype(jnp.bfloat16)
+    low = (state - high.astype(jnp.float32)).astype(jnp.bfloat16)
+    recalled = dot(high, q, NT) + dot(low, q, NT)
+    heads = []
+    for i in range(GROUPS):
+        read = recalled[:, part_of(i, rows)]
+        square = jnp.sum(read * read, axis=0, keepdims=True) * (1.0 / HEAD_DIM)
+        read = read * (lax.rsqrt(square + 1e-06) * reads)
+        heads.append(read * gain_ref[part_of(g * GROUPS + i, HEAD_DIM), :])
+    return heads
+
+
+def middle_kernel(
+    q_ref, own_ref, two_ref, summed_ref, stats_ref, gain_ref, state_ref, ready_ref
+):
+    rows = q_ref.shape[0]
+    part = lax.axis_index("kv")
+    first, same = first_document(own_ref, rows)
+    reads = jnp.where(same, 1.0, 0.0)
+    live = tail(two_ref, first, rows)
+    for g in range(KV_HEADS):
+        state_ref[part_of(g, HEAD_DIM), :] = block_state(two_ref, live, g, rows)
+
+    @pl.when(part == 0)
+    def _():
+        for g in range(KV_HEADS):
+            rest = stats_ref[2 * KV_HEADS + g : 2 * KV_HEADS + g + 1, :]
+            scaled = rest / stats_ref[KV_HEADS + g : KV_HEADS + g + 1, :]
+            group = part_of(g, HEAD_DIM)
+            ready_ref[group, :] = summed_ref[group, :] * scaled
+
+    @pl.when(part == 1)
+    def _():
+        for g in range(KV_HEADS):
+            state = state_ref[part_of(g, HEAD_DIM), :]
+            heads = memory_read(state, q_ref, g, gain_ref, reads)
+            ready_ref[part_of(g, HEAD_DIM), :] = jnp.concatenate(heads, axis=1)
+
+
+def join_kernel(
+    q_ref, own_ref, one_ref, summed_ref, stats_ref, gain_ref, state_ref, ready_ref,
+    out_ref, held, sems,
+):
+    rows = q_ref.shape[0]
+    part = lax.axis_index("kv")
+    first, same = first_document(own_ref, rows)
+    live = tail(one_ref, first, rows)
+
+    def copy(g):
+        wide = part_of(g, GROUPS * HEAD_DIM)
+        return pltpu.make_async_copy(held.at[:, wide], out_ref.at[:, wide], sems.at[g])
+
+    @pl.when(part == 0)
+    def _():
+        reads = jnp.where(same, 1.0, 0.0)
+        for g in range(KV_HEADS):
+            state = state_ref[part_of(g, HEAD_DIM), :] + block_state(one_ref, live, g, rows)
+            heads = memory_read(state, q_ref, g, gain_ref, reads)
+            for i in range(GROUPS):
+                mixed = heads[i] + ready_ref[part_of(g, HEAD_DIM), part_of(i, rows)]
+                held[:, part_of(g * GROUPS + i, HEAD_DIM)] = jnp.transpose(mixed)
+            copy(g).start()
+
+    @pl.when(part == 1)
+    def _():
+        bias = jnp.where(live & same, 0.0, LOWEST)
+        for g in range(KV_HEADS):
+            scores = dot(payload_keys(one_ref, g, rows), group_queries(q_ref, g), NT)
+            weights, factors, scales = [], [], []
+            for i in range(GROUPS):
+                cut = part_of(i, rows)
+                masked = scores[:, cut] * SCALE + bias
+                top_own = stats_ref[g : g + 1, cut]
+                top = jnp.maximum(jnp.max(masked, axis=0, keepdims=True), top_own)
+                weight = jnp.exp2(masked - top)
+                factor = jnp.exp2(top_own - top)
+                total = stats_ref[KV_HEADS + g : KV_HEADS + g + 1, cut] * factor
+                total = total + jnp.sum(weight, axis=0, keepdims=True)
+                factors.append(factor)
+                scales.append(stats_ref[2 * KV_HEADS + g : 2 * KV_HEADS + g + 1, cut] / total)
+                weights.append(weight.astype(jnp.bfloat16))
+            added = dot(payload_values(one_ref, g, rows), jnp.concatenate(weights, axis=1), TN)
+            for i in range(GROUPS):
+                cut, group = part_of(i, rows), part_of(g, HEAD_DIM)
+                summed = summed_ref[group, cut] * factors[i] + added[:, cut]
+                mixed = ready_ref[group, cut] + summed * scales[i]
+                held[:, part_of(g * GROUPS + i, HEAD_DIM)] = jnp.transpose(mixed)
+            copy(g).start()
+
+    for g in range(KV_HEADS):
+        copy(g).wait()
+
+
+def near_device(n_seq, n_kv, queries, keys, values, doc_ids, beta, lin_gain):
+    rows = queries.shape[0]
+    devices = n_seq * n_kv
+    vmem = pl.BlockSpec(memory_space=pltpu.VMEM)
+    smem = pl.BlockSpec(memory_space=pltpu.SMEM)
+    hbm = pl.BlockSpec(memory_space=pltpu.HBM)
+    params = pltpu.CompilerParams(vmem_limit_bytes=32 * 1024 * 1024)
+    wide = GROUPS * rows
+    group_shape = jax.ShapeDtypeStruct((KV_HEADS * HEAD_DIM, wide), jnp.float32)
+    deep = 2 * KV_HEADS * rows + DOC_ROWS
+    own = pl.pallas_call(
+        pack_kernel,
+        out_shape=jax.ShapeDtypeStruct((deep, HEAD_DIM), jnp.bfloat16),
+        in_specs=[hbm] * 3,
+        out_specs=hbm,
+        scratch_shapes=[
+            pltpu.VMEM((1, rows), jnp.int32),
+            pltpu.VMEM((DOC_ROWS, rows), jnp.bfloat16),
+            pltpu.SemaphoreType.DMA((2 * KV_HEADS + 2,)),
+        ],
+        compiler_params=pltpu.CompilerParams(vmem_limit_bytes=60 * 1024 * 1024),
+        cost_estimate=pl.CostEstimate(
+            flops=0, bytes_accessed=4 * deep * HEAD_DIM, transcendentals=0
+        ),
+    )(keys, values, doc_ids.reshape(1, rows))
+
+    def before(j):
+        pairs = [(b - j, b) for b in range(j, devices)]
+        return lax.ppermute(own, ("seq", "kv"), pairs)
+
+    one, two = before(1), before(2)
+    summed, stats, gains = pl.pallas_call(
+        own_kernel,
+        out_shape=[
+            group_shape,
+            jax.ShapeDtypeStruct((4 * KV_HEADS, wide), jnp.float32),
+            jax.ShapeDtypeStruct((HEADS * HEAD_DIM, rows), jnp.float32),
+        ],
+        in_specs=[smem, vmem, vmem, vmem],
+        out_specs=[vmem] * 3,
+        compiler_params=params,
+        cost_estimate=pl.CostEstimate(
+            flops=4 * HEADS * HEAD_DIM * rows * rows,
+            bytes_accessed=4 * 1024 * 1024,
+            transcendentals=HEADS * rows * rows,
+        ),
+    )(beta, queries, own, lin_gain.reshape(HEADS, HEAD_DIM))
+    state, ready = pl.pallas_call(
+        middle_kernel,
+        out_shape=[
+            jax.ShapeDtypeStruct((KV_HEADS * HEAD_DIM, HEAD_DIM), jnp.float32),
+            group_shape,
+        ],
+        in_specs=[vmem] * 6,
+        out_specs=[vmem] * 2,
+        compiler_params=params,
+        cost_estimate=pl.CostEstimate(
+            flops=4 * HEADS * HEAD_DIM * HEAD_DIM * rows,
+            bytes_accessed=4 * 1024 * 1024,
+            transcendentals=0,
+        ),
+    )(queries, own, two, summed, stats, gains)
+    return pl.pallas_call(
+        join_kernel,
+        out_shape=jax.ShapeDtypeStruct((rows, HEADS * HEAD_DIM), jnp.float32),
+        in_specs=[vmem] * 8,
+        out_specs=hbm,
+        scratch_shapes=[
+            pltpu.VMEM((rows, HEADS * HEAD_DIM), jnp.float32),
+            pltpu.SemaphoreType.DMA((KV_HEADS,)),
+        ],
+        compiler_params=params,
+    )(queries, own, one, summed, stats, gains, state, ready)
 
 
 def carried_in(part, axis, combine, identity):
@@ -81,7 +370,7 @@
     return (new_max, new_sum, new_accum)
 
 
-def on_device(queries, keys, values, doc_ids, beta, lin_gain):
+def far_device(queries, keys, values, doc_ids, beta, lin_gain):
     row_count = queries.shape[0]
     groups = HEADS // KV_HEADS
     query_heads = queries.reshape(row_count, KV_HEADS, groups, HEAD_DIM)
@@ -162,6 +451,7 @@
 
 
 def solution(mesh):
+    n_seq, n_kv = mesh.shape["seq"], mesh.shape["kv"]
     in_specs = (
         P(("dp", "seq", "kv"), None),
         P(("dp", "seq", "kv"), None),
@@ -171,6 +461,10 @@
         P(),
     )
     out_specs = P(("dp", "seq", "kv"), None)
+    if n_kv == 2 and n_seq * n_kv <= 2 * LONGEST:
+        on_device = functools.partial(near_device, n_seq, n_kv)
+    else:
+        on_device = far_device
     return jax.shard_map(
         on_device, mesh=mesh, in_specs=in_specs, out_specs=out_specs, check_vma=False
     )

time: 81.9 us -> 25.9 us (0.32)
  the two profiles are of different devices: /device:TPU:7 before, /device:TPU:1 now
where the time goes in v3:
time: 25.9 us; the launch traced here: 25.7 us
  Pallas kernels  13.3 us (51%)
  starting transfers between devices  7.66 us (30%)
  waiting for transfers between devices  3.06 us (12%)
  local copies, waits for them, and re-layouts  1.64 us (6%)
    pallas_call x1, Pallas kernels, near_device(): pl.pallas_call(pack_kernel, out_shape=jax.ShapeDtypeStruct((deep, HEAD_DI...  9.13 us
    ppermute x2, starting transfers between devices, before(): return lax.ppermute(own, ('seq', 'kv'), pairs)  7.66 us
    ppermute x2, waiting for transfers between devices, before(): return lax.ppermute(own, ('seq', 'kv'), pairs)  3.06 us
    pallas_call x1, Pallas kernels, near_device(): pl.pallas_call(join_kernel, out_shape=jax.ShapeDtypeStruct((rows, HEADS *...  2.06 us
    pallas_call x1, Pallas kernels, near_device(): pl.pallas_call(own_kernel, out_shape=[group_shape, jax.ShapeDtypeStruct((...  1.72 us
    unnamed x10, local copies, waits for them, and re-layouts  1.64 us
  transfers between devices with their start and end apart: 2, of which 1 were waited for; matrix products, arithmetic and copies ran while one was open for 0% of the time, Pallas kernels for 8%

profile of v3, /device:TPU:1, one launch (start us, length us, event | category | flops | bytes accessed | tf_op | source)
XLA Modules:
  0.0 25.7 jit_solution(8288206276607495893)
XLA Ops:
  0.0 0.0 copy-start
  0.0 0.0 copy-start.3
  0.0 9.1 %shard_map.64.own_ref = bf16[1040,128]{1,0:T(8,128)(2,1)} custom-call(bf16[128,512]{1,0:T(8,128)(2,1)} %key_ref.1, bf16[128,512]{1,0:T(8,128)(2,1)} %value_ref.1, s32[1,128]{1,0:T(1,128)} %bitcast.3), custom_call_target="tpu_custom_call" | custom-call | bytes 532480 | tf_op jit(solution)/shard_map/pallas_call | solution.py:235
  9.1 4.5 %collective-permute-start.1 = (bf16[1040,128]{1,0:T(8,128)(2,1)}, bf16[1040,128]{1,0:T(8,128)(2,1)S(1)}, u32[]{:S(2)}, u32[]{:S(2)}) collective-permute-start(bf16[1040,128]{1,0:T(8,128)(2,1)} %shard_map.64.own_ref), channel_id=1, source_target_pairs={{0,8},{4,12},{8,16},{12,20},{16,24},{20,28},{1,9},{5,13},{9,17},{1... | collective-permute-start | bytes 798728 | tf_op jit(solution)/shard_map/ppermute | solution.py:253
  13.7 3.1 %collective-permute-start = (bf16[1040,128]{1,0:T(8,128)(2,1)}, bf16[1040,128]{1,0:T(8,128)(2,1)S(1)}, u32[]{:S(2)}, u32[]{:S(2)}) collective-permute-start(bf16[1040,128]{1,0:T(8,128)(2,1)} %shard_map.64.own_ref), channel_id=1, source_target_pairs={{0,4},{4,8},{8,12},{12,16},{16,20},{20,24},{24,28},{1,5},{5,9},{9,... | collective-permute-start | bytes 798728 | tf_op jit(solution)/shard_map/ppermute | solution.py:253
  16.8 0.0 copy-done
  16.8 0.0 copy-done.3
  16.8 0.0 copy-start.1
  16.8 1.0 %copy-done.1 = bf16[1040,128]{1,0:T(8,128)(2,1)S(1)} copy-done((bf16[1040,128]{1,0:T(8,128)(2,1)S(1)}, bf16[1040,128]{1,0:T(8,128)(2,1)}, u32[]{:S(2)}) %copy-start.1) | copy-done | bytes 266264
  17.8 0.0 copy-start.4
  17.8 0.7 %copy-done.4 = f32[16]{0:T(128)S(1)} copy-done((f32[16]{0:T(128)S(1)}, f32[16]{0:T(128)}, u32[]{:S(2)}) %copy-start.4) | copy-done | bytes 88
  18.5 0.0 copy-start.2
  18.5 1.7 %shard_map.65 = (f32[512,512]{1,0:T(8,128)S(1)}, f32[16,512]{1,0:T(8,128)S(1)}, f32[2048,128]{1,0:T(8,128)S(1)}) custom-call(f32[16]{0:T(128)S(1)} %copy-done.4, bf16[128,2048]{1,0:T(8,128)(2,1)S(1)} %copy-done, bf16[1040,128]{1,0:T(8,128)(2,1)S(1)} %copy-done.1, f32[16,128]{1,0:T(8,128)S(1)} %bitcast.2), custom_call_target="tpu_custom_call" | custom-call | flops 134217728 | bytes 4194304 | tf_op jit(solution)/shard_map/pallas_call | solution.py:256
  20.2 0.0 collective-permute-done.1.two_ref
  20.2 0.0 copy-done.2
  20.2 0.4 %shard_map.66 = (f32[512,128]{1,0:T(8,128)S(1)}, f32[512,512]{1,0:T(8,128)S(1)}) custom-call(bf16[128,2048]{1,0:T(8,128)(2,1)S(1)} %copy-done, bf16[1040,128]{1,0:T(8,128)(2,1)S(1)} %copy-done.2, bf16[1040,128]{1,0:T(8,128)(2,1)S(1)} %collective-permute-done.1.two_ref, f32[512,512]{1,0:T(8,128)S(1)} %get-tuple-element.10.summed_ref, ...), custom_call_target="tpu_custom_call" | custom-call | flops 134217728 | bytes 4194304 | tf_op jit(solution)/shard_map/pallas_call | solution.py:272
  20.6 3.1 %collective-permute-done.one_ref = bf16[1040,128]{1,0:T(8,128)(2,1)S(1)} collective-permute-done((bf16[1040,128]{1,0:T(8,128)(2,1)}, bf16[1040,128]{1,0:T(8,128)(2,1)S(1)}, u32[]{:S(2)}, u32[]{:S(2)}) %collective-permute-start) | collective-permute-done | bytes 266272 | tf_op jit(solution)/shard_map/ppermute | solution.py:253
  23.7 2.1 %shard_map.67 = f32[128,2048]{1,0:T(8,128)} custom-call(bf16[128,2048]{1,0:T(8,128)(2,1)S(1)} %copy-done, bf16[1040,128]{1,0:T(8,128)(2,1)S(1)} %copy-done.2, bf16[1040,128]{1,0:T(8,128)(2,1)S(1)} %collective-permute-done.one_ref, f32[512,512]{1,0:T(8,128)S(1)} %get-tuple-element.10.summed_ref, f32[16,512]{1,0:T(8,128)S(1)} %get-tuple-element.11.stats_ref, ...), custom_call_target="tpu_custom_call" | custom-call | tf_op jit(solution)/shard_map/pallas_call | solution.py:287
Async XLA Ops:
  0.0 16.8 %copy-start = (bf16[128,2048]{1,0:T(8,128)(2,1)S(1)}, bf16[128,2048]{1,0:T(8,128)(2,1)}, u32[]{:S(2)}) copy-start(bf16[128,2048]{1,0:T(8,128)(2,1)} %q_ref.5) | copy-start | bytes 1572868
  0.0 16.8 %copy-start.3 = (f32[2048]{0:T(1024)S(1)}, f32[2048]{0:T(1024)}, u32[]{:S(2)}) copy-start(f32[2048]{0:T(1024)} %param.11) | copy-start | bytes 24580
  9.1 11.1 %collective-permute-start.1 = (bf16[1040,128]{1,0:T(8,128)(2,1)}, bf16[1040,128]{1,0:T(8,128)(2,1)S(1)}, u32[]{:S(2)}, u32[]{:S(2)}) collective-permute-start(bf16[1040,128]{1,0:T(8,128)(2,1)} %shard_map.64.own_ref), channel_id=1, source_target_pairs={{0,8},{4,12},{8,16},{12,20},{16,24},{20,28},{1,9},{5,13},{9,17},{1... | collective-permute-start | bytes 798728 | tf_op jit(solution)/shard_map/ppermute | solution.py:253
  13.7 10.0 %collective-permute-start = (bf16[1040,128]{1,0:T(8,128)(2,1)}, bf16[1040,128]{1,0:T(8,128)(2,1)S(1)}, u32[]{:S(2)}, u32[]{:S(2)}) collective-permute-start(bf16[1040,128]{1,0:T(8,128)(2,1)} %shard_map.64.own_ref), channel_id=1, source_target_pairs={{0,4},{4,8},{8,12},{12,16},{16,20},{20,24},{24,28},{1,5},{5,9},{9,... | collective-permute-start | bytes 798728 | tf_op jit(solution)/shard_map/ppermute | solution.py:253
  16.8 1.0 %copy-start.1 = (bf16[1040,128]{1,0:T(8,128)(2,1)S(1)}, bf16[1040,128]{1,0:T(8,128)(2,1)}, u32[]{:S(2)}) copy-start(bf16[1040,128]{1,0:T(8,128)(2,1)} %shard_map.64.own_ref) | copy-start | bytes 798724
  17.8 0.7 %copy-start.4 = (f32[16]{0:T(128)S(1)}, f32[16]{0:T(128)}, u32[]{:S(2)}) copy-start(f32[16]{0:T(128)} %beta_ref.1) | copy-start | bytes 196
  18.5 1.7 %copy-start.2 = (bf16[1040,128]{1,0:T(8,128)(2,1)S(1)}, bf16[1040,128]{1,0:T(8,128)(2,1)}, u32[]{:S(2)}) copy-start(bf16[1040,128]{1,0:T(8,128)(2,1)} %shard_map.64.own_ref) | copy-start | bytes 798724

commit v4 on v3

--- a/solution.py
+++ b/solution.py
@@ -51,7 +51,7 @@
     return ref[start : start + DOC_ROWS, :].astype(jnp.float32)[0:1, :]
 
 
-def pack_kernel(key_ref, value_ref, doc_ref, out_ref, doc_scratch, doc_rows, sems):
+def pack_kernel(key_ref, value_ref, doc_ref, out_ref, doc_scratch, sems):
     rows = key_ref.shape[0]
     doc_copy = pltpu.make_async_copy(doc_ref, doc_scratch, sems.at[2 * KV_HEADS])
     doc_copy.start()
@@ -67,15 +67,10 @@
         copies.append(copy)
     doc_copy.wait()
     docs = jnp.broadcast_to(doc_scratch[...].astype(jnp.float32), (DOC_ROWS, rows))
-    doc_rows[...] = docs.astype(jnp.bfloat16)
     start = 2 * KV_HEADS * rows
-    doc_copy = pltpu.make_async_copy(
-        doc_rows, out_ref.at[start : start + DOC_ROWS, :], sems.at[2 * KV_HEADS + 1]
-    )
-    doc_copy.start()
+    out_ref[start : start + DOC_ROWS, :] = docs.astype(jnp.bfloat16)
     for copy in copies:
         copy.wait()
-    doc_copy.wait()
 
 
 def own_kernel(beta_ref, q_ref, own_ref, gain_ref, summed_ref, stats_ref, gain_out_ref):
@@ -228,6 +223,7 @@
     vmem = pl.BlockSpec(memory_space=pltpu.VMEM)
     smem = pl.BlockSpec(memory_space=pltpu.SMEM)
     hbm = pl.BlockSpec(memory_space=pltpu.HBM)
+    in_hbm = functools.partial(pltpu.with_memory_space_constraint, memory_space=pltpu.HBM)
     params = pltpu.CompilerParams(vmem_limit_bytes=32 * 1024 * 1024)
     wide = GROUPS * rows
     group_shape = jax.ShapeDtypeStruct((KV_HEADS * HEAD_DIM, wide), jnp.float32)
@@ -236,17 +232,16 @@
         pack_kernel,
         out_shape=jax.ShapeDtypeStruct((deep, HEAD_DIM), jnp.bfloat16),
         in_specs=[hbm] * 3,
-        out_specs=hbm,
+        out_specs=vmem,
         scratch_shapes=[
             pltpu.VMEM((1, rows), jnp.int32),
-            pltpu.VMEM((DOC_ROWS, rows), jnp.bfloat16),
-            pltpu.SemaphoreType.DMA((2 * KV_HEADS + 2,)),
+            pltpu.SemaphoreType.DMA((2 * KV_HEADS + 1,)),
         ],
-        compiler_params=pltpu.CompilerParams(vmem_limit_bytes=60 * 1024 * 1024),
+        compiler_params=params,
         cost_estimate=pl.CostEstimate(
             flops=0, bytes_accessed=4 * deep * HEAD_DIM, transcendentals=0
         ),
-    )(keys, values, doc_ids.reshape(1, rows))
+    )(in_hbm(keys), in_hbm(values), in_hbm(doc_ids.reshape(1, rows)))
 
     def before(j):
         pairs = [(b - j, b) for b in range(j, devices)]

time: 25.9 us -> 17.6 us (0.68)
  Pallas kernels: 13.3 us -> 5.24 us
  local copies, waits for them, and re-layouts: 1.64 us -> 0.66 us
  waiting for transfers between devices: 3.06 us -> 3.83 us
    pallas_call x1, Pallas kernels: 9.13 us -> 1.03 us  [near_device(): pl.pallas_call(pack_kernel, out_shape=jax.ShapeDtypeStruct((deep, HEAD_DI...]
    unnamed x10 -> x6, local copies, waits for them, and re-layouts: 1.64 us -> 0.66 us
    ppermute x2, waiting for transfers between devices: 3.06 us -> 3.83 us  [before(): return lax.ppermute(own, ('seq', 'kv'), pairs)]
  transfers between devices with their start and end apart: 2 -> 2, of which waited for: 1 -> 1; matrix products, arithmetic and copies ran while one was open for 0% -> 0% of each run, Pallas kernels for 8% -> 12%
where the time goes in v4:
time: 17.6 us; the launch traced here: 17.5 us
  starting transfers between devices  7.66 us (44%)
  Pallas kernels  5.24 us (30%)
  waiting for transfers between devices  3.83 us (22%)
  local copies, waits for them, and re-layouts  0.66 us (4%)
    ppermute x2, starting transfers between devices, before(): return lax.ppermute(own, ('seq', 'kv'), pairs)  7.66 us
    ppermute x2, waiting for transfers between devices, before(): return lax.ppermute(own, ('seq', 'kv'), pairs)  3.83 us
    pallas_call x1, Pallas kernels, near_device(): pl.pallas_call(join_kernel, out_shape=jax.ShapeDtypeStruct((rows, HEADS *...  2.1 us
    pallas_call x1, Pallas kernels, near_device(): pl.pallas_call(own_kernel, out_shape=[group_shape, jax.ShapeDtypeStruct((...  1.72 us
    pallas_call x1, Pallas kernels, near_device(): pl.pallas_call(pack_kernel, out_shape=jax.ShapeDtypeStruct((deep, HEAD_DI...  1.03 us
    unnamed x6, local copies, waits for them, and re-layouts  0.66 us
    pallas_call x1, Pallas kernels, near_device(): pl.pallas_call(middle_kernel, out_shape=[jax.ShapeDtypeStruct((KV_HEADS *...  0.39 us
  transfers between devices with their start and end apart: 2, of which 1 were waited for; matrix products, arithmetic and copies ran while one was open for 0% of the time, Pallas kernels for 12%

profile of v4, /device:TPU:1, one launch (start us, length us, event | category | flops | bytes accessed | tf_op | source)
XLA Modules:
  0.0 17.5 jit_solution(45651847455572721)
XLA Ops:
  0.0 0.0 copy-start
  0.0 0.0 copy-start.1
  0.0 1.0 %shard_map.64.own_ref = bf16[1040,128]{1,0:T(8,128)(2,1)S(1)} custom-call(bf16[128,512]{1,0:T(8,128)(2,1)} %key_ref.1, bf16[128,512]{1,0:T(8,128)(2,1)} %value_ref.1, s32[1,128]{1,0:T(1,128)} %bitcast.3), custom_call_target="tpu_custom_call" | custom-call | bytes 532480 | tf_op jit(solution)/shard_map/pallas_call | solution.py:231
  1.0 4.5 %collective-permute-start.1 = (bf16[1040,128]{1,0:T(8,128)(2,1)S(1)}, bf16[1040,128]{1,0:T(8,128)(2,1)S(1)}, u32[]{:S(2)}, u32[]{:S(2)}) collective-permute-start(bf16[1040,128]{1,0:T(8,128)(2,1)S(1)} %shard_map.64.own_ref), channel_id=1, source_target_pairs={{0,8},{4,12},{8,16},{12,20},{16,24},{20,28},{1,9},{5,13},{9,17},{1... | collective-permute-start | bytes 798728 | tf_op jit(solution)/shard_map/ppermute | solution.py:248
  5.6 3.1 %collective-permute-start = (bf16[1040,128]{1,0:T(8,128)(2,1)S(1)}, bf16[1040,128]{1,0:T(8,128)(2,1)S(1)}, u32[]{:S(2)}, u32[]{:S(2)}) collective-permute-start(bf16[1040,128]{1,0:T(8,128)(2,1)S(1)} %shard_map.64.own_ref), channel_id=1, source_target_pairs={{0,4},{4,8},{8,12},{12,16},{16,20},{20,24},{24,28},{1,5},{5,9},{9,... | collective-permute-start | bytes 798728 | tf_op jit(solution)/shard_map/ppermute | solution.py:248
  8.7 0.0 copy-done
  8.7 0.0 copy-done.1
  8.7 0.0 copy-start.2
  8.7 0.6 %copy-done.2 = f32[16]{0:T(128)S(1)} copy-done((f32[16]{0:T(128)S(1)}, f32[16]{0:T(128)}, u32[]{:S(2)}) %copy-start.2) | copy-done | bytes 88
  9.4 1.7 %shard_map.65 = (f32[512,512]{1,0:T(8,128)S(1)}, f32[16,512]{1,0:T(8,128)S(1)}, f32[2048,128]{1,0:T(8,128)S(1)}) custom-call(f32[16]{0:T(128)S(1)} %copy-done.2, bf16[128,2048]{1,0:T(8,128)(2,1)S(1)} %copy-done, bf16[1040,128]{1,0:T(8,128)(2,1)S(1)} %shard_map.64.own_ref, f32[16,128]{1,0:T(8,128)S(1)} %bitcast.2), custom_call_target="tpu_custom_call" | custom-call | flops 134217728 | bytes 4194304 | tf_op jit(solution)/shard_map/pallas_call | solution.py:251
  11.1 0.0 collective-permute-done.1.two_ref
  11.1 0.4 %shard_map.66 = (f32[512,128]{1,0:T(8,128)S(1)}, f32[512,512]{1,0:T(8,128)S(1)}) custom-call(bf16[128,2048]{1,0:T(8,128)(2,1)S(1)} %copy-done, bf16[1040,128]{1,0:T(8,128)(2,1)S(1)} %shard_map.64.own_ref, bf16[1040,128]{1,0:T(8,128)(2,1)S(1)} %collective-permute-done.1.two_ref, f32[512,512]{1,0:T(8,128)S(1)} %get-tuple-element.10.summed_ref, ...), custom_call_target="tpu_custom_call" | custom-call | flops 134217728 | bytes 4194304 | tf_op jit(solution)/shard_map/pallas_call | solution.py:267
  11.5 3.8 %collective-permute-done.one_ref = bf16[1040,128]{1,0:T(8,128)(2,1)S(1)} collective-permute-done((bf16[1040,128]{1,0:T(8,128)(2,1)S(1)}, bf16[1040,128]{1,0:T(8,128)(2,1)S(1)}, u32[]{:S(2)}, u32[]{:S(2)}) %collective-permute-start) | collective-permute-done | bytes 266272 | tf_op jit(solution)/shard_map/ppermute | solution.py:248
  15.4 2.1 %shard_map.67 = f32[128,2048]{1,0:T(8,128)} custom-call(bf16[128,2048]{1,0:T(8,128)(2,1)S(1)} %copy-done, bf16[1040,128]{1,0:T(8,128)(2,1)S(1)} %shard_map.64.own_ref, bf16[1040,128]{1,0:T(8,128)(2,1)S(1)} %collective-permute-done.one_ref, f32[512,512]{1,0:T(8,128)S(1)} %get-tuple-element.10.summed_ref, f32[16,512]{1,0:T(8,128)S(1)} %get-tuple-element.11.stats_ref, ...), custom_call_target="tpu_custom_call" | custom-call | tf_op jit(solution)/shard_map/pallas_call | solution.py:282
Async XLA Ops:
  0.0 8.7 %copy-start = (bf16[128,2048]{1,0:T(8,128)(2,1)S(1)}, bf16[128,2048]{1,0:T(8,128)(2,1)}, u32[]{:S(2)}) copy-start(bf16[128,2048]{1,0:T(8,128)(2,1)} %q_ref.5) | copy-start | bytes 1572868
  0.0 8.7 %copy-start.1 = (f32[2048]{0:T(1024)S(1)}, f32[2048]{0:T(1024)}, u32[]{:S(2)}) copy-start(f32[2048]{0:T(1024)} %param.11) | copy-start | bytes 24580
  1.0 10.1 %collective-permute-start.1 = (bf16[1040,128]{1,0:T(8,128)(2,1)S(1)}, bf16[1040,128]{1,0:T(8,128)(2,1)S(1)}, u32[]{:S(2)}, u32[]{:S(2)}) collective-permute-start(bf16[1040,128]{1,0:T(8,128)(2,1)S(1)} %shard_map.64.own_ref), channel_id=1, source_target_pairs={{0,8},{4,12},{8,16},{12,20},{16,24},{20,28},{1,9},{5,13},{9,17},{1... | collective-permute-start | bytes 798728 | tf_op jit(solution)/shard_map/ppermute | solution.py:248
  5.6 9.8 %collective-permute-start = (bf16[1040,128]{1,0:T(8,128)(2,1)S(1)}, bf16[1040,128]{1,0:T(8,128)(2,1)S(1)}, u32[]{:S(2)}, u32[]{:S(2)}) collective-permute-start(bf16[1040,128]{1,0:T(8,128)(2,1)S(1)} %shard_map.64.own_ref), channel_id=1, source_target_pairs={{0,4},{4,8},{8,12},{12,16},{16,20},{20,24},{24,28},{1,5},{5,9},{9,... | collective-permute-start | bytes 798728 | tf_op jit(solution)/shard_map/ppermute | solution.py:248
  8.7 0.7 %copy-start.2 = (f32[16]{0:T(128)S(1)}, f32[16]{0:T(128)}, u32[]{:S(2)}) copy-start(f32[16]{0:T(128)} %beta_ref.1) | copy-start | bytes 196

commit v5 on v4

--- a/solution.py
+++ b/solution.py
@@ -51,24 +51,27 @@
     return ref[start : start + DOC_ROWS, :].astype(jnp.float32)[0:1, :]
 
 
-def pack_kernel(key_ref, value_ref, doc_ref, out_ref, doc_scratch, sems):
+def pack_kernel(key_ref, value_ref, doc_ref, next_ref, own_ref, doc_scratch, sems):
     rows = key_ref.shape[0]
-    doc_copy = pltpu.make_async_copy(doc_ref, doc_scratch, sems.at[2 * KV_HEADS])
+    doc_copy = pltpu.make_async_copy(doc_ref, doc_scratch, sems.at[0])
     doc_copy.start()
     copies = []
-    for g in range(2 * KV_HEADS):
-        source = key_ref if g < KV_HEADS else value_ref
-        copy = pltpu.make_async_copy(
-            source.at[:, part_of(g % KV_HEADS, HEAD_DIM)],
-            out_ref.at[part_of(g, rows), :],
-            sems.at[g],
-        )
-        copy.start()
-        copies.append(copy)
+    for out_ref in (next_ref, own_ref):
+        for g in range(2 * KV_HEADS):
+            source = key_ref if g < KV_HEADS else value_ref
+            copy = pltpu.make_async_copy(
+                source.at[:, part_of(g % KV_HEADS, HEAD_DIM)],
+                out_ref.at[part_of(g, rows), :],
+                sems.at[1 + len(copies)],
+            )
+            copy.start()
+            copies.append(copy)
     doc_copy.wait()
-    docs = jnp.broadcast_to(doc_scratch[...].astype(jnp.float32), (DOC_ROWS, rows))
     start = 2 * KV_HEADS * rows
-    out_ref[start : start + DOC_ROWS, :] = docs.astype(jnp.bfloat16)
+    for out_ref in (next_ref, own_ref):
+        count = out_ref.shape[0] - start
+        docs = jnp.broadcast_to(doc_scratch[...].astype(jnp.float32), (count, rows))
+        out_ref[start:, :] = docs.astype(jnp.bfloat16)
     for copy in copies:
         copy.wait()
 
@@ -228,14 +231,17 @@
     wide = GROUPS * rows
     group_shape = jax.ShapeDtypeStruct((KV_HEADS * HEAD_DIM, wide), jnp.float32)
     deep = 2 * KV_HEADS * rows + DOC_ROWS
-    own = pl.pallas_call(
+    ahead, own = pl.pallas_call(
         pack_kernel,
-        out_shape=jax.ShapeDtypeStruct((deep, HEAD_DIM), jnp.bfloat16),
+        out_shape=[
+            jax.ShapeDtypeStruct((deep + DOC_ROWS, HEAD_DIM), jnp.bfloat16),
+            jax.ShapeDtypeStruct((deep, HEAD_DIM), jnp.bfloat16),
+        ],
         in_specs=[hbm] * 3,
-        out_specs=vmem,
+        out_specs=[vmem] * 2,
         scratch_shapes=[
             pltpu.VMEM((1, rows), jnp.int32),
-            pltpu.SemaphoreType.DMA((2 * KV_HEADS + 1,)),
+            pltpu.SemaphoreType.DMA((4 * KV_HEADS + 1,)),
         ],
         compiler_params=params,
         cost_estimate=pl.CostEstimate(
@@ -243,11 +249,11 @@
         ),
     )(in_hbm(keys), in_hbm(values), in_hbm(doc_ids.reshape(1, rows)))
 
-    def before(j):
+    def before(j, payload):
         pairs = [(b - j, b) for b in range(j, devices)]
-        return lax.ppermute(own, ("seq", "kv"), pairs)
-
-    one, two = before(1), before(2)
+        return lax.ppermute(payload, ("seq", "kv"), pairs)
+
+    one, two = before(1, ahead), before(2, own)
     summed, stats, gains = pl.pallas_call(
         own_kernel,
         out_shape=[
@@ -273,11 +279,6 @@
         in_specs=[vmem] * 6,
         out_specs=[vmem] * 2,
         compiler_params=params,
-        cost_estimate=pl.CostEstimate(
-            flops=4 * HEADS * HEAD_DIM * HEAD_DIM * rows,
-            bytes_accessed=4 * 1024 * 1024,
-            transcendentals=0,
-        ),
     )(queries, own, two, summed, stats, gains)
     return pl.pallas_call(
         join_kernel,

time: 17.6 us -> 16.9 us (0.960)
  waiting for transfers between devices: 3.83 us -> 2.17 us
  local copies, waits for them, and re-layouts: 0.66 us -> 1.05 us
  starting transfers between devices: 7.66 us -> 7.94 us
    ppermute x2, waiting for transfers between devices: 3.83 us -> 2.17 us  [before(): return lax.ppermute(payload, ('seq', 'kv'), pairs)]
    unnamed x6 -> x8, local copies, waits for them, and re-layouts: 0.66 us -> 1.05 us
    ppermute x2, starting transfers between devices: 7.66 us -> 7.94 us  [before(): return lax.ppermute(payload, ('seq', 'kv'), pairs)]
  transfers between devices with their start and end apart: 2 -> 2, of which waited for: 1 -> 1; matrix products, arithmetic and copies ran while one was open for 0% -> 0% of each run, Pallas kernels for 12% -> 13%
where the time goes in v5:
time: 16.9 us; the launch traced here: 16.7 us
  starting transfers between devices  7.94 us (47%)
  Pallas kernels  5.41 us (32%)
  waiting for transfers between devices  2.17 us (13%)
  local copies, waits for them, and re-layouts  1.05 us (6%)
    ppermute x2, starting transfers between devices, before(): return lax.ppermute(payload, ('seq', 'kv'), pairs)  7.94 us
    ppermute x2, waiting for transfers between devices, before(): return lax.ppermute(payload, ('seq', 'kv'), pairs)  2.17 us
    pallas_call x1, Pallas kernels, near_device(): pl.pallas_call(join_kernel, out_shape=jax.ShapeDtypeStruct((rows, HEADS *...  2.12 us
    pallas_call x1, Pallas kernels, near_device(): pl.pallas_call(own_kernel, out_shape=[group_shape, jax.ShapeDtypeStruct((...  1.73 us
    pallas_call x1, Pallas kernels, near_device(): pl.pallas_call(pack_kernel, out_shape=[jax.ShapeDtypeStruct((deep + DOC_R...  1.18 us
    unnamed x8, local copies, waits for them, and re-layouts  1.05 us
    pallas_call x1, Pallas kernels, near_device(): pl.pallas_call(middle_kernel, out_shape=[jax.ShapeDtypeStruct((KV_HEADS *...  0.38 us
  transfers between devices with their start and end apart: 2, of which 1 were waited for; matrix products, arithmetic and copies ran while one was open for 0% of the time, Pallas kernels for 13%

profile of v5, /device:TPU:1, one launch (start us, length us, event | category | flops | bytes accessed | tf_op | source)
XLA Modules:
  0.0 16.7 jit_solution(8477857816844783213)
XLA Ops:
  0.0 0.0 copy-start.2
  0.0 1.2 %shard_map.64 = (bf16[1056,128]{1,0:T(8,128)(2,1)S(1)}, bf16[1040,128]{1,0:T(8,128)(2,1)S(1)}) custom-call(bf16[128,512]{1,0:T(8,128)(2,1)} %key_ref.1, bf16[128,512]{1,0:T(8,128)(2,1)} %value_ref.1, s32[1,128]{1,0:T(1,128)} %bitcast.3), custom_call_target="tpu_custom_call" | custom-call | bytes 532480 | tf_op jit(solution)/shard_map/pallas_call | solution.py:234
  1.2 3.9 %collective-permute-start = (bf16[1056,128]{1,0:T(8,128)(2,1)S(1)}, bf16[1056,128]{1,0:T(8,128)(2,1)S(1)}, u32[]{:S(2)}, u32[]{:S(2)}) collective-permute-start(bf16[1056,128]{1,0:T(8,128)(2,1)S(1)} %get-tuple-element.13), channel_id=1, source_target_pairs={{0,4},{4,8},{8,12},{12,16},{16,20},{20,24},{24,28},{1,5},{5,9},{9,... | collective-permute-start | bytes 811016 | tf_op jit(solution)/shard_map/ppermute | solution.py:254
  5.2 0.0 copy-start.3
  5.2 4.0 %collective-permute-start.1 = (bf16[1040,128]{1,0:T(8,128)(2,1)S(1)}, bf16[1040,128]{1,0:T(8,128)(2,1)S(1)}, u32[]{:S(2)}, u32[]{:S(2)}) collective-permute-start(bf16[1040,128]{1,0:T(8,128)(2,1)S(1)} %get-tuple-element.12.own_ref), channel_id=1, source_target_pairs={{0,8},{4,12},{8,16},{12,20},{16,24},{20,28},{1,9},{5,13},{9,17},{1... | collective-permute-start | bytes 798728 | tf_op jit(solution)/shard_map/ppermute | solution.py:254
  9.2 0.0 copy-done.2
  9.2 0.0 copy-done.3
  9.2 0.0 copy-start
  9.2 1.0 %copy-done = bf16[128,2048]{1,0:T(8,128)(2,1)S(1)} copy-done((bf16[128,2048]{1,0:T(8,128)(2,1)S(1)}, bf16[128,2048]{1,0:T(8,128)(2,1)}, u32[]{:S(2)}) %copy-start) | copy-done | bytes 524312
  10.2 0.0 copy-start.1
  10.2 1.7 %shard_map.65 = (f32[512,512]{1,0:T(8,128)S(1)}, f32[16,512]{1,0:T(8,128)S(1)}, f32[2048,128]{1,0:T(8,128)S(1)}) custom-call(f32[16]{0:T(128)S(1)} %copy-done.3, bf16[128,2048]{1,0:T(8,128)(2,1)S(1)} %copy-done, bf16[1040,128]{1,0:T(8,128)(2,1)S(1)} %get-tuple-element.12.own_ref, f32[16,128]{1,0:T(8,128)S(1)} %bitcast.2), custom_call_target="tpu_custom_call" | custom-call | flops 134217728 | bytes 4194304 | tf_op jit(solution)/shard_map/pallas_call | solution.py:257
  12.0 2.2 %collective-permute-done.1.two_ref = bf16[1040,128]{1,0:T(8,128)(2,1)S(1)} collective-permute-done((bf16[1040,128]{1,0:T(8,128)(2,1)S(1)}, bf16[1040,128]{1,0:T(8,128)(2,1)S(1)}, u32[]{:S(2)}, u32[]{:S(2)}) %collective-permute-start.1) | collective-permute-done | bytes 266272 | tf_op jit(solution)/shard_map/ppermute | solution.py:254
  14.1 0.0 copy-done.1
  14.1 0.4 %shard_map.66 = (f32[512,128]{1,0:T(8,128)S(1)}, f32[512,512]{1,0:T(8,128)S(1)}) custom-call(bf16[128,2048]{1,0:T(8,128)(2,1)S(1)} %copy-done.1, bf16[1040,128]{1,0:T(8,128)(2,1)S(1)} %get-tuple-element.12.own_ref, bf16[1040,128]{1,0:T(8,128)(2,1)S(1)} %collective-permute-done.1.two_ref, f32[512,512]{1,0:T(8,128)S(1)} %get-tuple-element.14.summed_ref, ...), custom_call_target="tpu_custom_call" | custom-call | tf_op jit(solution)/shard_map/pallas_call | solution.py:273
  14.5 0.0 collective-permute-done.one_ref
  14.5 2.1 %shard_map.67 = f32[128,2048]{1,0:T(8,128)} custom-call(bf16[128,2048]{1,0:T(8,128)(2,1)S(1)} %copy-done.1, bf16[1040,128]{1,0:T(8,128)(2,1)S(1)} %get-tuple-element.12.own_ref, bf16[1056,128]{1,0:T(8,128)(2,1)S(1)} %collective-permute-done.one_ref, f32[512,512]{1,0:T(8,128)S(1)} %get-tuple-element.14.summed_ref, f32[16,512]{1,0:T(8,128)S(1)} %get-tuple-element.15.stats_ref, ...), custom_call_target="tpu_custom_call" | custom-call | tf_op jit(solution)/shard_map/pallas_call | solution.py:283
Async XLA Ops:
  0.0 9.2 %copy-start.2 = (f32[2048]{0:T(1024)S(1)}, f32[2048]{0:T(1024)}, u32[]{:S(2)}) copy-start(f32[2048]{0:T(1024)} %param.11) | copy-start | bytes 24580
  1.2 13.3 %collective-permute-start = (bf16[1056,128]{1,0:T(8,128)(2,1)S(1)}, bf16[1056,128]{1,0:T(8,128)(2,1)S(1)}, u32[]{:S(2)}, u32[]{:S(2)}) collective-permute-start(bf16[1056,128]{1,0:T(8,128)(2,1)S(1)} %get-tuple-element.13), channel_id=1, source_target_pairs={{0,4},{4,8},{8,12},{12,16},{16,20},{20,24},{24,28},{1,5},{5,9},{9,... | collective-permute-start | bytes 811016 | tf_op jit(solution)/shard_map/ppermute | solution.py:254
  5.2 4.0 %copy-start.3 = (f32[16]{0:T(128)S(1)}, f32[16]{0:T(128)}, u32[]{:S(2)}) copy-start(f32[16]{0:T(128)} %beta_ref.1) | copy-start | bytes 196
  5.2 9.0 %collective-permute-start.1 = (bf16[1040,128]{1,0:T(8,128)(2,1)S(1)}, bf16[1040,128]{1,0:T(8,128)(2,1)S(1)}, u32[]{:S(2)}, u32[]{:S(2)}) collective-permute-start(bf16[1040,128]{1,0:T(8,128)(2,1)S(1)} %get-tuple-element.12.own_ref), channel_id=1, source_target_pairs={{0,8},{4,12},{8,16},{12,20},{16,24},{20,28},{1,9},{5,13},{9,17},{1... | collective-permute-start | bytes 798728 | tf_op jit(solution)/shard_map/ppermute | solution.py:254
  9.2 1.0 %copy-start = (bf16[128,2048]{1,0:T(8,128)(2,1)S(1)}, bf16[128,2048]{1,0:T(8,128)(2,1)}, u32[]{:S(2)}) copy-start(bf16[128,2048]{1,0:T(8,128)(2,1)} %q_ref.5) | copy-start | bytes 1572868
  10.2 3.9 %copy-start.1 = (bf16[128,2048]{1,0:T(8,128)(2,1)S(1)}, bf16[128,2048]{1,0:T(8,128)(2,1)}, u32[]{:S(2)}) copy-start(bf16[128,2048]{1,0:T(8,128)(2,1)} %q_ref.5) | copy-start | bytes 1572868

commit v6 on v0

--- a/solution.py
+++ b/solution.py
@@ -1,11 +1,364 @@
+import functools
+import math
+
 import jax
 import jax.numpy as jnp
 from jax import lax
+from jax.experimental import pallas as pl
+from jax.experimental.pallas import tpu as pltpu
 from jax.sharding import PartitionSpec as P
 
 HEADS = 16
 KV_HEADS = 4
 HEAD_DIM = 128
+GROUPS = HEADS // KV_HEADS
+LONGEST = 4
+SCALE = math.log2(math.e) / math.sqrt(HEAD_DIM)
+LOWEST = -1e30
+EXTRA = 16
+STEPS = 14.0
+
+NT = (((1,), (1,)), ((), ()))
+TN = (((0,), (0,)), ((), ()))
+
+
+def dot(a, b, dims):
+    return lax.dot_general(a, b, dims, preferred_element_type=jnp.float32)
+
+
+def column(row):
+    return jnp.transpose(jnp.broadcast_to(row, (HEAD_DIM, row.shape[1])))
+
+
+def part_of(i, size):
+    return slice(i * size, (i + 1) * size)
+
+
+def group_queries(q_ref, g):
+    heads = [q_ref[:, part_of(g * GROUPS + i, HEAD_DIM)] for i in range(GROUPS)]
+    return jnp.concatenate(heads, axis=0)
+
+
+def share_of(beta_ref, h):
+    return 1.0 / (1.0 + jnp.exp(-jnp.full((1, HEAD_DIM), beta_ref[h], jnp.float32)))
+
+
+def scaled_gains(beta_ref, gain_ref, out_ref):
+    for h in range(HEADS):
+        scaled = gain_ref[h : h + 1, :] * share_of(beta_ref, h)
+        out_ref[part_of(h, HEAD_DIM), :] = column(scaled)
+
+
+def suffix(others):
+    count = jnp.sum(others, axis=1, keepdims=True)
+    shape = (others.shape[1], HEAD_DIM)
+    return lax.broadcasted_iota(jnp.int32, shape, 0).astype(jnp.float32) >= count
+
+
+def first_document(docs):
+    first = jnp.broadcast_to(docs[:, 0:1], docs.shape)
+    return first, docs == first
+
+
+def load_block(key_ref, value_ref, doc_ref, out_ref, doc_scratch, sems):
+    rows = key_ref.shape[0]
+    doc_copy = pltpu.make_async_copy(doc_ref, doc_scratch, sems.at[0])
+    doc_copy.start()
+    copies = []
+    for g in range(2 * KV_HEADS):
+        source = key_ref if g < KV_HEADS else value_ref
+        copy = pltpu.make_async_copy(
+            source.at[:, part_of(g % KV_HEADS, HEAD_DIM)],
+            out_ref.at[part_of(g, rows), :],
+            sems.at[1 + g],
+        )
+        copy.start()
+        copies.append(copy)
+    doc_copy.wait()
+    docs = jnp.broadcast_to(doc_scratch[...].astype(jnp.float32), (EXTRA, rows))
+    start = 2 * KV_HEADS * rows
+    out_ref[start : start + EXTRA, :] = docs.astype(jnp.bfloat16)
+    for copy in copies:
+        copy.wait()
+
+
+def block_keys(ref, g):
+    return ref[part_of(g, HEAD_DIM), :]
+
+
+def block_values(ref, g):
+    return ref[part_of(KV_HEADS + g, HEAD_DIM), :]
+
+
+def block_docs(ref):
+    start = 2 * KV_HEADS * HEAD_DIM
+    return ref[start : start + EXTRA, :].astype(jnp.float32)[0:1, :]
+
+
+def pack_kernel(key_ref, value_ref, doc_ref, out_ref, doc_scratch, sems):
+    @pl.when(lax.axis_index("kv") == 0)
+    def _():
+        load_block(key_ref, value_ref, doc_ref, out_ref, doc_scratch, sems)
+
+
+def attend_own(q_ref, block_ref, g, bias):
+    rows = q_ref.shape[0]
+    scores = dot(block_keys(block_ref, g), group_queries(q_ref, g), NT)
+    tops, totals, weights = [], [], []
+    for i in range(GROUPS):
+        masked = scores[:, part_of(i, rows)] * SCALE + bias
+        top = jnp.max(masked, axis=0, keepdims=True)
+        weight = jnp.exp2(masked - top)
+        tops.append(top)
+        totals.append(jnp.sum(weight, axis=0, keepdims=True))
+        weights.append(weight.astype(jnp.bfloat16))
+    summed = dot(block_values(block_ref, g), jnp.concatenate(weights, axis=1), TN)
+    return summed, jnp.concatenate(tops, axis=1), jnp.concatenate(totals, axis=1)
+
+
+def own_bias(docs):
+    rows = docs.shape[1]
+    place = lax.broadcasted_iota(jnp.int32, (rows, rows), 0)
+    row = lax.broadcasted_iota(jnp.int32, (rows, rows), 1)
+    return jnp.where((place <= row) & (column(docs) == docs), 0.0, LOWEST)
+
+
+def block_state(block_ref, state_ref):
+    docs = block_docs(block_ref)
+    rows = docs.shape[1]
+    last = jnp.broadcast_to(docs[:, rows - 1 : rows], docs.shape)
+    live = suffix(jnp.where(docs == last, 0.0, 1.0))
+    extra = jnp.broadcast_to(last, (EXTRA, HEAD_DIM))
+    line = lax.broadcasted_iota(jnp.int32, (EXTRA, HEAD_DIM), 0)
+    for g in range(KV_HEADS):
+        keys = jnp.where(live, block_keys(block_ref, g).astype(jnp.float32), 0.0)
+        state = dot(block_values(block_ref, g), keys.astype(jnp.bfloat16), TN)
+        largest = jnp.max(jnp.abs(state), axis=0, keepdims=True)
+        power = jnp.ceil(jnp.log2(jnp.maximum(largest, 1e-30)))
+        steps = jnp.round(state * jnp.exp2(STEPS - power))
+        state_ref[part_of(g, HEAD_DIM), :] = steps.astype(jnp.int32).astype(jnp.int16)
+        extra = jnp.where(line == g, power, extra)
+    extra = jnp.where(line == KV_HEADS + 1, docs, extra)
+    start = KV_HEADS * HEAD_DIM
+    state_ref[start : start + EXTRA, :] = extra.astype(jnp.int32).astype(jnp.int16)
+
+
+def state_extra(ref):
+    start = KV_HEADS * HEAD_DIM
+    return ref[start : start + EXTRA, :].astype(jnp.int32).astype(jnp.float32)
+
+
+def state_docs(ref):
+    return state_extra(ref)[KV_HEADS + 1 : KV_HEADS + 2, :]
+
+
+def state_kernel(
+    q_ref, gain_ref, packed_ref, beta_ref, key_ref, value_ref, doc_ref,
+    state_ref, summed_ref, stats_ref, gains_ref,
+    own_ref, doc_scratch, beta_scratch, sems,
+):
+    part = lax.axis_index("kv")
+
+    @pl.when(part == 0)
+    def _():
+        block_state(packed_ref, state_ref)
+
+    @pl.when(part == 1)
+    def _():
+        beta_copy = pltpu.make_async_copy(beta_ref, beta_scratch, sems.at[2 * KV_HEADS + 1])
+        beta_copy.start()
+        load_block(key_ref, value_ref, doc_ref, own_ref, doc_scratch, sems)
+        beta_copy.wait()
+        block_state(own_ref, state_ref)
+        bias = own_bias(block_docs(own_ref))
+        for g in range(KV_HEADS):
+            summed, top, total = attend_own(q_ref, own_ref, g, bias)
+            summed_ref[part_of(g, HEAD_DIM), :] = summed
+            stats_ref[g : g + 1, :] = top
+            stats_ref[KV_HEADS + g : KV_HEADS + g + 1, :] = total
+            rest = [1.0 - share_of(beta_scratch, g * GROUPS + i) for i in range(GROUPS)]
+            stats_ref[2 * KV_HEADS + g : 2 * KV_HEADS + g + 1, :] = jnp.concatenate(rest, axis=1)
+        scaled_gains(beta_scratch, gain_ref, gains_ref)
+
+
+def own_kernel(beta_ref, q_ref, packed_ref, gain_ref, ready_ref, gains_ref):
+    @pl.when(lax.axis_index("kv") == 0)
+    def _():
+        bias = own_bias(block_docs(packed_ref))
+        for g in range(KV_HEADS):
+            summed, _, total = attend_own(q_ref, packed_ref, g, bias)
+            rest = [1.0 - share_of(beta_ref, g * GROUPS + i) for i in range(GROUPS)]
+            scale = jnp.concatenate(rest, axis=1) / total
+            ready_ref[part_of(g, HEAD_DIM), :] = summed * scale
+        scaled_gains(beta_ref, gain_ref, gains_ref)
+
+
+def before_kernel(q_ref, state_ref, one_ref, summed_ref, stats_ref, ready_ref):
+    @pl.when(lax.axis_index("kv") == 1)
+    def _():
+        docs = state_docs(state_ref)
+        rows = docs.shape[1]
+        first, same = first_document(docs)
+        live = suffix(jnp.where(block_docs(one_ref) == first, 0.0, 1.0))
+        bias = jnp.where(live & same, 0.0, LOWEST)
+        for g in range(KV_HEADS):
+            scores = dot(block_keys(one_ref, g), group_queries(q_ref, g), NT)
+            weights, factors, scales = [], [], []
+            for i in range(GROUPS):
+                cut = part_of(i, rows)
+                masked = scores[:, cut] * SCALE + bias
+                top_own = stats_ref[g : g + 1, cut]
+                top = jnp.maximum(jnp.max(masked, axis=0, keepdims=True), top_own)
+                weight = jnp.exp2(masked - top)
+                factor = jnp.exp2(top_own - top)
+                total = stats_ref[KV_HEADS + g : KV_HEADS + g + 1, cut] * factor
+                total = total + jnp.sum(weight, axis=0, keepdims=True)
+                factors.append(factor)
+                scales.append(stats_ref[2 * KV_HEADS + g : 2 * KV_HEADS + g + 1, cut] / total)
+                weights.append(weight.astype(jnp.bfloat16))
+            added = dot(block_values(one_ref, g), jnp.concatenate(weights, axis=1), TN)
+            group = part_of(g, HEAD_DIM)
+            summed = summed_ref[group, :] * jnp.concatenate(factors, axis=1) + added
+            ready_ref[group, :] = summed * jnp.concatenate(scales, axis=1)
+
+
+def join_kernel(
+    q_ref, state_ref, one_ref, two_ref, ready_zero, gains_zero, ready_one, gains_one,
+    out_ref, held, sems,
+):
+    docs = state_docs(state_ref)
+    rows = docs.shape[1]
+    first, same = first_document(docs)
+    reads = jnp.where(same, 1.0, 0.0)
+    extras = []
+    for ref in (one_ref, two_ref):
+        extra = state_extra(ref)
+        valid = jnp.where(extra[KV_HEADS : KV_HEADS + 1, :] == first, 1.0, 0.0)
+        extras.append(jnp.exp2(extra[0:KV_HEADS, :] - STEPS) * valid)
+
+    def copy(g):
+        wide = part_of(g, GROUPS * HEAD_DIM)
+        return pltpu.make_async_copy(held.at[:, wide], out_ref.at[:, wide], sems.at[g])
+
+    def finish(ready_ref, gains_ref):
+        for g in range(KV_HEADS):
+            group = part_of(g, HEAD_DIM)
+            one = one_ref[group, :].astype(jnp.int32).astype(jnp.float32)
+            two = two_ref[group, :].astype(jnp.int32).astype(jnp.float32)
+            state = one * extras[0][g : g + 1, :] + two * extras[1][g : g + 1, :]
+            q = group_queries(q_ref, g)
+            high = state.astype(jnp.bfloat16)
+            low = (state - high.astype(jnp.float32)).astype(jnp.bfloat16)
+            recalled = dot(high, q, NT) + dot(low, q, NT)
+            for i in range(GROUPS):
+                h, cut = g * GROUPS + i, part_of(i, rows)
+                read = recalled[:, cut]
+                square = jnp.sum(read * read, axis=0, keepdims=True) * (1.0 / HEAD_DIM)
+                read = read * (lax.rsqrt(square + 1e-06) * reads)
+                mixed = read * gains_ref[part_of(h, HEAD_DIM), :] + ready_ref[group, cut]
+                held[:, part_of(h, HEAD_DIM)] = jnp.transpose(mixed)
+            copy(g).start()
+
+    part = lax.axis_index("kv")
+
+    @pl.when(part == 0)
+    def _():
+        finish(ready_zero, gains_zero)
+
+    @pl.when(part == 1)
+    def _():
+        finish(ready_one, gains_one)
+
+    for g in range(KV_HEADS):
+        copy(g).wait()
+
+
+def near_device(n_seq, queries, keys, values, doc_ids, beta, lin_gain):
+    rows = queries.shape[0]
+    devices = 2 * n_seq
+    vmem = pl.BlockSpec(memory_space=pltpu.VMEM)
+    smem = pl.BlockSpec(memory_space=pltpu.SMEM)
+    hbm = pl.BlockSpec(memory_space=pltpu.HBM)
+    in_hbm = functools.partial(pltpu.with_memory_space_constraint, memory_space=pltpu.HBM)
+    params = pltpu.CompilerParams(vmem_limit_bytes=32 * 1024 * 1024)
+    wide = GROUPS * rows
+    group_shape = jax.ShapeDtypeStruct((KV_HEADS * HEAD_DIM, wide), jnp.float32)
+    gains_shape = jax.ShapeDtypeStruct((HEADS * HEAD_DIM, HEAD_DIM), jnp.float32)
+    docs = doc_ids.reshape(1, rows)
+    gain = lin_gain.reshape(HEADS, HEAD_DIM)
+    deep = 2 * KV_HEADS * rows + EXTRA
+
+    def estimate(share):
+        return pl.CostEstimate(
+            flops=int(share * 4 * HEADS * HEAD_DIM * rows * rows),
+            bytes_accessed=int(share * 4 * 1024 * 1024),
+            transcendentals=int(share * HEADS * rows * rows),
+        )
+
+    def send(payload, pairs):
+        return lax.ppermute(payload, ("seq", "kv"), pairs)
+
+    packed = pl.pallas_call(
+        pack_kernel,
+        out_shape=jax.ShapeDtypeStruct((deep, HEAD_DIM), jnp.bfloat16),
+        in_specs=[hbm] * 3,
+        out_specs=vmem,
+        scratch_shapes=[
+            pltpu.VMEM((1, rows), jnp.int32),
+            pltpu.SemaphoreType.DMA((2 * KV_HEADS + 1,)),
+        ],
+        compiler_params=params,
+        cost_estimate=estimate(0.1),
+    )(in_hbm(keys), in_hbm(values), in_hbm(docs))
+    block = send(packed, [(b, b + 1) for b in range(0, devices, 2)])
+    state, summed, stats, gains_one = pl.pallas_call(
+        state_kernel,
+        out_shape=[
+            jax.ShapeDtypeStruct((KV_HEADS * HEAD_DIM + EXTRA, HEAD_DIM), jnp.int16),
+            group_shape,
+            jax.ShapeDtypeStruct((4 * KV_HEADS, wide), jnp.float32),
+            gains_shape,
+        ],
+        in_specs=[vmem] * 3 + [hbm] * 4,
+        out_specs=[vmem] * 4,
+        scratch_shapes=[
+            pltpu.VMEM((deep, HEAD_DIM), jnp.bfloat16),
+            pltpu.VMEM((1, rows), jnp.int32),
+            pltpu.SMEM((HEADS,), jnp.float32),
+            pltpu.SemaphoreType.DMA((2 * KV_HEADS + 2,)),
+        ],
+        compiler_params=params,
+        cost_estimate=estimate(1.0),
+    )(queries, gain, packed, in_hbm(beta), in_hbm(keys), in_hbm(values), in_hbm(docs))
+    one = send(state, [(b, b + 1) for b in range(1, devices - 1, 2)])
+    two = send(state, [(b, b + 2) for b in range(devices - 2)])
+    ready_zero, gains_zero = pl.pallas_call(
+        own_kernel,
+        out_shape=[group_shape, gains_shape],
+        in_specs=[smem] + [vmem] * 3,
+        out_specs=[vmem] * 2,
+        compiler_params=params,
+        cost_estimate=estimate(1.0),
+    )(beta, queries, packed, gain)
+    ready_one = pl.pallas_call(
+        before_kernel,
+        out_shape=group_shape,
+        in_specs=[vmem] * 5,
+        out_specs=vmem,
+        compiler_params=params,
+        cost_estimate=estimate(1.0),
+    )(queries, state, block, summed, stats)
+    return pl.pallas_call(
+        join_kernel,
+        out_shape=jax.ShapeDtypeStruct((rows, HEADS * HEAD_DIM), jnp.float32),
+        in_specs=[vmem] * 8,
+        out_specs=hbm,
+        scratch_shapes=[
+            pltpu.VMEM((rows, HEADS * HEAD_DIM), jnp.float32),
+            pltpu.SemaphoreType.DMA((KV_HEADS,)),
+        ],
+        compiler_params=params,
+    )(queries, state, one, two, ready_zero, gains_zero, ready_one, gains_one)
 
 
 def carried_in(part, axis, combine, identity):
@@ -81,7 +434,7 @@
     return (new_max, new_sum, new_accum)
 
 
-def on_device(queries, keys, values, doc_ids, beta, lin_gain):
+def far_device(queries, keys, values, doc_ids, beta, lin_gain):
     row_count = queries.shape[0]
     groups = HEADS // KV_HEADS
     query_heads = queries.reshape(row_count, KV_HEADS, groups, HEAD_DIM)
@@ -162,6 +515,7 @@
 
 
 def solution(mesh):
+    n_seq, n_kv = mesh.shape["seq"], mesh.shape["kv"]
     in_specs = (
         P(("dp", "seq", "kv"), None),
         P(("dp", "seq", "kv"), None),
@@ -171,6 +525,10 @@
         P(),
     )
     out_specs = P(("dp", "seq", "kv"), None)
+    if n_kv == 2 and n_seq * n_kv <= 2 * LONGEST:
+        on_device = functools.partial(near_device, n_seq)
+    else:
+        on_device = far_device
     return jax.shard_map(
         on_device, mesh=mesh, in_specs=in_specs, out_specs=out_specs, check_vma=False
     )

time: 81.9 us -> 14.9 us (0.18)
  the two profiles are of different devices: /device:TPU:7 before, /device:TPU:1 now
where the time goes in v6:
time: 14.9 us; the launch traced here: 14.7 us
  starting transfers between devices  8.43 us (57%)
  Pallas kernels  4.75 us (32%)
  waiting for transfers between devices  1.39 us (9%)
    ppermute x3, starting transfers between devices, send(): return lax.ppermute(payload, ('seq', 'kv'), pairs)  8.43 us
    pallas_call x1, Pallas kernels, near_device(): pl.pallas_call(own_kernel, out_shape=[group_shape, gains_shape], in_specs...  1.75 us
    pallas_call x1, Pallas kernels, near_device(): pl.pallas_call(join_kernel, out_shape=jax.ShapeDtypeStruct((rows, HEADS *...  1.5 us
    ppermute x3, waiting for transfers between devices, send(): return lax.ppermute(payload, ('seq', 'kv'), pairs)  1.39 us
    pallas_call x1, Pallas kernels, near_device(): pl.pallas_call(pack_kernel, out_shape=jax.ShapeDtypeStruct((deep, HEAD_DI...  1.03 us
    pallas_call x1, Pallas kernels, near_device(): pl.pallas_call(state_kernel, out_shape=[jax.ShapeDtypeStruct((KV_HEADS *...  0.47 us
  transfers between devices with their start and end apart: 3, of which 1 were waited for; matrix products, arithmetic and copies ran while one was open for 0% of the time, Pallas kernels for 15%

profile of v6, /device:TPU:1, one launch (start us, length us, event | category | flops | bytes accessed | tf_op | source)
XLA Modules:
  0.0 14.7 jit_solution(15611222466939538617)
XLA Ops:
  0.0 0.0 copy-start
  0.0 0.0 copy-start.1
  0.0 1.0 %shard_map.64.packed_ref = bf16[1040,128]{1,0:T(8,128)(2,1)S(1)} custom-call(bf16[128,512]{1,0:T(8,128)(2,1)} %key_ref.3, bf16[128,512]{1,0:T(8,128)(2,1)} %value_ref.3, s32[1,128]{1,0:T(1,128)} %bitcast.4), custom_call_target="tpu_custom_call" | custom-call | flops 13421772 | bytes 419430 | tf_op jit(solution)/shard_map/pallas_call | solution.py:301
  1.0 3.1 %collective-permute-start.2 = (bf16[1040,128]{1,0:T(8,128)(2,1)S(1)}, bf16[1040,128]{1,0:T(8,128)(2,1)S(1)}, u32[]{:S(2)}, u32[]{:S(2)}) collective-permute-start(bf16[1040,128]{1,0:T(8,128)(2,1)S(1)} %shard_map.64.packed_ref), channel_id=1, source_target_pairs={{0,4},{8,12},{16,20},{24,28},{1,5},{9,13},{17,21},{25,29},{2,6},{1... | collective-permute-start | bytes 798728 | tf_op jit(solution)/shard_map/ppermute | solution.py:299
  4.2 0.0 copy-done
  4.2 0.0 copy-done.1
  4.2 0.5 %shard_map.65 = (s16[528,128]{1,0:T(8,128)(2,1)S(1)}, f32[512,512]{1,0:T(8,128)S(1)}, f32[16,512]{1,0:T(8,128)S(1)}, f32[2048,128]{1,0:T(8,128)S(1)}) custom-call(bf16[128,2048]{1,0:T(8,128)(2,1)S(1)} %copy-done, f32[16,128]{1,0:T(8,128)S(1)} %bitcast.2, bf16[1040,128]{1,0:T(8,128)(2,1)S(1)} %shard_map.64.packed_ref, f32[16]{0:T(128)} %beta_ref.3, ...), custom_call_target="tpu_custom_call" | custom-call | flops 134217728 | bytes 4194304 | tf_op jit(solution)/shard_map/pallas_call | solution.py:314
  4.7 0.0 copy-start.2
  4.7 1.3 %collective-permute-start = (s16[528,128]{1,0:T(8,128)(2,1)S(1)}, s16[528,128]{1,0:T(8,128)(2,1)S(1)}, u32[]{:S(2)}, u32[]{:S(2)}) collective-permute-start(s16[528,128]{1,0:T(8,128)(2,1)S(1)} %get-tuple-element.11.state_ref), channel_id=1, source_target_pairs={{4,8},{12,16},{20,24},{5,9},{13,17},{21,25},{6,10},{14,18},{22,26}... | collective-permute-start | bytes 405512 | tf_op jit(solution)/shard_map/ppermute | solution.py:299
  6.0 4.0 %collective-permute-start.1 = (s16[528,128]{1,0:T(8,128)(2,1)S(1)}, s16[528,128]{1,0:T(8,128)(2,1)S(1)}, u32[]{:S(2)}, u32[]{:S(2)}) collective-permute-start(s16[528,128]{1,0:T(8,128)(2,1)S(1)} %get-tuple-element.11.state_ref), channel_id=1, source_target_pairs={{0,8},{4,12},{8,16},{12,20},{16,24},{20,28},{1,9},{5,13},{9,17},{1... | collective-permute-start | bytes 405512 | tf_op jit(solution)/shard_map/ppermute | solution.py:299
  10.0 0.0 copy-done.2
  10.0 1.7 %shard_map.66 = (f32[512,512]{1,0:T(8,128)S(1)}, f32[2048,128]{1,0:T(8,128)S(1)}) custom-call(f32[16]{0:T(128)S(1)} %copy-done.2, bf16[128,2048]{1,0:T(8,128)(2,1)S(1)} %copy-done, bf16[1040,128]{1,0:T(8,128)(2,1)S(1)} %shard_map.64.packed_ref, f32[16,128]{1,0:T(8,128)S(1)} %bitcast.3), custom_call_target="tpu_custom_call" | custom-call | flops 134217728 | bytes 4194304 | tf_op jit(solution)/shard_map/pallas_call | solution.py:335
  11.8 0.0 collective-permute-done.2.one_ref
  11.8 0.0 collective-permute-done.one_ref
  11.8 1.4 %collective-permute-done.1.two_ref = s16[528,128]{1,0:T(8,128)(2,1)S(1)} collective-permute-done((s16[528,128]{1,0:T(8,128)(2,1)S(1)}, s16[528,128]{1,0:T(8,128)(2,1)S(1)}, u32[]{:S(2)}, u32[]{:S(2)}) %collective-permute-start.1) | collective-permute-done | bytes 135200 | tf_op jit(solution)/shard_map/ppermute | solution.py:299
  13.2 1.5 %shard_map.68 = f32[128,2048]{1,0:T(8,128)} custom-call(bf16[128,2048]{1,0:T(8,128)(2,1)S(1)} %copy-done, s16[528,128]{1,0:T(8,128)(2,1)S(1)} %get-tuple-element.11.state_ref, s16[528,128]{1,0:T(8,128)(2,1)S(1)} %collective-permute-done.one_ref, s16[528,128]{1,0:T(8,128)(2,1)S(1)} %collective-permute-done.1.two_ref, ...), custom_call_target="tpu_custom_call" | custom-call | tf_op jit(solution)/shard_map/pallas_call | solution.py:351
  (1 shorter events, 0.0 us)
Async XLA Ops:
  0.0 4.2 %copy-start = (bf16[128,2048]{1,0:T(8,128)(2,1)S(1)}, bf16[128,2048]{1,0:T(8,128)(2,1)}, u32[]{:S(2)}) copy-start(bf16[128,2048]{1,0:T(8,128)(2,1)} %q_ref.7) | copy-start | bytes 1572868
  0.0 4.2 %copy-start.1 = (f32[2048]{0:T(1024)S(1)}, f32[2048]{0:T(1024)}, u32[]{:S(2)}) copy-start(f32[2048]{0:T(1024)} %param.11) | copy-start | bytes 24580
  1.0 10.7 %collective-permute-start.2 = (bf16[1040,128]{1,0:T(8,128)(2,1)S(1)}, bf16[1040,128]{1,0:T(8,128)(2,1)S(1)}, u32[]{:S(2)}, u32[]{:S(2)}) collective-permute-start(bf16[1040,128]{1,0:T(8,128)(2,1)S(1)} %shard_map.64.packed_ref), channel_id=1, source_target_pairs={{0,4},{8,12},{16,20},{24,28},{1,5},{9,13},{17,21},{25,29},{2,6},{1... | collective-permute-start | bytes 798728 | tf_op jit(solution)/shard_map/ppermute | solution.py:299
  4.7 5.3 %copy-start.2 = (f32[16]{0:T(128)S(1)}, f32[16]{0:T(128)}, u32[]{:S(2)}) copy-start(f32[16]{0:T(128)} %beta_ref.3) | copy-start | bytes 196
  4.7 7.1 %collective-permute-start = (s16[528,128]{1,0:T(8,128)(2,1)S(1)}, s16[528,128]{1,0:T(8,128)(2,1)S(1)}, u32[]{:S(2)}, u32[]{:S(2)}) collective-permute-start(s16[528,128]{1,0:T(8,128)(2,1)S(1)} %get-tuple-element.11.state_ref), channel_id=1, source_target_pairs={{4,8},{12,16},{20,24},{5,9},{13,17},{21,25},{6,10},{14,18},{22,26}... | collective-permute-start | bytes 405512 | tf_op jit(solution)/shard_map/ppermute | solution.py:299
  6.0 7.2 %collective-permute-start.1 = (s16[528,128]{1,0:T(8,128)(2,1)S(1)}, s16[528,128]{1,0:T(8,128)(2,1)S(1)}, u32[]{:S(2)}, u32[]{:S(2)}) collective-permute-start(s16[528,128]{1,0:T(8,128)(2,1)S(1)} %get-tuple-element.11.state_ref), channel_id=1, source_target_pairs={{0,8},{4,12},{8,16},{12,20},{16,24},{20,28},{1,9},{5,13},{9,17},{1... | collective-permute-start | bytes 405512 | tf_op jit(solution)/shard_map/ppermute | solution.py:299

commit v7 on v0

--- a/solution.py
+++ b/solution.py
@@ -1,11 +1,387 @@
+import functools
+import math
+
 import jax
 import jax.numpy as jnp
 from jax import lax
+from jax.experimental import pallas as pl
+from jax.experimental.pallas import tpu as pltpu
 from jax.sharding import PartitionSpec as P
 
 HEADS = 16
 KV_HEADS = 4
 HEAD_DIM = 128
+GROUPS = HEADS // KV_HEADS
+LONGEST = 4
+SCALE = math.log2(math.e) / math.sqrt(HEAD_DIM)
+LOWEST = -1e30
+EXTRA = 16
+
+NT = (((1,), (1,)), ((), ()))
+TN = (((0,), (0,)), ((), ()))
+
+
+def dot(a, b, dims):
+    return lax.dot_general(a, b, dims, preferred_element_type=jnp.float32)
+
+
+def column(row):
+    return jnp.transpose(jnp.broadcast_to(row, (HEAD_DIM, row.shape[1])))
+
+
+def part_of(i, size):
+    return slice(i * size, (i + 1) * size)
+
+
+def group_queries(q_ref, g):
+    heads = [q_ref[:, part_of(g * GROUPS + i, HEAD_DIM)] for i in range(GROUPS)]
+    return jnp.concatenate(heads, axis=0)
+
+
+def share_of(beta_ref, h):
+    return 1.0 / (1.0 + jnp.exp(-jnp.full((1, HEAD_DIM), beta_ref[h], jnp.float32)))
+
+
+def scaled_gains(beta_ref, gain_ref, out_ref):
+    for h in range(HEADS):
+        scaled = gain_ref[h : h + 1, :] * share_of(beta_ref, h)
+        out_ref[part_of(h, HEAD_DIM), :] = column(scaled)
+
+
+def suffix(others):
+    count = jnp.sum(others, axis=1, keepdims=True)
+    shape = (others.shape[1], HEAD_DIM)
+    return lax.broadcasted_iota(jnp.int32, shape, 0).astype(jnp.float32) >= count
+
+
+def first_document(docs):
+    first = jnp.broadcast_to(docs[:, 0:1], docs.shape)
+    return first, docs == first
+
+
+def load_block(query_ref, key_ref, value_ref, doc_ref, q_ref, out_refs, doc_scratch, sems):
+    rows = key_ref.shape[0]
+    doc_copy = pltpu.make_async_copy(doc_ref, doc_scratch, sems.at[0])
+    doc_copy.start()
+    query_copy = pltpu.make_async_copy(query_ref, q_ref, sems.at[1])
+    copies = []
+    for out_ref in out_refs:
+        for g in range(2 * KV_HEADS):
+            source = key_ref if g < KV_HEADS else value_ref
+            copy = pltpu.make_async_copy(
+                source.at[:, part_of(g % KV_HEADS, HEAD_DIM)],
+                out_ref.at[part_of(g, rows), :],
+                sems.at[2 + len(copies)],
+            )
+            copy.start()
+            copies.append(copy)
+    query_copy.start()
+    copies.append(query_copy)
+    doc_copy.wait()
+    docs = jnp.broadcast_to(doc_scratch[...].astype(jnp.float32), (EXTRA, rows))
+    start = 2 * KV_HEADS * rows
+    for out_ref in out_refs:
+        out_ref[start : start + EXTRA, :] = docs.astype(jnp.bfloat16)
+    for copy in copies:
+        copy.wait()
+
+
+def block_keys(ref, g):
+    return ref[part_of(g, HEAD_DIM), :]
+
+
+def block_values(ref, g):
+    return ref[part_of(KV_HEADS + g, HEAD_DIM), :]
+
+
+def block_docs(ref):
+    start = 2 * KV_HEADS * HEAD_DIM
+    return ref[start : start + EXTRA, :].astype(jnp.float32)[0:1, :]
+
+
+class Plan:
+    def __init__(self, n_seq):
+        devices = 2 * n_seq
+        near = [(b, b + 1) for b in range(devices - 1)]
+        far = [(b, b + 2) for b in range(devices - 2)]
+        crossing = [p for p in far if p[0] // 2 % 2 == 1]
+        touched = {b for p in crossing for b in p}
+        targets = {p[1] for p in crossing}
+        early = [p for p in near if p[0] not in touched and p[1] not in targets]
+        self.pairs = [
+            crossing + early,
+            [p for p in near if p not in early],
+            [p for p in far if p not in crossing],
+        ]
+        self.senders = sorted({p[0] for p in self.pairs[0]})
+        busy = {b for p in self.pairs[1] for b in p}
+        self.idle = [b for b in range(devices) if b not in busy]
+        self.attend_first = [p[1] for p in early if p[1] % 2 == 1]
+
+
+def block_number():
+    return 2 * lax.axis_index("seq") + lax.axis_index("kv")
+
+
+def among(members):
+    block = block_number()
+    return functools.reduce(jnp.logical_or, [block == b for b in members])
+
+
+def pack_kernel(
+    plan, query_ref, key_ref, value_ref, doc_ref, first_ref, out_ref, q_ref, doc_scratch, sems
+):
+    @pl.when(among(plan.senders))
+    def _():
+        outs = (first_ref, out_ref)
+        load_block(query_ref, key_ref, value_ref, doc_ref, q_ref, outs, doc_scratch, sems)
+
+
+def attend_own(q_ref, block_ref, g, bias):
+    rows = q_ref.shape[0]
+    scores = dot(block_keys(block_ref, g), group_queries(q_ref, g), NT)
+    tops, totals, weights = [], [], []
+    for i in range(GROUPS):
+        masked = scores[:, part_of(i, rows)] * SCALE + bias
+        top = jnp.max(masked, axis=0, keepdims=True)
+        weight = jnp.exp2(masked - top)
+        tops.append(top)
+        totals.append(jnp.sum(weight, axis=0, keepdims=True))
+        weights.append(weight.astype(jnp.bfloat16))
+    summed = dot(block_values(block_ref, g), jnp.concatenate(weights, axis=1), TN)
+    return summed, jnp.concatenate(tops, axis=1), jnp.concatenate(totals, axis=1)
+
+
+def own_bias(docs):
+    rows = docs.shape[1]
+    place = lax.broadcasted_iota(jnp.int32, (rows, rows), 0)
+    row = lax.broadcasted_iota(jnp.int32, (rows, rows), 1)
+    return jnp.where((place <= row) & (column(docs) == docs), 0.0, LOWEST)
+
+
+def attend_itself(q_ref, block_ref, gain_ref, beta_ref, summed_ref, stats_ref, gains_ref, beta_copy):
+    bias = own_bias(block_docs(block_ref))
+    done = lax.axis_index("kv") == 0
+    for g in range(KV_HEADS):
+        summed, top, total = attend_own(q_ref, block_ref, g, bias)
+        summed_ref[part_of(g, HEAD_DIM), :] = summed
+        stats_ref[g : g + 1, :] = top
+        stats_ref[KV_HEADS + g : KV_HEADS + g + 1, :] = total
+    beta_copy.wait()
+    for g in range(KV_HEADS):
+        rest = [1.0 - share_of(beta_ref, g * GROUPS + i) for i in range(GROUPS)]
+        rest = jnp.concatenate(rest, axis=1)
+        stats_ref[2 * KV_HEADS + g : 2 * KV_HEADS + g + 1, :] = rest
+        scale = rest / stats_ref[KV_HEADS + g : KV_HEADS + g + 1, :]
+        group = part_of(g, HEAD_DIM)
+        summed_ref[group, :] = summed_ref[group, :] * jnp.where(done, scale, 1.0)
+    scaled_gains(beta_ref, gain_ref, gains_ref)
+
+
+def settle_kernel(
+    plan, gain_ref, packed_ref, q_in, beta_ref, query_ref, key_ref, value_ref, doc_ref,
+    out_ref, q_ref, summed_ref, stats_ref, gains_ref, beta_scratch, doc_scratch, sems,
+):
+    beta_copy = pltpu.make_async_copy(beta_ref, beta_scratch, sems.at[2 * KV_HEADS + 2])
+
+    @pl.when(among(plan.idle))
+    def _():
+        beta_copy.start()
+
+    @pl.when(jnp.logical_not(among(plan.senders)))
+    def _():
+        outs = (out_ref,)
+        load_block(query_ref, key_ref, value_ref, doc_ref, q_ref, outs, doc_scratch, sems)
+
+    @pl.when(among(plan.idle))
+    def _():
+        attend_itself(
+            q_ref, out_ref, gain_ref, beta_scratch, summed_ref, stats_ref, gains_ref, beta_copy
+        )
+
+
+def own_kernel(
+    plan, q_ref, own_ref, gain_ref, beta_ref, summed_in, stats_in, gains_in,
+    summed_ref, stats_ref, gains_ref, beta_scratch, sem,
+):
+    @pl.when(jnp.logical_not(among(plan.idle)))
+    def _():
+        beta_copy = pltpu.make_async_copy(beta_ref, beta_scratch, sem)
+        beta_copy.start()
+        attend_itself(
+            q_ref, own_ref, gain_ref, beta_scratch, summed_ref, stats_ref, gains_ref, beta_copy
+        )
+
+
+def before_kernel(plan, q_ref, own_ref, one_ref, two_ref, stats_ref, summed_in, summed_ref):
+    docs = block_docs(own_ref)
+    rows = docs.shape[1]
+    first, same = first_document(docs)
+
+    def attend(ref):
+        live = suffix(jnp.where(block_docs(ref) == first, 0.0, 1.0))
+        bias = jnp.where(live & same, 0.0, LOWEST)
+        for g in range(KV_HEADS):
+            scores = dot(block_keys(ref, g), group_queries(q_ref, g), NT)
+            weights, factors, scales = [], [], []
+            for i in range(GROUPS):
+                cut = part_of(i, rows)
+                masked = scores[:, cut] * SCALE + bias
+                top_own = stats_ref[g : g + 1, cut]
+                top = jnp.maximum(jnp.max(masked, axis=0, keepdims=True), top_own)
+                weight = jnp.exp2(masked - top)
+                factor = jnp.exp2(top_own - top)
+                total = stats_ref[KV_HEADS + g : KV_HEADS + g + 1, cut] * factor
+                total = total + jnp.sum(weight, axis=0, keepdims=True)
+                factors.append(factor)
+                scales.append(stats_ref[2 * KV_HEADS + g : 2 * KV_HEADS + g + 1, cut] / total)
+                weights.append(weight.astype(jnp.bfloat16))
+            added = dot(block_values(ref, g), jnp.concatenate(weights, axis=1), TN)
+            group = part_of(g, HEAD_DIM)
+            summed = summed_ref[group, :] * jnp.concatenate(factors, axis=1) + added
+            summed_ref[group, :] = summed * jnp.concatenate(scales, axis=1)
+
+    attend_first = among(plan.attend_first)
+
+    @pl.when(attend_first)
+    def _():
+        attend(one_ref)
+
+    @pl.when((lax.axis_index("kv") == 1) & jnp.logical_not(attend_first))
+    def _():
+        attend(two_ref)
+
+
+def join_kernel(
+    plan, q_ref, own_ref, one_ref, two_ref, three_ref, ready_ref, gains_ref, out_ref, held, sems
+):
+    docs = block_docs(own_ref)
+    rows = docs.shape[1]
+    first, same = first_document(docs)
+    reads = jnp.where(same, 1.0, 0.0)
+    sources = (one_ref, two_ref, three_ref)
+    attended = (among(plan.attend_first), lax.axis_index("kv") == 1, False)
+    lives = []
+    for ref, other in zip(sources, attended):
+        others = jnp.where((block_docs(ref) == first) & jnp.logical_not(other), 0.0, 1.0)
+        lives.append(suffix(others))
+
+    def copy(g):
+        wide = part_of(g, GROUPS * HEAD_DIM)
+        return pltpu.make_async_copy(held.at[:, wide], out_ref.at[:, wide], sems.at[g])
+
+    for g in range(KV_HEADS):
+        keys, values = [], []
+        for ref, live in zip(sources, lives):
+            masked = jnp.where(live, block_keys(ref, g).astype(jnp.float32), 0.0)
+            keys.append(masked.astype(jnp.bfloat16))
+            values.append(block_values(ref, g))
+        state = dot(jnp.concatenate(values, axis=0), jnp.concatenate(keys, axis=0), TN)
+        q = group_queries(q_ref, g)
+        high = state.astype(jnp.bfloat16)
+        state = state - high.astype(jnp.float32)
+        middle = state.astype(jnp.bfloat16)
+        low = (state - middle.astype(jnp.float32)).astype(jnp.bfloat16)
+        recalled = dot(high, q, NT) + (dot(middle, q, NT) + dot(low, q, NT))
+        for i in range(GROUPS):
+            h, cut = g * GROUPS + i, part_of(i, rows)
+            read = recalled[:, cut]
+            square = jnp.sum(read * read, axis=0, keepdims=True) * (1.0 / HEAD_DIM)
+            read = read * (lax.rsqrt(square + 1e-06) * reads)
+            mixed = read * gains_ref[part_of(h, HEAD_DIM), :]
+            mixed = mixed + ready_ref[part_of(g, HEAD_DIM), cut]
+            held[:, part_of(h, HEAD_DIM)] = jnp.transpose(mixed)
+        copy(g).start()
+    for g in range(KV_HEADS):
+        copy(g).wait()
+
+
+def near_device(n_seq, queries, keys, values, doc_ids, beta, lin_gain):
+    rows = queries.shape[0]
+    vmem = pl.BlockSpec(memory_space=pltpu.VMEM)
+    hbm = pl.BlockSpec(memory_space=pltpu.HBM)
+    in_hbm = functools.partial(pltpu.with_memory_space_constraint, memory_space=pltpu.HBM)
+    params = pltpu.CompilerParams(vmem_limit_bytes=32 * 1024 * 1024)
+    wide = GROUPS * rows
+    group_shape = jax.ShapeDtypeStruct((KV_HEADS * HEAD_DIM, wide), jnp.float32)
+    gains_shape = jax.ShapeDtypeStruct((HEADS * HEAD_DIM, HEAD_DIM), jnp.float32)
+    docs = doc_ids.reshape(1, rows)
+    gain = lin_gain.reshape(HEADS, HEAD_DIM)
+    deep = 2 * KV_HEADS * rows + EXTRA
+
+    def estimate(share):
+        return pl.CostEstimate(
+            flops=int(share * 4 * HEADS * HEAD_DIM * rows * rows),
+            bytes_accessed=int(share * 4 * 1024 * 1024),
+            transcendentals=int(share * HEADS * rows * rows),
+        )
+
+    def send(payload, pairs):
+        return lax.ppermute(payload, ("seq", "kv"), pairs)
+
+    plan = Plan(n_seq)
+    block_shape = jax.ShapeDtypeStruct((deep, HEAD_DIM), jnp.bfloat16)
+    stats_shape = jax.ShapeDtypeStruct((4 * KV_HEADS, wide), jnp.float32)
+    doc_scratch = pltpu.VMEM((1, rows), jnp.int32)
+    beta_scratch = pltpu.SMEM((HEADS,), jnp.float32)
+    query_shape = jax.ShapeDtypeStruct(queries.shape, queries.dtype)
+    block = (in_hbm(queries), in_hbm(keys), in_hbm(values), in_hbm(docs))
+    first, packed, q = pl.pallas_call(
+        functools.partial(pack_kernel, plan),
+        out_shape=[block_shape] * 2 + [query_shape],
+        in_specs=[hbm] * 4,
+        out_specs=[vmem] * 3,
+        scratch_shapes=[doc_scratch, pltpu.SemaphoreType.DMA((4 * KV_HEADS + 2,))],
+        compiler_params=params,
+        cost_estimate=estimate(0.1),
+    )(*block)
+    one = send(first, plan.pairs[0])
+    own, q, summed, stats, gains = pl.pallas_call(
+        functools.partial(settle_kernel, plan),
+        out_shape=[block_shape, query_shape, group_shape, stats_shape, gains_shape],
+        in_specs=[vmem] * 3 + [hbm] * 5,
+        out_specs=[vmem] * 5,
+        scratch_shapes=[
+            beta_scratch,
+            doc_scratch,
+            pltpu.SemaphoreType.DMA((2 * KV_HEADS + 3,)),
+        ],
+        input_output_aliases={1: 0, 2: 1},
+        compiler_params=params,
+        cost_estimate=estimate(1.0),
+    )(gain, packed, q, in_hbm(beta), *block)
+    two = send(own, plan.pairs[1])
+    three = send(own, plan.pairs[2])
+    summed, stats, gains = pl.pallas_call(
+        functools.partial(own_kernel, plan),
+        out_shape=[group_shape, stats_shape, gains_shape],
+        in_specs=[vmem] * 3 + [hbm] + [vmem] * 3,
+        out_specs=[vmem] * 3,
+        scratch_shapes=[beta_scratch, pltpu.SemaphoreType.DMA],
+        input_output_aliases={4: 0, 5: 1, 6: 2},
+        compiler_params=params,
+        cost_estimate=estimate(1.0),
+    )(q, own, gain, in_hbm(beta), summed, stats, gains)
+    ready = pl.pallas_call(
+        functools.partial(before_kernel, plan),
+        out_shape=group_shape,
+        in_specs=[vmem] * 6,
+        out_specs=vmem,
+        input_output_aliases={5: 0},
+        compiler_params=params,
+        cost_estimate=estimate(1.0),
+    )(q, own, one, two, stats, summed)
+    return pl.pallas_call(
+        functools.partial(join_kernel, plan),
+        out_shape=jax.ShapeDtypeStruct((rows, HEADS * HEAD_DIM), jnp.float32),
+        in_specs=[vmem] * 7,
+        out_specs=hbm,
+        scratch_shapes=[
+            pltpu.VMEM((rows, HEADS * HEAD_DIM), jnp.float32),
+            pltpu.SemaphoreType.DMA((KV_HEADS,)),
+        ],
+        compiler_params=params,
+    )(q, own, one, two, three, ready, gains)
 
 
 def carried_in(part, axis, combine, identity):
@@ -81,7 +457,7 @@
     return (new_max, new_sum, new_accum)
 
 
-def on_device(queries, keys, values, doc_ids, beta, lin_gain):
+def far_device(queries, keys, values, doc_ids, beta, lin_gain):
     row_count = queries.shape[0]
     groups = HEADS // KV_HEADS
     query_heads = queries.reshape(row_count, KV_HEADS, groups, HEAD_DIM)
@@ -162,6 +538,7 @@
 
 
 def solution(mesh):
+    n_seq, n_kv = mesh.shape["seq"], mesh.shape["kv"]
     in_specs = (
         P(("dp", "seq", "kv"), None),
         P(("dp", "seq", "kv"), None),
@@ -171,6 +548,10 @@
         P(),
     )
     out_specs = P(("dp", "seq", "kv"), None)
+    if n_kv == 2 and n_seq * n_kv <= 2 * LONGEST:
+        on_device = functools.partial(near_device, n_seq)
+    else:
+        on_device = far_device
     return jax.shard_map(
         on_device, mesh=mesh, in_specs=in_specs, out_specs=out_specs, check_vma=False
     )

time: 81.9 us -> 16.4 us (0.20)
  the two profiles are of different devices: /device:TPU:7 before, /device:TPU:27 now
where the time goes in v7:
time: 16.4 us; the launch traced here: 16.2 us
  Pallas kernels  6.69 us (41%)
  starting transfers between devices  6.11 us (37%)
  waiting for transfers between devices  3.26 us (20%)
    ppermute x3, starting transfers between devices, send(): return lax.ppermute(payload, ('seq', 'kv'), pairs)  6.11 us
    ppermute x3, waiting for transfers between devices, send(): return lax.ppermute(payload, ('seq', 'kv'), pairs)  3.26 us
    pallas_call x1, Pallas kernels, near_device(): pl.pallas_call(functools.partial(join_kernel, plan), out_shape=jax.ShapeD...  2.2 us
    pallas_call x1, Pallas kernels, near_device(): pl.pallas_call(functools.partial(own_kernel, plan), out_shape=[group_shap...  1.59 us
    pallas_call x1, Pallas kernels, near_device(): pl.pallas_call(functools.partial(pack_kernel, plan), out_shape=[block_sha...  1.52 us
    pallas_call x1, Pallas kernels, near_device(): pl.pallas_call(functools.partial(before_kernel, plan), out_shape=group_sh...  1.25 us
  transfers between devices with their start and end apart: 3, of which 1 were waited for; matrix products, arithmetic and copies ran while one was open for 0% of the time, Pallas kernels for 18%

profile of v7, /device:TPU:27, one launch (start us, length us, event | category | flops | bytes accessed | tf_op | source)
XLA Modules:
  0.0 16.2 jit_solution(17472089218846458042)
XLA Ops:
  0.0 0.0 copy-start
  0.0 1.5 %shard_map.64 = (bf16[1040,128]{1,0:T(8,128)(2,1)S(1)}, bf16[1040,128]{1,0:T(8,128)(2,1)S(1)}, bf16[128,2048]{1,0:T(8,128)(2,1)S(1)}) custom-call(bf16[128,2048]{1,0:T(8,128)(2,1)} %query_ref.3, bf16[128,512]{1,0:T(8,128)(2,1)} %key_ref.3, bf16[128,512]{1,0:T(8,128)(2,1)} %value_ref.3, s32[1,128]{1,0:T(1,128)} %bitcast.4), custom_call_target="tpu_custom_call" | custom-call | flops 13421772 | bytes 419430 | tf_op jit(solution)/shard_map/pallas_call | solution.py:329
  1.5 2.4 %collective-permute-start = (bf16[1040,128]{1,0:T(8,128)(2,1)S(1)}, bf16[1040,128]{1,0:T(8,128)(2,1)S(1)}, u32[]{:S(2)}, u32[]{:S(2)}) collective-permute-start(bf16[1040,128]{1,0:T(8,128)(2,1)S(1)} %get-tuple-element.20), channel_id=1, source_target_pairs={{8,16},{12,20},{0,4},{4,8},{24,28},{9,17},{13,21},{1,5},{5,9},{25,... | collective-permute-start | bytes 798728 | tf_op jit(solution)/shard_map/ppermute | solution.py:320
  3.9 0.0 copy-done
  3.9 0.1 shard_map.65
  4.0 2.5 %collective-permute-start.1 = (bf16[1040,128]{1,0:T(8,128)(2,1)S(1)}, bf16[1040,128]{1,0:T(8,128)(2,1)S(1)}, u32[]{:S(2)}, u32[]{:S(2)}) collective-permute-start(bf16[1040,128]{1,0:T(8,128)(2,1)S(1)} %get-tuple-element.19.own_ref), channel_id=1, source_target_pairs={{8,12},{12,16},{16,20},{20,24},{9,13},{13,17},{17,21},{21,25},{10,... | collective-permute-start | bytes 798728 | tf_op jit(solution)/shard_map/ppermute | solution.py:320
  6.5 1.3 %collective-permute-start.2 = (bf16[1040,128]{1,0:T(8,128)(2,1)S(1)}, bf16[1040,128]{1,0:T(8,128)(2,1)S(1)}, u32[]{:S(2)}, u32[]{:S(2)}) collective-permute-start(bf16[1040,128]{1,0:T(8,128)(2,1)S(1)} %get-tuple-element.19.own_ref), channel_id=1, source_target_pairs={{0,8},{4,12},{16,24},{20,28},{1,9},{5,13},{17,25},{21,29},{2,10},{... | collective-permute-start | bytes 798728 | tf_op jit(solution)/shard_map/ppermute | solution.py:320
  7.8 1.6 %shard_map.66 = (f32[512,512]{1,0:T(8,128)S(1)}, f32[16,512]{1,0:T(8,128)S(1)}, f32[2048,128]{1,0:T(8,128)S(1)}) custom-call(bf16[128,2048]{1,0:T(8,128)(2,1)S(1)} %get-tuple-element.18.q_ref, bf16[1040,128]{1,0:T(8,128)(2,1)S(1)} %get-tuple-element.19.own_ref, f32[16,128]{1,0:T(8,128)S(1)} %bitcast.3, ...), custom_call_target="tpu_custom_call", output_to_operand_aliasing={{0}: (4, {}), {1}: (5, {}), {2}: (6, {})} | custom-call | flops 134217728 | bytes 4194304 | tf_op jit(solution)/shard_map/pallas_call | solution.py:355
  9.4 0.0 collective-permute-done.one_ref
  9.4 3.3 %collective-permute-done.1.two_ref = bf16[1040,128]{1,0:T(8,128)(2,1)S(1)} collective-permute-done((bf16[1040,128]{1,0:T(8,128)(2,1)S(1)}, bf16[1040,128]{1,0:T(8,128)(2,1)S(1)}, u32[]{:S(2)}, u32[]{:S(2)}) %collective-permute-start.1) | collective-permute-done | bytes 266272 | tf_op jit(solution)/shard_map/ppermute | solution.py:320
  12.7 1.3 %shard_map.67.ready_ref = f32[512,512]{1,0:T(8,128)S(1)} custom-call(bf16[128,2048]{1,0:T(8,128)(2,1)S(1)} %get-tuple-element.18.q_ref, bf16[1040,128]{1,0:T(8,128)(2,1)S(1)} %get-tuple-element.19.own_ref, bf16[1040,128]{1,0:T(8,128)(2,1)S(1)} %collective-permute-done.one_ref, ...), custom_call_target="tpu_custom_call", output_to_operand_aliasing={{}: (5, {})} | custom-call | flops 134217728 | bytes 4194304 | tf_op jit(solution)/shard_map/pallas_call | solution.py:365
  13.9 0.0 collective-permute-done.2.three_ref
  13.9 2.2 %shard_map.68 = f32[128,2048]{1,0:T(8,128)} custom-call(bf16[128,2048]{1,0:T(8,128)(2,1)S(1)} %get-tuple-element.18.q_ref, bf16[1040,128]{1,0:T(8,128)(2,1)S(1)} %get-tuple-element.19.own_ref, bf16[1040,128]{1,0:T(8,128)(2,1)S(1)} %collective-permute-done.one_ref, bf16[1040,128]{1,0:T(8,128)(2,1)S(1)} %collective-permute-done.1.two_ref, ...), custom_call_target="tpu_custom_call" | custom-call | tf_op jit(solution)/shard_map/pallas_call | solution.py:374
Async XLA Ops:
  0.0 3.9 %copy-start = (f32[2048]{0:T(1024)S(1)}, f32[2048]{0:T(1024)}, u32[]{:S(2)}) copy-start(f32[2048]{0:T(1024)} %param.11) | copy-start | bytes 24580
  1.5 7.9 %collective-permute-start = (bf16[1040,128]{1,0:T(8,128)(2,1)S(1)}, bf16[1040,128]{1,0:T(8,128)(2,1)S(1)}, u32[]{:S(2)}, u32[]{:S(2)}) collective-permute-start(bf16[1040,128]{1,0:T(8,128)(2,1)S(1)} %get-tuple-element.20), channel_id=1, source_target_pairs={{8,16},{12,20},{0,4},{4,8},{24,28},{9,17},{13,21},{1,5},{5,9},{25,... | collective-permute-start | bytes 798728 | tf_op jit(solution)/shard_map/ppermute | solution.py:320
  4.0 8.6 %collective-permute-start.1 = (bf16[1040,128]{1,0:T(8,128)(2,1)S(1)}, bf16[1040,128]{1,0:T(8,128)(2,1)S(1)}, u32[]{:S(2)}, u32[]{:S(2)}) collective-permute-start(bf16[1040,128]{1,0:T(8,128)(2,1)S(1)} %get-tuple-element.19.own_ref), channel_id=1, source_target_pairs={{8,12},{12,16},{16,20},{20,24},{9,13},{13,17},{17,21},{21,25},{10,... | collective-permute-start | bytes 798728 | tf_op jit(solution)/shard_map/ppermute | solution.py:320
  6.5 7.4 %collective-permute-start.2 = (bf16[1040,128]{1,0:T(8,128)(2,1)S(1)}, bf16[1040,128]{1,0:T(8,128)(2,1)S(1)}, u32[]{:S(2)}, u32[]{:S(2)}) collective-permute-start(bf16[1040,128]{1,0:T(8,128)(2,1)S(1)} %get-tuple-element.19.own_ref), channel_id=1, source_target_pairs={{0,8},{4,12},{16,24},{20,28},{1,9},{5,13},{17,25},{21,29},{2,10},{... | collective-permute-start | bytes 798728 | tf_op jit(solution)/shard_map/ppermute | solution.py:320

commit v8 on v7

--- a/solution.py
+++ b/solution.py
@@ -59,29 +59,24 @@
     return first, docs == first
 
 
-def load_block(query_ref, key_ref, value_ref, doc_ref, q_ref, out_refs, doc_scratch, sems):
+def load_block(key_ref, value_ref, doc_ref, out_ref, doc_scratch, sems):
     rows = key_ref.shape[0]
     doc_copy = pltpu.make_async_copy(doc_ref, doc_scratch, sems.at[0])
     doc_copy.start()
-    query_copy = pltpu.make_async_copy(query_ref, q_ref, sems.at[1])
     copies = []
-    for out_ref in out_refs:
-        for g in range(2 * KV_HEADS):
-            source = key_ref if g < KV_HEADS else value_ref
-            copy = pltpu.make_async_copy(
-                source.at[:, part_of(g % KV_HEADS, HEAD_DIM)],
-                out_ref.at[part_of(g, rows), :],
-                sems.at[2 + len(copies)],
-            )
-            copy.start()
-            copies.append(copy)
-    query_copy.start()
-    copies.append(query_copy)
+    for g in range(2 * KV_HEADS):
+        source = key_ref if g < KV_HEADS else value_ref
+        copy = pltpu.make_async_copy(
+            source.at[:, part_of(g % KV_HEADS, HEAD_DIM)],
+            out_ref.at[part_of(g, rows), :],
+            sems.at[1 + g],
+        )
+        copy.start()
+        copies.append(copy)
     doc_copy.wait()
     docs = jnp.broadcast_to(doc_scratch[...].astype(jnp.float32), (EXTRA, rows))
     start = 2 * KV_HEADS * rows
-    for out_ref in out_refs:
-        out_ref[start : start + EXTRA, :] = docs.astype(jnp.bfloat16)
+    out_ref[start : start + EXTRA, :] = docs.astype(jnp.bfloat16)
     for copy in copies:
         copy.wait()
 
@@ -104,37 +99,24 @@
         devices = 2 * n_seq
         near = [(b, b + 1) for b in range(devices - 1)]
         far = [(b, b + 2) for b in range(devices - 2)]
-        crossing = [p for p in far if p[0] // 2 % 2 == 1]
-        touched = {b for p in crossing for b in p}
-        targets = {p[1] for p in crossing}
-        early = [p for p in near if p[0] not in touched and p[1] not in targets]
-        self.pairs = [
-            crossing + early,
-            [p for p in near if p not in early],
-            [p for p in far if p not in crossing],
-        ]
-        self.senders = sorted({p[0] for p in self.pairs[0]})
-        busy = {b for p in self.pairs[1] for b in p}
+        first = [p for p in near if p[0] % 2 == 0 or p[0] // 2 % 2 == 1]
+        last = [p for p in far if p[0] // 2 % 2 == 0]
+        second = [p for p in near + far if p not in first + last]
+        self.pairs = [first, second, last]
+        self.senders = sorted({p[0] for p in first})
+        busy = {b for p in second for b in p}
         self.idle = [b for b in range(devices) if b not in busy]
-        self.attend_first = [p[1] for p in early if p[1] % 2 == 1]
-
-
-def block_number():
-    return 2 * lax.axis_index("seq") + lax.axis_index("kv")
 
 
 def among(members):
-    block = block_number()
+    block = 2 * lax.axis_index("seq") + lax.axis_index("kv")
     return functools.reduce(jnp.logical_or, [block == b for b in members])
 
 
-def pack_kernel(
-    plan, query_ref, key_ref, value_ref, doc_ref, first_ref, out_ref, q_ref, doc_scratch, sems
-):
+def pack_kernel(plan, key_ref, value_ref, doc_ref, out_ref, doc_scratch, sems):
     @pl.when(among(plan.senders))
     def _():
-        outs = (first_ref, out_ref)
-        load_block(query_ref, key_ref, value_ref, doc_ref, q_ref, outs, doc_scratch, sems)
+        load_block(key_ref, value_ref, doc_ref, out_ref, doc_scratch, sems)
 
 
 def attend_own(q_ref, block_ref, g, bias):
@@ -159,70 +141,78 @@
     return jnp.where((place <= row) & (column(docs) == docs), 0.0, LOWEST)
 
 
-def attend_itself(q_ref, block_ref, gain_ref, beta_ref, summed_ref, stats_ref, gains_ref, beta_copy):
+def attend_itself(
+    query_ref, block_ref, gain_ref, beta_ref, q_ref, summed_ref, stats_ref, gains_ref,
+    beta_scratch, sems,
+):
+    copies = []
+    for g in range(KV_HEADS):
+        wide = part_of(g, GROUPS * HEAD_DIM)
+        copies.append(
+            pltpu.make_async_copy(query_ref.at[:, wide], q_ref.at[:, wide], sems.at[g])
+        )
+        copies[g].start()
+    beta_copy = pltpu.make_async_copy(beta_ref, beta_scratch, sems.at[KV_HEADS])
+    beta_copy.start()
     bias = own_bias(block_docs(block_ref))
     done = lax.axis_index("kv") == 0
+    beta_copy.wait()
+    scaled_gains(beta_scratch, gain_ref, gains_ref)
     for g in range(KV_HEADS):
+        copies[g].wait()
         summed, top, total = attend_own(q_ref, block_ref, g, bias)
-        summed_ref[part_of(g, HEAD_DIM), :] = summed
+        rest = [1.0 - share_of(beta_scratch, g * GROUPS + i) for i in range(GROUPS)]
+        rest = jnp.concatenate(rest, axis=1)
+        summed_ref[part_of(g, HEAD_DIM), :] = summed * jnp.where(done, rest / total, 1.0)
         stats_ref[g : g + 1, :] = top
         stats_ref[KV_HEADS + g : KV_HEADS + g + 1, :] = total
-    beta_copy.wait()
-    for g in range(KV_HEADS):
-        rest = [1.0 - share_of(beta_ref, g * GROUPS + i) for i in range(GROUPS)]
-        rest = jnp.concatenate(rest, axis=1)
         stats_ref[2 * KV_HEADS + g : 2 * KV_HEADS + g + 1, :] = rest
-        scale = rest / stats_ref[KV_HEADS + g : KV_HEADS + g + 1, :]
-        group = part_of(g, HEAD_DIM)
-        summed_ref[group, :] = summed_ref[group, :] * jnp.where(done, scale, 1.0)
-    scaled_gains(beta_ref, gain_ref, gains_ref)
 
 
 def settle_kernel(
-    plan, gain_ref, packed_ref, q_in, beta_ref, query_ref, key_ref, value_ref, doc_ref,
+    plan, gain_ref, packed_ref, query_ref, key_ref, value_ref, doc_ref, beta_ref,
     out_ref, q_ref, summed_ref, stats_ref, gains_ref, beta_scratch, doc_scratch, sems,
 ):
-    beta_copy = pltpu.make_async_copy(beta_ref, beta_scratch, sems.at[2 * KV_HEADS + 2])
-
-    @pl.when(among(plan.idle))
+    sender = among(plan.senders)
+
+    @pl.when(sender)
     def _():
-        beta_copy.start()
-
-    @pl.when(jnp.logical_not(among(plan.senders)))
+        out_ref[...] = packed_ref[...]
+
+    @pl.when(jnp.logical_not(sender))
     def _():
-        outs = (out_ref,)
-        load_block(query_ref, key_ref, value_ref, doc_ref, q_ref, outs, doc_scratch, sems)
+        load_block(key_ref, value_ref, doc_ref, out_ref, doc_scratch, sems)
 
     @pl.when(among(plan.idle))
     def _():
         attend_itself(
-            q_ref, out_ref, gain_ref, beta_scratch, summed_ref, stats_ref, gains_ref, beta_copy
+            query_ref, out_ref, gain_ref, beta_ref, q_ref, summed_ref, stats_ref, gains_ref,
+            beta_scratch, sems,
         )
 
 
 def own_kernel(
-    plan, q_ref, own_ref, gain_ref, beta_ref, summed_in, stats_in, gains_in,
-    summed_ref, stats_ref, gains_ref, beta_scratch, sem,
+    plan, gain_ref, own_ref, query_ref, beta_ref, q_in, summed_in, stats_in, gains_in,
+    q_ref, summed_ref, stats_ref, gains_ref, beta_scratch, sems,
 ):
     @pl.when(jnp.logical_not(among(plan.idle)))
     def _():
-        beta_copy = pltpu.make_async_copy(beta_ref, beta_scratch, sem)
-        beta_copy.start()
         attend_itself(
-            q_ref, own_ref, gain_ref, beta_scratch, summed_ref, stats_ref, gains_ref, beta_copy
-        )
-
-
-def before_kernel(plan, q_ref, own_ref, one_ref, two_ref, stats_ref, summed_in, summed_ref):
-    docs = block_docs(own_ref)
-    rows = docs.shape[1]
-    first, same = first_document(docs)
-
-    def attend(ref):
-        live = suffix(jnp.where(block_docs(ref) == first, 0.0, 1.0))
+            query_ref, own_ref, gain_ref, beta_ref, q_ref, summed_ref, stats_ref, gains_ref,
+            beta_scratch, sems,
+        )
+
+
+def before_kernel(q_ref, own_ref, one_ref, stats_ref, summed_in, summed_ref):
+    @pl.when(lax.axis_index("kv") == 1)
+    def _():
+        docs = block_docs(own_ref)
+        rows = docs.shape[1]
+        first, same = first_document(docs)
+        live = suffix(jnp.where(block_docs(one_ref) == first, 0.0, 1.0))
         bias = jnp.where(live & same, 0.0, LOWEST)
         for g in range(KV_HEADS):
-            scores = dot(block_keys(ref, g), group_queries(q_ref, g), NT)
+            scores = dot(block_keys(one_ref, g), group_queries(q_ref, g), NT)
             weights, factors, scales = [], [], []
             for i in range(GROUPS):
                 cut = part_of(i, rows)
@@ -236,31 +226,21 @@
                 factors.append(factor)
                 scales.append(stats_ref[2 * KV_HEADS + g : 2 * KV_HEADS + g + 1, cut] / total)
                 weights.append(weight.astype(jnp.bfloat16))
-            added = dot(block_values(ref, g), jnp.concatenate(weights, axis=1), TN)
+            added = dot(block_values(one_ref, g), jnp.concatenate(weights, axis=1), TN)
             group = part_of(g, HEAD_DIM)
             summed = summed_ref[group, :] * jnp.concatenate(factors, axis=1) + added
             summed_ref[group, :] = summed * jnp.concatenate(scales, axis=1)
 
-    attend_first = among(plan.attend_first)
-
-    @pl.when(attend_first)
-    def _():
-        attend(one_ref)
-
-    @pl.when((lax.axis_index("kv") == 1) & jnp.logical_not(attend_first))
-    def _():
-        attend(two_ref)
-
 
 def join_kernel(
-    plan, q_ref, own_ref, one_ref, two_ref, three_ref, ready_ref, gains_ref, out_ref, held, sems
+    q_ref, own_ref, one_ref, three_ref, two_ref, ready_ref, gains_ref, out_ref, held, sems
 ):
     docs = block_docs(own_ref)
     rows = docs.shape[1]
     first, same = first_document(docs)
     reads = jnp.where(same, 1.0, 0.0)
     sources = (one_ref, two_ref, three_ref)
-    attended = (among(plan.attend_first), lax.axis_index("kv") == 1, False)
+    attended = (lax.axis_index("kv") == 1, False, False)
     lives = []
     for ref, other in zip(sources, attended):
         others = jnp.where((block_docs(ref) == first) & jnp.logical_not(other), 0.0, 1.0)
@@ -277,12 +257,14 @@
             keys.append(masked.astype(jnp.bfloat16))
             values.append(block_values(ref, g))
         state = dot(jnp.concatenate(values, axis=0), jnp.concatenate(keys, axis=0), TN)
-        q = group_queries(q_ref, g)
         high = state.astype(jnp.bfloat16)
         state = state - high.astype(jnp.float32)
         middle = state.astype(jnp.bfloat16)
         low = (state - middle.astype(jnp.float32)).astype(jnp.bfloat16)
-        recalled = dot(high, q, NT) + (dot(middle, q, NT) + dot(low, q, NT))
+        pieces = dot(jnp.concatenate([high, middle, low], axis=0), group_queries(q_ref, g), NT)
+        recalled = pieces[part_of(0, HEAD_DIM), :] + (
+            pieces[part_of(1, HEAD_DIM), :] + pieces[part_of(2, HEAD_DIM), :]
+        )
         for i in range(GROUPS):
             h, cut = g * GROUPS + i, part_of(i, rows)
             read = recalled[:, cut]
@@ -321,58 +303,56 @@
 
     plan = Plan(n_seq)
     block_shape = jax.ShapeDtypeStruct((deep, HEAD_DIM), jnp.bfloat16)
+    query_shape = jax.ShapeDtypeStruct(queries.shape, queries.dtype)
     stats_shape = jax.ShapeDtypeStruct((4 * KV_HEADS, wide), jnp.float32)
+    results = [query_shape, group_shape, stats_shape, gains_shape]
     doc_scratch = pltpu.VMEM((1, rows), jnp.int32)
     beta_scratch = pltpu.SMEM((HEADS,), jnp.float32)
-    query_shape = jax.ShapeDtypeStruct(queries.shape, queries.dtype)
-    block = (in_hbm(queries), in_hbm(keys), in_hbm(values), in_hbm(docs))
-    first, packed, q = pl.pallas_call(
+    sems = pltpu.SemaphoreType.DMA((2 * KV_HEADS + 1,))
+    block = (in_hbm(keys), in_hbm(values), in_hbm(docs))
+    queries, beta = in_hbm(queries), in_hbm(beta)
+    packed = pl.pallas_call(
         functools.partial(pack_kernel, plan),
-        out_shape=[block_shape] * 2 + [query_shape],
-        in_specs=[hbm] * 4,
-        out_specs=[vmem] * 3,
-        scratch_shapes=[doc_scratch, pltpu.SemaphoreType.DMA((4 * KV_HEADS + 2,))],
+        out_shape=block_shape,
+        in_specs=[hbm] * 3,
+        out_specs=vmem,
+        scratch_shapes=[doc_scratch, sems],
         compiler_params=params,
         cost_estimate=estimate(0.1),
     )(*block)
-    one = send(first, plan.pairs[0])
+    one = send(packed, plan.pairs[0])
     own, q, summed, stats, gains = pl.pallas_call(
         functools.partial(settle_kernel, plan),
-        out_shape=[block_shape, query_shape, group_shape, stats_shape, gains_shape],
-        in_specs=[vmem] * 3 + [hbm] * 5,
+        out_shape=[block_shape] + results,
+        in_specs=[vmem] * 2 + [hbm] * 5,
         out_specs=[vmem] * 5,
-        scratch_shapes=[
-            beta_scratch,
-            doc_scratch,
-            pltpu.SemaphoreType.DMA((2 * KV_HEADS + 3,)),
-        ],
-        input_output_aliases={1: 0, 2: 1},
+        scratch_shapes=[beta_scratch, doc_scratch, sems],
         compiler_params=params,
         cost_estimate=estimate(1.0),
-    )(gain, packed, q, in_hbm(beta), *block)
+    )(gain, packed, queries, *block, beta)
     two = send(own, plan.pairs[1])
     three = send(own, plan.pairs[2])
-    summed, stats, gains = pl.pallas_call(
+    q, summed, stats, gains = pl.pallas_call(
         functools.partial(own_kernel, plan),
-        out_shape=[group_shape, stats_shape, gains_shape],
-        in_specs=[vmem] * 3 + [hbm] + [vmem] * 3,
-        out_specs=[vmem] * 3,
-        scratch_shapes=[beta_scratch, pltpu.SemaphoreType.DMA],
-        input_output_aliases={4: 0, 5: 1, 6: 2},
+        out_shape=results,
+        in_specs=[vmem] * 2 + [hbm] * 2 + [vmem] * 4,
+        out_specs=[vmem] * 4,
+        scratch_shapes=[beta_scratch, sems],
+        input_output_aliases={4: 0, 5: 1, 6: 2, 7: 3},
         compiler_params=params,
         cost_estimate=estimate(1.0),
-    )(q, own, gain, in_hbm(beta), summed, stats, gains)
+    )(gain, own, queries, beta, q, summed, stats, gains)
     ready = pl.pallas_call(
-        functools.partial(before_kernel, plan),
+        before_kernel,
         out_shape=group_shape,
-        in_specs=[vmem] * 6,
+        in_specs=[vmem] * 5,
         out_specs=vmem,
-        input_output_aliases={5: 0},
+        input_output_aliases={4: 0},
         compiler_params=params,
         cost_estimate=estimate(1.0),
-    )(q, own, one, two, stats, summed)
+    )(q, own, one, stats, summed)
     return pl.pallas_call(
-        functools.partial(join_kernel, plan),
+        join_kernel,
         out_shape=jax.ShapeDtypeStruct((rows, HEADS * HEAD_DIM), jnp.float32),
         in_specs=[vmem] * 7,
         out_specs=hbm,
@@ -381,7 +361,7 @@
             pltpu.SemaphoreType.DMA((KV_HEADS,)),
         ],
         compiler_params=params,
-    )(q, own, one, two, three, ready, gains)
+    )(q, own, one, three, two, ready, gains)
 
 
 def carried_in(part, axis, combine, identity):

time: 16.4 us -> 15.8 us (0.963)
  the two profiles are of different devices: /device:TPU:27 before, /device:TPU:1 now
where the time goes in v8:
time: 15.8 us; the launch traced here: 15.5 us
  starting transfers between devices  8.33 us (53%)
  Pallas kernels  6.22 us (39%)
  waiting for transfers between devices  0.92 us (6%)
    ppermute x3, starting transfers between devices, send(): return lax.ppermute(payload, ('seq', 'kv'), pairs)  8.33 us
    pallas_call x1, Pallas kernels, near_device(): pl.pallas_call(functools.partial(own_kernel, plan), out_shape=results, in...  2.9 us
    pallas_call x1, Pallas kernels, near_device(): pl.pallas_call(join_kernel, out_shape=jax.ShapeDtypeStruct((rows, HEADS *...  2.19 us
    pallas_call x1, Pallas kernels, near_device(): pl.pallas_call(functools.partial(pack_kernel, plan), out_shape=block_shap...  0.98 us
    ppermute x3, waiting for transfers between devices, send(): return lax.ppermute(payload, ('seq', 'kv'), pairs)  0.92 us
  transfers between devices with their start and end apart: 3, of which 1 were waited for; matrix products, arithmetic and copies ran while one was open for 0% of the time, Pallas kernels for 20%

profile of v8, /device:TPU:1, one launch (start us, length us, event | category | flops | bytes accessed | tf_op | source)
XLA Modules:
  0.0 15.5 jit_solution(14734098306931862889)
XLA Ops:
  0.0 0.0 copy-start
  0.0 1.0 %shard_map.64.packed_ref = bf16[1040,128]{1,0:T(8,128)(2,1)S(1)} custom-call(bf16[128,512]{1,0:T(8,128)(2,1)} %key_ref.3, bf16[128,512]{1,0:T(8,128)(2,1)} %value_ref.3, s32[1,128]{1,0:T(1,128)} %bitcast.4), custom_call_target="tpu_custom_call" | custom-call | flops 13421772 | bytes 419430 | tf_op jit(solution)/shard_map/pallas_call | solution.py:314
  1.0 4.0 %collective-permute-start = (bf16[1040,128]{1,0:T(8,128)(2,1)S(1)}, bf16[1040,128]{1,0:T(8,128)(2,1)S(1)}, u32[]{:S(2)}, u32[]{:S(2)}) collective-permute-start(bf16[1040,128]{1,0:T(8,128)(2,1)S(1)} %shard_map.64.packed_ref), channel_id=1, source_target_pairs={{0,4},{8,12},{12,16},{16,20},{24,28},{1,5},{9,13},{13,17},{17,21},... | collective-permute-start | bytes 798728 | tf_op jit(solution)/shard_map/ppermute | solution.py:302
  5.0 0.0 copy-done
  5.0 0.1 shard_map.65
  5.1 3.1 %collective-permute-start.2 = (bf16[1040,128]{1,0:T(8,128)(2,1)S(1)}, bf16[1040,128]{1,0:T(8,128)(2,1)S(1)}, u32[]{:S(2)}, u32[]{:S(2)}) collective-permute-start(bf16[1040,128]{1,0:T(8,128)(2,1)S(1)} %get-tuple-element.14.own_ref), channel_id=1, source_target_pairs={{4,8},{20,24},{8,16},{12,20},{5,9},{21,25},{9,17},{13,21},{6,10},{... | collective-permute-start | bytes 798728 | tf_op jit(solution)/shard_map/ppermute | solution.py:302
  8.2 1.3 %collective-permute-start.1 = (bf16[1040,128]{1,0:T(8,128)(2,1)S(1)}, bf16[1040,128]{1,0:T(8,128)(2,1)S(1)}, u32[]{:S(2)}, u32[]{:S(2)}) collective-permute-start(bf16[1040,128]{1,0:T(8,128)(2,1)S(1)} %get-tuple-element.14.own_ref), channel_id=1, source_target_pairs={{0,8},{4,12},{16,24},{20,28},{1,9},{5,13},{17,25},{21,29},{2,10},{... | collective-permute-start | bytes 798728 | tf_op jit(solution)/shard_map/ppermute | solution.py:302
  9.5 2.9 %shard_map.66 = (bf16[128,2048]{1,0:T(8,128)(2,1)S(1)}, f32[512,512]{1,0:T(8,128)S(1)}, f32[16,512]{1,0:T(8,128)S(1)}, f32[2048,128]{1,0:T(8,128)S(1)}) custom-call(f32[16,128]{1,0:T(8,128)S(1)} %bitcast.3, bf16[1040,128]{1,0:T(8,128)(2,1)S(1)} %get-tuple-element.14.own_ref, ...), custom_call_target="tpu_custom_call", output_to_operand_aliasing={{0}: (4, {}), {1}: (5, {}), {2}: (6, {}), {3}: (7, {})} | custom-call | flops 134217728 | bytes 4194304 | tf_op jit(solution)/shard_map/pallas_call | solution.py:335
  12.4 0.0 collective-permute-done.one_ref
  12.4 0.9 %collective-permute-done.2.two_ref = bf16[1040,128]{1,0:T(8,128)(2,1)S(1)} collective-permute-done((bf16[1040,128]{1,0:T(8,128)(2,1)S(1)}, bf16[1040,128]{1,0:T(8,128)(2,1)S(1)}, u32[]{:S(2)}, u32[]{:S(2)}) %collective-permute-start.2) | collective-permute-done | bytes 266272 | tf_op jit(solution)/shard_map/ppermute | solution.py:302
  13.4 0.0 collective-permute-done.1.three_ref
  13.4 2.2 %shard_map.68 = f32[128,2048]{1,0:T(8,128)} custom-call(bf16[128,2048]{1,0:T(8,128)(2,1)S(1)} %get-tuple-element.19.q_ref, bf16[1040,128]{1,0:T(8,128)(2,1)S(1)} %get-tuple-element.14.own_ref, bf16[1040,128]{1,0:T(8,128)(2,1)S(1)} %collective-permute-done.one_ref, bf16[1040,128]{1,0:T(8,128)(2,1)S(1)} %collective-permute-done.1.three_ref, ...), custom_call_target="tpu_custom_call" | custom-call | tf_op jit(solution)/shard_map/pallas_call | solution.py:354
  (1 shorter events, 0.0 us)
Async XLA Ops:
  0.0 5.0 %copy-start = (f32[2048]{0:T(1024)S(1)}, f32[2048]{0:T(1024)}, u32[]{:S(2)}) copy-start(f32[2048]{0:T(1024)} %param.11) | copy-start | bytes 24580
  1.0 11.4 %collective-permute-start = (bf16[1040,128]{1,0:T(8,128)(2,1)S(1)}, bf16[1040,128]{1,0:T(8,128)(2,1)S(1)}, u32[]{:S(2)}, u32[]{:S(2)}) collective-permute-start(bf16[1040,128]{1,0:T(8,128)(2,1)S(1)} %shard_map.64.packed_ref), channel_id=1, source_target_pairs={{0,4},{8,12},{12,16},{16,20},{24,28},{1,5},{9,13},{13,17},{17,21},... | collective-permute-start | bytes 798728 | tf_op jit(solution)/shard_map/ppermute | solution.py:302
  5.1 8.2 %collective-permute-start.2 = (bf16[1040,128]{1,0:T(8,128)(2,1)S(1)}, bf16[1040,128]{1,0:T(8,128)(2,1)S(1)}, u32[]{:S(2)}, u32[]{:S(2)}) collective-permute-start(bf16[1040,128]{1,0:T(8,128)(2,1)S(1)} %get-tuple-element.14.own_ref), channel_id=1, source_target_pairs={{4,8},{20,24},{8,16},{12,20},{5,9},{21,25},{9,17},{13,21},{6,10},{... | collective-permute-start | bytes 798728 | tf_op jit(solution)/shard_map/ppermute | solution.py:302
  8.2 5.2 %collective-permute-start.1 = (bf16[1040,128]{1,0:T(8,128)(2,1)S(1)}, bf16[1040,128]{1,0:T(8,128)(2,1)S(1)}, u32[]{:S(2)}, u32[]{:S(2)}) collective-permute-start(bf16[1040,128]{1,0:T(8,128)(2,1)S(1)} %get-tuple-element.14.own_ref), channel_id=1, source_target_pairs={{0,8},{4,12},{16,24},{20,28},{1,9},{5,13},{17,25},{21,29},{2,10},{... | collective-permute-start | bytes 798728 | tf_op jit(solution)/shard_map/ppermute | solution.py:302

commit v9 on v8

--- a/solution.py
+++ b/solution.py
@@ -19,6 +19,7 @@
 
 NT = (((1,), (1,)), ((), ()))
 TN = (((0,), (0,)), ((), ()))
+NN = (((1,), (0,)), ((), ()))
 
 
 def dot(a, b, dims):
@@ -40,12 +41,6 @@
 
 def share_of(beta_ref, h):
     return 1.0 / (1.0 + jnp.exp(-jnp.full((1, HEAD_DIM), beta_ref[h], jnp.float32)))
-
-
-def scaled_gains(beta_ref, gain_ref, out_ref):
-    for h in range(HEADS):
-        scaled = gain_ref[h : h + 1, :] * share_of(beta_ref, h)
-        out_ref[part_of(h, HEAD_DIM), :] = column(scaled)
 
 
 def suffix(others):
@@ -104,8 +99,8 @@
         second = [p for p in near + far if p not in first + last]
         self.pairs = [first, second, last]
         self.senders = sorted({p[0] for p in first})
-        busy = {b for p in second for b in p}
-        self.idle = [b for b in range(devices) if b not in busy]
+        busy = {p[0] for p in second if p[0] in self.senders} | {p[1] for p in second}
+        self.early = [b for b in range(devices) if b not in busy]
 
 
 def among(members):
@@ -142,38 +137,49 @@
 
 
 def attend_itself(
-    query_ref, block_ref, gain_ref, beta_ref, q_ref, summed_ref, stats_ref, gains_ref,
-    beta_scratch, sems,
+    q_ref, block_ref, gain_ref, beta_ref, beta_copy, ready_ref, summed_ref, stats_ref, gains_ref
 ):
-    copies = []
+    bias = own_bias(block_docs(block_ref))
+    rows = bias.shape[0]
+    done = lax.axis_index("kv") == 0
     for g in range(KV_HEADS):
-        wide = part_of(g, GROUPS * HEAD_DIM)
-        copies.append(
-            pltpu.make_async_copy(query_ref.at[:, wide], q_ref.at[:, wide], sems.at[g])
-        )
-        copies[g].start()
-    beta_copy = pltpu.make_async_copy(beta_ref, beta_scratch, sems.at[KV_HEADS])
-    beta_copy.start()
-    bias = own_bias(block_docs(block_ref))
-    done = lax.axis_index("kv") == 0
-    beta_copy.wait()
-    scaled_gains(beta_scratch, gain_ref, gains_ref)
-    for g in range(KV_HEADS):
-        copies[g].wait()
         summed, top, total = attend_own(q_ref, block_ref, g, bias)
-        rest = [1.0 - share_of(beta_scratch, g * GROUPS + i) for i in range(GROUPS)]
-        rest = jnp.concatenate(rest, axis=1)
-        summed_ref[part_of(g, HEAD_DIM), :] = summed * jnp.where(done, rest / total, 1.0)
-        stats_ref[g : g + 1, :] = top
-        stats_ref[KV_HEADS + g : KV_HEADS + g + 1, :] = total
-        stats_ref[2 * KV_HEADS + g : 2 * KV_HEADS + g + 1, :] = rest
+        if g == 0:
+            beta_copy.wait()
+        shares = [share_of(beta_ref, g * GROUPS + i) for i in range(GROUPS)]
+        rest = jnp.concatenate([1.0 - share for share in shares], axis=1)
+        for i in range(GROUPS):
+            h = g * GROUPS + i
+            gains_ref[h : h + 1, :] = gain_ref[h : h + 1, :] * shares[i]
+
+        @pl.when(done)
+        def _():
+            scaled = summed * (rest / total)
+            for i in range(GROUPS):
+                part = jnp.transpose(scaled[:, part_of(i, rows)])
+                ready_ref[:, part_of(g * GROUPS + i, HEAD_DIM)] = part
+
+        @pl.when(jnp.logical_not(done))
+        def _():
+            summed_ref[part_of(g, HEAD_DIM), :] = summed
+            stats_ref[g : g + 1, :] = top
+            stats_ref[KV_HEADS + g : KV_HEADS + g + 1, :] = total
+            stats_ref[2 * KV_HEADS + g : 2 * KV_HEADS + g + 1, :] = rest
 
 
 def settle_kernel(
     plan, gain_ref, packed_ref, query_ref, key_ref, value_ref, doc_ref, beta_ref,
-    out_ref, q_ref, summed_ref, stats_ref, gains_ref, beta_scratch, doc_scratch, sems,
+    out_ref, ready_ref, summed_ref, stats_ref, gains_ref,
+    q_scratch, beta_scratch, doc_scratch, sems, early_sems,
 ):
-    sender = among(plan.senders)
+    sender, early = among(plan.senders), among(plan.early)
+    query_copy = pltpu.make_async_copy(query_ref, q_scratch, early_sems.at[0])
+    beta_copy = pltpu.make_async_copy(beta_ref, beta_scratch, early_sems.at[1])
+
+    @pl.when(early)
+    def _():
+        query_copy.start()
+        beta_copy.start()
 
     @pl.when(sender)
     def _():
@@ -183,27 +189,30 @@
     def _():
         load_block(key_ref, value_ref, doc_ref, out_ref, doc_scratch, sems)
 
-    @pl.when(among(plan.idle))
-    def _():
+    @pl.when(early)
+    def _():
+        query_copy.wait()
         attend_itself(
-            query_ref, out_ref, gain_ref, beta_ref, q_ref, summed_ref, stats_ref, gains_ref,
-            beta_scratch, sems,
+            q_scratch, out_ref, gain_ref, beta_scratch, beta_copy,
+            ready_ref, summed_ref, stats_ref, gains_ref,
         )
 
 
 def own_kernel(
-    plan, gain_ref, own_ref, query_ref, beta_ref, q_in, summed_in, stats_in, gains_in,
-    q_ref, summed_ref, stats_ref, gains_ref, beta_scratch, sems,
+    plan, q_ref, gain_ref, own_ref, beta_ref, ready_in, summed_in, stats_in, gains_in,
+    ready_ref, summed_ref, stats_ref, gains_ref, beta_scratch, sem,
 ):
-    @pl.when(jnp.logical_not(among(plan.idle)))
-    def _():
+    @pl.when(jnp.logical_not(among(plan.early)))
+    def _():
+        beta_copy = pltpu.make_async_copy(beta_ref, beta_scratch, sem)
+        beta_copy.start()
         attend_itself(
-            query_ref, own_ref, gain_ref, beta_ref, q_ref, summed_ref, stats_ref, gains_ref,
-            beta_scratch, sems,
-        )
-
-
-def before_kernel(q_ref, own_ref, one_ref, stats_ref, summed_in, summed_ref):
+            q_ref, own_ref, gain_ref, beta_scratch, beta_copy,
+            ready_ref, summed_ref, stats_ref, gains_ref,
+        )
+
+
+def before_kernel(q_ref, own_ref, one_ref, stats_ref, summed_ref, ready_in, ready_ref):
     @pl.when(lax.axis_index("kv") == 1)
     def _():
         docs = block_docs(own_ref)
@@ -229,7 +238,10 @@
             added = dot(block_values(one_ref, g), jnp.concatenate(weights, axis=1), TN)
             group = part_of(g, HEAD_DIM)
             summed = summed_ref[group, :] * jnp.concatenate(factors, axis=1) + added
-            summed_ref[group, :] = summed * jnp.concatenate(scales, axis=1)
+            summed = summed * jnp.concatenate(scales, axis=1)
+            for i in range(GROUPS):
+                part = jnp.transpose(summed[:, part_of(i, rows)])
+                ready_ref[:, part_of(g * GROUPS + i, HEAD_DIM)] = part
 
 
 def join_kernel(
@@ -238,7 +250,8 @@
     docs = block_docs(own_ref)
     rows = docs.shape[1]
     first, same = first_document(docs)
-    reads = jnp.where(same, 1.0, 0.0)
+    reads = column(jnp.where(same, 1.0, 0.0))
+    ones = jnp.full((2 * HEAD_DIM, HEAD_DIM), 1.0 / HEAD_DIM, jnp.bfloat16)
     sources = (one_ref, two_ref, three_ref)
     attended = (lax.axis_index("kv") == 1, False, False)
     lives = []
@@ -256,23 +269,24 @@
             masked = jnp.where(live, block_keys(ref, g).astype(jnp.float32), 0.0)
             keys.append(masked.astype(jnp.bfloat16))
             values.append(block_values(ref, g))
-        state = dot(jnp.concatenate(values, axis=0), jnp.concatenate(keys, axis=0), TN)
+        state = dot(jnp.concatenate(keys, axis=0), jnp.concatenate(values, axis=0), TN)
         high = state.astype(jnp.bfloat16)
         state = state - high.astype(jnp.float32)
         middle = state.astype(jnp.bfloat16)
         low = (state - middle.astype(jnp.float32)).astype(jnp.bfloat16)
-        pieces = dot(jnp.concatenate([high, middle, low], axis=0), group_queries(q_ref, g), NT)
-        recalled = pieces[part_of(0, HEAD_DIM), :] + (
-            pieces[part_of(1, HEAD_DIM), :] + pieces[part_of(2, HEAD_DIM), :]
-        )
+        pieces = dot(group_queries(q_ref, g), jnp.concatenate([high, middle, low], axis=1), NN)
+        recalled = pieces[:, part_of(0, HEAD_DIM)] + (
+            pieces[:, part_of(1, HEAD_DIM)] + pieces[:, part_of(2, HEAD_DIM)]
+        )
+        square = recalled * recalled
+        high = square.astype(jnp.bfloat16)
+        low = (square - high.astype(jnp.float32)).astype(jnp.bfloat16)
+        mean = dot(jnp.concatenate([high, low], axis=1), ones, NN)
         for i in range(GROUPS):
             h, cut = g * GROUPS + i, part_of(i, rows)
-            read = recalled[:, cut]
-            square = jnp.sum(read * read, axis=0, keepdims=True) * (1.0 / HEAD_DIM)
-            read = read * (lax.rsqrt(square + 1e-06) * reads)
-            mixed = read * gains_ref[part_of(h, HEAD_DIM), :]
-            mixed = mixed + ready_ref[part_of(g, HEAD_DIM), cut]
-            held[:, part_of(h, HEAD_DIM)] = jnp.transpose(mixed)
+            wide = part_of(h, HEAD_DIM)
+            read = recalled[cut, :] * (lax.rsqrt(mean[cut, :] + 1e-06) * reads)
+            held[:, wide] = read * gains_ref[h : h + 1, :] + ready_ref[:, wide]
         copy(g).start()
     for g in range(KV_HEADS):
         copy(g).wait()
@@ -286,7 +300,6 @@
     params = pltpu.CompilerParams(vmem_limit_bytes=32 * 1024 * 1024)
     wide = GROUPS * rows
     group_shape = jax.ShapeDtypeStruct((KV_HEADS * HEAD_DIM, wide), jnp.float32)
-    gains_shape = jax.ShapeDtypeStruct((HEADS * HEAD_DIM, HEAD_DIM), jnp.float32)
     docs = doc_ids.reshape(1, rows)
     gain = lin_gain.reshape(HEADS, HEAD_DIM)
     deep = 2 * KV_HEADS * rows + EXTRA
@@ -303,14 +316,15 @@
 
     plan = Plan(n_seq)
     block_shape = jax.ShapeDtypeStruct((deep, HEAD_DIM), jnp.bfloat16)
-    query_shape = jax.ShapeDtypeStruct(queries.shape, queries.dtype)
     stats_shape = jax.ShapeDtypeStruct((4 * KV_HEADS, wide), jnp.float32)
-    results = [query_shape, group_shape, stats_shape, gains_shape]
+    out_shape = jax.ShapeDtypeStruct((rows, HEADS * HEAD_DIM), jnp.float32)
+    gains_shape = jax.ShapeDtypeStruct((HEADS, HEAD_DIM), jnp.float32)
+    results = [out_shape, group_shape, stats_shape, gains_shape]
     doc_scratch = pltpu.VMEM((1, rows), jnp.int32)
     beta_scratch = pltpu.SMEM((HEADS,), jnp.float32)
     sems = pltpu.SemaphoreType.DMA((2 * KV_HEADS + 1,))
     block = (in_hbm(keys), in_hbm(values), in_hbm(docs))
-    queries, beta = in_hbm(queries), in_hbm(beta)
+    beta = in_hbm(beta)
     packed = pl.pallas_call(
         functools.partial(pack_kernel, plan),
         out_shape=block_shape,
@@ -321,39 +335,45 @@
         cost_estimate=estimate(0.1),
     )(*block)
     one = send(packed, plan.pairs[0])
-    own, q, summed, stats, gains = pl.pallas_call(
+    own, ready, summed, stats, gains = pl.pallas_call(
         functools.partial(settle_kernel, plan),
         out_shape=[block_shape] + results,
         in_specs=[vmem] * 2 + [hbm] * 5,
         out_specs=[vmem] * 5,
-        scratch_shapes=[beta_scratch, doc_scratch, sems],
+        scratch_shapes=[
+            pltpu.VMEM(queries.shape, queries.dtype),
+            beta_scratch,
+            doc_scratch,
+            sems,
+            pltpu.SemaphoreType.DMA((2,)),
+        ],
         compiler_params=params,
         cost_estimate=estimate(1.0),
-    )(gain, packed, queries, *block, beta)
+    )(gain, packed, in_hbm(queries), *block, beta)
     two = send(own, plan.pairs[1])
     three = send(own, plan.pairs[2])
-    q, summed, stats, gains = pl.pallas_call(
+    ready, summed, stats, gains = pl.pallas_call(
         functools.partial(own_kernel, plan),
         out_shape=results,
-        in_specs=[vmem] * 2 + [hbm] * 2 + [vmem] * 4,
+        in_specs=[vmem] * 3 + [hbm] + [vmem] * 4,
         out_specs=[vmem] * 4,
-        scratch_shapes=[beta_scratch, sems],
+        scratch_shapes=[beta_scratch, pltpu.SemaphoreType.DMA],
         input_output_aliases={4: 0, 5: 1, 6: 2, 7: 3},
         compiler_params=params,
         cost_estimate=estimate(1.0),
-    )(gain, own, queries, beta, q, summed, stats, gains)
+    )(queries, gain, own, beta, ready, summed, stats, gains)
     ready = pl.pallas_call(
         before_kernel,
-        out_shape=group_shape,
-        in_specs=[vmem] * 5,
+        out_shape=out_shape,
+        in_specs=[vmem] * 6,
         out_specs=vmem,
-        input_output_aliases={4: 0},
+        input_output_aliases={5: 0},
         compiler_params=params,
         cost_estimate=estimate(1.0),
-    )(q, own, one, stats, summed)
+    )(queries, own, one, stats, summed, ready)
     return pl.pallas_call(
         join_kernel,
-        out_shape=jax.ShapeDtypeStruct((rows, HEADS * HEAD_DIM), jnp.float32),
+        out_shape=out_shape,
         in_specs=[vmem] * 7,
         out_specs=hbm,
         scratch_shapes=[
@@ -361,7 +381,7 @@
             pltpu.SemaphoreType.DMA((KV_HEADS,)),
         ],
         compiler_params=params,
-    )(q, own, one, three, two, ready, gains)
+    )(queries, own, one, three, two, ready, gains)
 
 
 def carried_in(part, axis, combine, identity):

time: 15.8 us -> 16.2 us (1.025)
  waiting for transfers between devices: 0.92 us -> 1.29 us
    pallas_call x1, Pallas kernels: 2.9 us -> 2.5 us  [near_device(): pl.pallas_call(functools.partial(own_kernel, plan), out_shape=results, in...]
    pallas_call x2, Pallas kernels: 2.21 us -> 2.6 us  [the longest x1 2.58 us: near_device(): pl.pallas_call(join_kernel, out_shape=out_shape, in_specs=[vmem] * 7, out...]
    ppermute x3, waiting for transfers between devices: 0.92 us -> 1.29 us  [send(): return lax.ppermute(payload, ('seq', 'kv'), pairs)]
  transfers between devices with their start and end apart: 3 -> 3, of which waited for: 1 -> 1; matrix products, arithmetic and copies ran while one was open for 0% -> 0% of each run, Pallas kernels for 20% -> 17%
where the time goes in v9:
time: 16.2 us; the launch traced here: 15.9 us
  starting transfers between devices  8.33 us (51%)
  Pallas kernels  6.22 us (38%)
  waiting for transfers between devices  1.29 us (8%)
    ppermute x3, starting transfers between devices, send(): return lax.ppermute(payload, ('seq', 'kv'), pairs)  8.33 us
    pallas_call x1, Pallas kernels, near_device(): pl.pallas_call(join_kernel, out_shape=out_shape, in_specs=[vmem] * 7, out...  2.58 us
    pallas_call x1, Pallas kernels, near_device(): pl.pallas_call(functools.partial(own_kernel, plan), out_shape=results, in...  2.5 us
    ppermute x3, waiting for transfers between devices, send(): return lax.ppermute(payload, ('seq', 'kv'), pairs)  1.29 us
    pallas_call x1, Pallas kernels, near_device(): pl.pallas_call(functools.partial(pack_kernel, plan), out_shape=block_shap...  0.98 us
  transfers between devices with their start and end apart: 3, of which 1 were waited for; matrix products, arithmetic and copies ran while one was open for 0% of the time, Pallas kernels for 17%

profile of v9, /device:TPU:1, one launch (start us, length us, event | category | flops | bytes accessed | tf_op | source)
XLA Modules:
  0.0 15.9 jit_solution(1745828663022825817)
XLA Ops:
  0.0 0.0 copy-start.1
  0.0 1.0 %shard_map.64.packed_ref = bf16[1040,128]{1,0:T(8,128)(2,1)S(1)} custom-call(bf16[128,512]{1,0:T(8,128)(2,1)} %key_ref.3, bf16[128,512]{1,0:T(8,128)(2,1)} %value_ref.3, s32[1,128]{1,0:T(1,128)} %bitcast.4), custom_call_target="tpu_custom_call" | custom-call | flops 13421772 | bytes 419430 | tf_op jit(solution)/shard_map/pallas_call | solution.py:328
  1.0 4.0 %collective-permute-start = (bf16[1040,128]{1,0:T(8,128)(2,1)S(1)}, bf16[1040,128]{1,0:T(8,128)(2,1)S(1)}, u32[]{:S(2)}, u32[]{:S(2)}) collective-permute-start(bf16[1040,128]{1,0:T(8,128)(2,1)S(1)} %shard_map.64.packed_ref), channel_id=1, source_target_pairs={{0,4},{8,12},{12,16},{16,20},{24,28},{1,5},{9,13},{13,17},{17,21},... | collective-permute-start | bytes 798728 | tf_op jit(solution)/shard_map/ppermute | solution.py:315
  5.0 0.0 copy-done.1
  5.0 0.0 copy-start
  5.0 0.1 shard_map.65
  5.1 3.1 %collective-permute-start.2 = (bf16[1040,128]{1,0:T(8,128)(2,1)S(1)}, bf16[1040,128]{1,0:T(8,128)(2,1)S(1)}, u32[]{:S(2)}, u32[]{:S(2)}) collective-permute-start(bf16[1040,128]{1,0:T(8,128)(2,1)S(1)} %get-tuple-element.14.own_ref), channel_id=1, source_target_pairs={{4,8},{20,24},{8,16},{12,20},{5,9},{21,25},{9,17},{13,21},{6,10},{... | collective-permute-start | bytes 798728 | tf_op jit(solution)/shard_map/ppermute | solution.py:315
  8.2 1.3 %collective-permute-start.1 = (bf16[1040,128]{1,0:T(8,128)(2,1)S(1)}, bf16[1040,128]{1,0:T(8,128)(2,1)S(1)}, u32[]{:S(2)}, u32[]{:S(2)}) collective-permute-start(bf16[1040,128]{1,0:T(8,128)(2,1)S(1)} %get-tuple-element.14.own_ref), channel_id=1, source_target_pairs={{0,8},{4,12},{16,24},{20,28},{1,9},{5,13},{17,25},{21,29},{2,10},{... | collective-permute-start | bytes 798728 | tf_op jit(solution)/shard_map/ppermute | solution.py:315
  9.5 0.0 copy-done
  9.5 2.5 %shard_map.66 = (f32[128,2048]{1,0:T(8,128)S(1)}, f32[512,512]{1,0:T(8,128)S(1)}, f32[16,512]{1,0:T(8,128)S(1)}, f32[16,128]{1,0:T(8,128)S(1)}) custom-call(bf16[128,2048]{1,0:T(8,128)(2,1)S(1)} %copy-done, f32[16,128]{1,0:T(8,128)S(1)} %bitcast.3, ...), custom_call_target="tpu_custom_call", output_to_operand_aliasing={{0}: (4, {}), {1}: (5, {}), {2}: (6, {}), {3}: (7, {})} | custom-call | flops 134217728 | bytes 4194304 | tf_op jit(solution)/shard_map/pallas_call | solution.py:355
  12.0 0.0 collective-permute-done.one_ref
  12.1 1.3 %collective-permute-done.2.two_ref = bf16[1040,128]{1,0:T(8,128)(2,1)S(1)} collective-permute-done((bf16[1040,128]{1,0:T(8,128)(2,1)S(1)}, bf16[1040,128]{1,0:T(8,128)(2,1)S(1)}, u32[]{:S(2)}, u32[]{:S(2)}) %collective-permute-start.2) | collective-permute-done | bytes 266272 | tf_op jit(solution)/shard_map/ppermute | solution.py:315
  13.4 0.0 collective-permute-done.1.three_ref
  13.4 2.6 %shard_map.68 = f32[128,2048]{1,0:T(8,128)} custom-call(bf16[128,2048]{1,0:T(8,128)(2,1)S(1)} %copy-done, bf16[1040,128]{1,0:T(8,128)(2,1)S(1)} %get-tuple-element.14.own_ref, bf16[1040,128]{1,0:T(8,128)(2,1)S(1)} %collective-permute-done.one_ref, bf16[1040,128]{1,0:T(8,128)(2,1)S(1)} %collective-permute-done.1.three_ref, ...), custom_call_target="tpu_custom_call" | custom-call | tf_op jit(solution)/shard_map/pallas_call | solution.py:374
  (1 shorter events, 0.0 us)
Async XLA Ops:
  0.0 5.0 %copy-start.1 = (f32[2048]{0:T(1024)S(1)}, f32[2048]{0:T(1024)}, u32[]{:S(2)}) copy-start(f32[2048]{0:T(1024)} %param.11) | copy-start | bytes 24580
  1.0 11.0 %collective-permute-start = (bf16[1040,128]{1,0:T(8,128)(2,1)S(1)}, bf16[1040,128]{1,0:T(8,128)(2,1)S(1)}, u32[]{:S(2)}, u32[]{:S(2)}) collective-permute-start(bf16[1040,128]{1,0:T(8,128)(2,1)S(1)} %shard_map.64.packed_ref), channel_id=1, source_target_pairs={{0,4},{8,12},{12,16},{16,20},{24,28},{1,5},{9,13},{13,17},{17,21},... | collective-permute-start | bytes 798728 | tf_op jit(solution)/shard_map/ppermute | solution.py:315
  5.0 4.5 %copy-start = (bf16[128,2048]{1,0:T(8,128)(2,1)S(1)}, bf16[128,2048]{1,0:T(8,128)(2,1)}, u32[]{:S(2)}) copy-start(bf16[128,2048]{1,0:T(8,128)(2,1)} %q_ref.5) | copy-start | bytes 1572868
  5.1 8.2 %collective-permute-start.2 = (bf16[1040,128]{1,0:T(8,128)(2,1)S(1)}, bf16[1040,128]{1,0:T(8,128)(2,1)S(1)}, u32[]{:S(2)}, u32[]{:S(2)}) collective-permute-start(bf16[1040,128]{1,0:T(8,128)(2,1)S(1)} %get-tuple-element.14.own_ref), channel_id=1, source_target_pairs={{4,8},{20,24},{8,16},{12,20},{5,9},{21,25},{9,17},{13,21},{6,10},{... | collective-permute-start | bytes 798728 | tf_op jit(solution)/shard_map/ppermute | solution.py:315
  8.2 5.1 %collective-permute-start.1 = (bf16[1040,128]{1,0:T(8,128)(2,1)S(1)}, bf16[1040,128]{1,0:T(8,128)(2,1)S(1)}, u32[]{:S(2)}, u32[]{:S(2)}) collective-permute-start(bf16[1040,128]{1,0:T(8,128)(2,1)S(1)} %get-tuple-element.14.own_ref), channel_id=1, source_target_pairs={{0,8},{4,12},{16,24},{20,28},{1,9},{5,13},{17,25},{21,29},{2,10},{... | collective-permute-start | bytes 798728 | tf_op jit(solution)/shard_map/ppermute | solution.py:315

commit v10 on v8

--- a/solution.py
+++ b/solution.py
@@ -74,9 +74,10 @@
         copy.start()
         copies.append(copy)
     doc_copy.wait()
-    docs = jnp.broadcast_to(doc_scratch[...].astype(jnp.float32), (EXTRA, rows))
     start = 2 * KV_HEADS * rows
-    out_ref[start : start + EXTRA, :] = docs.astype(jnp.bfloat16)
+    docs = doc_scratch[...].astype(jnp.float32)
+    docs = jnp.broadcast_to(docs, (out_ref.shape[0] - start, rows))
+    out_ref[start:, :] = docs.astype(jnp.bfloat16)
     for copy in copies:
         copy.wait()
 
@@ -104,8 +105,8 @@
         second = [p for p in near + far if p not in first + last]
         self.pairs = [first, second, last]
         self.senders = sorted({p[0] for p in first})
-        busy = {b for p in second for b in p}
-        self.idle = [b for b in range(devices) if b not in busy]
+        busy = {p[0] for p in second if p[0] in self.senders} | {p[1] for p in second}
+        self.early = [b for b in range(devices) if b not in busy]
 
 
 def among(members):
@@ -142,26 +143,15 @@
 
 
 def attend_itself(
-    query_ref, block_ref, gain_ref, beta_ref, q_ref, summed_ref, stats_ref, gains_ref,
-    beta_scratch, sems,
+    q_ref, block_ref, gain_ref, beta_ref, beta_copy, summed_ref, stats_ref, gains_ref
 ):
-    copies = []
-    for g in range(KV_HEADS):
-        wide = part_of(g, GROUPS * HEAD_DIM)
-        copies.append(
-            pltpu.make_async_copy(query_ref.at[:, wide], q_ref.at[:, wide], sems.at[g])
-        )
-        copies[g].start()
-    beta_copy = pltpu.make_async_copy(beta_ref, beta_scratch, sems.at[KV_HEADS])
-    beta_copy.start()
     bias = own_bias(block_docs(block_ref))
+    results = [attend_own(q_ref, block_ref, g, bias) for g in range(KV_HEADS)]
+    beta_copy.wait()
+    scaled_gains(beta_ref, gain_ref, gains_ref)
     done = lax.axis_index("kv") == 0
-    beta_copy.wait()
-    scaled_gains(beta_scratch, gain_ref, gains_ref)
-    for g in range(KV_HEADS):
-        copies[g].wait()
-        summed, top, total = attend_own(q_ref, block_ref, g, bias)
-        rest = [1.0 - share_of(beta_scratch, g * GROUPS + i) for i in range(GROUPS)]
+    for g, (summed, top, total) in enumerate(results):
+        rest = [1.0 - share_of(beta_ref, g * GROUPS + i) for i in range(GROUPS)]
         rest = jnp.concatenate(rest, axis=1)
         summed_ref[part_of(g, HEAD_DIM), :] = summed * jnp.where(done, rest / total, 1.0)
         stats_ref[g : g + 1, :] = top
@@ -171,44 +161,73 @@
 
 def settle_kernel(
     plan, gain_ref, packed_ref, query_ref, key_ref, value_ref, doc_ref, beta_ref,
-    out_ref, q_ref, summed_ref, stats_ref, gains_ref, beta_scratch, doc_scratch, sems,
+    second_ref, own_ref, summed_ref, stats_ref, gains_ref,
+    q_scratch, beta_scratch, doc_scratch, sems, early_sems,
 ):
-    sender = among(plan.senders)
+    sender, early = among(plan.senders), among(plan.early)
+    query_copy = pltpu.make_async_copy(query_ref, q_scratch, early_sems.at[0])
+    beta_copy = pltpu.make_async_copy(beta_ref, beta_scratch, early_sems.at[1])
+    deep = own_ref.shape[0]
+
+    @pl.when(early)
+    def _():
+        query_copy.start()
+        beta_copy.start()
 
     @pl.when(sender)
     def _():
-        out_ref[...] = packed_ref[...]
+        own_ref[...] = packed_ref[0:deep, :]
 
     @pl.when(jnp.logical_not(sender))
     def _():
-        load_block(key_ref, value_ref, doc_ref, out_ref, doc_scratch, sems)
-
-    @pl.when(among(plan.idle))
-    def _():
+        load_block(key_ref, value_ref, doc_ref, own_ref, doc_scratch, sems)
+
+    second_ref[0:deep, :] = own_ref[...]
+    second_ref[deep:, :] = jnp.zeros((EXTRA, HEAD_DIM), jnp.bfloat16)
+
+    @pl.when(early)
+    def _():
+        query_copy.wait()
         attend_itself(
-            query_ref, out_ref, gain_ref, beta_ref, q_ref, summed_ref, stats_ref, gains_ref,
-            beta_scratch, sems,
+            q_scratch, own_ref, gain_ref, beta_scratch, beta_copy,
+            summed_ref, stats_ref, gains_ref,
         )
 
 
 def own_kernel(
-    plan, gain_ref, own_ref, query_ref, beta_ref, q_in, summed_in, stats_in, gains_in,
-    q_ref, summed_ref, stats_ref, gains_ref, beta_scratch, sems,
+    plan, q_ref, gain_ref, own_ref, beta_ref, summed_in, stats_in, gains_in,
+    summed_ref, stats_ref, gains_ref, beta_scratch, sem,
 ):
-    @pl.when(jnp.logical_not(among(plan.idle)))
-    def _():
+    @pl.when(jnp.logical_not(among(plan.early)))
+    def _():
+        beta_copy = pltpu.make_async_copy(beta_ref, beta_scratch, sem)
+        beta_copy.start()
         attend_itself(
-            query_ref, own_ref, gain_ref, beta_ref, q_ref, summed_ref, stats_ref, gains_ref,
-            beta_scratch, sems,
-        )
-
-
-def before_kernel(q_ref, own_ref, one_ref, stats_ref, summed_in, summed_ref):
+            q_ref, own_ref, gain_ref, beta_scratch, beta_copy, summed_ref, stats_ref, gains_ref
+        )
+
+
+def memory_state(ref, first, g):
+    live = suffix(jnp.where(block_docs(ref) == first, 0.0, 1.0))
+    keys = jnp.where(live, block_keys(ref, g).astype(jnp.float32), 0.0).astype(jnp.bfloat16)
+    return dot(block_values(ref, g), keys, TN)
+
+
+def before_kernel(
+    q_ref, own_ref, one_ref, three_ref, stats_ref, summed_in, state_ref, summed_ref
+):
+    docs = block_docs(own_ref)
+    rows = docs.shape[1]
+    first, same = first_document(docs)
+
+    @pl.when(lax.axis_index("kv") == 0)
+    def _():
+        for g in range(KV_HEADS):
+            state = memory_state(one_ref, first, g) + memory_state(three_ref, first, g)
+            state_ref[part_of(g, HEAD_DIM), :] = state
+
     @pl.when(lax.axis_index("kv") == 1)
     def _():
-        docs = block_docs(own_ref)
-        rows = docs.shape[1]
-        first, same = first_document(docs)
         live = suffix(jnp.where(block_docs(one_ref) == first, 0.0, 1.0))
         bias = jnp.where(live & same, 0.0, LOWEST)
         for g in range(KV_HEADS):
@@ -230,40 +249,31 @@
             group = part_of(g, HEAD_DIM)
             summed = summed_ref[group, :] * jnp.concatenate(factors, axis=1) + added
             summed_ref[group, :] = summed * jnp.concatenate(scales, axis=1)
+            state_ref[group, :] = memory_state(three_ref, first, g)
 
 
 def join_kernel(
-    q_ref, own_ref, one_ref, three_ref, two_ref, ready_ref, gains_ref, out_ref, held, sems
+    q_ref, own_ref, two_ref, state_ref, ready_ref, gains_ref, out_ref, held, sems
 ):
     docs = block_docs(own_ref)
     rows = docs.shape[1]
     first, same = first_document(docs)
     reads = jnp.where(same, 1.0, 0.0)
-    sources = (one_ref, two_ref, three_ref)
-    attended = (lax.axis_index("kv") == 1, False, False)
-    lives = []
-    for ref, other in zip(sources, attended):
-        others = jnp.where((block_docs(ref) == first) & jnp.logical_not(other), 0.0, 1.0)
-        lives.append(suffix(others))
-
-    def copy(g):
-        wide = part_of(g, GROUPS * HEAD_DIM)
-        return pltpu.make_async_copy(held.at[:, wide], out_ref.at[:, wide], sems.at[g])
-
-    for g in range(KV_HEADS):
-        keys, values = [], []
-        for ref, live in zip(sources, lives):
-            masked = jnp.where(live, block_keys(ref, g).astype(jnp.float32), 0.0)
-            keys.append(masked.astype(jnp.bfloat16))
-            values.append(block_values(ref, g))
-        state = dot(jnp.concatenate(values, axis=0), jnp.concatenate(keys, axis=0), TN)
+    groups = range(KV_HEADS)
+    states = [state_ref[part_of(g, HEAD_DIM), :] + memory_state(two_ref, first, g) for g in groups]
+    pieces = []
+    for state in states:
         high = state.astype(jnp.bfloat16)
         state = state - high.astype(jnp.float32)
         middle = state.astype(jnp.bfloat16)
         low = (state - middle.astype(jnp.float32)).astype(jnp.bfloat16)
-        pieces = dot(jnp.concatenate([high, middle, low], axis=0), group_queries(q_ref, g), NT)
-        recalled = pieces[part_of(0, HEAD_DIM), :] + (
-            pieces[part_of(1, HEAD_DIM), :] + pieces[part_of(2, HEAD_DIM), :]
+        pieces.append(jnp.concatenate([high, middle, low], axis=0))
+    products = [dot(pieces[g], group_queries(q_ref, g), NT) for g in groups]
+
+    copies = []
+    for g in groups:
+        recalled = products[g][part_of(0, HEAD_DIM), :] + (
+            products[g][part_of(1, HEAD_DIM), :] + products[g][part_of(2, HEAD_DIM), :]
         )
         for i in range(GROUPS):
             h, cut = g * GROUPS + i, part_of(i, rows)
@@ -273,9 +283,13 @@
             mixed = read * gains_ref[part_of(h, HEAD_DIM), :]
             mixed = mixed + ready_ref[part_of(g, HEAD_DIM), cut]
             held[:, part_of(h, HEAD_DIM)] = jnp.transpose(mixed)
-        copy(g).start()
-    for g in range(KV_HEADS):
-        copy(g).wait()
+        wide = part_of(g, GROUPS * HEAD_DIM)
+        copies.append(
+            pltpu.make_async_copy(held.at[:, wide], out_ref.at[:, wide], sems.at[g])
+        )
+        copies[g].start()
+    for copy in copies:
+        copy.wait()
 
 
 def near_device(n_seq, queries, keys, values, doc_ids, beta, lin_gain):
@@ -303,17 +317,18 @@
 
     plan = Plan(n_seq)
     block_shape = jax.ShapeDtypeStruct((deep, HEAD_DIM), jnp.bfloat16)
-    query_shape = jax.ShapeDtypeStruct(queries.shape, queries.dtype)
+    longer_shape = jax.ShapeDtypeStruct((deep + EXTRA, HEAD_DIM), jnp.bfloat16)
     stats_shape = jax.ShapeDtypeStruct((4 * KV_HEADS, wide), jnp.float32)
-    results = [query_shape, group_shape, stats_shape, gains_shape]
+    state_shape = jax.ShapeDtypeStruct((KV_HEADS * HEAD_DIM, HEAD_DIM), jnp.float32)
+    results = [group_shape, stats_shape, gains_shape]
     doc_scratch = pltpu.VMEM((1, rows), jnp.int32)
     beta_scratch = pltpu.SMEM((HEADS,), jnp.float32)
     sems = pltpu.SemaphoreType.DMA((2 * KV_HEADS + 1,))
     block = (in_hbm(keys), in_hbm(values), in_hbm(docs))
-    queries, beta = in_hbm(queries), in_hbm(beta)
+    beta = in_hbm(beta)
     packed = pl.pallas_call(
         functools.partial(pack_kernel, plan),
-        out_shape=block_shape,
+        out_shape=longer_shape,
         in_specs=[hbm] * 3,
         out_specs=vmem,
         scratch_shapes=[doc_scratch, sems],
@@ -321,47 +336,52 @@
         cost_estimate=estimate(0.1),
     )(*block)
     one = send(packed, plan.pairs[0])
-    own, q, summed, stats, gains = pl.pallas_call(
+    second, own, summed, stats, gains = pl.pallas_call(
         functools.partial(settle_kernel, plan),
-        out_shape=[block_shape] + results,
+        out_shape=[longer_shape, block_shape] + results,
         in_specs=[vmem] * 2 + [hbm] * 5,
         out_specs=[vmem] * 5,
-        scratch_shapes=[beta_scratch, doc_scratch, sems],
+        scratch_shapes=[
+            pltpu.VMEM(queries.shape, queries.dtype),
+            beta_scratch,
+            doc_scratch,
+            sems,
+            pltpu.SemaphoreType.DMA((2,)),
+        ],
         compiler_params=params,
         cost_estimate=estimate(1.0),
-    )(gain, packed, queries, *block, beta)
-    two = send(own, plan.pairs[1])
+    )(gain, packed, in_hbm(queries), *block, beta)
+    two = send(second, plan.pairs[1])
     three = send(own, plan.pairs[2])
-    q, summed, stats, gains = pl.pallas_call(
+    summed, stats, gains = pl.pallas_call(
         functools.partial(own_kernel, plan),
         out_shape=results,
-        in_specs=[vmem] * 2 + [hbm] * 2 + [vmem] * 4,
-        out_specs=[vmem] * 4,
-        scratch_shapes=[beta_scratch, sems],
-        input_output_aliases={4: 0, 5: 1, 6: 2, 7: 3},
+        in_specs=[vmem] * 3 + [hbm] + [vmem] * 3,
+        out_specs=[vmem] * 3,
+        scratch_shapes=[beta_scratch, pltpu.SemaphoreType.DMA],
+        input_output_aliases={4: 0, 5: 1, 6: 2},
         compiler_params=params,
         cost_estimate=estimate(1.0),
-    )(gain, own, queries, beta, q, summed, stats, gains)
-    ready = pl.pallas_call(
+    )(queries, gain, own, beta, summed, stats, gains)
+    state, ready = pl.pallas_call(
         before_kernel,
-        out_shape=group_shape,
-        in_specs=[vmem] * 5,
-        out_specs=vmem,
-        input_output_aliases={4: 0},
+        out_shape=[state_shape, group_shape],
+        in_specs=[vmem] * 6,
+        out_specs=[vmem] * 2,
+        input_output_aliases={5: 1},
         compiler_params=params,
-        cost_estimate=estimate(1.0),
-    )(q, own, one, stats, summed)
+    )(queries, own, one, three, stats, summed)
     return pl.pallas_call(
         join_kernel,
         out_shape=jax.ShapeDtypeStruct((rows, HEADS * HEAD_DIM), jnp.float32),
-        in_specs=[vmem] * 7,
+        in_specs=[vmem] * 6,
         out_specs=hbm,
         scratch_shapes=[
             pltpu.VMEM((rows, HEADS * HEAD_DIM), jnp.float32),
             pltpu.SemaphoreType.DMA((KV_HEADS,)),
         ],
         compiler_params=params,
-    )(q, own, one, three, two, ready, gains)
+    )(queries, own, two, state, ready, gains)
 
 
 def carried_in(part, axis, combine, identity):

time: 15.8 us -> 15.5 us (0.981)
  Pallas kernels: 6.22 us -> 5.15 us
  waiting for transfers between devices: 0.92 us -> 1.62 us
    pallas_call x1, Pallas kernels: 2.9 us -> 1.88 us  [near_device(): pl.pallas_call(functools.partial(own_kernel, plan), out_shape=results, in...]
    ppermute x3, waiting for transfers between devices: 0.92 us -> 1.62 us  [send(): return lax.ppermute(payload, ('seq', 'kv'), pairs)]
    pallas_call x1, Pallas kernels: 2.19 us -> 1.76 us  [near_device(): pl.pallas_call(join_kernel, out_shape=jax.ShapeDtypeStruct((rows, HEADS *...]
    pallas_call x3, Pallas kernels: 1.12 us -> 1.52 us  [the longest x1 0.98 us: near_device(): pl.pallas_call(functools.partial(pack_kernel, plan), out_shape=longer_sha...]
  transfers between devices with their start and end apart: 3 -> 3, of which waited for: 1 -> 2; matrix products, arithmetic and copies ran while one was open for 0% -> 0% of each run, Pallas kernels for 20% -> 16%
where the time goes in v10:
time: 15.5 us; the launch traced here: 15.2 us
  starting transfers between devices  8.33 us (54%)
  Pallas kernels  5.15 us (33%)
  waiting for transfers between devices  1.62 us (10%)
    ppermute x3, starting transfers between devices, send(): return lax.ppermute(payload, ('seq', 'kv'), pairs)  8.33 us
    pallas_call x1, Pallas kernels, near_device(): pl.pallas_call(functools.partial(own_kernel, plan), out_shape=results, in...  1.88 us
    pallas_call x1, Pallas kernels, near_device(): pl.pallas_call(join_kernel, out_shape=jax.ShapeDtypeStruct((rows, HEADS *...  1.76 us
    ppermute x3, waiting for transfers between devices, send(): return lax.ppermute(payload, ('seq', 'kv'), pairs)  1.62 us
    pallas_call x1, Pallas kernels, near_device(): pl.pallas_call(functools.partial(pack_kernel, plan), out_shape=longer_sha...  0.98 us
    pallas_call x1, Pallas kernels, near_device(): pl.pallas_call(before_kernel, out_shape=[state_shape, group_shape], in_sp...  0.38 us
  transfers between devices with their start and end apart: 3, of which 2 were waited for; matrix products, arithmetic and copies ran while one was open for 0% of the time, Pallas kernels for 16%

profile of v10, /device:TPU:1, one launch (start us, length us, event | category | flops | bytes accessed | tf_op | source)
XLA Modules:
  0.0 15.2 jit_solution(6816698006653559522)
XLA Ops:
  0.0 0.0 copy-start.1
  0.0 1.0 %shard_map.64.packed_ref = bf16[1056,128]{1,0:T(8,128)(2,1)S(1)} custom-call(bf16[128,512]{1,0:T(8,128)(2,1)} %key_ref.3, bf16[128,512]{1,0:T(8,128)(2,1)} %value_ref.3, s32[1,128]{1,0:T(1,128)} %bitcast.4), custom_call_target="tpu_custom_call" | custom-call | flops 13421772 | bytes 419430 | tf_op jit(solution)/shard_map/pallas_call | solution.py:329
  1.0 4.0 %collective-permute-start.1 = (bf16[1056,128]{1,0:T(8,128)(2,1)S(1)}, bf16[1056,128]{1,0:T(8,128)(2,1)S(1)}, u32[]{:S(2)}, u32[]{:S(2)}) collective-permute-start(bf16[1056,128]{1,0:T(8,128)(2,1)S(1)} %shard_map.64.packed_ref), channel_id=1, source_target_pairs={{0,4},{8,12},{12,16},{16,20},{24,28},{1,5},{9,13},{13,17},{17,21},... | collective-permute-start | bytes 811016 | tf_op jit(solution)/shard_map/ppermute | solution.py:316
  5.0 0.0 copy-done.1
  5.0 0.0 copy-start
  5.0 0.2 %shard_map.65 = (bf16[1056,128]{1,0:T(8,128)(2,1)S(1)}, bf16[1040,128]{1,0:T(8,128)(2,1)S(1)}, f32[512,512]{1,0:T(8,128)S(1)}, f32[16,512]{1,0:T(8,128)S(1)}, f32[2048,128]{1,0:T(8,128)S(1)}) custom-call(f32[16,128]{1,0:T(8,128)S(1)} %bitcast.2, bf16[1056,128]{1,0:T(8,128)(2,1)S(1)} %shard_map.64.packed_ref, bf16[128,2048]{1,0:T(8,128)(2,1)} %q_ref.5, ...), custom_call_target="tpu_custom_call" | custom-call | flops 134217728 | bytes 4194304 | tf_op jit(solution)/shard_map/pallas_call | solution.py:339
  5.1 3.1 %collective-permute-start = (bf16[1056,128]{1,0:T(8,128)(2,1)S(1)}, bf16[1056,128]{1,0:T(8,128)(2,1)S(1)}, u32[]{:S(2)}, u32[]{:S(2)}) collective-permute-start(bf16[1056,128]{1,0:T(8,128)(2,1)S(1)} %get-tuple-element.16), channel_id=1, source_target_pairs={{4,8},{20,24},{8,16},{12,20},{5,9},{21,25},{9,17},{13,21},{6,10},{... | collective-permute-start | bytes 811016 | tf_op jit(solution)/shard_map/ppermute | solution.py:316
  8.2 1.3 %collective-permute-start.2 = (bf16[1040,128]{1,0:T(8,128)(2,1)S(1)}, bf16[1040,128]{1,0:T(8,128)(2,1)S(1)}, u32[]{:S(2)}, u32[]{:S(2)}) collective-permute-start(bf16[1040,128]{1,0:T(8,128)(2,1)S(1)} %get-tuple-element.15.own_ref), channel_id=1, source_target_pairs={{0,8},{4,12},{16,24},{20,28},{1,9},{5,13},{17,25},{21,29},{2,10},{... | collective-permute-start | bytes 798728 | tf_op jit(solution)/shard_map/ppermute | solution.py:316
  9.5 0.0 copy-done
  9.5 1.9 %shard_map.66 = (f32[512,512]{1,0:T(8,128)S(1)}, f32[16,512]{1,0:T(8,128)S(1)}, f32[2048,128]{1,0:T(8,128)S(1)}) custom-call(bf16[128,2048]{1,0:T(8,128)(2,1)S(1)} %copy-done, f32[16,128]{1,0:T(8,128)S(1)} %bitcast.3, bf16[1040,128]{1,0:T(8,128)(2,1)S(1)} %get-tuple-element.15.own_ref, ...), custom_call_target="tpu_custom_call", output_to_operand_aliasing={{0}: (4, {}), {1}: (5, {}), {2}: (6, {})} | custom-call | flops 134217728 | bytes 4194304 | tf_op jit(solution)/shard_map/pallas_call | solution.py:356
  11.4 0.2 %collective-permute-done.2.three_ref = bf16[1040,128]{1,0:T(8,128)(2,1)S(1)} collective-permute-done((bf16[1040,128]{1,0:T(8,128)(2,1)S(1)}, bf16[1040,128]{1,0:T(8,128)(2,1)S(1)}, u32[]{:S(2)}, u32[]{:S(2)}) %collective-permute-start.2) | collective-permute-done | bytes 266272 | tf_op jit(solution)/shard_map/ppermute | solution.py:316
  11.7 0.0 collective-permute-done.1.one_ref
  11.7 0.4 %shard_map.67 = (f32[512,128]{1,0:T(8,128)S(1)}, f32[512,512]{1,0:T(8,128)S(1)}) custom-call(bf16[128,2048]{1,0:T(8,128)(2,1)S(1)} %copy-done, bf16[1040,128]{1,0:T(8,128)(2,1)S(1)} %get-tuple-element.15.own_ref, bf16[1056,128]{1,0:T(8,128)(2,1)S(1)} %collective-permute-done.1.one_ref, ...), custom_call_target="tpu_custom_call", output_to_operand_aliasing={{1}: (5, {})} | custom-call | tf_op jit(solution)/shard_map/pallas_call | solution.py:366
  12.1 1.4 %collective-permute-done.two_ref = bf16[1056,128]{1,0:T(8,128)(2,1)S(1)} collective-permute-done((bf16[1056,128]{1,0:T(8,128)(2,1)S(1)}, bf16[1056,128]{1,0:T(8,128)(2,1)S(1)}, u32[]{:S(2)}, u32[]{:S(2)}) %collective-permute-start) | collective-permute-done | bytes 270368 | tf_op jit(solution)/shard_map/ppermute | solution.py:316
  13.4 1.8 %shard_map.68 = f32[128,2048]{1,0:T(8,128)} custom-call(bf16[128,2048]{1,0:T(8,128)(2,1)S(1)} %copy-done, bf16[1040,128]{1,0:T(8,128)(2,1)S(1)} %get-tuple-element.15.own_ref, bf16[1056,128]{1,0:T(8,128)(2,1)S(1)} %collective-permute-done.two_ref, f32[512,128]{1,0:T(8,128)S(1)} %get-tuple-element.22.state_ref, f32[512,512]{1,0:T(8,128)S(1)} %get-tuple-element.23.ready_ref, ...), custom_call_target="tpu_custom_call" | custom-call | tf_op jit(solution)/shard_map/pallas_call | solution.py:374
Async XLA Ops:
  0.0 5.0 %copy-start.1 = (f32[2048]{0:T(1024)S(1)}, f32[2048]{0:T(1024)}, u32[]{:S(2)}) copy-start(f32[2048]{0:T(1024)} %param.11) | copy-start | bytes 24580
  1.0 10.7 %collective-permute-start.1 = (bf16[1056,128]{1,0:T(8,128)(2,1)S(1)}, bf16[1056,128]{1,0:T(8,128)(2,1)S(1)}, u32[]{:S(2)}, u32[]{:S(2)}) collective-permute-start(bf16[1056,128]{1,0:T(8,128)(2,1)S(1)} %shard_map.64.packed_ref), channel_id=1, source_target_pairs={{0,4},{8,12},{12,16},{16,20},{24,28},{1,5},{9,13},{13,17},{17,21},... | collective-permute-start | bytes 811016 | tf_op jit(solution)/shard_map/ppermute | solution.py:316
  5.0 4.6 %copy-start = (bf16[128,2048]{1,0:T(8,128)(2,1)S(1)}, bf16[128,2048]{1,0:T(8,128)(2,1)}, u32[]{:S(2)}) copy-start(bf16[128,2048]{1,0:T(8,128)(2,1)} %q_ref.5) | copy-start | bytes 1572868
  5.1 8.3 %collective-permute-start = (bf16[1056,128]{1,0:T(8,128)(2,1)S(1)}, bf16[1056,128]{1,0:T(8,128)(2,1)S(1)}, u32[]{:S(2)}, u32[]{:S(2)}) collective-permute-start(bf16[1056,128]{1,0:T(8,128)(2,1)S(1)} %get-tuple-element.16), channel_id=1, source_target_pairs={{4,8},{20,24},{8,16},{12,20},{5,9},{21,25},{9,17},{13,21},{6,10},{... | collective-permute-start | bytes 811016 | tf_op jit(solution)/shard_map/ppermute | solution.py:316
  8.2 3.4 %collective-permute-start.2 = (bf16[1040,128]{1,0:T(8,128)(2,1)S(1)}, bf16[1040,128]{1,0:T(8,128)(2,1)S(1)}, u32[]{:S(2)}, u32[]{:S(2)}) collective-permute-start(bf16[1040,128]{1,0:T(8,128)(2,1)S(1)} %get-tuple-element.15.own_ref), channel_id=1, source_target_pairs={{0,8},{4,12},{16,24},{20,28},{1,9},{5,13},{17,25},{21,29},{2,10},{... | collective-permute-start | bytes 798728 | tf_op jit(solution)/shard_map/ppermute | solution.py:316

commit v11 on v10

--- a/solution.py
+++ b/solution.py
@@ -100,13 +100,14 @@
         devices = 2 * n_seq
         near = [(b, b + 1) for b in range(devices - 1)]
         far = [(b, b + 2) for b in range(devices - 2)]
-        first = [p for p in near if p[0] % 2 == 0 or p[0] // 2 % 2 == 1]
+        first = [p for p in near if p[0] % 2 == 0 or p[0] // 2 % 2 == 1 or p[0] == 1]
         last = [p for p in far if p[0] // 2 % 2 == 0]
         second = [p for p in near + far if p not in first + last]
         self.pairs = [first, second, last]
         self.senders = sorted({p[0] for p in first})
-        busy = {p[0] for p in second if p[0] in self.senders} | {p[1] for p in second}
+        busy = {b for p in second for b in p}
         self.early = [b for b in range(devices) if b not in busy]
+        self.late = sorted({p[1] for p in second})
 
 
 def among(members):
@@ -213,54 +214,14 @@
     return dot(block_values(ref, g), keys, TN)
 
 
-def before_kernel(
-    q_ref, own_ref, one_ref, three_ref, stats_ref, summed_in, state_ref, summed_ref
-):
-    docs = block_docs(own_ref)
-    rows = docs.shape[1]
-    first, same = first_document(docs)
-
-    @pl.when(lax.axis_index("kv") == 0)
-    def _():
-        for g in range(KV_HEADS):
-            state = memory_state(one_ref, first, g) + memory_state(three_ref, first, g)
-            state_ref[part_of(g, HEAD_DIM), :] = state
-
-    @pl.when(lax.axis_index("kv") == 1)
-    def _():
-        live = suffix(jnp.where(block_docs(one_ref) == first, 0.0, 1.0))
-        bias = jnp.where(live & same, 0.0, LOWEST)
-        for g in range(KV_HEADS):
-            scores = dot(block_keys(one_ref, g), group_queries(q_ref, g), NT)
-            weights, factors, scales = [], [], []
-            for i in range(GROUPS):
-                cut = part_of(i, rows)
-                masked = scores[:, cut] * SCALE + bias
-                top_own = stats_ref[g : g + 1, cut]
-                top = jnp.maximum(jnp.max(masked, axis=0, keepdims=True), top_own)
-                weight = jnp.exp2(masked - top)
-                factor = jnp.exp2(top_own - top)
-                total = stats_ref[KV_HEADS + g : KV_HEADS + g + 1, cut] * factor
-                total = total + jnp.sum(weight, axis=0, keepdims=True)
-                factors.append(factor)
-                scales.append(stats_ref[2 * KV_HEADS + g : 2 * KV_HEADS + g + 1, cut] / total)
-                weights.append(weight.astype(jnp.bfloat16))
-            added = dot(block_values(one_ref, g), jnp.concatenate(weights, axis=1), TN)
-            group = part_of(g, HEAD_DIM)
-            summed = summed_ref[group, :] * jnp.concatenate(factors, axis=1) + added
-            summed_ref[group, :] = summed * jnp.concatenate(scales, axis=1)
-            state_ref[group, :] = memory_state(three_ref, first, g)
-
-
-def join_kernel(
-    q_ref, own_ref, two_ref, state_ref, ready_ref, gains_ref, out_ref, held, sems
-):
-    docs = block_docs(own_ref)
-    rows = docs.shape[1]
-    first, same = first_document(docs)
-    reads = jnp.where(same, 1.0, 0.0)
-    groups = range(KV_HEADS)
-    states = [state_ref[part_of(g, HEAD_DIM), :] + memory_state(two_ref, first, g) for g in groups]
+def memory_states(refs, first):
+    return [
+        functools.reduce(jnp.add, [memory_state(ref, first, g) for ref in refs])
+        for g in range(KV_HEADS)
+    ]
+
+
+def read_memory(states, q_ref, gains_ref, reads):
     pieces = []
     for state in states:
         high = state.astype(jnp.bfloat16)
@@ -268,28 +229,132 @@
         middle = state.astype(jnp.bfloat16)
         low = (state - middle.astype(jnp.float32)).astype(jnp.bfloat16)
         pieces.append(jnp.concatenate([high, middle, low], axis=0))
-    products = [dot(pieces[g], group_queries(q_ref, g), NT) for g in groups]
-
-    copies = []
-    for g in groups:
+    products = [dot(pieces[g], group_queries(q_ref, g), NT) for g in range(KV_HEADS)]
+    rows = q_ref.shape[0]
+    heads = []
+    for g in range(KV_HEADS):
         recalled = products[g][part_of(0, HEAD_DIM), :] + (
             products[g][part_of(1, HEAD_DIM), :] + products[g][part_of(2, HEAD_DIM), :]
         )
         for i in range(GROUPS):
-            h, cut = g * GROUPS + i, part_of(i, rows)
-            read = recalled[:, cut]
+            read = recalled[:, part_of(i, rows)]
             square = jnp.sum(read * read, axis=0, keepdims=True) * (1.0 / HEAD_DIM)
             read = read * (lax.rsqrt(square + 1e-06) * reads)
-            mixed = read * gains_ref[part_of(h, HEAD_DIM), :]
-            mixed = mixed + ready_ref[part_of(g, HEAD_DIM), cut]
-            held[:, part_of(h, HEAD_DIM)] = jnp.transpose(mixed)
+            heads.append(read * gains_ref[part_of(g * GROUPS + i, HEAD_DIM), :])
+    return heads
+
+
+def attend_before(q_ref, one_ref, stats_ref, summed_ref, first, same):
+    rows = q_ref.shape[0]
+    live = suffix(jnp.where(block_docs(one_ref) == first, 0.0, 1.0))
+    bias = jnp.where(live & same, 0.0, LOWEST)
+    results = []
+    for g in range(KV_HEADS):
+        scores = dot(block_keys(one_ref, g), group_queries(q_ref, g), NT)
+        weights, factors, scales = [], [], []
+        for i in range(GROUPS):
+            cut = part_of(i, rows)
+            masked = scores[:, cut] * SCALE + bias
+            top_own = stats_ref[g : g + 1, cut]
+            top = jnp.maximum(jnp.max(masked, axis=0, keepdims=True), top_own)
+            weight = jnp.exp2(masked - top)
+            factor = jnp.exp2(top_own - top)
+            total = stats_ref[KV_HEADS + g : KV_HEADS + g + 1, cut] * factor
+            total = total + jnp.sum(weight, axis=0, keepdims=True)
+            factors.append(factor)
+            scales.append(stats_ref[2 * KV_HEADS + g : 2 * KV_HEADS + g + 1, cut] / total)
+            weights.append(weight.astype(jnp.bfloat16))
+        added = dot(block_values(one_ref, g), jnp.concatenate(weights, axis=1), TN)
+        summed = summed_ref[part_of(g, HEAD_DIM), :] * jnp.concatenate(factors, axis=1) + added
+        results.append(summed * jnp.concatenate(scales, axis=1))
+    return results
+
+
+def store_heads(mixed, out_ref, held, sems):
+    copies = []
+    for g in range(KV_HEADS):
+        for i in range(GROUPS):
+            h = g * GROUPS + i
+            held[:, part_of(h, HEAD_DIM)] = jnp.transpose(mixed(g, i))
         wide = part_of(g, GROUPS * HEAD_DIM)
-        copies.append(
-            pltpu.make_async_copy(held.at[:, wide], out_ref.at[:, wide], sems.at[g])
-        )
+        copies.append(pltpu.make_async_copy(held.at[:, wide], out_ref.at[:, wide], sems.at[g]))
         copies[g].start()
     for copy in copies:
         copy.wait()
+
+
+def read_kernel(plan, q_ref, own_ref, three_ref, gains_ref, read_ref):
+    kv = lax.axis_index("kv")
+
+    @pl.when((kv == 1) & jnp.logical_not(among(plan.late)))
+    def _():
+        first, same = first_document(block_docs(own_ref))
+        states = memory_states([three_ref], first)
+        heads = read_memory(states, q_ref, gains_ref, jnp.where(same, 1.0, 0.0))
+        for h, head in enumerate(heads):
+            read_ref[part_of(h, HEAD_DIM), :] = head
+
+
+def early_kernel(
+    plan, q_ref, own_ref, one_ref, three_ref, stats_ref, gains_ref, read_ref, summed_in,
+    summed_ref, state_ref, out_ref, held, sems,
+):
+    first, same = first_document(block_docs(own_ref))
+    rows = q_ref.shape[0]
+    kv = lax.axis_index("kv")
+    late = among(plan.late)
+
+    def summed_part(g, i):
+        return summed_ref[part_of(g, HEAD_DIM), part_of(i, rows)]
+
+    @pl.when((kv == 0) & jnp.logical_not(late))
+    def _():
+        states = memory_states([one_ref, three_ref], first)
+        heads = read_memory(states, q_ref, gains_ref, jnp.where(same, 1.0, 0.0))
+        store_heads(lambda g, i: heads[g * GROUPS + i] + summed_part(g, i), out_ref, held, sems)
+
+    @pl.when((kv == 1) & jnp.logical_not(late))
+    def _():
+        results = attend_before(q_ref, one_ref, stats_ref, summed_ref, first, same)
+
+        def mixed(g, i):
+            read = read_ref[part_of(g * GROUPS + i, HEAD_DIM), :]
+            return read + results[g][:, part_of(i, rows)]
+
+        store_heads(mixed, out_ref, held, sems)
+
+    @pl.when((kv == 0) & late)
+    def _():
+        for g, state in enumerate(memory_states([one_ref, three_ref], first)):
+            state_ref[part_of(g, HEAD_DIM), :] = state
+
+    @pl.when((kv == 1) & late)
+    def _():
+        for g, state in enumerate(memory_states([three_ref], first)):
+            state_ref[part_of(g, HEAD_DIM), :] = state
+        results = attend_before(q_ref, one_ref, stats_ref, summed_ref, first, same)
+        for g in range(KV_HEADS):
+            summed_ref[part_of(g, HEAD_DIM), :] = results[g]
+
+
+def late_kernel(
+    plan, q_ref, own_ref, two_ref, state_ref, summed_ref, gains_ref, out_in, out_ref, held, sems
+):
+    @pl.when(among(plan.late))
+    def _():
+        first, same = first_document(block_docs(own_ref))
+        rows = q_ref.shape[0]
+        states = [
+            state_ref[part_of(g, HEAD_DIM), :] + memory_state(two_ref, first, g)
+            for g in range(KV_HEADS)
+        ]
+        heads = read_memory(states, q_ref, gains_ref, jnp.where(same, 1.0, 0.0))
+
+        def mixed(g, i):
+            summed = summed_ref[part_of(g, HEAD_DIM), part_of(i, rows)]
+            return heads[g * GROUPS + i] + summed
+
+        store_heads(mixed, out_ref, held, sems)
 
 
 def near_device(n_seq, queries, keys, values, doc_ids, beta, lin_gain):
@@ -363,25 +428,36 @@
         compiler_params=params,
         cost_estimate=estimate(1.0),
     )(queries, gain, own, beta, summed, stats, gains)
-    state, ready = pl.pallas_call(
-        before_kernel,
-        out_shape=[state_shape, group_shape],
-        in_specs=[vmem] * 6,
-        out_specs=[vmem] * 2,
-        input_output_aliases={5: 1},
+    read = pl.pallas_call(
+        functools.partial(read_kernel, plan),
+        out_shape=gains_shape,
+        in_specs=[vmem] * 4,
+        out_specs=vmem,
         compiler_params=params,
-    )(queries, own, one, three, stats, summed)
+    )(queries, own, three, gains)
+    out_shape = jax.ShapeDtypeStruct((rows, HEADS * HEAD_DIM), jnp.float32)
+    store_scratch = [
+        pltpu.VMEM((rows, HEADS * HEAD_DIM), jnp.float32),
+        pltpu.SemaphoreType.DMA((KV_HEADS,)),
+    ]
+    summed, state, out = pl.pallas_call(
+        functools.partial(early_kernel, plan),
+        out_shape=[group_shape, state_shape, out_shape],
+        in_specs=[vmem] * 8,
+        out_specs=[vmem] * 2 + [hbm],
+        scratch_shapes=store_scratch,
+        input_output_aliases={7: 0},
+        compiler_params=params,
+    )(queries, own, one, three, stats, gains, read, summed)
     return pl.pallas_call(
-        join_kernel,
-        out_shape=jax.ShapeDtypeStruct((rows, HEADS * HEAD_DIM), jnp.float32),
-        in_specs=[vmem] * 6,
+        functools.partial(late_kernel, plan),
+        out_shape=out_shape,
+        in_specs=[vmem] * 6 + [hbm],
         out_specs=hbm,
-        scratch_shapes=[
-            pltpu.VMEM((rows, HEADS * HEAD_DIM), jnp.float32),
-            pltpu.SemaphoreType.DMA((KV_HEADS,)),
-        ],
+        scratch_shapes=store_scratch,
+        input_output_aliases={6: 0},
         compiler_params=params,
-    )(queries, own, two, state, ready, gains)
+    )(queries, own, two, state, summed, gains, out)
 
 
 def carried_in(part, axis, combine, identity):

time: 15.5 us -> 15.5 us (level)
  the two profiles are of different devices: /device:TPU:1 before, /device:TPU:28 now
where the time goes in v11:
time: 15.5 us; the launch traced here: 15.2 us
  starting transfers between devices  5.28 us (34%)
  Pallas kernels  5.2 us (34%)
  waiting for transfers between devices  4.61 us (30%)
    ppermute x3, starting transfers between devices, send(): return lax.ppermute(payload, ('seq', 'kv'), pairs)  5.28 us
    ppermute x3, waiting for transfers between devices, send(): return lax.ppermute(payload, ('seq', 'kv'), pairs)  4.61 us
    pallas_call x1, Pallas kernels, near_device(): pl.pallas_call(functools.partial(own_kernel, plan), out_shape=results, in...  1.88 us
    pallas_call x1, Pallas kernels, near_device(): pl.pallas_call(functools.partial(late_kernel, plan), out_shape=out_shape,...  1.74 us
    pallas_call x1, Pallas kernels, near_device(): pl.pallas_call(functools.partial(pack_kernel, plan), out_shape=longer_sha...  0.98 us
    pallas_call x1, Pallas kernels, near_device(): pl.pallas_call(functools.partial(early_kernel, plan), out_shape=[group_sh...  0.41 us
  transfers between devices with their start and end apart: 3, of which 2 were waited for; matrix products, arithmetic and copies ran while one was open for 0% of the time, Pallas kernels for 16%

profile of v11, /device:TPU:28, one launch (start us, length us, event | category | flops | bytes accessed | tf_op | source)
XLA Modules:
  0.0 15.2 jit_solution(17351959099193761564)
XLA Ops:
  0.0 0.0 copy-start.1
  0.0 1.0 %shard_map.64.packed_ref = bf16[1056,128]{1,0:T(8,128)(2,1)S(1)} custom-call(bf16[128,512]{1,0:T(8,128)(2,1)} %key_ref.3, bf16[128,512]{1,0:T(8,128)(2,1)} %value_ref.3, s32[1,128]{1,0:T(1,128)} %bitcast.4), custom_call_target="tpu_custom_call" | custom-call | flops 13421772 | bytes 419430 | tf_op jit(solution)/shard_map/pallas_call | solution.py:394
  1.0 2.5 %collective-permute-start.1 = (bf16[1056,128]{1,0:T(8,128)(2,1)S(1)}, bf16[1056,128]{1,0:T(8,128)(2,1)S(1)}, u32[]{:S(2)}, u32[]{:S(2)}) collective-permute-start(bf16[1056,128]{1,0:T(8,128)(2,1)S(1)} %shard_map.64.packed_ref), channel_id=1, source_target_pairs={{0,4},{4,8},{8,12},{12,16},{16,20},{24,28},{1,5},{5,9},{9,13},{13,... | collective-permute-start | bytes 811016 | tf_op jit(solution)/shard_map/ppermute | solution.py:381
  3.5 0.0 copy-done.1
  3.5 0.0 copy-start
  3.5 0.2 %shard_map.65 = (bf16[1056,128]{1,0:T(8,128)(2,1)S(1)}, bf16[1040,128]{1,0:T(8,128)(2,1)S(1)}, f32[512,512]{1,0:T(8,128)S(1)}, f32[16,512]{1,0:T(8,128)S(1)}, f32[2048,128]{1,0:T(8,128)S(1)}) custom-call(f32[16,128]{1,0:T(8,128)S(1)} %bitcast.2, bf16[1056,128]{1,0:T(8,128)(2,1)S(1)} %shard_map.64.packed_ref, bf16[128,2048]{1,0:T(8,128)(2,1)} %q_ref.7, ...), custom_call_target="tpu_custom_call" | custom-call | flops 134217728 | bytes 4194304 | tf_op jit(solution)/shard_map/pallas_call | solution.py:404
  3.7 1.3 %collective-permute-start = (bf16[1056,128]{1,0:T(8,128)(2,1)S(1)}, bf16[1056,128]{1,0:T(8,128)(2,1)S(1)}, u32[]{:S(2)}, u32[]{:S(2)}) collective-permute-start(bf16[1056,128]{1,0:T(8,128)(2,1)S(1)} %get-tuple-element.17), channel_id=1, source_target_pairs={{20,24},{8,16},{12,20},{21,25},{9,17},{13,21},{22,26},{10,18},{14,... | collective-permute-start | bytes 811016 | tf_op jit(solution)/shard_map/ppermute | solution.py:381
  5.0 1.5 %collective-permute-start.2 = (bf16[1040,128]{1,0:T(8,128)(2,1)S(1)}, bf16[1040,128]{1,0:T(8,128)(2,1)S(1)}, u32[]{:S(2)}, u32[]{:S(2)}) collective-permute-start(bf16[1040,128]{1,0:T(8,128)(2,1)S(1)} %get-tuple-element.16.own_ref), channel_id=1, source_target_pairs={{0,8},{4,12},{16,24},{20,28},{1,9},{5,13},{17,25},{21,29},{2,10},{... | collective-permute-start | bytes 798728 | tf_op jit(solution)/shard_map/ppermute | solution.py:381
  6.5 0.0 copy-done
  6.5 1.9 %shard_map.66 = (f32[512,512]{1,0:T(8,128)S(1)}, f32[16,512]{1,0:T(8,128)S(1)}, f32[2048,128]{1,0:T(8,128)S(1)}) custom-call(bf16[128,2048]{1,0:T(8,128)(2,1)S(1)} %copy-done, f32[16,128]{1,0:T(8,128)S(1)} %bitcast.3, bf16[1040,128]{1,0:T(8,128)(2,1)S(1)} %get-tuple-element.16.own_ref, ...), custom_call_target="tpu_custom_call", output_to_operand_aliasing={{0}: (4, {}), {1}: (5, {}), {2}: (6, {})} | custom-call | flops 134217728 | bytes 4194304 | tf_op jit(solution)/shard_map/pallas_call | solution.py:421
  8.4 0.0 collective-permute-done.2.three_ref
  8.4 3.3 %collective-permute-done.1.one_ref = bf16[1056,128]{1,0:T(8,128)(2,1)S(1)} collective-permute-done((bf16[1056,128]{1,0:T(8,128)(2,1)S(1)}, bf16[1056,128]{1,0:T(8,128)(2,1)S(1)}, u32[]{:S(2)}, u32[]{:S(2)}) %collective-permute-start.1) | collective-permute-done | bytes 270368 | tf_op jit(solution)/shard_map/ppermute | solution.py:381
  11.8 0.4 %shard_map.68 = (f32[512,512]{1,0:T(8,128)S(1)}, f32[512,128]{1,0:T(8,128)S(1)}, f32[128,2048]{1,0:T(8,128)}) custom-call(bf16[128,2048]{1,0:T(8,128)(2,1)S(1)} %copy-done, bf16[1040,128]{1,0:T(8,128)(2,1)S(1)} %get-tuple-element.16.own_ref, bf16[1056,128]{1,0:T(8,128)(2,1)S(1)} %collective-permute-done.1.one_ref, ...), custom_call_target="tpu_custom_call", output_to_operand_aliasing={{0}: (7, {})} | custom-call | tf_op jit(solution)/shard_map/pallas_call | solution.py:443
  12.2 1.3 %collective-permute-done.two_ref = bf16[1056,128]{1,0:T(8,128)(2,1)S(1)} collective-permute-done((bf16[1056,128]{1,0:T(8,128)(2,1)S(1)}, bf16[1056,128]{1,0:T(8,128)(2,1)S(1)}, u32[]{:S(2)}, u32[]{:S(2)}) %collective-permute-start) | collective-permute-done | bytes 270368 | tf_op jit(solution)/shard_map/ppermute | solution.py:381
  13.5 1.7 %shard_map.69 = f32[128,2048]{1,0:T(8,128)} custom-call(bf16[128,2048]{1,0:T(8,128)(2,1)S(1)} %copy-done, bf16[1040,128]{1,0:T(8,128)(2,1)S(1)} %get-tuple-element.16.own_ref, bf16[1056,128]{1,0:T(8,128)(2,1)S(1)} %collective-permute-done.two_ref, f32[512,128]{1,0:T(8,128)S(1)} %get-tuple-element.24.state_ref, ...), custom_call_target="tpu_custom_call", output_to_operand_aliasing={{}: (6, {})} | custom-call | tf_op jit(solution)/shard_map/pallas_call | solution.py:452
  (1 shorter events, 0.0 us)
Async XLA Ops:
  0.0 3.5 %copy-start.1 = (f32[2048]{0:T(1024)S(1)}, f32[2048]{0:T(1024)}, u32[]{:S(2)}) copy-start(f32[2048]{0:T(1024)} %param.11) | copy-start | bytes 24580
  1.0 10.8 %collective-permute-start.1 = (bf16[1056,128]{1,0:T(8,128)(2,1)S(1)}, bf16[1056,128]{1,0:T(8,128)(2,1)S(1)}, u32[]{:S(2)}, u32[]{:S(2)}) collective-permute-start(bf16[1056,128]{1,0:T(8,128)(2,1)S(1)} %shard_map.64.packed_ref), channel_id=1, source_target_pairs={{0,4},{4,8},{8,12},{12,16},{16,20},{24,28},{1,5},{5,9},{9,13},{13,... | collective-permute-start | bytes 811016 | tf_op jit(solution)/shard_map/ppermute | solution.py:381
  3.5 3.0 %copy-start = (bf16[128,2048]{1,0:T(8,128)(2,1)S(1)}, bf16[128,2048]{1,0:T(8,128)(2,1)}, u32[]{:S(2)}) copy-start(bf16[128,2048]{1,0:T(8,128)(2,1)} %q_ref.7) | copy-start | bytes 1572868
  3.7 9.8 %collective-permute-start = (bf16[1056,128]{1,0:T(8,128)(2,1)S(1)}, bf16[1056,128]{1,0:T(8,128)(2,1)S(1)}, u32[]{:S(2)}, u32[]{:S(2)}) collective-permute-start(bf16[1056,128]{1,0:T(8,128)(2,1)S(1)} %get-tuple-element.17), channel_id=1, source_target_pairs={{20,24},{8,16},{12,20},{21,25},{9,17},{13,21},{22,26},{10,18},{14,... | collective-permute-start | bytes 811016 | tf_op jit(solution)/shard_map/ppermute | solution.py:381
  5.0 3.4 %collective-permute-start.2 = (bf16[1040,128]{1,0:T(8,128)(2,1)S(1)}, bf16[1040,128]{1,0:T(8,128)(2,1)S(1)}, u32[]{:S(2)}, u32[]{:S(2)}) collective-permute-start(bf16[1040,128]{1,0:T(8,128)(2,1)S(1)} %get-tuple-element.16.own_ref), channel_id=1, source_target_pairs={{0,8},{4,12},{16,24},{20,28},{1,9},{5,13},{17,25},{21,29},{2,10},{... | collective-permute-start | bytes 798728 | tf_op jit(solution)/shard_map/ppermute | solution.py:381

commit v12 on v11

--- a/solution.py
+++ b/solution.py
@@ -101,13 +101,15 @@
         near = [(b, b + 1) for b in range(devices - 1)]
         far = [(b, b + 2) for b in range(devices - 2)]
         first = [p for p in near if p[0] % 2 == 0 or p[0] // 2 % 2 == 1 or p[0] == 1]
+        first = [p for p in first if p[0] > 0]
         last = [p for p in far if p[0] // 2 % 2 == 0]
         second = [p for p in near + far if p not in first + last]
         self.pairs = [first, second, last]
         self.senders = sorted({p[0] for p in first})
-        busy = {b for p in second for b in p}
+        busy = {b for p in first for b in p} & {b for p in second for b in p}
         self.early = [b for b in range(devices) if b not in busy]
         self.late = sorted({p[1] for p in second})
+        self.attend_late = [b for a, b in second if a + 1 == b and b % 2 == 1]
 
 
 def among(members):
@@ -284,9 +286,9 @@
 
 
 def read_kernel(plan, q_ref, own_ref, three_ref, gains_ref, read_ref):
-    kv = lax.axis_index("kv")
-
-    @pl.when((kv == 1) & jnp.logical_not(among(plan.late)))
+    ready = jnp.logical_not(among(plan.late)) | among(plan.attend_late)
+
+    @pl.when((lax.axis_index("kv") == 1) & ready)
     def _():
         first, same = first_document(block_docs(own_ref))
         states = memory_states([three_ref], first)
@@ -328,7 +330,7 @@
         for g, state in enumerate(memory_states([one_ref, three_ref], first)):
             state_ref[part_of(g, HEAD_DIM), :] = state
 
-    @pl.when((kv == 1) & late)
+    @pl.when((kv == 1) & late & jnp.logical_not(among(plan.attend_late)))
     def _():
         for g, state in enumerate(memory_states([three_ref], first)):
             state_ref[part_of(g, HEAD_DIM), :] = state
@@ -338,12 +340,25 @@
 
 
 def late_kernel(
-    plan, q_ref, own_ref, two_ref, state_ref, summed_ref, gains_ref, out_in, out_ref, held, sems
+    plan, q_ref, own_ref, two_ref, state_ref, summed_ref, stats_ref, gains_ref, read_ref, out_in,
+    out_ref, held, sems,
 ):
-    @pl.when(among(plan.late))
-    def _():
-        first, same = first_document(block_docs(own_ref))
-        rows = q_ref.shape[0]
+    first, same = first_document(block_docs(own_ref))
+    rows = q_ref.shape[0]
+    attend_late = among(plan.attend_late)
+
+    @pl.when(attend_late)
+    def _():
+        results = attend_before(q_ref, two_ref, stats_ref, summed_ref, first, same)
+
+        def mixed(g, i):
+            read = read_ref[part_of(g * GROUPS + i, HEAD_DIM), :]
+            return read + results[g][:, part_of(i, rows)]
+
+        store_heads(mixed, out_ref, held, sems)
+
+    @pl.when(among(plan.late) & jnp.logical_not(attend_late))
+    def _():
         states = [
             state_ref[part_of(g, HEAD_DIM), :] + memory_state(two_ref, first, g)
             for g in range(KV_HEADS)
@@ -452,12 +467,12 @@
     return pl.pallas_call(
         functools.partial(late_kernel, plan),
         out_shape=out_shape,
-        in_specs=[vmem] * 6 + [hbm],
+        in_specs=[vmem] * 8 + [hbm],
         out_specs=hbm,
         scratch_shapes=store_scratch,
-        input_output_aliases={6: 0},
+        input_output_aliases={8: 0},
         compiler_params=params,
-    )(queries, own, two, state, summed, gains, out)
+    )(queries, own, two, state, summed, stats, gains, read, out)
 
 
 def carried_in(part, axis, combine, identity):

time: 15.5 us -> 15.5 us (level)
  the two profiles are of different devices: /device:TPU:28 before, /device:TPU:4 now
where the time goes in v12:
time: 15.5 us; the launch traced here: 15.2 us
  starting transfers between devices  5.28 us (34%)
  Pallas kernels  5.19 us (33%)
  waiting for transfers between devices  4.66 us (30%)
    ppermute x3, starting transfers between devices, send(): return lax.ppermute(payload, ('seq', 'kv'), pairs)  5.28 us
    ppermute x3, waiting for transfers between devices, send(): return lax.ppermute(payload, ('seq', 'kv'), pairs)  4.66 us
    pallas_call x1, Pallas kernels, near_device(): pl.pallas_call(functools.partial(own_kernel, plan), out_shape=results, in...  1.88 us
    pallas_call x1, Pallas kernels, near_device(): pl.pallas_call(functools.partial(late_kernel, plan), out_shape=out_shape,...  1.74 us
    pallas_call x1, Pallas kernels, near_device(): pl.pallas_call(functools.partial(pack_kernel, plan), out_shape=longer_sha...  0.98 us
    pallas_call x1, Pallas kernels, near_device(): pl.pallas_call(functools.partial(early_kernel, plan), out_shape=[group_sh...  0.41 us
  transfers between devices with their start and end apart: 3, of which 2 were waited for; matrix products, arithmetic and copies ran while one was open for 0% of the time, Pallas kernels for 16%

profile of v12, /device:TPU:4, one launch (start us, length us, event | category | flops | bytes accessed | tf_op | source)
XLA Modules:
  0.0 15.2 jit_solution(5784676597405343121)
XLA Ops:
  0.0 0.0 copy-start.1
  0.0 1.0 %shard_map.64.packed_ref = bf16[1056,128]{1,0:T(8,128)(2,1)S(1)} custom-call(bf16[128,512]{1,0:T(8,128)(2,1)} %key_ref.3, bf16[128,512]{1,0:T(8,128)(2,1)} %value_ref.3, s32[1,128]{1,0:T(1,128)} %bitcast.4), custom_call_target="tpu_custom_call" | custom-call | flops 13421772 | bytes 419430 | tf_op jit(solution)/shard_map/pallas_call | solution.py:409
  1.0 2.5 %collective-permute-start.1 = (bf16[1056,128]{1,0:T(8,128)(2,1)S(1)}, bf16[1056,128]{1,0:T(8,128)(2,1)S(1)}, u32[]{:S(2)}, u32[]{:S(2)}) collective-permute-start(bf16[1056,128]{1,0:T(8,128)(2,1)S(1)} %shard_map.64.packed_ref), channel_id=1, source_target_pairs={{4,8},{8,12},{12,16},{16,20},{24,28},{5,9},{9,13},{13,17},{17,21},... | collective-permute-start | bytes 811016 | tf_op jit(solution)/shard_map/ppermute | solution.py:396
  3.5 0.0 copy-done.1
  3.5 0.0 copy-start
  3.5 0.2 %shard_map.65 = (bf16[1056,128]{1,0:T(8,128)(2,1)S(1)}, bf16[1040,128]{1,0:T(8,128)(2,1)S(1)}, f32[512,512]{1,0:T(8,128)S(1)}, f32[16,512]{1,0:T(8,128)S(1)}, f32[2048,128]{1,0:T(8,128)S(1)}) custom-call(f32[16,128]{1,0:T(8,128)S(1)} %bitcast.2, bf16[1056,128]{1,0:T(8,128)(2,1)S(1)} %shard_map.64.packed_ref, bf16[128,2048]{1,0:T(8,128)(2,1)} %q_ref.7, ...), custom_call_target="tpu_custom_call" | custom-call | flops 134217728 | bytes 4194304 | tf_op jit(solution)/shard_map/pallas_call | solution.py:419
  3.7 1.3 %collective-permute-start = (bf16[1056,128]{1,0:T(8,128)(2,1)S(1)}, bf16[1056,128]{1,0:T(8,128)(2,1)S(1)}, u32[]{:S(2)}, u32[]{:S(2)}) collective-permute-start(bf16[1056,128]{1,0:T(8,128)(2,1)S(1)} %get-tuple-element.17), channel_id=1, source_target_pairs={{0,4},{20,24},{8,16},{12,20},{1,5},{21,25},{9,17},{13,21},{2,6},{2... | collective-permute-start | bytes 811016 | tf_op jit(solution)/shard_map/ppermute | solution.py:396
  5.0 1.5 %collective-permute-start.2 = (bf16[1040,128]{1,0:T(8,128)(2,1)S(1)}, bf16[1040,128]{1,0:T(8,128)(2,1)S(1)}, u32[]{:S(2)}, u32[]{:S(2)}) collective-permute-start(bf16[1040,128]{1,0:T(8,128)(2,1)S(1)} %get-tuple-element.16.own_ref), channel_id=1, source_target_pairs={{0,8},{4,12},{16,24},{20,28},{1,9},{5,13},{17,25},{21,29},{2,10},{... | collective-permute-start | bytes 798728 | tf_op jit(solution)/shard_map/ppermute | solution.py:396
  6.5 0.0 copy-done
  6.5 1.9 %shard_map.66 = (f32[512,512]{1,0:T(8,128)S(1)}, f32[16,512]{1,0:T(8,128)S(1)}, f32[2048,128]{1,0:T(8,128)S(1)}) custom-call(bf16[128,2048]{1,0:T(8,128)(2,1)S(1)} %copy-done, f32[16,128]{1,0:T(8,128)S(1)} %bitcast.3, bf16[1040,128]{1,0:T(8,128)(2,1)S(1)} %get-tuple-element.16.own_ref, ...), custom_call_target="tpu_custom_call", output_to_operand_aliasing={{0}: (4, {}), {1}: (5, {}), {2}: (6, {})} | custom-call | flops 134217728 | bytes 4194304 | tf_op jit(solution)/shard_map/pallas_call | solution.py:436
  8.4 0.0 collective-permute-done.2.three_ref
  8.4 2.7 %collective-permute-done.1.one_ref = bf16[1056,128]{1,0:T(8,128)(2,1)S(1)} collective-permute-done((bf16[1056,128]{1,0:T(8,128)(2,1)S(1)}, bf16[1056,128]{1,0:T(8,128)(2,1)S(1)}, u32[]{:S(2)}, u32[]{:S(2)}) %collective-permute-start.1) | collective-permute-done | bytes 270368 | tf_op jit(solution)/shard_map/ppermute | solution.py:396
  11.1 0.4 %shard_map.68 = (f32[512,512]{1,0:T(8,128)S(1)}, f32[512,128]{1,0:T(8,128)S(1)}, f32[128,2048]{1,0:T(8,128)}) custom-call(bf16[128,2048]{1,0:T(8,128)(2,1)S(1)} %copy-done, bf16[1040,128]{1,0:T(8,128)(2,1)S(1)} %get-tuple-element.16.own_ref, bf16[1056,128]{1,0:T(8,128)(2,1)S(1)} %collective-permute-done.1.one_ref, ...), custom_call_target="tpu_custom_call", output_to_operand_aliasing={{0}: (7, {})} | custom-call | tf_op jit(solution)/shard_map/pallas_call | solution.py:458
  11.6 1.9 %collective-permute-done.two_ref = bf16[1056,128]{1,0:T(8,128)(2,1)S(1)} collective-permute-done((bf16[1056,128]{1,0:T(8,128)(2,1)S(1)}, bf16[1056,128]{1,0:T(8,128)(2,1)S(1)}, u32[]{:S(2)}, u32[]{:S(2)}) %collective-permute-start) | collective-permute-done | bytes 270368 | tf_op jit(solution)/shard_map/ppermute | solution.py:396
  13.5 1.7 %shard_map.69 = f32[128,2048]{1,0:T(8,128)} custom-call(bf16[128,2048]{1,0:T(8,128)(2,1)S(1)} %copy-done, bf16[1040,128]{1,0:T(8,128)(2,1)S(1)} %get-tuple-element.16.own_ref, bf16[1056,128]{1,0:T(8,128)(2,1)S(1)} %collective-permute-done.two_ref, f32[512,128]{1,0:T(8,128)S(1)} %get-tuple-element.24.state_ref, ...), custom_call_target="tpu_custom_call", output_to_operand_aliasing={{}: (8, {})} | custom-call | tf_op jit(solution)/shard_map/pallas_call | solution.py:467
  (1 shorter events, 0.0 us)
Async XLA Ops:
  0.0 3.5 %copy-start.1 = (f32[2048]{0:T(1024)S(1)}, f32[2048]{0:T(1024)}, u32[]{:S(2)}) copy-start(f32[2048]{0:T(1024)} %param.11) | copy-start | bytes 24580
  1.0 10.2 %collective-permute-start.1 = (bf16[1056,128]{1,0:T(8,128)(2,1)S(1)}, bf16[1056,128]{1,0:T(8,128)(2,1)S(1)}, u32[]{:S(2)}, u32[]{:S(2)}) collective-permute-start(bf16[1056,128]{1,0:T(8,128)(2,1)S(1)} %shard_map.64.packed_ref), channel_id=1, source_target_pairs={{4,8},{8,12},{12,16},{16,20},{24,28},{5,9},{9,13},{13,17},{17,21},... | collective-permute-start | bytes 811016 | tf_op jit(solution)/shard_map/ppermute | solution.py:396
  3.5 3.0 %copy-start = (bf16[128,2048]{1,0:T(8,128)(2,1)S(1)}, bf16[128,2048]{1,0:T(8,128)(2,1)}, u32[]{:S(2)}) copy-start(bf16[128,2048]{1,0:T(8,128)(2,1)} %q_ref.7) | copy-start | bytes 1572868
  3.7 9.8 %collective-permute-start = (bf16[1056,128]{1,0:T(8,128)(2,1)S(1)}, bf16[1056,128]{1,0:T(8,128)(2,1)S(1)}, u32[]{:S(2)}, u32[]{:S(2)}) collective-permute-start(bf16[1056,128]{1,0:T(8,128)(2,1)S(1)} %get-tuple-element.17), channel_id=1, source_target_pairs={{0,4},{20,24},{8,16},{12,20},{1,5},{21,25},{9,17},{13,21},{2,6},{2... | collective-permute-start | bytes 811016 | tf_op jit(solution)/shard_map/ppermute | solution.py:396
  5.0 3.4 %collective-permute-start.2 = (bf16[1040,128]{1,0:T(8,128)(2,1)S(1)}, bf16[1040,128]{1,0:T(8,128)(2,1)S(1)}, u32[]{:S(2)}, u32[]{:S(2)}) collective-permute-start(bf16[1040,128]{1,0:T(8,128)(2,1)S(1)} %get-tuple-element.16.own_ref), channel_id=1, source_target_pairs={{0,8},{4,12},{16,24},{20,28},{1,9},{5,13},{17,25},{21,29},{2,10},{... | collective-permute-start | bytes 798728 | tf_op jit(solution)/shard_map/ppermute | solution.py:396

commit v13 on v12

--- a/solution.py
+++ b/solution.py
@@ -100,16 +100,18 @@
         devices = 2 * n_seq
         near = [(b, b + 1) for b in range(devices - 1)]
         far = [(b, b + 2) for b in range(devices - 2)]
-        first = [p for p in near if p[0] % 2 == 0 or p[0] // 2 % 2 == 1 or p[0] == 1]
-        first = [p for p in first if p[0] > 0]
-        last = [p for p in far if p[0] // 2 % 2 == 0]
-        second = [p for p in near + far if p not in first + last]
+        crossing = [p for p in far if p[0] // 2 % 2 == 1]
+        touched = {b for p in crossing for b in p}
+        targets = {p[1] for p in crossing}
+        first = crossing + [p for p in near if p[0] not in touched and p[1] not in targets]
+        second = [p for p in near if p not in first]
+        last = [p for p in far if p not in first]
         self.pairs = [first, second, last]
         self.senders = sorted({p[0] for p in first})
         busy = {b for p in first for b in p} & {b for p in second for b in p}
         self.early = [b for b in range(devices) if b not in busy]
         self.late = sorted({p[1] for p in second})
-        self.attend_late = [b for a, b in second if a + 1 == b and b % 2 == 1]
+        self.memory_first = [p[1] for p in crossing if p[1] % 2 == 1]
 
 
 def among(members):
@@ -285,91 +287,97 @@
         copy.wait()
 
 
+def read_into(read_ref, refs, q_ref, own_ref, gains_ref):
+    first, same = first_document(block_docs(own_ref))
+    heads = read_memory(
+        memory_states(refs, first), q_ref, gains_ref, jnp.where(same, 1.0, 0.0)
+    )
+    for h, head in enumerate(heads):
+        read_ref[part_of(h, HEAD_DIM), :] = head
+
+
 def read_kernel(plan, q_ref, own_ref, three_ref, gains_ref, read_ref):
-    ready = jnp.logical_not(among(plan.late)) | among(plan.attend_late)
-
-    @pl.when((lax.axis_index("kv") == 1) & ready)
-    def _():
-        first, same = first_document(block_docs(own_ref))
-        states = memory_states([three_ref], first)
-        heads = read_memory(states, q_ref, gains_ref, jnp.where(same, 1.0, 0.0))
-        for h, head in enumerate(heads):
-            read_ref[part_of(h, HEAD_DIM), :] = head
-
-
-def early_kernel(
-    plan, q_ref, own_ref, one_ref, three_ref, stats_ref, gains_ref, read_ref, summed_in,
-    summed_ref, state_ref, out_ref, held, sems,
+    @pl.when((lax.axis_index("kv") == 1) & jnp.logical_not(among(plan.memory_first)))
+    def _():
+        read_into(read_ref, [three_ref], q_ref, own_ref, gains_ref)
+
+
+def attend_and_store(
+    q_ref, own_ref, earlier_ref, stats_ref, summed_ref, read_ref, out_ref, held, sems
 ):
     first, same = first_document(block_docs(own_ref))
+    results = attend_before(q_ref, earlier_ref, stats_ref, summed_ref, first, same)
     rows = q_ref.shape[0]
+
+    def mixed(g, i):
+        read = read_ref[part_of(g * GROUPS + i, HEAD_DIM), :]
+        return read + results[g][:, part_of(i, rows)]
+
+    store_heads(mixed, out_ref, held, sems)
+
+
+def read_and_store(states, q_ref, gains_ref, same, summed_ref, out_ref, held, sems):
+    rows = q_ref.shape[0]
+    heads = read_memory(states, q_ref, gains_ref, jnp.where(same, 1.0, 0.0))
+
+    def mixed(g, i):
+        summed = summed_ref[part_of(g, HEAD_DIM), part_of(i, rows)]
+        return heads[g * GROUPS + i] + summed
+
+    store_heads(mixed, out_ref, held, sems)
+
+
+def early_kernel(
+    plan, q_ref, own_ref, one_ref, three_ref, stats_ref, gains_ref, summed_ref, read_in,
+    read_ref, state_ref, out_ref, held, sems,
+):
     kv = lax.axis_index("kv")
     late = among(plan.late)
 
-    def summed_part(g, i):
-        return summed_ref[part_of(g, HEAD_DIM), part_of(i, rows)]
-
     @pl.when((kv == 0) & jnp.logical_not(late))
     def _():
+        first, same = first_document(block_docs(own_ref))
         states = memory_states([one_ref, three_ref], first)
-        heads = read_memory(states, q_ref, gains_ref, jnp.where(same, 1.0, 0.0))
-        store_heads(lambda g, i: heads[g * GROUPS + i] + summed_part(g, i), out_ref, held, sems)
+        read_and_store(states, q_ref, gains_ref, same, summed_ref, out_ref, held, sems)
 
     @pl.when((kv == 1) & jnp.logical_not(late))
     def _():
-        results = attend_before(q_ref, one_ref, stats_ref, summed_ref, first, same)
-
-        def mixed(g, i):
-            read = read_ref[part_of(g * GROUPS + i, HEAD_DIM), :]
-            return read + results[g][:, part_of(i, rows)]
-
-        store_heads(mixed, out_ref, held, sems)
+        attend_and_store(
+            q_ref, own_ref, one_ref, stats_ref, summed_ref, read_ref, out_ref, held, sems
+        )
 
     @pl.when((kv == 0) & late)
     def _():
+        first, _ = first_document(block_docs(own_ref))
         for g, state in enumerate(memory_states([one_ref, three_ref], first)):
             state_ref[part_of(g, HEAD_DIM), :] = state
 
-    @pl.when((kv == 1) & late & jnp.logical_not(among(plan.attend_late)))
-    def _():
-        for g, state in enumerate(memory_states([three_ref], first)):
-            state_ref[part_of(g, HEAD_DIM), :] = state
-        results = attend_before(q_ref, one_ref, stats_ref, summed_ref, first, same)
-        for g in range(KV_HEADS):
-            summed_ref[part_of(g, HEAD_DIM), :] = results[g]
+    @pl.when((kv == 1) & among(plan.memory_first))
+    def _():
+        read_into(read_ref, [one_ref, three_ref], q_ref, own_ref, gains_ref)
 
 
 def late_kernel(
     plan, q_ref, own_ref, two_ref, state_ref, summed_ref, stats_ref, gains_ref, read_ref, out_in,
     out_ref, held, sems,
 ):
-    first, same = first_document(block_docs(own_ref))
-    rows = q_ref.shape[0]
-    attend_late = among(plan.attend_late)
-
-    @pl.when(attend_late)
-    def _():
-        results = attend_before(q_ref, two_ref, stats_ref, summed_ref, first, same)
-
-        def mixed(g, i):
-            read = read_ref[part_of(g * GROUPS + i, HEAD_DIM), :]
-            return read + results[g][:, part_of(i, rows)]
-
-        store_heads(mixed, out_ref, held, sems)
-
-    @pl.when(among(plan.late) & jnp.logical_not(attend_late))
-    def _():
+    kv = lax.axis_index("kv")
+    late = among(plan.late)
+
+    @pl.when((kv == 1) & late)
+    def _():
+        attend_and_store(
+            q_ref, own_ref, two_ref, stats_ref, summed_ref, read_ref, out_ref, held, sems
+        )
+
+    @pl.when((kv == 0) & late)
+    def _():
+        first, same = first_document(block_docs(own_ref))
         states = [
             state_ref[part_of(g, HEAD_DIM), :] + memory_state(two_ref, first, g)
             for g in range(KV_HEADS)
         ]
-        heads = read_memory(states, q_ref, gains_ref, jnp.where(same, 1.0, 0.0))
-
-        def mixed(g, i):
-            summed = summed_ref[part_of(g, HEAD_DIM), part_of(i, rows)]
-            return heads[g * GROUPS + i] + summed
-
-        store_heads(mixed, out_ref, held, sems)
+        read_and_store(states, q_ref, gains_ref, same, summed_ref, out_ref, held, sems)
 
 
 def near_device(n_seq, queries, keys, values, doc_ids, beta, lin_gain):
@@ -455,15 +463,15 @@
         pltpu.VMEM((rows, HEADS * HEAD_DIM), jnp.float32),
         pltpu.SemaphoreType.DMA((KV_HEADS,)),
     ]
-    summed, state, out = pl.pallas_call(
+    read, state, out = pl.pallas_call(
         functools.partial(early_kernel, plan),
-        out_shape=[group_shape, state_shape, out_shape],
+        out_shape=[gains_shape, state_shape, out_shape],
         in_specs=[vmem] * 8,
         out_specs=[vmem] * 2 + [hbm],
         scratch_shapes=store_scratch,
         input_output_aliases={7: 0},
         compiler_params=params,
-    )(queries, own, one, three, stats, gains, read, summed)
+    )(queries, own, one, three, stats, gains, summed, read)
     return pl.pallas_call(
         functools.partial(late_kernel, plan),
         out_shape=out_shape,

time: 15.5 us -> 14.5 us (0.935)
  the two profiles are of different devices: /device:TPU:4 before, /device:TPU:27 now
where the time goes in v13:
time: 14.5 us; the launch traced here: 14.3 us
  starting transfers between devices  6.29 us (43%)
  Pallas kernels  6.02 us (42%)
  waiting for transfers between devices  1.87 us (13%)
    ppermute x3, starting transfers between devices, send(): return lax.ppermute(payload, ('seq', 'kv'), pairs)  6.29 us
    pallas_call x1, Pallas kernels, near_device(): pl.pallas_call(functools.partial(late_kernel, plan), out_shape=out_shape,...  2.05 us
    pallas_call x1, Pallas kernels, near_device(): pl.pallas_call(functools.partial(own_kernel, plan), out_shape=results, in...  1.88 us
    ppermute x3, waiting for transfers between devices, send(): return lax.ppermute(payload, ('seq', 'kv'), pairs)  1.87 us
    pallas_call x1, Pallas kernels, near_device(): pl.pallas_call(functools.partial(pack_kernel, plan), out_shape=longer_sha...  0.98 us
    pallas_call x1, Pallas kernels, near_device(): pl.pallas_call(functools.partial(read_kernel, plan), out_shape=gains_shap...  0.88 us
  transfers between devices with their start and end apart: 3, of which 2 were waited for; matrix products, arithmetic and copies ran while one was open for 0% of the time, Pallas kernels for 21%

profile of v13, /device:TPU:27, one launch (start us, length us, event | category | flops | bytes accessed | tf_op | source)
XLA Modules:
  0.0 14.3 jit_solution(17475185224658927689)
XLA Ops:
  0.0 0.0 copy-start.1
  0.0 1.0 %shard_map.64.packed_ref = bf16[1056,128]{1,0:T(8,128)(2,1)S(1)} custom-call(bf16[128,512]{1,0:T(8,128)(2,1)} %key_ref.3, bf16[128,512]{1,0:T(8,128)(2,1)} %value_ref.3, s32[1,128]{1,0:T(1,128)} %bitcast.4), custom_call_target="tpu_custom_call" | custom-call | flops 13421772 | bytes 419430 | tf_op jit(solution)/shard_map/pallas_call | solution.py:417
  1.0 2.8 %collective-permute-start.1 = (bf16[1056,128]{1,0:T(8,128)(2,1)S(1)}, bf16[1056,128]{1,0:T(8,128)(2,1)S(1)}, u32[]{:S(2)}, u32[]{:S(2)}) collective-permute-start(bf16[1056,128]{1,0:T(8,128)(2,1)S(1)} %shard_map.64.packed_ref), channel_id=1, source_target_pairs={{8,16},{12,20},{0,4},{4,8},{24,28},{9,17},{13,21},{1,5},{5,9},{25,... | collective-permute-start | bytes 811016 | tf_op jit(solution)/shard_map/ppermute | solution.py:404
  3.8 0.0 copy-done.1
  3.8 0.0 copy-start
  3.8 0.2 %shard_map.65 = (bf16[1056,128]{1,0:T(8,128)(2,1)S(1)}, bf16[1040,128]{1,0:T(8,128)(2,1)S(1)}, f32[512,512]{1,0:T(8,128)S(1)}, f32[16,512]{1,0:T(8,128)S(1)}, f32[2048,128]{1,0:T(8,128)S(1)}) custom-call(f32[16,128]{1,0:T(8,128)S(1)} %bitcast.2, bf16[1056,128]{1,0:T(8,128)(2,1)S(1)} %shard_map.64.packed_ref, bf16[128,2048]{1,0:T(8,128)(2,1)} %q_ref.7, ...), custom_call_target="tpu_custom_call" | custom-call | flops 134217728 | bytes 4194304 | tf_op jit(solution)/shard_map/pallas_call | solution.py:427
  4.0 2.2 %collective-permute-start = (bf16[1056,128]{1,0:T(8,128)(2,1)S(1)}, bf16[1056,128]{1,0:T(8,128)(2,1)S(1)}, u32[]{:S(2)}, u32[]{:S(2)}) collective-permute-start(bf16[1056,128]{1,0:T(8,128)(2,1)S(1)} %get-tuple-element.17), channel_id=1, source_target_pairs={{8,12},{12,16},{16,20},{20,24},{9,13},{13,17},{17,21},{21,25},{10,... | collective-permute-start | bytes 811016 | tf_op jit(solution)/shard_map/ppermute | solution.py:404
  6.2 1.3 %collective-permute-start.2 = (bf16[1040,128]{1,0:T(8,128)(2,1)S(1)}, bf16[1040,128]{1,0:T(8,128)(2,1)S(1)}, u32[]{:S(2)}, u32[]{:S(2)}) collective-permute-start(bf16[1040,128]{1,0:T(8,128)(2,1)S(1)} %get-tuple-element.16.own_ref), channel_id=1, source_target_pairs={{0,8},{4,12},{16,24},{20,28},{1,9},{5,13},{17,25},{21,29},{2,10},{... | collective-permute-start | bytes 798728 | tf_op jit(solution)/shard_map/ppermute | solution.py:404
  7.5 0.0 copy-done
  7.5 1.9 %shard_map.66 = (f32[512,512]{1,0:T(8,128)S(1)}, f32[16,512]{1,0:T(8,128)S(1)}, f32[2048,128]{1,0:T(8,128)S(1)}) custom-call(bf16[128,2048]{1,0:T(8,128)(2,1)S(1)} %copy-done, f32[16,128]{1,0:T(8,128)S(1)} %bitcast.3, bf16[1040,128]{1,0:T(8,128)(2,1)S(1)} %get-tuple-element.16.own_ref, ...), custom_call_target="tpu_custom_call", output_to_operand_aliasing={{0}: (4, {}), {1}: (5, {}), {2}: (6, {})} | custom-call | flops 134217728 | bytes 4194304 | tf_op jit(solution)/shard_map/pallas_call | solution.py:444
  9.4 0.2 %collective-permute-done.2.three_ref = bf16[1040,128]{1,0:T(8,128)(2,1)S(1)} collective-permute-done((bf16[1040,128]{1,0:T(8,128)(2,1)S(1)}, bf16[1040,128]{1,0:T(8,128)(2,1)S(1)}, u32[]{:S(2)}, u32[]{:S(2)}) %collective-permute-start.2) | collective-permute-done | bytes 266272 | tf_op jit(solution)/shard_map/ppermute | solution.py:404
  9.6 0.9 %shard_map.67.read_in = f32[2048,128]{1,0:T(8,128)S(1)} custom-call(bf16[128,2048]{1,0:T(8,128)(2,1)S(1)} %copy-done, bf16[1040,128]{1,0:T(8,128)(2,1)S(1)} %get-tuple-element.16.own_ref, bf16[1040,128]{1,0:T(8,128)(2,1)S(1)} %collective-permute-done.2.three_ref, f32[2048,128]{1,0:T(8,128)S(1)} %get-tuple-element.22.gains_ref), custom_call_target="tpu_custom_call" | custom-call | tf_op jit(solution)/shard_map/pallas_call | solution.py:454
  10.5 0.0 collective-permute-done.1.one_ref
  10.5 0.1 shard_map.68
  10.6 1.6 %collective-permute-done.two_ref = bf16[1056,128]{1,0:T(8,128)(2,1)S(1)} collective-permute-done((bf16[1056,128]{1,0:T(8,128)(2,1)S(1)}, bf16[1056,128]{1,0:T(8,128)(2,1)S(1)}, u32[]{:S(2)}, u32[]{:S(2)}) %collective-permute-start) | collective-permute-done | bytes 270368 | tf_op jit(solution)/shard_map/ppermute | solution.py:404
  12.2 2.0 %shard_map.69 = f32[128,2048]{1,0:T(8,128)} custom-call(bf16[128,2048]{1,0:T(8,128)(2,1)S(1)} %copy-done, bf16[1040,128]{1,0:T(8,128)(2,1)S(1)} %get-tuple-element.16.own_ref, bf16[1056,128]{1,0:T(8,128)(2,1)S(1)} %collective-permute-done.two_ref, f32[512,128]{1,0:T(8,128)S(1)} %get-tuple-element.24.state_ref, ...), custom_call_target="tpu_custom_call", output_to_operand_aliasing={{}: (8, {})} | custom-call | tf_op jit(solution)/shard_map/pallas_call | solution.py:475
Async XLA Ops:
  0.0 3.8 %copy-start.1 = (f32[2048]{0:T(1024)S(1)}, f32[2048]{0:T(1024)}, u32[]{:S(2)}) copy-start(f32[2048]{0:T(1024)} %param.11) | copy-start | bytes 24580
  1.0 9.5 %collective-permute-start.1 = (bf16[1056,128]{1,0:T(8,128)(2,1)S(1)}, bf16[1056,128]{1,0:T(8,128)(2,1)S(1)}, u32[]{:S(2)}, u32[]{:S(2)}) collective-permute-start(bf16[1056,128]{1,0:T(8,128)(2,1)S(1)} %shard_map.64.packed_ref), channel_id=1, source_target_pairs={{8,16},{12,20},{0,4},{4,8},{24,28},{9,17},{13,21},{1,5},{5,9},{25,... | collective-permute-start | bytes 811016 | tf_op jit(solution)/shard_map/ppermute | solution.py:404
  3.8 3.7 %copy-start = (bf16[128,2048]{1,0:T(8,128)(2,1)S(1)}, bf16[128,2048]{1,0:T(8,128)(2,1)}, u32[]{:S(2)}) copy-start(bf16[128,2048]{1,0:T(8,128)(2,1)} %q_ref.7) | copy-start | bytes 1572868
  4.0 8.2 %collective-permute-start = (bf16[1056,128]{1,0:T(8,128)(2,1)S(1)}, bf16[1056,128]{1,0:T(8,128)(2,1)S(1)}, u32[]{:S(2)}, u32[]{:S(2)}) collective-permute-start(bf16[1056,128]{1,0:T(8,128)(2,1)S(1)} %get-tuple-element.17), channel_id=1, source_target_pairs={{8,12},{12,16},{16,20},{20,24},{9,13},{13,17},{17,21},{21,25},{10,... | collective-permute-start | bytes 811016 | tf_op jit(solution)/shard_map/ppermute | solution.py:404
  6.2 3.4 %collective-permute-start.2 = (bf16[1040,128]{1,0:T(8,128)(2,1)S(1)}, bf16[1040,128]{1,0:T(8,128)(2,1)S(1)}, u32[]{:S(2)}, u32[]{:S(2)}) collective-permute-start(bf16[1040,128]{1,0:T(8,128)(2,1)S(1)} %get-tuple-element.16.own_ref), channel_id=1, source_target_pairs={{0,8},{4,12},{16,24},{20,28},{1,9},{5,13},{17,25},{21,29},{2,10},{... | collective-permute-start | bytes 798728 | tf_op jit(solution)/shard_map/ppermute | solution.py:404

commit v14 on v13

--- a/solution.py
+++ b/solution.py
@@ -275,12 +275,18 @@
 
 
 def store_heads(mixed, out_ref, held, sems):
+    rows = held.shape[0]
+    line = lax.broadcasted_iota(jnp.int32, (rows, 2 * rows), 0)
+    place = lax.broadcasted_iota(jnp.int32, (rows, 2 * rows), 1)
+    same = (place == line) | (place == line + rows)
+    identity = jnp.where(same, 1.0, 0.0).astype(jnp.bfloat16)
     copies = []
     for g in range(KV_HEADS):
-        for i in range(GROUPS):
-            h = g * GROUPS + i
-            held[:, part_of(h, HEAD_DIM)] = jnp.transpose(mixed(g, i))
+        heads = jnp.concatenate([mixed(g, i) for i in range(GROUPS)], axis=0)
+        high = heads.astype(jnp.bfloat16)
+        low = (heads - high.astype(jnp.float32)).astype(jnp.bfloat16)
         wide = part_of(g, GROUPS * HEAD_DIM)
+        held[:, wide] = dot(identity, jnp.concatenate([high, low], axis=1), NT)
         copies.append(pltpu.make_async_copy(held.at[:, wide], out_ref.at[:, wide], sems.at[g]))
         copies[g].start()
     for copy in copies:

time: 14.5 us -> 14.8 us (1.021)
  Pallas kernels: 6.02 us -> 6.26 us
    pallas_call x1, Pallas kernels: 2.05 us -> 2.3 us  [near_device(): pl.pallas_call(functools.partial(late_kernel, plan), out_shape=out_shape,...]
where the time goes in v14:
time: 14.8 us; the launch traced here: 14.5 us
  starting transfers between devices  6.29 us (42%)
  Pallas kernels  6.26 us (42%)
  waiting for transfers between devices  1.87 us (13%)
    ppermute x3, starting transfers between devices, send(): return lax.ppermute(payload, ('seq', 'kv'), pairs)  6.29 us
    pallas_call x1, Pallas kernels, near_device(): pl.pallas_call(functools.partial(late_kernel, plan), out_shape=out_shape,...  2.3 us
    pallas_call x1, Pallas kernels, near_device(): pl.pallas_call(functools.partial(own_kernel, plan), out_shape=results, in...  1.88 us
    ppermute x3, waiting for transfers between devices, send(): return lax.ppermute(payload, ('seq', 'kv'), pairs)  1.87 us
    pallas_call x1, Pallas kernels, near_device(): pl.pallas_call(functools.partial(pack_kernel, plan), out_shape=longer_sha...  0.98 us
    pallas_call x1, Pallas kernels, near_device(): pl.pallas_call(functools.partial(read_kernel, plan), out_shape=gains_shap...  0.88 us
  transfers between devices with their start and end apart: 3, of which 2 were waited for; matrix products, arithmetic and copies ran while one was open for 0% of the time, Pallas kernels for 21%

profile of v14, /device:TPU:27, one launch (start us, length us, event | category | flops | bytes accessed | tf_op | source)
XLA Modules:
  0.0 14.5 jit_solution(5050519998811970268)
XLA Ops:
  0.0 0.0 copy-start.1
  0.0 1.0 %shard_map.64.packed_ref = bf16[1056,128]{1,0:T(8,128)(2,1)S(1)} custom-call(bf16[128,512]{1,0:T(8,128)(2,1)} %key_ref.3, bf16[128,512]{1,0:T(8,128)(2,1)} %value_ref.3, s32[1,128]{1,0:T(1,128)} %bitcast.4), custom_call_target="tpu_custom_call" | custom-call | flops 13421772 | bytes 419430 | tf_op jit(solution)/shard_map/pallas_call | solution.py:423
  1.0 2.8 %collective-permute-start.1 = (bf16[1056,128]{1,0:T(8,128)(2,1)S(1)}, bf16[1056,128]{1,0:T(8,128)(2,1)S(1)}, u32[]{:S(2)}, u32[]{:S(2)}) collective-permute-start(bf16[1056,128]{1,0:T(8,128)(2,1)S(1)} %shard_map.64.packed_ref), channel_id=1, source_target_pairs={{8,16},{12,20},{0,4},{4,8},{24,28},{9,17},{13,21},{1,5},{5,9},{25,... | collective-permute-start | bytes 811016 | tf_op jit(solution)/shard_map/ppermute | solution.py:410
  3.8 0.0 copy-done.1
  3.8 0.0 copy-start
  3.8 0.2 %shard_map.65 = (bf16[1056,128]{1,0:T(8,128)(2,1)S(1)}, bf16[1040,128]{1,0:T(8,128)(2,1)S(1)}, f32[512,512]{1,0:T(8,128)S(1)}, f32[16,512]{1,0:T(8,128)S(1)}, f32[2048,128]{1,0:T(8,128)S(1)}) custom-call(f32[16,128]{1,0:T(8,128)S(1)} %bitcast.2, bf16[1056,128]{1,0:T(8,128)(2,1)S(1)} %shard_map.64.packed_ref, bf16[128,2048]{1,0:T(8,128)(2,1)} %q_ref.7, ...), custom_call_target="tpu_custom_call" | custom-call | flops 134217728 | bytes 4194304 | tf_op jit(solution)/shard_map/pallas_call | solution.py:433
  4.0 2.2 %collective-permute-start = (bf16[1056,128]{1,0:T(8,128)(2,1)S(1)}, bf16[1056,128]{1,0:T(8,128)(2,1)S(1)}, u32[]{:S(2)}, u32[]{:S(2)}) collective-permute-start(bf16[1056,128]{1,0:T(8,128)(2,1)S(1)} %get-tuple-element.17), channel_id=1, source_target_pairs={{8,12},{12,16},{16,20},{20,24},{9,13},{13,17},{17,21},{21,25},{10,... | collective-permute-start | bytes 811016 | tf_op jit(solution)/shard_map/ppermute | solution.py:410
  6.2 1.3 %collective-permute-start.2 = (bf16[1040,128]{1,0:T(8,128)(2,1)S(1)}, bf16[1040,128]{1,0:T(8,128)(2,1)S(1)}, u32[]{:S(2)}, u32[]{:S(2)}) collective-permute-start(bf16[1040,128]{1,0:T(8,128)(2,1)S(1)} %get-tuple-element.16.own_ref), channel_id=1, source_target_pairs={{0,8},{4,12},{16,24},{20,28},{1,9},{5,13},{17,25},{21,29},{2,10},{... | collective-permute-start | bytes 798728 | tf_op jit(solution)/shard_map/ppermute | solution.py:410
  7.5 0.0 copy-done
  7.5 1.9 %shard_map.66 = (f32[512,512]{1,0:T(8,128)S(1)}, f32[16,512]{1,0:T(8,128)S(1)}, f32[2048,128]{1,0:T(8,128)S(1)}) custom-call(bf16[128,2048]{1,0:T(8,128)(2,1)S(1)} %copy-done, f32[16,128]{1,0:T(8,128)S(1)} %bitcast.3, bf16[1040,128]{1,0:T(8,128)(2,1)S(1)} %get-tuple-element.16.own_ref, ...), custom_call_target="tpu_custom_call", output_to_operand_aliasing={{0}: (4, {}), {1}: (5, {}), {2}: (6, {})} | custom-call | flops 134217728 | bytes 4194304 | tf_op jit(solution)/shard_map/pallas_call | solution.py:450
  9.4 0.2 %collective-permute-done.2.three_ref = bf16[1040,128]{1,0:T(8,128)(2,1)S(1)} collective-permute-done((bf16[1040,128]{1,0:T(8,128)(2,1)S(1)}, bf16[1040,128]{1,0:T(8,128)(2,1)S(1)}, u32[]{:S(2)}, u32[]{:S(2)}) %collective-permute-start.2) | collective-permute-done | bytes 266272 | tf_op jit(solution)/shard_map/ppermute | solution.py:410
  9.6 0.9 %shard_map.67.read_in = f32[2048,128]{1,0:T(8,128)S(1)} custom-call(bf16[128,2048]{1,0:T(8,128)(2,1)S(1)} %copy-done, bf16[1040,128]{1,0:T(8,128)(2,1)S(1)} %get-tuple-element.16.own_ref, bf16[1040,128]{1,0:T(8,128)(2,1)S(1)} %collective-permute-done.2.three_ref, f32[2048,128]{1,0:T(8,128)S(1)} %get-tuple-element.22.gains_ref), custom_call_target="tpu_custom_call" | custom-call | tf_op jit(solution)/shard_map/pallas_call | solution.py:460
  10.5 0.0 collective-permute-done.1.one_ref
  10.5 0.1 shard_map.68
  10.6 1.6 %collective-permute-done.two_ref = bf16[1056,128]{1,0:T(8,128)(2,1)S(1)} collective-permute-done((bf16[1056,128]{1,0:T(8,128)(2,1)S(1)}, bf16[1056,128]{1,0:T(8,128)(2,1)S(1)}, u32[]{:S(2)}, u32[]{:S(2)}) %collective-permute-start) | collective-permute-done | bytes 270368 | tf_op jit(solution)/shard_map/ppermute | solution.py:410
  12.2 2.3 %shard_map.69 = f32[128,2048]{1,0:T(8,128)} custom-call(bf16[128,2048]{1,0:T(8,128)(2,1)S(1)} %copy-done, bf16[1040,128]{1,0:T(8,128)(2,1)S(1)} %get-tuple-element.16.own_ref, bf16[1056,128]{1,0:T(8,128)(2,1)S(1)} %collective-permute-done.two_ref, f32[512,128]{1,0:T(8,128)S(1)} %get-tuple-element.24.state_ref, ...), custom_call_target="tpu_custom_call", output_to_operand_aliasing={{}: (8, {})} | custom-call | tf_op jit(solution)/shard_map/pallas_call | solution.py:481
Async XLA Ops:
  0.0 3.8 %copy-start.1 = (f32[2048]{0:T(1024)S(1)}, f32[2048]{0:T(1024)}, u32[]{:S(2)}) copy-start(f32[2048]{0:T(1024)} %param.11) | copy-start | bytes 24580
  1.0 9.5 %collective-permute-start.1 = (bf16[1056,128]{1,0:T(8,128)(2,1)S(1)}, bf16[1056,128]{1,0:T(8,128)(2,1)S(1)}, u32[]{:S(2)}, u32[]{:S(2)}) collective-permute-start(bf16[1056,128]{1,0:T(8,128)(2,1)S(1)} %shard_map.64.packed_ref), channel_id=1, source_target_pairs={{8,16},{12,20},{0,4},{4,8},{24,28},{9,17},{13,21},{1,5},{5,9},{25,... | collective-permute-start | bytes 811016 | tf_op jit(solution)/shard_map/ppermute | solution.py:410
  3.8 3.7 %copy-start = (bf16[128,2048]{1,0:T(8,128)(2,1)S(1)}, bf16[128,2048]{1,0:T(8,128)(2,1)}, u32[]{:S(2)}) copy-start(bf16[128,2048]{1,0:T(8,128)(2,1)} %q_ref.7) | copy-start | bytes 1572868
  4.0 8.2 %collective-permute-start = (bf16[1056,128]{1,0:T(8,128)(2,1)S(1)}, bf16[1056,128]{1,0:T(8,128)(2,1)S(1)}, u32[]{:S(2)}, u32[]{:S(2)}) collective-permute-start(bf16[1056,128]{1,0:T(8,128)(2,1)S(1)} %get-tuple-element.17), channel_id=1, source_target_pairs={{8,12},{12,16},{16,20},{20,24},{9,13},{13,17},{17,21},{21,25},{10,... | collective-permute-start | bytes 811016 | tf_op jit(solution)/shard_map/ppermute | solution.py:410
  6.2 3.4 %collective-permute-start.2 = (bf16[1040,128]{1,0:T(8,128)(2,1)S(1)}, bf16[1040,128]{1,0:T(8,128)(2,1)S(1)}, u32[]{:S(2)}, u32[]{:S(2)}) collective-permute-start(bf16[1040,128]{1,0:T(8,128)(2,1)S(1)} %get-tuple-element.16.own_ref), channel_id=1, source_target_pairs={{0,8},{4,12},{16,24},{20,28},{1,9},{5,13},{17,25},{21,29},{2,10},{... | collective-permute-start | bytes 798728 | tf_op jit(solution)/shard_map/ppermute | solution.py:410

commit v15 on v13

--- a/solution.py
+++ b/solution.py
@@ -48,8 +48,8 @@
         out_ref[part_of(h, HEAD_DIM), :] = column(scaled)
 
 
-def suffix(others):
-    count = jnp.sum(others, axis=1, keepdims=True)
+def suffix(others, least=0.0):
+    count = jnp.maximum(jnp.sum(others, axis=1, keepdims=True), least)
     shape = (others.shape[1], HEAD_DIM)
     return lax.broadcasted_iota(jnp.int32, shape, 0).astype(jnp.float32) >= count
 
@@ -166,13 +166,12 @@
 
 def settle_kernel(
     plan, gain_ref, packed_ref, query_ref, key_ref, value_ref, doc_ref, beta_ref,
-    second_ref, own_ref, summed_ref, stats_ref, gains_ref,
+    own_ref, short_ref, summed_ref, stats_ref, gains_ref,
     q_scratch, beta_scratch, doc_scratch, sems, early_sems,
 ):
     sender, early = among(plan.senders), among(plan.early)
     query_copy = pltpu.make_async_copy(query_ref, q_scratch, early_sems.at[0])
     beta_copy = pltpu.make_async_copy(beta_ref, beta_scratch, early_sems.at[1])
-    deep = own_ref.shape[0]
 
     @pl.when(early)
     def _():
@@ -181,14 +180,17 @@
 
     @pl.when(sender)
     def _():
-        own_ref[...] = packed_ref[0:deep, :]
+        own_ref[...] = packed_ref[...]
 
     @pl.when(jnp.logical_not(sender))
     def _():
         load_block(key_ref, value_ref, doc_ref, own_ref, doc_scratch, sems)
 
-    second_ref[0:deep, :] = own_ref[...]
-    second_ref[deep:, :] = jnp.zeros((EXTRA, HEAD_DIM), jnp.bfloat16)
+    short_ref[...] = own_ref[0 : short_ref.shape[0], :]
+    line = lax.broadcasted_iota(jnp.int32, (EXTRA, HEAD_DIM), 0)
+    keys = own_ref[0:EXTRA, :].astype(jnp.float32)
+    keys = jnp.where(line == 0, block_docs(own_ref), keys)
+    short_ref[0:EXTRA, :] = keys.astype(jnp.bfloat16)
 
     @pl.when(early)
     def _():
@@ -213,7 +215,9 @@
 
 
 def memory_state(ref, first, g):
-    live = suffix(jnp.where(block_docs(ref) == first, 0.0, 1.0))
+    short = ref.shape[0] == 2 * KV_HEADS * HEAD_DIM
+    docs = ref[0:EXTRA, :].astype(jnp.float32)[0:1, :] if short else block_docs(ref)
+    live = suffix(jnp.where(docs == first, 0.0, 1.0), 1.0 if short else 0.0)
     keys = jnp.where(live, block_keys(ref, g).astype(jnp.float32), 0.0).astype(jnp.bfloat16)
     return dot(block_values(ref, g), keys, TN)
 
@@ -252,13 +256,15 @@
     rows = q_ref.shape[0]
     live = suffix(jnp.where(block_docs(one_ref) == first, 0.0, 1.0))
     bias = jnp.where(live & same, 0.0, LOWEST)
-    results = []
-    for g in range(KV_HEADS):
-        scores = dot(block_keys(one_ref, g), group_queries(q_ref, g), NT)
+    scores = [
+        dot(block_keys(one_ref, g), group_queries(q_ref, g), NT) for g in range(KV_HEADS)
+    ]
+
+    def attend(g):
         weights, factors, scales = [], [], []
         for i in range(GROUPS):
             cut = part_of(i, rows)
-            masked = scores[:, cut] * SCALE + bias
+            masked = scores[g][:, cut] * SCALE + bias
             top_own = stats_ref[g : g + 1, cut]
             top = jnp.maximum(jnp.max(masked, axis=0, keepdims=True), top_own)
             weight = jnp.exp2(masked - top)
@@ -270,16 +276,16 @@
             weights.append(weight.astype(jnp.bfloat16))
         added = dot(block_values(one_ref, g), jnp.concatenate(weights, axis=1), TN)
         summed = summed_ref[part_of(g, HEAD_DIM), :] * jnp.concatenate(factors, axis=1) + added
-        results.append(summed * jnp.concatenate(scales, axis=1))
-    return results
+        return summed * jnp.concatenate(scales, axis=1)
+
+    return attend
 
 
 def store_heads(mixed, out_ref, held, sems):
     copies = []
     for g in range(KV_HEADS):
-        for i in range(GROUPS):
-            h = g * GROUPS + i
-            held[:, part_of(h, HEAD_DIM)] = jnp.transpose(mixed(g, i))
+        for i, head in enumerate(mixed(g)):
+            held[:, part_of(g * GROUPS + i, HEAD_DIM)] = jnp.transpose(head)
         wide = part_of(g, GROUPS * HEAD_DIM)
         copies.append(pltpu.make_async_copy(held.at[:, wide], out_ref.at[:, wide], sems.at[g]))
         copies[g].start()
@@ -306,12 +312,15 @@
     q_ref, own_ref, earlier_ref, stats_ref, summed_ref, read_ref, out_ref, held, sems
 ):
     first, same = first_document(block_docs(own_ref))
-    results = attend_before(q_ref, earlier_ref, stats_ref, summed_ref, first, same)
+    attend = attend_before(q_ref, earlier_ref, stats_ref, summed_ref, first, same)
     rows = q_ref.shape[0]
 
-    def mixed(g, i):
-        read = read_ref[part_of(g * GROUPS + i, HEAD_DIM), :]
-        return read + results[g][:, part_of(i, rows)]
+    def mixed(g):
+        attended = attend(g)
+        return [
+            read_ref[part_of(g * GROUPS + i, HEAD_DIM), :] + attended[:, part_of(i, rows)]
+            for i in range(GROUPS)
+        ]
 
     store_heads(mixed, out_ref, held, sems)
 
@@ -320,9 +329,11 @@
     rows = q_ref.shape[0]
     heads = read_memory(states, q_ref, gains_ref, jnp.where(same, 1.0, 0.0))
 
-    def mixed(g, i):
-        summed = summed_ref[part_of(g, HEAD_DIM), part_of(i, rows)]
-        return heads[g * GROUPS + i] + summed
+    def mixed(g):
+        return [
+            heads[g * GROUPS + i] + summed_ref[part_of(g, HEAD_DIM), part_of(i, rows)]
+            for i in range(GROUPS)
+        ]
 
     store_heads(mixed, out_ref, held, sems)
 
@@ -405,7 +416,7 @@
 
     plan = Plan(n_seq)
     block_shape = jax.ShapeDtypeStruct((deep, HEAD_DIM), jnp.bfloat16)
-    longer_shape = jax.ShapeDtypeStruct((deep + EXTRA, HEAD_DIM), jnp.bfloat16)
+    short_shape = jax.ShapeDtypeStruct((deep - EXTRA, HEAD_DIM), jnp.bfloat16)
     stats_shape = jax.ShapeDtypeStruct((4 * KV_HEADS, wide), jnp.float32)
     state_shape = jax.ShapeDtypeStruct((KV_HEADS * HEAD_DIM, HEAD_DIM), jnp.float32)
     results = [group_shape, stats_shape, gains_shape]
@@ -416,7 +427,7 @@
     beta = in_hbm(beta)
     packed = pl.pallas_call(
         functools.partial(pack_kernel, plan),
-        out_shape=longer_shape,
+        out_shape=block_shape,
         in_specs=[hbm] * 3,
         out_specs=vmem,
         scratch_shapes=[doc_scratch, sems],
@@ -424,9 +435,9 @@
         cost_estimate=estimate(0.1),
     )(*block)
     one = send(packed, plan.pairs[0])
-    second, own, summed, stats, gains = pl.pallas_call(
+    own, short, summed, stats, gains = pl.pallas_call(
         functools.partial(settle_kernel, plan),
-        out_shape=[longer_shape, block_shape] + results,
+        out_shape=[block_shape, short_shape] + results,
         in_specs=[vmem] * 2 + [hbm] * 5,
         out_specs=[vmem] * 5,
         scratch_shapes=[
@@ -439,8 +450,8 @@
         compiler_params=params,
         cost_estimate=estimate(1.0),
     )(gain, packed, in_hbm(queries), *block, beta)
-    two = send(second, plan.pairs[1])
-    three = send(own, plan.pairs[2])
+    two = send(own, plan.pairs[1])
+    three = send(short, plan.pairs[2])
     summed, stats, gains = pl.pallas_call(
         functools.partial(own_kernel, plan),
         out_shape=results,

time: 14.5 us -> 14.1 us (0.972)
  Pallas kernels: 6.02 us -> 5.72 us
    pallas_call x1, Pallas kernels: 2.05 us -> 1.73 us  [near_device(): pl.pallas_call(functools.partial(late_kernel, plan), out_shape=out_shape,...]
  transfers between devices with their start and end apart: 3 -> 3, of which waited for: 2 -> 2; matrix products, arithmetic and copies ran while one was open for 0% -> 0% of each run, Pallas kernels for 21% -> 22%
where the time goes in v15:
time: 14.1 us; the launch traced here: 13.9 us
  starting transfers between devices  6.29 us (45%)
  Pallas kernels  5.72 us (41%)
  waiting for transfers between devices  1.75 us (12%)
    ppermute x3, starting transfers between devices, send(): return lax.ppermute(payload, ('seq', 'kv'), pairs)  6.29 us
    pallas_call x1, Pallas kernels, near_device(): pl.pallas_call(functools.partial(own_kernel, plan), out_shape=results, in...  1.89 us
    ppermute x3, waiting for transfers between devices, send(): return lax.ppermute(payload, ('seq', 'kv'), pairs)  1.75 us
    pallas_call x1, Pallas kernels, near_device(): pl.pallas_call(functools.partial(late_kernel, plan), out_shape=out_shape,...  1.73 us
    pallas_call x1, Pallas kernels, near_device(): pl.pallas_call(functools.partial(pack_kernel, plan), out_shape=block_shap...  0.98 us
    pallas_call x1, Pallas kernels, near_device(): pl.pallas_call(functools.partial(read_kernel, plan), out_shape=gains_shap...  0.89 us
  transfers between devices with their start and end apart: 3, of which 2 were waited for; matrix products, arithmetic and copies ran while one was open for 0% of the time, Pallas kernels for 22%

profile of v15, /device:TPU:27, one launch (start us, length us, event | category | flops | bytes accessed | tf_op | source)
XLA Modules:
  0.0 13.9 jit_solution(5446528643454022954)
XLA Ops:
  0.0 0.0 copy-start.1
  0.0 1.0 %shard_map.64.packed_ref = bf16[1040,128]{1,0:T(8,128)(2,1)S(1)} custom-call(bf16[128,512]{1,0:T(8,128)(2,1)} %key_ref.3, bf16[128,512]{1,0:T(8,128)(2,1)} %value_ref.3, s32[1,128]{1,0:T(1,128)} %bitcast.4), custom_call_target="tpu_custom_call" | custom-call | flops 13421772 | bytes 419430 | tf_op jit(solution)/shard_map/pallas_call | solution.py:428
  1.0 2.8 %collective-permute-start.1 = (bf16[1040,128]{1,0:T(8,128)(2,1)S(1)}, bf16[1040,128]{1,0:T(8,128)(2,1)S(1)}, u32[]{:S(2)}, u32[]{:S(2)}) collective-permute-start(bf16[1040,128]{1,0:T(8,128)(2,1)S(1)} %shard_map.64.packed_ref), channel_id=1, source_target_pairs={{8,16},{12,20},{0,4},{4,8},{24,28},{9,17},{13,21},{1,5},{5,9},{25,... | collective-permute-start | bytes 798728 | tf_op jit(solution)/shard_map/ppermute | solution.py:415
  3.8 0.0 copy-done.1
  3.8 0.0 copy-start
  3.8 0.2 %shard_map.65 = (bf16[1040,128]{1,0:T(8,128)(2,1)S(1)}, bf16[1024,128]{1,0:T(8,128)(2,1)S(1)}, f32[512,512]{1,0:T(8,128)S(1)}, f32[16,512]{1,0:T(8,128)S(1)}, f32[2048,128]{1,0:T(8,128)S(1)}) custom-call(f32[16,128]{1,0:T(8,128)S(1)} %bitcast.2, bf16[1040,128]{1,0:T(8,128)(2,1)S(1)} %shard_map.64.packed_ref, bf16[128,2048]{1,0:T(8,128)(2,1)} %q_ref.7, ...), custom_call_target="tpu_custom_call" | custom-call | flops 134217728 | bytes 4194304 | tf_op jit(solution)/shard_map/pallas_call | solution.py:438
  4.0 2.2 %collective-permute-start = (bf16[1040,128]{1,0:T(8,128)(2,1)S(1)}, bf16[1040,128]{1,0:T(8,128)(2,1)S(1)}, u32[]{:S(2)}, u32[]{:S(2)}) collective-permute-start(bf16[1040,128]{1,0:T(8,128)(2,1)S(1)} %get-tuple-element.16.own_ref), channel_id=1, source_target_pairs={{8,12},{12,16},{16,20},{20,24},{9,13},{13,17},{17,21},{21,25},{10,... | collective-permute-start | bytes 798728 | tf_op jit(solution)/shard_map/ppermute | solution.py:415
  6.2 1.3 %collective-permute-start.2 = (bf16[1024,128]{1,0:T(8,128)(2,1)S(1)}, bf16[1024,128]{1,0:T(8,128)(2,1)S(1)}, u32[]{:S(2)}, u32[]{:S(2)}) collective-permute-start(bf16[1024,128]{1,0:T(8,128)(2,1)S(1)} %get-tuple-element.17), channel_id=1, source_target_pairs={{0,8},{4,12},{16,24},{20,28},{1,9},{5,13},{17,25},{21,29},{2,10},{... | collective-permute-start | bytes 786440 | tf_op jit(solution)/shard_map/ppermute | solution.py:415
  7.5 0.0 copy-done
  7.5 1.9 %shard_map.66 = (f32[512,512]{1,0:T(8,128)S(1)}, f32[16,512]{1,0:T(8,128)S(1)}, f32[2048,128]{1,0:T(8,128)S(1)}) custom-call(bf16[128,2048]{1,0:T(8,128)(2,1)S(1)} %copy-done, f32[16,128]{1,0:T(8,128)S(1)} %bitcast.3, bf16[1040,128]{1,0:T(8,128)(2,1)S(1)} %get-tuple-element.16.own_ref, ...), custom_call_target="tpu_custom_call", output_to_operand_aliasing={{0}: (4, {}), {1}: (5, {}), {2}: (6, {})} | custom-call | flops 134217728 | bytes 4194304 | tf_op jit(solution)/shard_map/pallas_call | solution.py:455
  9.4 0.2 %collective-permute-done.2.three_ref = bf16[1024,128]{1,0:T(8,128)(2,1)S(1)} collective-permute-done((bf16[1024,128]{1,0:T(8,128)(2,1)S(1)}, bf16[1024,128]{1,0:T(8,128)(2,1)S(1)}, u32[]{:S(2)}, u32[]{:S(2)}) %collective-permute-start.2) | collective-permute-done | bytes 262176 | tf_op jit(solution)/shard_map/ppermute | solution.py:415
  9.6 0.9 %shard_map.67.read_in = f32[2048,128]{1,0:T(8,128)S(1)} custom-call(bf16[128,2048]{1,0:T(8,128)(2,1)S(1)} %copy-done, bf16[1040,128]{1,0:T(8,128)(2,1)S(1)} %get-tuple-element.16.own_ref, bf16[1024,128]{1,0:T(8,128)(2,1)S(1)} %collective-permute-done.2.three_ref, f32[2048,128]{1,0:T(8,128)S(1)} %get-tuple-element.22.gains_ref), custom_call_target="tpu_custom_call" | custom-call | tf_op jit(solution)/shard_map/pallas_call | solution.py:465
  10.5 0.0 collective-permute-done.1.one_ref
  10.5 0.1 shard_map.68
  10.6 1.5 %collective-permute-done.two_ref = bf16[1040,128]{1,0:T(8,128)(2,1)S(1)} collective-permute-done((bf16[1040,128]{1,0:T(8,128)(2,1)S(1)}, bf16[1040,128]{1,0:T(8,128)(2,1)S(1)}, u32[]{:S(2)}, u32[]{:S(2)}) %collective-permute-start) | collective-permute-done | bytes 266272 | tf_op jit(solution)/shard_map/ppermute | solution.py:415
  12.1 1.7 %shard_map.69 = f32[128,2048]{1,0:T(8,128)} custom-call(bf16[128,2048]{1,0:T(8,128)(2,1)S(1)} %copy-done, bf16[1040,128]{1,0:T(8,128)(2,1)S(1)} %get-tuple-element.16.own_ref, bf16[1040,128]{1,0:T(8,128)(2,1)S(1)} %collective-permute-done.two_ref, f32[512,128]{1,0:T(8,128)S(1)} %get-tuple-element.24.state_ref, ...), custom_call_target="tpu_custom_call", output_to_operand_aliasing={{}: (8, {})} | custom-call | tf_op jit(solution)/shard_map/pallas_call | solution.py:486
Async XLA Ops:
  0.0 3.8 %copy-start.1 = (f32[2048]{0:T(1024)S(1)}, f32[2048]{0:T(1024)}, u32[]{:S(2)}) copy-start(f32[2048]{0:T(1024)} %param.11) | copy-start | bytes 24580
  1.0 9.5 %collective-permute-start.1 = (bf16[1040,128]{1,0:T(8,128)(2,1)S(1)}, bf16[1040,128]{1,0:T(8,128)(2,1)S(1)}, u32[]{:S(2)}, u32[]{:S(2)}) collective-permute-start(bf16[1040,128]{1,0:T(8,128)(2,1)S(1)} %shard_map.64.packed_ref), channel_id=1, source_target_pairs={{8,16},{12,20},{0,4},{4,8},{24,28},{9,17},{13,21},{1,5},{5,9},{25,... | collective-permute-start | bytes 798728 | tf_op jit(solution)/shard_map/ppermute | solution.py:415
  3.8 3.7 %copy-start = (bf16[128,2048]{1,0:T(8,128)(2,1)S(1)}, bf16[128,2048]{1,0:T(8,128)(2,1)}, u32[]{:S(2)}) copy-start(bf16[128,2048]{1,0:T(8,128)(2,1)} %q_ref.7) | copy-start | bytes 1572868
  4.0 8.1 %collective-permute-start = (bf16[1040,128]{1,0:T(8,128)(2,1)S(1)}, bf16[1040,128]{1,0:T(8,128)(2,1)S(1)}, u32[]{:S(2)}, u32[]{:S(2)}) collective-permute-start(bf16[1040,128]{1,0:T(8,128)(2,1)S(1)} %get-tuple-element.16.own_ref), channel_id=1, source_target_pairs={{8,12},{12,16},{16,20},{20,24},{9,13},{13,17},{17,21},{21,25},{10,... | collective-permute-start | bytes 798728 | tf_op jit(solution)/shard_map/ppermute | solution.py:415
  6.2 3.4 %collective-permute-start.2 = (bf16[1024,128]{1,0:T(8,128)(2,1)S(1)}, bf16[1024,128]{1,0:T(8,128)(2,1)S(1)}, u32[]{:S(2)}, u32[]{:S(2)}) collective-permute-start(bf16[1024,128]{1,0:T(8,128)(2,1)S(1)} %get-tuple-element.17), channel_id=1, source_target_pairs={{0,8},{4,12},{16,24},{20,28},{1,9},{5,13},{17,25},{21,29},{2,10},{... | collective-permute-start | bytes 786440 | tf_op jit(solution)/shard_map/ppermute | solution.py:415

commit v16 on v15

--- a/solution.py
+++ b/solution.py
@@ -111,6 +111,8 @@
         busy = {b for p in first for b in p} & {b for p in second for b in p}
         self.early = [b for b in range(devices) if b not in busy]
         self.late = sorted({p[1] for p in second})
+        received = {p[1] for pairs in self.pairs for p in pairs}
+        self.alone = [b for b in range(devices) if b not in received]
         self.memory_first = [p[1] for p in crossing if p[1] % 2 == 1]
 
 
@@ -203,8 +205,14 @@
 
 def own_kernel(
     plan, q_ref, gain_ref, own_ref, beta_ref, summed_in, stats_in, gains_in,
-    summed_ref, stats_ref, gains_ref, beta_scratch, sem,
+    summed_ref, stats_ref, gains_ref, out_ref, beta_scratch, sem, held, sems,
 ):
+    @pl.when(among(plan.alone))
+    def _():
+        _, same = first_document(block_docs(own_ref))
+        states = [jnp.zeros((HEAD_DIM, HEAD_DIM), jnp.float32)] * KV_HEADS
+        read_and_store(states, q_ref, gains_ref, same, summed_ref, out_ref, held, sems)
+
     @pl.when(jnp.logical_not(among(plan.early)))
     def _():
         beta_copy = pltpu.make_async_copy(beta_ref, beta_scratch, sem)
@@ -230,41 +238,53 @@
 
 
 def read_memory(states, q_ref, gains_ref, reads):
-    pieces = []
-    for state in states:
-        high = state.astype(jnp.bfloat16)
-        state = state - high.astype(jnp.float32)
-        middle = state.astype(jnp.bfloat16)
-        low = (state - middle.astype(jnp.float32)).astype(jnp.bfloat16)
-        pieces.append(jnp.concatenate([high, middle, low], axis=0))
-    products = [dot(pieces[g], group_queries(q_ref, g), NT) for g in range(KV_HEADS)]
     rows = q_ref.shape[0]
-    heads = []
-    for g in range(KV_HEADS):
-        recalled = products[g][part_of(0, HEAD_DIM), :] + (
-            products[g][part_of(1, HEAD_DIM), :] + products[g][part_of(2, HEAD_DIM), :]
-        )
+    ahead = {}
+
+    def product(g):
+        if g < KV_HEADS and g not in ahead:
+            state = states[g]
+            high = state.astype(jnp.bfloat16)
+            state = state - high.astype(jnp.float32)
+            middle = state.astype(jnp.bfloat16)
+            low = (state - middle.astype(jnp.float32)).astype(jnp.bfloat16)
+            pieces = jnp.concatenate([high, middle, low], axis=0)
+            ahead[g] = dot(pieces, group_queries(q_ref, g), NT)
+
+    def read(g):
+        product(g)
+        product(g + 1)
+        recalled = ahead[g][part_of(0, HEAD_DIM), :] + (
+            ahead[g][part_of(1, HEAD_DIM), :] + ahead[g][part_of(2, HEAD_DIM), :]
+        )
+        heads = []
         for i in range(GROUPS):
-            read = recalled[:, part_of(i, rows)]
-            square = jnp.sum(read * read, axis=0, keepdims=True) * (1.0 / HEAD_DIM)
-            read = read * (lax.rsqrt(square + 1e-06) * reads)
-            heads.append(read * gains_ref[part_of(g * GROUPS + i, HEAD_DIM), :])
-    return heads
+            head = recalled[:, part_of(i, rows)]
+            square = jnp.sum(head * head, axis=0, keepdims=True) * (1.0 / HEAD_DIM)
+            head = head * (lax.rsqrt(square + 1e-06) * reads)
+            heads.append(head * gains_ref[part_of(g * GROUPS + i, HEAD_DIM), :])
+        return heads
+
+    return read
 
 
 def attend_before(q_ref, one_ref, stats_ref, summed_ref, first, same):
     rows = q_ref.shape[0]
     live = suffix(jnp.where(block_docs(one_ref) == first, 0.0, 1.0))
     bias = jnp.where(live & same, 0.0, LOWEST)
-    scores = [
-        dot(block_keys(one_ref, g), group_queries(q_ref, g), NT) for g in range(KV_HEADS)
-    ]
+    ahead = {}
+
+    def score(g):
+        if g < KV_HEADS and g not in ahead:
+            ahead[g] = dot(block_keys(one_ref, g), group_queries(q_ref, g), NT)
 
     def attend(g):
+        score(g)
+        score(g + 1)
         weights, factors, scales = [], [], []
         for i in range(GROUPS):
             cut = part_of(i, rows)
-            masked = scores[g][:, cut] * SCALE + bias
+            masked = ahead[g][:, cut] * SCALE + bias
             top_own = stats_ref[g : g + 1, cut]
             top = jnp.maximum(jnp.max(masked, axis=0, keepdims=True), top_own)
             weight = jnp.exp2(masked - top)
@@ -285,21 +305,27 @@
     copies = []
     for g in range(KV_HEADS):
         for i, head in enumerate(mixed(g)):
-            held[:, part_of(g * GROUPS + i, HEAD_DIM)] = jnp.transpose(head)
-        wide = part_of(g, GROUPS * HEAD_DIM)
-        copies.append(pltpu.make_async_copy(held.at[:, wide], out_ref.at[:, wide], sems.at[g]))
-        copies[g].start()
+            h = g * GROUPS + i
+            held[:, part_of(h, HEAD_DIM)] = jnp.transpose(head)
+            if h % 2 == 1:
+                wide = part_of(h // 2, 2 * HEAD_DIM)
+                copy = pltpu.make_async_copy(
+                    held.at[:, wide], out_ref.at[:, wide], sems.at[h // 2]
+                )
+                copy.start()
+                copies.append(copy)
     for copy in copies:
         copy.wait()
 
 
 def read_into(read_ref, refs, q_ref, own_ref, gains_ref):
     first, same = first_document(block_docs(own_ref))
-    heads = read_memory(
+    read = read_memory(
         memory_states(refs, first), q_ref, gains_ref, jnp.where(same, 1.0, 0.0)
     )
-    for h, head in enumerate(heads):
-        read_ref[part_of(h, HEAD_DIM), :] = head
+    for g in range(KV_HEADS):
+        for i, head in enumerate(read(g)):
+            read_ref[part_of(g * GROUPS + i, HEAD_DIM), :] = head
 
 
 def read_kernel(plan, q_ref, own_ref, three_ref, gains_ref, read_ref):
@@ -327,25 +353,25 @@
 
 def read_and_store(states, q_ref, gains_ref, same, summed_ref, out_ref, held, sems):
     rows = q_ref.shape[0]
-    heads = read_memory(states, q_ref, gains_ref, jnp.where(same, 1.0, 0.0))
+    read = read_memory(states, q_ref, gains_ref, jnp.where(same, 1.0, 0.0))
 
     def mixed(g):
         return [
-            heads[g * GROUPS + i] + summed_ref[part_of(g, HEAD_DIM), part_of(i, rows)]
-            for i in range(GROUPS)
+            head + summed_ref[part_of(g, HEAD_DIM), part_of(i, rows)]
+            for i, head in enumerate(read(g))
         ]
 
     store_heads(mixed, out_ref, held, sems)
 
 
 def early_kernel(
-    plan, q_ref, own_ref, one_ref, three_ref, stats_ref, gains_ref, summed_ref, read_in,
+    plan, q_ref, own_ref, one_ref, three_ref, stats_ref, gains_ref, summed_ref, read_in, out_in,
     read_ref, state_ref, out_ref, held, sems,
 ):
     kv = lax.axis_index("kv")
     late = among(plan.late)
 
-    @pl.when((kv == 0) & jnp.logical_not(late))
+    @pl.when((kv == 0) & jnp.logical_not(late | among(plan.alone)))
     def _():
         first, same = first_document(block_docs(own_ref))
         states = memory_states([one_ref, three_ref], first)
@@ -452,12 +478,17 @@
     )(gain, packed, in_hbm(queries), *block, beta)
     two = send(own, plan.pairs[1])
     three = send(short, plan.pairs[2])
-    summed, stats, gains = pl.pallas_call(
+    out_shape = jax.ShapeDtypeStruct((rows, HEADS * HEAD_DIM), jnp.float32)
+    store_scratch = [
+        pltpu.VMEM((rows, HEADS * HEAD_DIM), jnp.float32),
+        pltpu.SemaphoreType.DMA((HEADS // 2,)),
+    ]
+    summed, stats, gains, out = pl.pallas_call(
         functools.partial(own_kernel, plan),
-        out_shape=results,
+        out_shape=results + [out_shape],
         in_specs=[vmem] * 3 + [hbm] + [vmem] * 3,
-        out_specs=[vmem] * 3,
-        scratch_shapes=[beta_scratch, pltpu.SemaphoreType.DMA],
+        out_specs=[vmem] * 3 + [hbm],
+        scratch_shapes=[beta_scratch, pltpu.SemaphoreType.DMA] + store_scratch,
         input_output_aliases={4: 0, 5: 1, 6: 2},
         compiler_params=params,
         cost_estimate=estimate(1.0),
@@ -469,20 +500,15 @@
         out_specs=vmem,
         compiler_params=params,
     )(queries, own, three, gains)
-    out_shape = jax.ShapeDtypeStruct((rows, HEADS * HEAD_DIM), jnp.float32)
-    store_scratch = [
-        pltpu.VMEM((rows, HEADS * HEAD_DIM), jnp.float32),
-        pltpu.SemaphoreType.DMA((KV_HEADS,)),
-    ]
     read, state, out = pl.pallas_call(
         functools.partial(early_kernel, plan),
         out_shape=[gains_shape, state_shape, out_shape],
-        in_specs=[vmem] * 8,
+        in_specs=[vmem] * 8 + [hbm],
         out_specs=[vmem] * 2 + [hbm],
         scratch_shapes=store_scratch,
-        input_output_aliases={7: 0},
+        input_output_aliases={7: 0, 8: 2},
         compiler_params=params,
-    )(queries, own, one, three, stats, gains, summed, read)
+    )(queries, own, one, three, stats, gains, summed, read, out)
     return pl.pallas_call(
         functools.partial(late_kernel, plan),
         out_shape=out_shape,

time: 14.1 us -> 14.1 us (level)
  no operation moved by 1% of the time
where the time goes in v16:
time: 14.1 us; the launch traced here: 13.9 us
  starting transfers between devices  6.29 us (45%)
  Pallas kernels  5.82 us (41%)
  waiting for transfers between devices  1.64 us (12%)
    ppermute x3, starting transfers between devices, send(): return lax.ppermute(payload, ('seq', 'kv'), pairs)  6.29 us
    pallas_call x1, Pallas kernels, near_device(): pl.pallas_call(functools.partial(own_kernel, plan), out_shape=results + [...  1.96 us
    pallas_call x1, Pallas kernels, near_device(): pl.pallas_call(functools.partial(late_kernel, plan), out_shape=out_shape,...  1.72 us
    ppermute x3, waiting for transfers between devices, send(): return lax.ppermute(payload, ('seq', 'kv'), pairs)  1.64 us
    pallas_call x1, Pallas kernels, near_device(): pl.pallas_call(functools.partial(pack_kernel, plan), out_shape=block_shap...  0.98 us
    pallas_call x1, Pallas kernels, near_device(): pl.pallas_call(functools.partial(read_kernel, plan), out_shape=gains_shap...  0.89 us
  transfers between devices with their start and end apart: 3, of which 2 were waited for; matrix products, arithmetic and copies ran while one was open for 0% of the time, Pallas kernels for 22%

profile of v16, /device:TPU:27, one launch (start us, length us, event | category | flops | bytes accessed | tf_op | source)
XLA Modules:
  0.0 13.9 jit_solution(14309147600816188911)
XLA Ops:
  0.0 0.0 copy-start.1
  0.0 1.0 %shard_map.64.packed_ref = bf16[1040,128]{1,0:T(8,128)(2,1)S(1)} custom-call(bf16[128,512]{1,0:T(8,128)(2,1)} %key_ref.3, bf16[128,512]{1,0:T(8,128)(2,1)} %value_ref.3, s32[1,128]{1,0:T(1,128)} %bitcast.4), custom_call_target="tpu_custom_call" | custom-call | flops 13421772 | bytes 419430 | tf_op jit(solution)/shard_map/pallas_call | solution.py:454
  1.0 2.8 %collective-permute-start.1 = (bf16[1040,128]{1,0:T(8,128)(2,1)S(1)}, bf16[1040,128]{1,0:T(8,128)(2,1)S(1)}, u32[]{:S(2)}, u32[]{:S(2)}) collective-permute-start(bf16[1040,128]{1,0:T(8,128)(2,1)S(1)} %shard_map.64.packed_ref), channel_id=1, source_target_pairs={{8,16},{12,20},{0,4},{4,8},{24,28},{9,17},{13,21},{1,5},{5,9},{25,... | collective-permute-start | bytes 798728 | tf_op jit(solution)/shard_map/ppermute | solution.py:441
  3.8 0.0 copy-done.1
  3.8 0.0 copy-start
  3.8 0.2 %shard_map.65 = (bf16[1040,128]{1,0:T(8,128)(2,1)S(1)}, bf16[1024,128]{1,0:T(8,128)(2,1)S(1)}, f32[512,512]{1,0:T(8,128)S(1)}, f32[16,512]{1,0:T(8,128)S(1)}, f32[2048,128]{1,0:T(8,128)S(1)}) custom-call(f32[16,128]{1,0:T(8,128)S(1)} %bitcast.2, bf16[1040,128]{1,0:T(8,128)(2,1)S(1)} %shard_map.64.packed_ref, bf16[128,2048]{1,0:T(8,128)(2,1)} %q_ref.7, ...), custom_call_target="tpu_custom_call" | custom-call | flops 134217728 | bytes 4194304 | tf_op jit(solution)/shard_map/pallas_call | solution.py:464
  4.0 2.2 %collective-permute-start = (bf16[1040,128]{1,0:T(8,128)(2,1)S(1)}, bf16[1040,128]{1,0:T(8,128)(2,1)S(1)}, u32[]{:S(2)}, u32[]{:S(2)}) collective-permute-start(bf16[1040,128]{1,0:T(8,128)(2,1)S(1)} %get-tuple-element.17.own_ref), channel_id=1, source_target_pairs={{8,12},{12,16},{16,20},{20,24},{9,13},{13,17},{17,21},{21,25},{10,... | collective-permute-start | bytes 798728 | tf_op jit(solution)/shard_map/ppermute | solution.py:441
  6.2 1.3 %collective-permute-start.2 = (bf16[1024,128]{1,0:T(8,128)(2,1)S(1)}, bf16[1024,128]{1,0:T(8,128)(2,1)S(1)}, u32[]{:S(2)}, u32[]{:S(2)}) collective-permute-start(bf16[1024,128]{1,0:T(8,128)(2,1)S(1)} %get-tuple-element.18), channel_id=1, source_target_pairs={{0,8},{4,12},{16,24},{20,28},{1,9},{5,13},{17,25},{21,29},{2,10},{... | collective-permute-start | bytes 786440 | tf_op jit(solution)/shard_map/ppermute | solution.py:441
  7.5 0.0 copy-done
  7.5 2.0 %shard_map.66 = (f32[512,512]{1,0:T(8,128)S(1)}, f32[16,512]{1,0:T(8,128)S(1)}, f32[2048,128]{1,0:T(8,128)S(1)}, f32[128,2048]{1,0:T(8,128)}) custom-call(bf16[128,2048]{1,0:T(8,128)(2,1)S(1)} %copy-done, f32[16,128]{1,0:T(8,128)S(1)} %bitcast.3, ...), custom_call_target="tpu_custom_call", output_to_operand_aliasing={{0}: (4, {}), {1}: (5, {}), {2}: (6, {})} | custom-call | flops 134217728 | bytes 4194304 | tf_op jit(solution)/shard_map/pallas_call | solution.py:486
  9.5 0.2 %collective-permute-done.2.three_ref = bf16[1024,128]{1,0:T(8,128)(2,1)S(1)} collective-permute-done((bf16[1024,128]{1,0:T(8,128)(2,1)S(1)}, bf16[1024,128]{1,0:T(8,128)(2,1)S(1)}, u32[]{:S(2)}, u32[]{:S(2)}) %collective-permute-start.2) | collective-permute-done | bytes 262176 | tf_op jit(solution)/shard_map/ppermute | solution.py:441
  9.6 0.9 %shard_map.67.read_in = f32[2048,128]{1,0:T(8,128)S(1)} custom-call(bf16[128,2048]{1,0:T(8,128)(2,1)S(1)} %copy-done, bf16[1040,128]{1,0:T(8,128)(2,1)S(1)} %get-tuple-element.17.own_ref, bf16[1024,128]{1,0:T(8,128)(2,1)S(1)} %collective-permute-done.2.three_ref, f32[2048,128]{1,0:T(8,128)S(1)} %get-tuple-element.23.gains_ref), custom_call_target="tpu_custom_call" | custom-call | tf_op jit(solution)/shard_map/pallas_call | solution.py:496
  10.5 0.0 collective-permute-done.1.one_ref
  10.5 0.1 shard_map.68
  10.7 1.5 %collective-permute-done.two_ref = bf16[1040,128]{1,0:T(8,128)(2,1)S(1)} collective-permute-done((bf16[1040,128]{1,0:T(8,128)(2,1)S(1)}, bf16[1040,128]{1,0:T(8,128)(2,1)S(1)}, u32[]{:S(2)}, u32[]{:S(2)}) %collective-permute-start) | collective-permute-done | bytes 266272 | tf_op jit(solution)/shard_map/ppermute | solution.py:441
  12.1 1.7 %shard_map.69 = f32[128,2048]{1,0:T(8,128)} custom-call(bf16[128,2048]{1,0:T(8,128)(2,1)S(1)} %copy-done, bf16[1040,128]{1,0:T(8,128)(2,1)S(1)} %get-tuple-element.17.own_ref, bf16[1040,128]{1,0:T(8,128)(2,1)S(1)} %collective-permute-done.two_ref, f32[512,128]{1,0:T(8,128)S(1)} %get-tuple-element.26.state_ref, ...), custom_call_target="tpu_custom_call", output_to_operand_aliasing={{}: (8, {})} | custom-call | tf_op jit(solution)/shard_map/pallas_call | solution.py:512
Async XLA Ops:
  0.0 3.8 %copy-start.1 = (f32[2048]{0:T(1024)S(1)}, f32[2048]{0:T(1024)}, u32[]{:S(2)}) copy-start(f32[2048]{0:T(1024)} %param.11) | copy-start | bytes 24580
  1.0 9.5 %collective-permute-start.1 = (bf16[1040,128]{1,0:T(8,128)(2,1)S(1)}, bf16[1040,128]{1,0:T(8,128)(2,1)S(1)}, u32[]{:S(2)}, u32[]{:S(2)}) collective-permute-start(bf16[1040,128]{1,0:T(8,128)(2,1)S(1)} %shard_map.64.packed_ref), channel_id=1, source_target_pairs={{8,16},{12,20},{0,4},{4,8},{24,28},{9,17},{13,21},{1,5},{5,9},{25,... | collective-permute-start | bytes 798728 | tf_op jit(solution)/shard_map/ppermute | solution.py:441
  3.8 3.7 %copy-start = (bf16[128,2048]{1,0:T(8,128)(2,1)S(1)}, bf16[128,2048]{1,0:T(8,128)(2,1)}, u32[]{:S(2)}) copy-start(bf16[128,2048]{1,0:T(8,128)(2,1)} %q_ref.7) | copy-start | bytes 1572868
  4.0 8.1 %collective-permute-start = (bf16[1040,128]{1,0:T(8,128)(2,1)S(1)}, bf16[1040,128]{1,0:T(8,128)(2,1)S(1)}, u32[]{:S(2)}, u32[]{:S(2)}) collective-permute-start(bf16[1040,128]{1,0:T(8,128)(2,1)S(1)} %get-tuple-element.17.own_ref), channel_id=1, source_target_pairs={{8,12},{12,16},{16,20},{20,24},{9,13},{13,17},{17,21},{21,25},{10,... | collective-permute-start | bytes 798728 | tf_op jit(solution)/shard_map/ppermute | solution.py:441
  6.2 3.4 %collective-permute-start.2 = (bf16[1024,128]{1,0:T(8,128)(2,1)S(1)}, bf16[1024,128]{1,0:T(8,128)(2,1)S(1)}, u32[]{:S(2)}, u32[]{:S(2)}) collective-permute-start(bf16[1024,128]{1,0:T(8,128)(2,1)S(1)} %get-tuple-element.18), channel_id=1, source_target_pairs={{0,8},{4,12},{16,24},{20,28},{1,9},{5,13},{17,25},{21,29},{2,10},{... | collective-permute-start | bytes 786440 | tf_op jit(solution)/shard_map/ppermute | solution.py:441

commit v17 on v16

--- a/solution.py
+++ b/solution.py
@@ -19,6 +19,7 @@
 
 NT = (((1,), (1,)), ((), ()))
 TN = (((0,), (0,)), ((), ()))
+NN = (((1,), (0,)), ((), ()))
 
 
 def dot(a, b, dims):
@@ -205,13 +206,19 @@
 
 def own_kernel(
     plan, q_ref, gain_ref, own_ref, beta_ref, summed_in, stats_in, gains_in,
-    summed_ref, stats_ref, gains_ref, out_ref, beta_scratch, sem, held, sems,
+    summed_ref, stats_ref, gains_ref, out_ref, turned_ref, beta_scratch, sem, held, sems,
 ):
+    rows = q_ref.shape[0]
+    for g in range(KV_HEADS):
+        for i in range(GROUPS):
+            head = q_ref[:, part_of(g * GROUPS + i, HEAD_DIM)]
+            turned_ref[part_of(g, HEAD_DIM), part_of(i, rows)] = jnp.transpose(head)
+
     @pl.when(among(plan.alone))
     def _():
         _, same = first_document(block_docs(own_ref))
         states = [jnp.zeros((HEAD_DIM, HEAD_DIM), jnp.float32)] * KV_HEADS
-        read_and_store(states, q_ref, gains_ref, same, summed_ref, out_ref, held, sems)
+        read_and_store(states, turned_ref, gains_ref, same, summed_ref, out_ref, held, sems)
 
     @pl.when(jnp.logical_not(among(plan.early)))
     def _():
@@ -222,23 +229,27 @@
         )
 
 
-def memory_state(ref, first, g):
-    short = ref.shape[0] == 2 * KV_HEADS * HEAD_DIM
-    docs = ref[0:EXTRA, :].astype(jnp.float32)[0:1, :] if short else block_docs(ref)
-    live = suffix(jnp.where(docs == first, 0.0, 1.0), 1.0 if short else 0.0)
-    keys = jnp.where(live, block_keys(ref, g).astype(jnp.float32), 0.0).astype(jnp.bfloat16)
-    return dot(block_values(ref, g), keys, TN)
-
-
 def memory_states(refs, first):
+    lives = []
+    for ref in refs:
+        short = ref.shape[0] == 2 * KV_HEADS * HEAD_DIM
+        docs = ref[0:EXTRA, :].astype(jnp.float32)[0:1, :] if short else block_docs(ref)
+        live = suffix(jnp.where(docs == first, 0.0, 1.0), 1.0 if short else 0.0)
+        lives.append(jnp.where(live, 1.0, 0.0).astype(jnp.bfloat16))
     return [
-        functools.reduce(jnp.add, [memory_state(ref, first, g) for ref in refs])
+        functools.reduce(
+            jnp.add,
+            [
+                dot(block_values(ref, g), block_keys(ref, g) * live, TN)
+                for ref, live in zip(refs, lives)
+            ],
+        )
         for g in range(KV_HEADS)
     ]
 
 
-def read_memory(states, q_ref, gains_ref, reads):
-    rows = q_ref.shape[0]
+def read_memory(states, turned_ref, gains_ref, reads):
+    rows = (turned_ref.shape[1] // GROUPS)
     ahead = {}
 
     def product(g):
@@ -249,7 +260,7 @@
             middle = state.astype(jnp.bfloat16)
             low = (state - middle.astype(jnp.float32)).astype(jnp.bfloat16)
             pieces = jnp.concatenate([high, middle, low], axis=0)
-            ahead[g] = dot(pieces, group_queries(q_ref, g), NT)
+            ahead[g] = dot(pieces, turned_ref[part_of(g, HEAD_DIM), :], NN)
 
     def read(g):
         product(g)
@@ -268,15 +279,15 @@
     return read
 
 
-def attend_before(q_ref, one_ref, stats_ref, summed_ref, first, same):
-    rows = q_ref.shape[0]
+def attend_before(turned_ref, one_ref, stats_ref, summed_ref, first, same):
+    rows = (turned_ref.shape[1] // GROUPS)
     live = suffix(jnp.where(block_docs(one_ref) == first, 0.0, 1.0))
     bias = jnp.where(live & same, 0.0, LOWEST)
     ahead = {}
 
     def score(g):
         if g < KV_HEADS and g not in ahead:
-            ahead[g] = dot(block_keys(one_ref, g), group_queries(q_ref, g), NT)
+            ahead[g] = dot(block_keys(one_ref, g), turned_ref[part_of(g, HEAD_DIM), :], NN)
 
     def attend(g):
         score(g)
@@ -318,28 +329,28 @@
         copy.wait()
 
 
-def read_into(read_ref, refs, q_ref, own_ref, gains_ref):
+def read_into(read_ref, refs, turned_ref, own_ref, gains_ref):
     first, same = first_document(block_docs(own_ref))
     read = read_memory(
-        memory_states(refs, first), q_ref, gains_ref, jnp.where(same, 1.0, 0.0)
+        memory_states(refs, first), turned_ref, gains_ref, jnp.where(same, 1.0, 0.0)
     )
     for g in range(KV_HEADS):
         for i, head in enumerate(read(g)):
             read_ref[part_of(g * GROUPS + i, HEAD_DIM), :] = head
 
 
-def read_kernel(plan, q_ref, own_ref, three_ref, gains_ref, read_ref):
+def read_kernel(plan, turned_ref, own_ref, three_ref, gains_ref, read_ref):
     @pl.when((lax.axis_index("kv") == 1) & jnp.logical_not(among(plan.memory_first)))
     def _():
-        read_into(read_ref, [three_ref], q_ref, own_ref, gains_ref)
+        read_into(read_ref, [three_ref], turned_ref, own_ref, gains_ref)
 
 
 def attend_and_store(
-    q_ref, own_ref, earlier_ref, stats_ref, summed_ref, read_ref, out_ref, held, sems
+    turned_ref, own_ref, earlier_ref, stats_ref, summed_ref, read_ref, out_ref, held, sems
 ):
     first, same = first_document(block_docs(own_ref))
-    attend = attend_before(q_ref, earlier_ref, stats_ref, summed_ref, first, same)
-    rows = q_ref.shape[0]
+    attend = attend_before(turned_ref, earlier_ref, stats_ref, summed_ref, first, same)
+    rows = (turned_ref.shape[1] // GROUPS)
 
     def mixed(g):
         attended = attend(g)
@@ -351,9 +362,9 @@
     store_heads(mixed, out_ref, held, sems)
 
 
-def read_and_store(states, q_ref, gains_ref, same, summed_ref, out_ref, held, sems):
-    rows = q_ref.shape[0]
-    read = read_memory(states, q_ref, gains_ref, jnp.where(same, 1.0, 0.0))
+def read_and_store(states, turned_ref, gains_ref, same, summed_ref, out_ref, held, sems):
+    rows = (turned_ref.shape[1] // GROUPS)
+    read = read_memory(states, turned_ref, gains_ref, jnp.where(same, 1.0, 0.0))
 
     def mixed(g):
         return [
@@ -365,7 +376,7 @@
 
 
 def early_kernel(
-    plan, q_ref, own_ref, one_ref, three_ref, stats_ref, gains_ref, summed_ref, read_in, out_in,
+    plan, turned_ref, own_ref, one_ref, three_ref, stats_ref, gains_ref, summed_ref, read_in, out_in,
     read_ref, state_ref, out_ref, held, sems,
 ):
     kv = lax.axis_index("kv")
@@ -375,12 +386,12 @@
     def _():
         first, same = first_document(block_docs(own_ref))
         states = memory_states([one_ref, three_ref], first)
-        read_and_store(states, q_ref, gains_ref, same, summed_ref, out_ref, held, sems)
+        read_and_store(states, turned_ref, gains_ref, same, summed_ref, out_ref, held, sems)
 
     @pl.when((kv == 1) & jnp.logical_not(late))
     def _():
         attend_and_store(
-            q_ref, own_ref, one_ref, stats_ref, summed_ref, read_ref, out_ref, held, sems
+            turned_ref, own_ref, one_ref, stats_ref, summed_ref, read_ref, out_ref, held, sems
         )
 
     @pl.when((kv == 0) & late)
@@ -391,11 +402,11 @@
 
     @pl.when((kv == 1) & among(plan.memory_first))
     def _():
-        read_into(read_ref, [one_ref, three_ref], q_ref, own_ref, gains_ref)
+        read_into(read_ref, [one_ref, three_ref], turned_ref, own_ref, gains_ref)
 
 
 def late_kernel(
-    plan, q_ref, own_ref, two_ref, state_ref, summed_ref, stats_ref, gains_ref, read_ref, out_in,
+    plan, turned_ref, own_ref, two_ref, state_ref, summed_ref, stats_ref, gains_ref, read_ref, out_in,
     out_ref, held, sems,
 ):
     kv = lax.axis_index("kv")
@@ -404,17 +415,17 @@
     @pl.when((kv == 1) & late)
     def _():
         attend_and_store(
-            q_ref, own_ref, two_ref, stats_ref, summed_ref, read_ref, out_ref, held, sems
+            turned_ref, own_ref, two_ref, stats_ref, summed_ref, read_ref, out_ref, held, sems
         )
 
     @pl.when((kv == 0) & late)
     def _():
         first, same = first_document(block_docs(own_ref))
         states = [
-            state_ref[part_of(g, HEAD_DIM), :] + memory_state(two_ref, first, g)
-            for g in range(KV_HEADS)
+            state_ref[part_of(g, HEAD_DIM), :] + state
+            for g, state in enumerate(memory_states([two_ref], first))
         ]
-        read_and_store(states, q_ref, gains_ref, same, summed_ref, out_ref, held, sems)
+        read_and_store(states, turned_ref, gains_ref, same, summed_ref, out_ref, held, sems)
 
 
 def near_device(n_seq, queries, keys, values, doc_ids, beta, lin_gain):
@@ -483,11 +494,12 @@
         pltpu.VMEM((rows, HEADS * HEAD_DIM), jnp.float32),
         pltpu.SemaphoreType.DMA((HEADS // 2,)),
     ]
-    summed, stats, gains, out = pl.pallas_call(
+    turned_shape = jax.ShapeDtypeStruct((KV_HEADS * HEAD_DIM, wide), queries.dtype)
+    summed, stats, gains, out, turned = pl.pallas_call(
         functools.partial(own_kernel, plan),
-        out_shape=results + [out_shape],
+        out_shape=results + [out_shape, turned_shape],
         in_specs=[vmem] * 3 + [hbm] + [vmem] * 3,
-        out_specs=[vmem] * 3 + [hbm],
+        out_specs=[vmem] * 3 + [hbm, vmem],
         scratch_shapes=[beta_scratch, pltpu.SemaphoreType.DMA] + store_scratch,
         input_output_aliases={4: 0, 5: 1, 6: 2},
         compiler_params=params,
@@ -499,7 +511,7 @@
         in_specs=[vmem] * 4,
         out_specs=vmem,
         compiler_params=params,
-    )(queries, own, three, gains)
+    )(turned, own, three, gains)
     read, state, out = pl.pallas_call(
         functools.partial(early_kernel, plan),
         out_shape=[gains_shape, state_shape, out_shape],
@@ -508,7 +520,7 @@
         scratch_shapes=store_scratch,
         input_output_aliases={7: 0, 8: 2},
         compiler_params=params,
-    )(queries, own, one, three, stats, gains, summed, read, out)
+    )(turned, own, one, three, stats, gains, summed, read, out)
     return pl.pallas_call(
         functools.partial(late_kernel, plan),
         out_shape=out_shape,
@@ -517,7 +529,7 @@
         scratch_shapes=store_scratch,
         input_output_aliases={8: 0},
         compiler_params=params,
-    )(queries, own, two, state, summed, stats, gains, read, out)
+    )(turned, own, two, state, summed, stats, gains, read, out)
 
 
 def carried_in(part, axis, combine, identity):

time: 14.1 us -> 14.1 us (level)
  waiting for transfers between devices: 1.64 us -> 1.44 us
  Pallas kernels: 5.82 us -> 5.99 us
    ppermute x3, waiting for transfers between devices: 1.64 us -> 1.44 us  [send(): return lax.ppermute(payload, ('seq', 'kv'), pairs)]
    pallas_call x1, Pallas kernels: 1.96 us -> 2.13 us  [near_device(): pl.pallas_call(functools.partial(own_kernel, plan), out_shape=results + [...]
  transfers between devices with their start and end apart: 3 -> 3, of which waited for: 2 -> 1; matrix products, arithmetic and copies ran while one was open for 0% -> 0% of each run, Pallas kernels for 22% -> 24%
where the time goes in v17:
time: 14.1 us; the launch traced here: 13.8 us
  starting transfers between devices  6.29 us (45%)
  Pallas kernels  5.99 us (42%)
  waiting for transfers between devices  1.44 us (10%)
    ppermute x3, starting transfers between devices, send(): return lax.ppermute(payload, ('seq', 'kv'), pairs)  6.29 us
    pallas_call x1, Pallas kernels, near_device(): pl.pallas_call(functools.partial(own_kernel, plan), out_shape=results + [...  2.13 us
    pallas_call x1, Pallas kernels, near_device(): pl.pallas_call(functools.partial(late_kernel, plan), out_shape=out_shape,...  1.7 us
    ppermute x3, waiting for transfers between devices, send(): return lax.ppermute(payload, ('seq', 'kv'), pairs)  1.44 us
    pallas_call x1, Pallas kernels, near_device(): pl.pallas_call(functools.partial(pack_kernel, plan), out_shape=block_shap...  0.98 us
    pallas_call x1, Pallas kernels, near_device(): pl.pallas_call(functools.partial(read_kernel, plan), out_shape=gains_shap...  0.91 us
  transfers between devices with their start and end apart: 3, of which 1 were waited for; matrix products, arithmetic and copies ran while one was open for 0% of the time, Pallas kernels for 24%

profile of v17, /device:TPU:27, one launch (start us, length us, event | category | flops | bytes accessed | tf_op | source)
XLA Modules:
  0.0 13.8 jit_solution(13180613689893659415)
XLA Ops:
  0.0 0.0 copy-start.1
  0.0 1.0 %shard_map.64.packed_ref = bf16[1040,128]{1,0:T(8,128)(2,1)S(1)} custom-call(bf16[128,512]{1,0:T(8,128)(2,1)} %key_ref.3, bf16[128,512]{1,0:T(8,128)(2,1)} %value_ref.3, s32[1,128]{1,0:T(1,128)} %bitcast.4), custom_call_target="tpu_custom_call" | custom-call | flops 13421772 | bytes 419430 | tf_op jit(solution)/shard_map/pallas_call | solution.py:465
  1.0 2.8 %collective-permute-start.1 = (bf16[1040,128]{1,0:T(8,128)(2,1)S(1)}, bf16[1040,128]{1,0:T(8,128)(2,1)S(1)}, u32[]{:S(2)}, u32[]{:S(2)}) collective-permute-start(bf16[1040,128]{1,0:T(8,128)(2,1)S(1)} %shard_map.64.packed_ref), channel_id=1, source_target_pairs={{8,16},{12,20},{0,4},{4,8},{24,28},{9,17},{13,21},{1,5},{5,9},{25,... | collective-permute-start | bytes 798728 | tf_op jit(solution)/shard_map/ppermute | solution.py:452
  3.8 0.0 copy-done.1
  3.8 0.0 copy-start
  3.8 0.2 %shard_map.65 = (bf16[1040,128]{1,0:T(8,128)(2,1)S(1)}, bf16[1024,128]{1,0:T(8,128)(2,1)S(1)}, f32[512,512]{1,0:T(8,128)S(1)}, f32[16,512]{1,0:T(8,128)S(1)}, f32[2048,128]{1,0:T(8,128)S(1)}) custom-call(f32[16,128]{1,0:T(8,128)S(1)} %bitcast.2, bf16[1040,128]{1,0:T(8,128)(2,1)S(1)} %shard_map.64.packed_ref, bf16[128,2048]{1,0:T(8,128)(2,1)} %q_ref.1, ...), custom_call_target="tpu_custom_call" | custom-call | flops 134217728 | bytes 4194304 | tf_op jit(solution)/shard_map/pallas_call | solution.py:475
  4.0 2.2 %collective-permute-start = (bf16[1040,128]{1,0:T(8,128)(2,1)S(1)}, bf16[1040,128]{1,0:T(8,128)(2,1)S(1)}, u32[]{:S(2)}, u32[]{:S(2)}) collective-permute-start(bf16[1040,128]{1,0:T(8,128)(2,1)S(1)} %get-tuple-element.18.own_ref), channel_id=1, source_target_pairs={{8,12},{12,16},{16,20},{20,24},{9,13},{13,17},{17,21},{21,25},{10,... | collective-permute-start | bytes 798728 | tf_op jit(solution)/shard_map/ppermute | solution.py:452
  6.2 1.3 %collective-permute-start.2 = (bf16[1024,128]{1,0:T(8,128)(2,1)S(1)}, bf16[1024,128]{1,0:T(8,128)(2,1)S(1)}, u32[]{:S(2)}, u32[]{:S(2)}) collective-permute-start(bf16[1024,128]{1,0:T(8,128)(2,1)S(1)} %get-tuple-element.23), channel_id=1, source_target_pairs={{0,8},{4,12},{16,24},{20,28},{1,9},{5,13},{17,25},{21,29},{2,10},{... | collective-permute-start | bytes 786440 | tf_op jit(solution)/shard_map/ppermute | solution.py:452
  7.5 0.0 copy-done
  7.5 2.1 %shard_map.66 = (f32[512,512]{1,0:T(8,128)S(1)}, f32[16,512]{1,0:T(8,128)S(1)}, f32[2048,128]{1,0:T(8,128)S(1)}, f32[128,2048]{1,0:T(8,128)}, bf16[512,512]{1,0:T(8,128)(2,1)S(1)}) custom-call(bf16[128,2048]{1,0:T(8,128)(2,1)S(1)} %copy-done, f32[16,128]{1,0:T(8,128)S(1)} %bitcast.3, ...), custom_call_target="tpu_custom_call", output_to_operand_aliasing={{0}: (4, {}), {1}: (5, {}), {2}: (6, {})} | custom-call | flops 134217728 | bytes 4194304 | tf_op jit(solution)/shard_map/pallas_call | solution.py:498
  9.6 0.0 collective-permute-done.2.three_ref
  9.7 0.9 %shard_map.67.read_in = f32[2048,128]{1,0:T(8,128)S(1)} custom-call(bf16[512,512]{1,0:T(8,128)(2,1)S(1)} %get-tuple-element.22.turned_ref, bf16[1040,128]{1,0:T(8,128)(2,1)S(1)} %get-tuple-element.18.own_ref, bf16[1024,128]{1,0:T(8,128)(2,1)S(1)} %collective-permute-done.2.three_ref, f32[2048,128]{1,0:T(8,128)S(1)} %get-tuple-element.25.gains_ref), custom_call_target="tpu_custom_call" | custom-call | tf_op jit(solution)/shard_map/pallas_call | solution.py:508
  10.6 0.0 collective-permute-done.1.one_ref
  10.6 0.1 shard_map.68
  10.7 1.4 %collective-permute-done.two_ref = bf16[1040,128]{1,0:T(8,128)(2,1)S(1)} collective-permute-done((bf16[1040,128]{1,0:T(8,128)(2,1)S(1)}, bf16[1040,128]{1,0:T(8,128)(2,1)S(1)}, u32[]{:S(2)}, u32[]{:S(2)}) %collective-permute-start) | collective-permute-done | bytes 266272 | tf_op jit(solution)/shard_map/ppermute | solution.py:452
  12.1 1.7 %shard_map.69 = f32[128,2048]{1,0:T(8,128)} custom-call(bf16[512,512]{1,0:T(8,128)(2,1)S(1)} %get-tuple-element.22.turned_ref, bf16[1040,128]{1,0:T(8,128)(2,1)S(1)} %get-tuple-element.18.own_ref, bf16[1040,128]{1,0:T(8,128)(2,1)S(1)} %collective-permute-done.two_ref, f32[512,128]{1,0:T(8,128)S(1)} %get-tuple-element.28.state_ref, ...), custom_call_target="tpu_custom_call", output_to_operand_aliasing={{}: (8, {})} | custom-call | tf_op jit(solution)/shard_map/pallas_call | solution.py:524
Async XLA Ops:
  0.0 3.8 %copy-start.1 = (f32[2048]{0:T(1024)S(1)}, f32[2048]{0:T(1024)}, u32[]{:S(2)}) copy-start(f32[2048]{0:T(1024)} %param.11) | copy-start | bytes 24580
  1.0 9.6 %collective-permute-start.1 = (bf16[1040,128]{1,0:T(8,128)(2,1)S(1)}, bf16[1040,128]{1,0:T(8,128)(2,1)S(1)}, u32[]{:S(2)}, u32[]{:S(2)}) collective-permute-start(bf16[1040,128]{1,0:T(8,128)(2,1)S(1)} %shard_map.64.packed_ref), channel_id=1, source_target_pairs={{8,16},{12,20},{0,4},{4,8},{24,28},{9,17},{13,21},{1,5},{5,9},{25,... | collective-permute-start | bytes 798728 | tf_op jit(solution)/shard_map/ppermute | solution.py:452
  3.8 3.7 %copy-start = (bf16[128,2048]{1,0:T(8,128)(2,1)S(1)}, bf16[128,2048]{1,0:T(8,128)(2,1)}, u32[]{:S(2)}) copy-start(bf16[128,2048]{1,0:T(8,128)(2,1)} %q_ref.1) | copy-start | bytes 1572868
  4.0 8.1 %collective-permute-start = (bf16[1040,128]{1,0:T(8,128)(2,1)S(1)}, bf16[1040,128]{1,0:T(8,128)(2,1)S(1)}, u32[]{:S(2)}, u32[]{:S(2)}) collective-permute-start(bf16[1040,128]{1,0:T(8,128)(2,1)S(1)} %get-tuple-element.18.own_ref), channel_id=1, source_target_pairs={{8,12},{12,16},{16,20},{20,24},{9,13},{13,17},{17,21},{21,25},{10,... | collective-permute-start | bytes 798728 | tf_op jit(solution)/shard_map/ppermute | solution.py:452
  6.2 3.4 %collective-permute-start.2 = (bf16[1024,128]{1,0:T(8,128)(2,1)S(1)}, bf16[1024,128]{1,0:T(8,128)(2,1)S(1)}, u32[]{:S(2)}, u32[]{:S(2)}) collective-permute-start(bf16[1024,128]{1,0:T(8,128)(2,1)S(1)} %get-tuple-element.23), channel_id=1, source_target_pairs={{0,8},{4,12},{16,24},{20,28},{1,9},{5,13},{17,25},{21,29},{2,10},{... | collective-permute-start | bytes 786440 | tf_op jit(solution)/shard_map/ppermute | solution.py:452

commit v18 on v17

--- a/solution.py
+++ b/solution.py
@@ -217,7 +217,7 @@
     @pl.when(among(plan.alone))
     def _():
         _, same = first_document(block_docs(own_ref))
-        states = [jnp.zeros((HEAD_DIM, HEAD_DIM), jnp.float32)] * KV_HEADS
+        states = lambda g: jnp.zeros((HEAD_DIM, HEAD_DIM), jnp.float32)
         read_and_store(states, turned_ref, gains_ref, same, summed_ref, out_ref, held, sems)
 
     @pl.when(jnp.logical_not(among(plan.early)))
@@ -236,16 +236,15 @@
         docs = ref[0:EXTRA, :].astype(jnp.float32)[0:1, :] if short else block_docs(ref)
         live = suffix(jnp.where(docs == first, 0.0, 1.0), 1.0 if short else 0.0)
         lives.append(jnp.where(live, 1.0, 0.0).astype(jnp.bfloat16))
-    return [
-        functools.reduce(
-            jnp.add,
-            [
-                dot(block_values(ref, g), block_keys(ref, g) * live, TN)
-                for ref, live in zip(refs, lives)
-            ],
-        )
-        for g in range(KV_HEADS)
-    ]
+
+    def state(g):
+        terms = [
+            dot(block_values(ref, g), block_keys(ref, g) * live, TN)
+            for ref, live in zip(refs, lives)
+        ]
+        return functools.reduce(jnp.add, terms)
+
+    return state
 
 
 def read_memory(states, turned_ref, gains_ref, reads):
@@ -254,7 +253,7 @@
 
     def product(g):
         if g < KV_HEADS and g not in ahead:
-            state = states[g]
+            state = states(g)
             high = state.astype(jnp.bfloat16)
             state = state - high.astype(jnp.float32)
             middle = state.astype(jnp.bfloat16)
@@ -397,8 +396,9 @@
     @pl.when((kv == 0) & late)
     def _():
         first, _ = first_document(block_docs(own_ref))
-        for g, state in enumerate(memory_states([one_ref, three_ref], first)):
-            state_ref[part_of(g, HEAD_DIM), :] = state
+        states = memory_states([one_ref, three_ref], first)
+        for g in range(KV_HEADS):
+            state_ref[part_of(g, HEAD_DIM), :] = states(g)
 
     @pl.when((kv == 1) & among(plan.memory_first))
     def _():
@@ -421,10 +421,8 @@
     @pl.when((kv == 0) & late)
     def _():
         first, same = first_document(block_docs(own_ref))
-        states = [
-            state_ref[part_of(g, HEAD_DIM), :] + state
-            for g, state in enumerate(memory_states([two_ref], first))
-        ]
+        added = memory_states([two_ref], first)
+        states = lambda g: state_ref[part_of(g, HEAD_DIM), :] + added(g)
         read_and_store(states, turned_ref, gains_ref, same, summed_ref, out_ref, held, sems)
 
 

time: 14.1 us -> 14.3 us (1.014)
  the two profiles are of different devices: /device:TPU:27 before, /device:TPU:1 now
where the time goes in v18:
time: 14.3 us; the launch traced here: 14.1 us
  starting transfers between devices  8.07 us (56%)
  Pallas kernels  5.61 us (39%)
  waiting for transfers between devices  0.3 us (2%)
    ppermute x3, starting transfers between devices, send(): return lax.ppermute(payload, ('seq', 'kv'), pairs)  8.07 us
    pallas_call x1, Pallas kernels, near_device(): pl.pallas_call(functools.partial(early_kernel, plan), out_shape=[gains_sh...  2.24 us
    pallas_call x1, Pallas kernels, near_device(): pl.pallas_call(functools.partial(own_kernel, plan), out_shape=results + [...  2.13 us
    pallas_call x1, Pallas kernels, near_device(): pl.pallas_call(functools.partial(pack_kernel, plan), out_shape=block_shap...  0.98 us
    ppermute x3, waiting for transfers between devices, send(): return lax.ppermute(payload, ('seq', 'kv'), pairs)  0.3 us
  transfers between devices with their start and end apart: 3, of which 1 were waited for; matrix products, arithmetic and copies ran while one was open for 0% of the time, Pallas kernels for 32%

profile of v18, /device:TPU:1, one launch (start us, length us, event | category | flops | bytes accessed | tf_op | source)
XLA Modules:
  0.0 14.1 jit_solution(3530398907516925451)
XLA Ops:
  0.0 0.0 copy-start.1
  0.0 1.0 %shard_map.64.packed_ref = bf16[1040,128]{1,0:T(8,128)(2,1)S(1)} custom-call(bf16[128,512]{1,0:T(8,128)(2,1)} %key_ref.3, bf16[128,512]{1,0:T(8,128)(2,1)} %value_ref.3, s32[1,128]{1,0:T(1,128)} %bitcast.4), custom_call_target="tpu_custom_call" | custom-call | flops 13421772 | bytes 419430 | tf_op jit(solution)/shard_map/pallas_call | solution.py:463
  1.0 3.6 %collective-permute-start.1 = (bf16[1040,128]{1,0:T(8,128)(2,1)S(1)}, bf16[1040,128]{1,0:T(8,128)(2,1)S(1)}, u32[]{:S(2)}, u32[]{:S(2)}) collective-permute-start(bf16[1040,128]{1,0:T(8,128)(2,1)S(1)} %shard_map.64.packed_ref), channel_id=1, source_target_pairs={{8,16},{12,20},{0,4},{4,8},{24,28},{9,17},{13,21},{1,5},{5,9},{25,... | collective-permute-start | bytes 798728 | tf_op jit(solution)/shard_map/ppermute | solution.py:450
  4.6 0.0 copy-done.1
  4.6 0.0 copy-start
  4.7 0.2 %shard_map.65 = (bf16[1040,128]{1,0:T(8,128)(2,1)S(1)}, bf16[1024,128]{1,0:T(8,128)(2,1)S(1)}, f32[512,512]{1,0:T(8,128)S(1)}, f32[16,512]{1,0:T(8,128)S(1)}, f32[2048,128]{1,0:T(8,128)S(1)}) custom-call(f32[16,128]{1,0:T(8,128)S(1)} %bitcast.2, bf16[1040,128]{1,0:T(8,128)(2,1)S(1)} %shard_map.64.packed_ref, bf16[128,2048]{1,0:T(8,128)(2,1)} %q_ref.1, ...), custom_call_target="tpu_custom_call" | custom-call | flops 134217728 | bytes 4194304 | tf_op jit(solution)/shard_map/pallas_call | solution.py:473
  4.8 3.1 %collective-permute-start = (bf16[1040,128]{1,0:T(8,128)(2,1)S(1)}, bf16[1040,128]{1,0:T(8,128)(2,1)S(1)}, u32[]{:S(2)}, u32[]{:S(2)}) collective-permute-start(bf16[1040,128]{1,0:T(8,128)(2,1)S(1)} %get-tuple-element.18.own_ref), channel_id=1, source_target_pairs={{8,12},{12,16},{16,20},{20,24},{9,13},{13,17},{17,21},{21,25},{10,... | collective-permute-start | bytes 798728 | tf_op jit(solution)/shard_map/ppermute | solution.py:450
  8.0 1.3 %collective-permute-start.2 = (bf16[1024,128]{1,0:T(8,128)(2,1)S(1)}, bf16[1024,128]{1,0:T(8,128)(2,1)S(1)}, u32[]{:S(2)}, u32[]{:S(2)}) collective-permute-start(bf16[1024,128]{1,0:T(8,128)(2,1)S(1)} %get-tuple-element.23), channel_id=1, source_target_pairs={{0,8},{4,12},{16,24},{20,28},{1,9},{5,13},{17,25},{21,29},{2,10},{... | collective-permute-start | bytes 786440 | tf_op jit(solution)/shard_map/ppermute | solution.py:450
  9.3 0.0 copy-done
  9.3 2.1 %shard_map.66 = (f32[512,512]{1,0:T(8,128)S(1)}, f32[16,512]{1,0:T(8,128)S(1)}, f32[2048,128]{1,0:T(8,128)S(1)}, f32[128,2048]{1,0:T(8,128)}, bf16[512,512]{1,0:T(8,128)(2,1)S(1)}) custom-call(bf16[128,2048]{1,0:T(8,128)(2,1)S(1)} %copy-done, f32[16,128]{1,0:T(8,128)S(1)} %bitcast.3, ...), custom_call_target="tpu_custom_call", output_to_operand_aliasing={{0}: (4, {}), {1}: (5, {}), {2}: (6, {})} | custom-call | flops 134217728 | bytes 4194304 | tf_op jit(solution)/shard_map/pallas_call | solution.py:496
  11.4 0.3 %collective-permute-done.2.three_ref = bf16[1024,128]{1,0:T(8,128)(2,1)S(1)} collective-permute-done((bf16[1024,128]{1,0:T(8,128)(2,1)S(1)}, bf16[1024,128]{1,0:T(8,128)(2,1)S(1)}, u32[]{:S(2)}, u32[]{:S(2)}) %collective-permute-start.2) | collective-permute-done | bytes 262176 | tf_op jit(solution)/shard_map/ppermute | solution.py:450
  11.7 0.0 collective-permute-done.1.one_ref
  11.7 2.2 %shard_map.68 = (f32[2048,128]{1,0:T(8,128)S(1)}, f32[512,128]{1,0:T(8,128)S(1)}, f32[128,2048]{1,0:T(8,128)}) custom-call(bf16[512,512]{1,0:T(8,128)(2,1)S(1)} %get-tuple-element.22.turned_ref, bf16[1040,128]{1,0:T(8,128)(2,1)S(1)} %get-tuple-element.18.own_ref, ...), custom_call_target="tpu_custom_call", output_to_operand_aliasing={{0}: (7, {}), {2}: (8, {})} | custom-call | tf_op jit(solution)/shard_map/pallas_call | solution.py:513
  14.0 0.0 collective-permute-done.two_ref
  14.0 0.1 shard_map.69
  (1 shorter events, 0.0 us)
Async XLA Ops:
  0.0 4.6 %copy-start.1 = (f32[2048]{0:T(1024)S(1)}, f32[2048]{0:T(1024)}, u32[]{:S(2)}) copy-start(f32[2048]{0:T(1024)} %param.11) | copy-start | bytes 24580
  1.0 10.7 %collective-permute-start.1 = (bf16[1040,128]{1,0:T(8,128)(2,1)S(1)}, bf16[1040,128]{1,0:T(8,128)(2,1)S(1)}, u32[]{:S(2)}, u32[]{:S(2)}) collective-permute-start(bf16[1040,128]{1,0:T(8,128)(2,1)S(1)} %shard_map.64.packed_ref), channel_id=1, source_target_pairs={{8,16},{12,20},{0,4},{4,8},{24,28},{9,17},{13,21},{1,5},{5,9},{25,... | collective-permute-start | bytes 798728 | tf_op jit(solution)/shard_map/ppermute | solution.py:450
  4.6 4.6 %copy-start = (bf16[128,2048]{1,0:T(8,128)(2,1)S(1)}, bf16[128,2048]{1,0:T(8,128)(2,1)}, u32[]{:S(2)}) copy-start(bf16[128,2048]{1,0:T(8,128)(2,1)} %q_ref.1) | copy-start | bytes 1572868
  4.8 9.1 %collective-permute-start = (bf16[1040,128]{1,0:T(8,128)(2,1)S(1)}, bf16[1040,128]{1,0:T(8,128)(2,1)S(1)}, u32[]{:S(2)}, u32[]{:S(2)}) collective-permute-start(bf16[1040,128]{1,0:T(8,128)(2,1)S(1)} %get-tuple-element.18.own_ref), channel_id=1, source_target_pairs={{8,12},{12,16},{16,20},{20,24},{9,13},{13,17},{17,21},{21,25},{10,... | collective-permute-start | bytes 798728 | tf_op jit(solution)/shard_map/ppermute | solution.py:450
  8.0 3.7 %collective-permute-start.2 = (bf16[1024,128]{1,0:T(8,128)(2,1)S(1)}, bf16[1024,128]{1,0:T(8,128)(2,1)S(1)}, u32[]{:S(2)}, u32[]{:S(2)}) collective-permute-start(bf16[1024,128]{1,0:T(8,128)(2,1)S(1)} %get-tuple-element.23), channel_id=1, source_target_pairs={{0,8},{4,12},{16,24},{20,28},{1,9},{5,13},{17,25},{21,29},{2,10},{... | collective-permute-start | bytes 786440 | tf_op jit(solution)/shard_map/ppermute | solution.py:450

commit v19 on v17

--- a/solution.py
+++ b/solution.py
@@ -249,24 +249,21 @@
 
 
 def read_memory(states, turned_ref, gains_ref, reads):
-    rows = (turned_ref.shape[1] // GROUPS)
-    ahead = {}
-
-    def product(g):
-        if g < KV_HEADS and g not in ahead:
-            state = states[g]
-            high = state.astype(jnp.bfloat16)
-            state = state - high.astype(jnp.float32)
-            middle = state.astype(jnp.bfloat16)
-            low = (state - middle.astype(jnp.float32)).astype(jnp.bfloat16)
-            pieces = jnp.concatenate([high, middle, low], axis=0)
-            ahead[g] = dot(pieces, turned_ref[part_of(g, HEAD_DIM), :], NN)
+    rows = turned_ref.shape[1] // GROUPS
+    pieces = []
+    for state in states:
+        high = state.astype(jnp.bfloat16)
+        state = state - high.astype(jnp.float32)
+        middle = state.astype(jnp.bfloat16)
+        low = (state - middle.astype(jnp.float32)).astype(jnp.bfloat16)
+        pieces.append(jnp.concatenate([high, middle, low], axis=0))
+    products = [
+        dot(pieces[g], turned_ref[part_of(g, HEAD_DIM), :], NN) for g in range(KV_HEADS)
+    ]
 
     def read(g):
-        product(g)
-        product(g + 1)
-        recalled = ahead[g][part_of(0, HEAD_DIM), :] + (
-            ahead[g][part_of(1, HEAD_DIM), :] + ahead[g][part_of(2, HEAD_DIM), :]
+        recalled = products[g][part_of(0, HEAD_DIM), :] + (
+            products[g][part_of(1, HEAD_DIM), :] + products[g][part_of(2, HEAD_DIM), :]
         )
         heads = []
         for i in range(GROUPS):
@@ -290,8 +287,8 @@
             ahead[g] = dot(block_keys(one_ref, g), turned_ref[part_of(g, HEAD_DIM), :], NN)
 
     def attend(g):
-        score(g)
-        score(g + 1)
+        for later in range(3):
+            score(g + later)
         weights, factors, scales = [], [], []
         for i in range(GROUPS):
             cut = part_of(i, rows)
@@ -314,17 +311,14 @@
 
 def store_heads(mixed, out_ref, held, sems):
     copies = []
+    ahead = mixed(0)
     for g in range(KV_HEADS):
-        for i, head in enumerate(mixed(g)):
-            h = g * GROUPS + i
-            held[:, part_of(h, HEAD_DIM)] = jnp.transpose(head)
-            if h % 2 == 1:
-                wide = part_of(h // 2, 2 * HEAD_DIM)
-                copy = pltpu.make_async_copy(
-                    held.at[:, wide], out_ref.at[:, wide], sems.at[h // 2]
-                )
-                copy.start()
-                copies.append(copy)
+        heads, ahead = ahead, mixed(g + 1) if g + 1 < KV_HEADS else None
+        for i, head in enumerate(heads):
+            held[:, part_of(g * GROUPS + i, HEAD_DIM)] = jnp.transpose(head)
+        wide = part_of(g, GROUPS * HEAD_DIM)
+        copies.append(pltpu.make_async_copy(held.at[:, wide], out_ref.at[:, wide], sems.at[g]))
+        copies[g].start()
     for copy in copies:
         copy.wait()
 
@@ -492,7 +486,7 @@
     out_shape = jax.ShapeDtypeStruct((rows, HEADS * HEAD_DIM), jnp.float32)
     store_scratch = [
         pltpu.VMEM((rows, HEADS * HEAD_DIM), jnp.float32),
-        pltpu.SemaphoreType.DMA((HEADS // 2,)),
+        pltpu.SemaphoreType.DMA((KV_HEADS,)),
     ]
     turned_shape = jax.ShapeDtypeStruct((KV_HEADS * HEAD_DIM, wide), queries.dtype)
     summed, stats, gains, out, turned = pl.pallas_call(

time: 14.1 us -> 14 us (level)
  transfers between devices with their start and end apart: 3 -> 3, of which waited for: 1 -> 1; matrix products, arithmetic and copies ran while one was open for 0% -> 0% of each run, Pallas kernels for 24% -> 23%
where the time goes in v19:
time: 14 us; the launch traced here: 13.8 us
  starting transfers between devices  6.29 us (45%)
  Pallas kernels  5.86 us (42%)
  waiting for transfers between devices  1.53 us (11%)
    ppermute x3, starting transfers between devices, send(): return lax.ppermute(payload, ('seq', 'kv'), pairs)  6.29 us
    pallas_call x1, Pallas kernels, near_device(): pl.pallas_call(functools.partial(own_kernel, plan), out_shape=results + [...  2.09 us
    pallas_call x1, Pallas kernels, near_device(): pl.pallas_call(functools.partial(late_kernel, plan), out_shape=out_shape,...  1.65 us
    ppermute x3, waiting for transfers between devices, send(): return lax.ppermute(payload, ('seq', 'kv'), pairs)  1.53 us
    pallas_call x1, Pallas kernels, near_device(): pl.pallas_call(functools.partial(pack_kernel, plan), out_shape=block_shap...  0.98 us
    pallas_call x1, Pallas kernels, near_device(): pl.pallas_call(functools.partial(read_kernel, plan), out_shape=gains_shap...  0.9 us
  transfers between devices with their start and end apart: 3, of which 1 were waited for; matrix products, arithmetic and copies ran while one was open for 0% of the time, Pallas kernels for 23%

profile of v19, /device:TPU:27, one launch (start us, length us, event | category | flops | bytes accessed | tf_op | source)
XLA Modules:
  0.0 13.8 jit_solution(9483161481556893908)
XLA Ops:
  0.0 0.0 copy-start.1
  0.0 1.0 %shard_map.64.packed_ref = bf16[1040,128]{1,0:T(8,128)(2,1)S(1)} custom-call(bf16[128,512]{1,0:T(8,128)(2,1)} %key_ref.3, bf16[128,512]{1,0:T(8,128)(2,1)} %value_ref.3, s32[1,128]{1,0:T(1,128)} %bitcast.4), custom_call_target="tpu_custom_call" | custom-call | flops 13421772 | bytes 419430 | tf_op jit(solution)/shard_map/pallas_call | solution.py:459
  1.0 2.8 %collective-permute-start.1 = (bf16[1040,128]{1,0:T(8,128)(2,1)S(1)}, bf16[1040,128]{1,0:T(8,128)(2,1)S(1)}, u32[]{:S(2)}, u32[]{:S(2)}) collective-permute-start(bf16[1040,128]{1,0:T(8,128)(2,1)S(1)} %shard_map.64.packed_ref), channel_id=1, source_target_pairs={{8,16},{12,20},{0,4},{4,8},{24,28},{9,17},{13,21},{1,5},{5,9},{25,... | collective-permute-start | bytes 798728 | tf_op jit(solution)/shard_map/ppermute | solution.py:446
  3.8 0.0 copy-done.1
  3.8 0.0 copy-start
  3.8 0.2 %shard_map.65 = (bf16[1040,128]{1,0:T(8,128)(2,1)S(1)}, bf16[1024,128]{1,0:T(8,128)(2,1)S(1)}, f32[512,512]{1,0:T(8,128)S(1)}, f32[16,512]{1,0:T(8,128)S(1)}, f32[2048,128]{1,0:T(8,128)S(1)}) custom-call(f32[16,128]{1,0:T(8,128)S(1)} %bitcast.2, bf16[1040,128]{1,0:T(8,128)(2,1)S(1)} %shard_map.64.packed_ref, bf16[128,2048]{1,0:T(8,128)(2,1)} %q_ref.1, ...), custom_call_target="tpu_custom_call" | custom-call | flops 134217728 | bytes 4194304 | tf_op jit(solution)/shard_map/pallas_call | solution.py:469
  4.0 2.2 %collective-permute-start = (bf16[1040,128]{1,0:T(8,128)(2,1)S(1)}, bf16[1040,128]{1,0:T(8,128)(2,1)S(1)}, u32[]{:S(2)}, u32[]{:S(2)}) collective-permute-start(bf16[1040,128]{1,0:T(8,128)(2,1)S(1)} %get-tuple-element.18.own_ref), channel_id=1, source_target_pairs={{8,12},{12,16},{16,20},{20,24},{9,13},{13,17},{17,21},{21,25},{10,... | collective-permute-start | bytes 798728 | tf_op jit(solution)/shard_map/ppermute | solution.py:446
  6.2 1.3 %collective-permute-start.2 = (bf16[1024,128]{1,0:T(8,128)(2,1)S(1)}, bf16[1024,128]{1,0:T(8,128)(2,1)S(1)}, u32[]{:S(2)}, u32[]{:S(2)}) collective-permute-start(bf16[1024,128]{1,0:T(8,128)(2,1)S(1)} %get-tuple-element.23), channel_id=1, source_target_pairs={{0,8},{4,12},{16,24},{20,28},{1,9},{5,13},{17,25},{21,29},{2,10},{... | collective-permute-start | bytes 786440 | tf_op jit(solution)/shard_map/ppermute | solution.py:446
  7.5 0.0 copy-done
  7.5 2.1 %shard_map.66 = (f32[512,512]{1,0:T(8,128)S(1)}, f32[16,512]{1,0:T(8,128)S(1)}, f32[2048,128]{1,0:T(8,128)S(1)}, f32[128,2048]{1,0:T(8,128)}, bf16[512,512]{1,0:T(8,128)(2,1)S(1)}) custom-call(bf16[128,2048]{1,0:T(8,128)(2,1)S(1)} %copy-done, f32[16,128]{1,0:T(8,128)S(1)} %bitcast.3, ...), custom_call_target="tpu_custom_call", output_to_operand_aliasing={{0}: (4, {}), {1}: (5, {}), {2}: (6, {})} | custom-call | flops 134217728 | bytes 4194304 | tf_op jit(solution)/shard_map/pallas_call | solution.py:492
  9.6 0.0 collective-permute-done.2.three_ref
  9.6 0.9 %shard_map.67.read_in = f32[2048,128]{1,0:T(8,128)S(1)} custom-call(bf16[512,512]{1,0:T(8,128)(2,1)S(1)} %get-tuple-element.22.turned_ref, bf16[1040,128]{1,0:T(8,128)(2,1)S(1)} %get-tuple-element.18.own_ref, bf16[1024,128]{1,0:T(8,128)(2,1)S(1)} %collective-permute-done.2.three_ref, f32[2048,128]{1,0:T(8,128)S(1)} %get-tuple-element.25.gains_ref), custom_call_target="tpu_custom_call" | custom-call | tf_op jit(solution)/shard_map/pallas_call | solution.py:502
  10.5 0.0 collective-permute-done.1.one_ref
  10.5 0.1 shard_map.68
  10.6 1.5 %collective-permute-done.two_ref = bf16[1040,128]{1,0:T(8,128)(2,1)S(1)} collective-permute-done((bf16[1040,128]{1,0:T(8,128)(2,1)S(1)}, bf16[1040,128]{1,0:T(8,128)(2,1)S(1)}, u32[]{:S(2)}, u32[]{:S(2)}) %collective-permute-start) | collective-permute-done | bytes 266272 | tf_op jit(solution)/shard_map/ppermute | solution.py:446
  12.1 1.6 %shard_map.69 = f32[128,2048]{1,0:T(8,128)} custom-call(bf16[512,512]{1,0:T(8,128)(2,1)S(1)} %get-tuple-element.22.turned_ref, bf16[1040,128]{1,0:T(8,128)(2,1)S(1)} %get-tuple-element.18.own_ref, bf16[1040,128]{1,0:T(8,128)(2,1)S(1)} %collective-permute-done.two_ref, f32[512,128]{1,0:T(8,128)S(1)} %get-tuple-element.28.state_ref, ...), custom_call_target="tpu_custom_call", output_to_operand_aliasing={{}: (8, {})} | custom-call | tf_op jit(solution)/shard_map/pallas_call | solution.py:518
Async XLA Ops:
  0.0 3.8 %copy-start.1 = (f32[2048]{0:T(1024)S(1)}, f32[2048]{0:T(1024)}, u32[]{:S(2)}) copy-start(f32[2048]{0:T(1024)} %param.11) | copy-start | bytes 24580
  1.0 9.5 %collective-permute-start.1 = (bf16[1040,128]{1,0:T(8,128)(2,1)S(1)}, bf16[1040,128]{1,0:T(8,128)(2,1)S(1)}, u32[]{:S(2)}, u32[]{:S(2)}) collective-permute-start(bf16[1040,128]{1,0:T(8,128)(2,1)S(1)} %shard_map.64.packed_ref), channel_id=1, source_target_pairs={{8,16},{12,20},{0,4},{4,8},{24,28},{9,17},{13,21},{1,5},{5,9},{25,... | collective-permute-start | bytes 798728 | tf_op jit(solution)/shard_map/ppermute | solution.py:446
  3.8 3.7 %copy-start = (bf16[128,2048]{1,0:T(8,128)(2,1)S(1)}, bf16[128,2048]{1,0:T(8,128)(2,1)}, u32[]{:S(2)}) copy-start(bf16[128,2048]{1,0:T(8,128)(2,1)} %q_ref.1) | copy-start | bytes 1572868
  4.0 8.1 %collective-permute-start = (bf16[1040,128]{1,0:T(8,128)(2,1)S(1)}, bf16[1040,128]{1,0:T(8,128)(2,1)S(1)}, u32[]{:S(2)}, u32[]{:S(2)}) collective-permute-start(bf16[1040,128]{1,0:T(8,128)(2,1)S(1)} %get-tuple-element.18.own_ref), channel_id=1, source_target_pairs={{8,12},{12,16},{16,20},{20,24},{9,13},{13,17},{17,21},{21,25},{10,... | collective-permute-start | bytes 798728 | tf_op jit(solution)/shard_map/ppermute | solution.py:446
  6.2 3.4 %collective-permute-start.2 = (bf16[1024,128]{1,0:T(8,128)(2,1)S(1)}, bf16[1024,128]{1,0:T(8,128)(2,1)S(1)}, u32[]{:S(2)}, u32[]{:S(2)}) collective-permute-start(bf16[1024,128]{1,0:T(8,128)(2,1)S(1)} %get-tuple-element.23), channel_id=1, source_target_pairs={{0,8},{4,12},{16,24},{20,28},{1,9},{5,13},{17,25},{21,29},{2,10},{... | collective-permute-start | bytes 786440 | tf_op jit(solution)/shard_map/ppermute | solution.py:446

commit v20 on v19

--- a/solution.py
+++ b/solution.py
@@ -316,9 +316,11 @@
         heads, ahead = ahead, mixed(g + 1) if g + 1 < KV_HEADS else None
         for i, head in enumerate(heads):
             held[:, part_of(g * GROUPS + i, HEAD_DIM)] = jnp.transpose(head)
-        wide = part_of(g, GROUPS * HEAD_DIM)
-        copies.append(pltpu.make_async_copy(held.at[:, wide], out_ref.at[:, wide], sems.at[g]))
-        copies[g].start()
+        for half in range(2 * g, 2 * g + 2):
+            wide = part_of(half, GROUPS // 2 * HEAD_DIM)
+            copy = pltpu.make_async_copy(held.at[:, wide], out_ref.at[:, wide], sems.at[half])
+            copy.start(priority=half % 2)
+            copies.append(copy)
     for copy in copies:
         copy.wait()
 
@@ -486,7 +488,7 @@
     out_shape = jax.ShapeDtypeStruct((rows, HEADS * HEAD_DIM), jnp.float32)
     store_scratch = [
         pltpu.VMEM((rows, HEADS * HEAD_DIM), jnp.float32),
-        pltpu.SemaphoreType.DMA((KV_HEADS,)),
+        pltpu.SemaphoreType.DMA((2 * KV_HEADS,)),
     ]
     turned_shape = jax.ShapeDtypeStruct((KV_HEADS * HEAD_DIM, wide), queries.dtype)
     summed, stats, gains, out, turned = pl.pallas_call(

time: 14 us -> 14.1 us (level)
  transfers between devices with their start and end apart: 3 -> 3, of which waited for: 1 -> 1; matrix products, arithmetic and copies ran while one was open for 0% -> 0% of each run, Pallas kernels for 23% -> 24%
where the time goes in v20:
time: 14.1 us; the launch traced here: 13.8 us
  starting transfers between devices  6.29 us (45%)
  Pallas kernels  5.97 us (42%)
  waiting for transfers between devices  1.44 us (10%)
    ppermute x3, starting transfers between devices, send(): return lax.ppermute(payload, ('seq', 'kv'), pairs)  6.29 us
    pallas_call x1, Pallas kernels, near_device(): pl.pallas_call(functools.partial(own_kernel, plan), out_shape=results + [...  2.13 us
    pallas_call x1, Pallas kernels, near_device(): pl.pallas_call(functools.partial(late_kernel, plan), out_shape=out_shape,...  1.68 us
    ppermute x3, waiting for transfers between devices, send(): return lax.ppermute(payload, ('seq', 'kv'), pairs)  1.44 us
    pallas_call x1, Pallas kernels, near_device(): pl.pallas_call(functools.partial(pack_kernel, plan), out_shape=block_shap...  0.98 us
    pallas_call x1, Pallas kernels, near_device(): pl.pallas_call(functools.partial(read_kernel, plan), out_shape=gains_shap...  0.91 us
  transfers between devices with their start and end apart: 3, of which 1 were waited for; matrix products, arithmetic and copies ran while one was open for 0% of the time, Pallas kernels for 24%

profile of v20, /device:TPU:27, one launch (start us, length us, event | category | flops | bytes accessed | tf_op | source)
XLA Modules:
  0.0 13.8 jit_solution(9085218084415521809)
XLA Ops:
  0.0 0.0 copy-start.1
  0.0 1.0 %shard_map.64.packed_ref = bf16[1040,128]{1,0:T(8,128)(2,1)S(1)} custom-call(bf16[128,512]{1,0:T(8,128)(2,1)} %key_ref.3, bf16[128,512]{1,0:T(8,128)(2,1)} %value_ref.3, s32[1,128]{1,0:T(1,128)} %bitcast.4), custom_call_target="tpu_custom_call" | custom-call | flops 13421772 | bytes 419430 | tf_op jit(solution)/shard_map/pallas_call | solution.py:461
  1.0 2.8 %collective-permute-start.1 = (bf16[1040,128]{1,0:T(8,128)(2,1)S(1)}, bf16[1040,128]{1,0:T(8,128)(2,1)S(1)}, u32[]{:S(2)}, u32[]{:S(2)}) collective-permute-start(bf16[1040,128]{1,0:T(8,128)(2,1)S(1)} %shard_map.64.packed_ref), channel_id=1, source_target_pairs={{8,16},{12,20},{0,4},{4,8},{24,28},{9,17},{13,21},{1,5},{5,9},{25,... | collective-permute-start | bytes 798728 | tf_op jit(solution)/shard_map/ppermute | solution.py:448
  3.8 0.0 copy-done.1
  3.8 0.0 copy-start
  3.8 0.2 %shard_map.65 = (bf16[1040,128]{1,0:T(8,128)(2,1)S(1)}, bf16[1024,128]{1,0:T(8,128)(2,1)S(1)}, f32[512,512]{1,0:T(8,128)S(1)}, f32[16,512]{1,0:T(8,128)S(1)}, f32[2048,128]{1,0:T(8,128)S(1)}) custom-call(f32[16,128]{1,0:T(8,128)S(1)} %bitcast.2, bf16[1040,128]{1,0:T(8,128)(2,1)S(1)} %shard_map.64.packed_ref, bf16[128,2048]{1,0:T(8,128)(2,1)} %q_ref.1, ...), custom_call_target="tpu_custom_call" | custom-call | flops 134217728 | bytes 4194304 | tf_op jit(solution)/shard_map/pallas_call | solution.py:471
  4.0 2.2 %collective-permute-start = (bf16[1040,128]{1,0:T(8,128)(2,1)S(1)}, bf16[1040,128]{1,0:T(8,128)(2,1)S(1)}, u32[]{:S(2)}, u32[]{:S(2)}) collective-permute-start(bf16[1040,128]{1,0:T(8,128)(2,1)S(1)} %get-tuple-element.18.own_ref), channel_id=1, source_target_pairs={{8,12},{12,16},{16,20},{20,24},{9,13},{13,17},{17,21},{21,25},{10,... | collective-permute-start | bytes 798728 | tf_op jit(solution)/shard_map/ppermute | solution.py:448
  6.2 1.3 %collective-permute-start.2 = (bf16[1024,128]{1,0:T(8,128)(2,1)S(1)}, bf16[1024,128]{1,0:T(8,128)(2,1)S(1)}, u32[]{:S(2)}, u32[]{:S(2)}) collective-permute-start(bf16[1024,128]{1,0:T(8,128)(2,1)S(1)} %get-tuple-element.23), channel_id=1, source_target_pairs={{0,8},{4,12},{16,24},{20,28},{1,9},{5,13},{17,25},{21,29},{2,10},{... | collective-permute-start | bytes 786440 | tf_op jit(solution)/shard_map/ppermute | solution.py:448
  7.5 0.0 copy-done
  7.5 2.1 %shard_map.66 = (f32[512,512]{1,0:T(8,128)S(1)}, f32[16,512]{1,0:T(8,128)S(1)}, f32[2048,128]{1,0:T(8,128)S(1)}, f32[128,2048]{1,0:T(8,128)}, bf16[512,512]{1,0:T(8,128)(2,1)S(1)}) custom-call(bf16[128,2048]{1,0:T(8,128)(2,1)S(1)} %copy-done, f32[16,128]{1,0:T(8,128)S(1)} %bitcast.3, ...), custom_call_target="tpu_custom_call", output_to_operand_aliasing={{0}: (4, {}), {1}: (5, {}), {2}: (6, {})} | custom-call | flops 134217728 | bytes 4194304 | tf_op jit(solution)/shard_map/pallas_call | solution.py:494
  9.6 0.0 collective-permute-done.2.three_ref
  9.7 0.9 %shard_map.67.read_in = f32[2048,128]{1,0:T(8,128)S(1)} custom-call(bf16[512,512]{1,0:T(8,128)(2,1)S(1)} %get-tuple-element.22.turned_ref, bf16[1040,128]{1,0:T(8,128)(2,1)S(1)} %get-tuple-element.18.own_ref, bf16[1024,128]{1,0:T(8,128)(2,1)S(1)} %collective-permute-done.2.three_ref, f32[2048,128]{1,0:T(8,128)S(1)} %get-tuple-element.25.gains_ref), custom_call_target="tpu_custom_call" | custom-call | tf_op jit(solution)/shard_map/pallas_call | solution.py:504
  10.6 0.0 collective-permute-done.1.one_ref
  10.6 0.1 shard_map.68
  10.7 1.4 %collective-permute-done.two_ref = bf16[1040,128]{1,0:T(8,128)(2,1)S(1)} collective-permute-done((bf16[1040,128]{1,0:T(8,128)(2,1)S(1)}, bf16[1040,128]{1,0:T(8,128)(2,1)S(1)}, u32[]{:S(2)}, u32[]{:S(2)}) %collective-permute-start) | collective-permute-done | bytes 266272 | tf_op jit(solution)/shard_map/ppermute | solution.py:448
  12.1 1.7 %shard_map.69 = f32[128,2048]{1,0:T(8,128)} custom-call(bf16[512,512]{1,0:T(8,128)(2,1)S(1)} %get-tuple-element.22.turned_ref, bf16[1040,128]{1,0:T(8,128)(2,1)S(1)} %get-tuple-element.18.own_ref, bf16[1040,128]{1,0:T(8,128)(2,1)S(1)} %collective-permute-done.two_ref, f32[512,128]{1,0:T(8,128)S(1)} %get-tuple-element.28.state_ref, ...), custom_call_target="tpu_custom_call", output_to_operand_aliasing={{}: (8, {})} | custom-call | tf_op jit(solution)/shard_map/pallas_call | solution.py:520
Async XLA Ops:
  0.0 3.8 %copy-start.1 = (f32[2048]{0:T(1024)S(1)}, f32[2048]{0:T(1024)}, u32[]{:S(2)}) copy-start(f32[2048]{0:T(1024)} %param.11) | copy-start | bytes 24580
  1.0 9.6 %collective-permute-start.1 = (bf16[1040,128]{1,0:T(8,128)(2,1)S(1)}, bf16[1040,128]{1,0:T(8,128)(2,1)S(1)}, u32[]{:S(2)}, u32[]{:S(2)}) collective-permute-start(bf16[1040,128]{1,0:T(8,128)(2,1)S(1)} %shard_map.64.packed_ref), channel_id=1, source_target_pairs={{8,16},{12,20},{0,4},{4,8},{24,28},{9,17},{13,21},{1,5},{5,9},{25,... | collective-permute-start | bytes 798728 | tf_op jit(solution)/shard_map/ppermute | solution.py:448
  3.8 3.7 %copy-start = (bf16[128,2048]{1,0:T(8,128)(2,1)S(1)}, bf16[128,2048]{1,0:T(8,128)(2,1)}, u32[]{:S(2)}) copy-start(bf16[128,2048]{1,0:T(8,128)(2,1)} %q_ref.1) | copy-start | bytes 1572868
  4.0 8.1 %collective-permute-start = (bf16[1040,128]{1,0:T(8,128)(2,1)S(1)}, bf16[1040,128]{1,0:T(8,128)(2,1)S(1)}, u32[]{:S(2)}, u32[]{:S(2)}) collective-permute-start(bf16[1040,128]{1,0:T(8,128)(2,1)S(1)} %get-tuple-element.18.own_ref), channel_id=1, source_target_pairs={{8,12},{12,16},{16,20},{20,24},{9,13},{13,17},{17,21},{21,25},{10,... | collective-permute-start | bytes 798728 | tf_op jit(solution)/shard_map/ppermute | solution.py:448
  6.2 3.4 %collective-permute-start.2 = (bf16[1024,128]{1,0:T(8,128)(2,1)S(1)}, bf16[1024,128]{1,0:T(8,128)(2,1)S(1)}, u32[]{:S(2)}, u32[]{:S(2)}) collective-permute-start(bf16[1024,128]{1,0:T(8,128)(2,1)S(1)} %get-tuple-element.23), channel_id=1, source_target_pairs={{0,8},{4,12},{16,24},{20,28},{1,9},{5,13},{17,25},{21,29},{2,10},{... | collective-permute-start | bytes 786440 | tf_op jit(solution)/shard_map/ppermute | solution.py:448

commit v21 on v19

--- a/solution.py
+++ b/solution.py
@@ -168,9 +168,9 @@
 
 
 def settle_kernel(
-    plan, gain_ref, packed_ref, query_ref, key_ref, value_ref, doc_ref, beta_ref,
+    plan, gain_ref, packed_ref, key_ref, value_ref, doc_ref, query_ref, beta_ref,
     own_ref, short_ref, summed_ref, stats_ref, gains_ref,
-    q_scratch, beta_scratch, doc_scratch, sems, early_sems,
+    q_scratch, beta_scratch, early_sems,
 ):
     sender, early = among(plan.senders), among(plan.early)
     query_copy = pltpu.make_async_copy(query_ref, q_scratch, early_sems.at[0])
@@ -187,7 +187,13 @@
 
     @pl.when(jnp.logical_not(sender))
     def _():
-        load_block(key_ref, value_ref, doc_ref, own_ref, doc_scratch, sems)
+        for g in range(KV_HEADS):
+            cols = part_of(g, HEAD_DIM)
+            own_ref[part_of(g, HEAD_DIM), :] = key_ref[:, cols]
+            own_ref[part_of(KV_HEADS + g, HEAD_DIM), :] = value_ref[:, cols]
+        start = 2 * KV_HEADS * HEAD_DIM
+        docs = jnp.broadcast_to(doc_ref[...].astype(jnp.float32), (EXTRA, HEAD_DIM))
+        own_ref[start:, :] = docs.astype(jnp.bfloat16)
 
     short_ref[...] = own_ref[0 : short_ref.shape[0], :]
     line = lax.broadcasted_iota(jnp.int32, (EXTRA, HEAD_DIM), 0)
@@ -469,18 +475,16 @@
     own, short, summed, stats, gains = pl.pallas_call(
         functools.partial(settle_kernel, plan),
         out_shape=[block_shape, short_shape] + results,
-        in_specs=[vmem] * 2 + [hbm] * 5,
+        in_specs=[vmem] * 5 + [hbm] * 2,
         out_specs=[vmem] * 5,
         scratch_shapes=[
             pltpu.VMEM(queries.shape, queries.dtype),
             beta_scratch,
-            doc_scratch,
-            sems,
             pltpu.SemaphoreType.DMA((2,)),
         ],
         compiler_params=params,
         cost_estimate=estimate(1.0),
-    )(gain, packed, in_hbm(queries), *block, beta)
+    )(gain, packed, keys, values, docs, in_hbm(queries), beta)
     two = send(own, plan.pairs[1])
     three = send(short, plan.pairs[2])
     out_shape = jax.ShapeDtypeStruct((rows, HEADS * HEAD_DIM), jnp.float32)

time: 14 us -> 14 us (level)
  no operation moved by 1% of the time
where the time goes in v21:
time: 14 us; the launch traced here: 13.9 us
  starting transfers between devices  6.27 us (45%)
  Pallas kernels  5.82 us (42%)
  waiting for transfers between devices  1.61 us (12%)
    ppermute x3, starting transfers between devices, send(): return lax.ppermute(payload, ('seq', 'kv'), pairs)  6.27 us
    pallas_call x1, Pallas kernels, near_device(): pl.pallas_call(functools.partial(own_kernel, plan), out_shape=results + [...  2.09 us
    pallas_call x1, Pallas kernels, near_device(): pl.pallas_call(functools.partial(late_kernel, plan), out_shape=out_shape,...  1.65 us
    ppermute x3, waiting for transfers between devices, send(): return lax.ppermute(payload, ('seq', 'kv'), pairs)  1.61 us
    pallas_call x1, Pallas kernels, near_device(): pl.pallas_call(functools.partial(pack_kernel, plan), out_shape=block_shap...  1.02 us
    pallas_call x1, Pallas kernels, near_device(): pl.pallas_call(functools.partial(read_kernel, plan), out_shape=gains_shap...  0.9 us
  transfers between devices with their start and end apart: 3, of which 1 were waited for; matrix products, arithmetic and copies ran while one was open for 0% of the time, Pallas kernels for 23%

profile of v21, /device:TPU:27, one launch (start us, length us, event | category | flops | bytes accessed | tf_op | source)
XLA Modules:
  0.0 13.9 jit_solution(7475126192199888360)
XLA Ops:
  0.0 0.0 copy-start.1
  0.0 0.0 copy-start.2
  0.0 0.0 copy-start.3
  0.0 1.0 %shard_map.64.packed_ref = bf16[1040,128]{1,0:T(8,128)(2,1)S(1)} custom-call(bf16[128,512]{1,0:T(8,128)(2,1)} %key_ref.3, bf16[128,512]{1,0:T(8,128)(2,1)} %value_ref.3, s32[1,128]{1,0:T(1,128)} %bitcast.4), custom_call_target="tpu_custom_call" | custom-call | flops 13421772 | bytes 419430 | tf_op jit(solution)/shard_map/pallas_call | solution.py:465
  1.0 0.0 copy-start.4
  1.1 2.9 %collective-permute-start.1 = (bf16[1040,128]{1,0:T(8,128)(2,1)S(1)}, bf16[1040,128]{1,0:T(8,128)(2,1)S(1)}, u32[]{:S(2)}, u32[]{:S(2)}) collective-permute-start(bf16[1040,128]{1,0:T(8,128)(2,1)S(1)} %shard_map.64.packed_ref), channel_id=1, source_target_pairs={{8,16},{12,20},{0,4},{4,8},{24,28},{9,17},{13,21},{1,5},{5,9},{25,... | collective-permute-start | bytes 798728 | tf_op jit(solution)/shard_map/ppermute | solution.py:452
  4.0 0.0 copy-done.1
  4.0 0.0 copy-done.2
  4.0 0.0 copy-done.3
  4.0 0.0 copy-done.4
  4.0 0.0 copy-start
  4.0 0.1 shard_map.65
  4.1 2.1 %collective-permute-start = (bf16[1040,128]{1,0:T(8,128)(2,1)S(1)}, bf16[1040,128]{1,0:T(8,128)(2,1)S(1)}, u32[]{:S(2)}, u32[]{:S(2)}) collective-permute-start(bf16[1040,128]{1,0:T(8,128)(2,1)S(1)} %get-tuple-element.18.own_ref), channel_id=1, source_target_pairs={{8,12},{12,16},{16,20},{20,24},{9,13},{13,17},{17,21},{21,25},{10,... | collective-permute-start | bytes 798728 | tf_op jit(solution)/shard_map/ppermute | solution.py:452
  6.2 1.3 %collective-permute-start.2 = (bf16[1024,128]{1,0:T(8,128)(2,1)S(1)}, bf16[1024,128]{1,0:T(8,128)(2,1)S(1)}, u32[]{:S(2)}, u32[]{:S(2)}) collective-permute-start(bf16[1024,128]{1,0:T(8,128)(2,1)S(1)} %get-tuple-element.23), channel_id=1, source_target_pairs={{0,8},{4,12},{16,24},{20,28},{1,9},{5,13},{17,25},{21,29},{2,10},{... | collective-permute-start | bytes 786440 | tf_op jit(solution)/shard_map/ppermute | solution.py:452
  7.5 0.0 copy-done
  7.5 2.1 %shard_map.66 = (f32[512,512]{1,0:T(8,128)S(1)}, f32[16,512]{1,0:T(8,128)S(1)}, f32[2048,128]{1,0:T(8,128)S(1)}, f32[128,2048]{1,0:T(8,128)}, bf16[512,512]{1,0:T(8,128)(2,1)S(1)}) custom-call(bf16[128,2048]{1,0:T(8,128)(2,1)S(1)} %copy-done, f32[16,128]{1,0:T(8,128)S(1)} %bitcast.3, ...), custom_call_target="tpu_custom_call", output_to_operand_aliasing={{0}: (4, {}), {1}: (5, {}), {2}: (6, {})} | custom-call | flops 134217728 | bytes 4194304 | tf_op jit(solution)/shard_map/pallas_call | solution.py:496
  9.6 0.0 collective-permute-done.2.three_ref
  9.6 0.9 %shard_map.67.read_in = f32[2048,128]{1,0:T(8,128)S(1)} custom-call(bf16[512,512]{1,0:T(8,128)(2,1)S(1)} %get-tuple-element.22.turned_ref, bf16[1040,128]{1,0:T(8,128)(2,1)S(1)} %get-tuple-element.18.own_ref, bf16[1024,128]{1,0:T(8,128)(2,1)S(1)} %collective-permute-done.2.three_ref, f32[2048,128]{1,0:T(8,128)S(1)} %get-tuple-element.25.gains_ref), custom_call_target="tpu_custom_call" | custom-call | tf_op jit(solution)/shard_map/pallas_call | solution.py:506
  10.5 0.0 collective-permute-done.1.one_ref
  10.5 0.1 shard_map.68
  10.6 1.6 %collective-permute-done.two_ref = bf16[1040,128]{1,0:T(8,128)(2,1)S(1)} collective-permute-done((bf16[1040,128]{1,0:T(8,128)(2,1)S(1)}, bf16[1040,128]{1,0:T(8,128)(2,1)S(1)}, u32[]{:S(2)}, u32[]{:S(2)}) %collective-permute-start) | collective-permute-done | bytes 266272 | tf_op jit(solution)/shard_map/ppermute | solution.py:452
  12.2 1.7 %shard_map.69 = f32[128,2048]{1,0:T(8,128)} custom-call(bf16[512,512]{1,0:T(8,128)(2,1)S(1)} %get-tuple-element.22.turned_ref, bf16[1040,128]{1,0:T(8,128)(2,1)S(1)} %get-tuple-element.18.own_ref, bf16[1040,128]{1,0:T(8,128)(2,1)S(1)} %collective-permute-done.two_ref, f32[512,128]{1,0:T(8,128)S(1)} %get-tuple-element.28.state_ref, ...), custom_call_target="tpu_custom_call", output_to_operand_aliasing={{}: (8, {})} | custom-call | tf_op jit(solution)/shard_map/pallas_call | solution.py:522
Async XLA Ops:
  0.0 4.0 %copy-start.1 = (bf16[128,512]{1,0:T(8,128)(2,1)S(1)}, bf16[128,512]{1,0:T(8,128)(2,1)}, u32[]{:S(2)}) copy-start(bf16[128,512]{1,0:T(8,128)(2,1)} %key_ref.3) | copy-start | bytes 393220
  0.0 4.0 %copy-start.2 = (bf16[128,512]{1,0:T(8,128)(2,1)S(1)}, bf16[128,512]{1,0:T(8,128)(2,1)}, u32[]{:S(2)}) copy-start(bf16[128,512]{1,0:T(8,128)(2,1)} %value_ref.3) | copy-start | bytes 393220
  0.0 4.0 %copy-start.3 = (f32[2048]{0:T(1024)S(1)}, f32[2048]{0:T(1024)}, u32[]{:S(2)}) copy-start(f32[2048]{0:T(1024)} %param.11) | copy-start | bytes 24580
  1.0 3.0 %copy-start.4 = (s32[128]{0:T(128)S(1)}, s32[128]{0:T(128)}, u32[]{:S(2)}) copy-start(s32[128]{0:T(128)} %param.9) | copy-start | bytes 1540
  1.1 9.5 %collective-permute-start.1 = (bf16[1040,128]{1,0:T(8,128)(2,1)S(1)}, bf16[1040,128]{1,0:T(8,128)(2,1)S(1)}, u32[]{:S(2)}, u32[]{:S(2)}) collective-permute-start(bf16[1040,128]{1,0:T(8,128)(2,1)S(1)} %shard_map.64.packed_ref), channel_id=1, source_target_pairs={{8,16},{12,20},{0,4},{4,8},{24,28},{9,17},{13,21},{1,5},{5,9},{25,... | collective-permute-start | bytes 798728 | tf_op jit(solution)/shard_map/ppermute | solution.py:452
  4.0 3.5 %copy-start = (bf16[128,2048]{1,0:T(8,128)(2,1)S(1)}, bf16[128,2048]{1,0:T(8,128)(2,1)}, u32[]{:S(2)}) copy-start(bf16[128,2048]{1,0:T(8,128)(2,1)} %q_ref.1) | copy-start | bytes 1572868
  4.1 8.1 %collective-permute-start = (bf16[1040,128]{1,0:T(8,128)(2,1)S(1)}, bf16[1040,128]{1,0:T(8,128)(2,1)S(1)}, u32[]{:S(2)}, u32[]{:S(2)}) collective-permute-start(bf16[1040,128]{1,0:T(8,128)(2,1)S(1)} %get-tuple-element.18.own_ref), channel_id=1, source_target_pairs={{8,12},{12,16},{16,20},{20,24},{9,13},{13,17},{17,21},{21,25},{10,... | collective-permute-start | bytes 798728 | tf_op jit(solution)/shard_map/ppermute | solution.py:452
  6.2 3.4 %collective-permute-start.2 = (bf16[1024,128]{1,0:T(8,128)(2,1)S(1)}, bf16[1024,128]{1,0:T(8,128)(2,1)S(1)}, u32[]{:S(2)}, u32[]{:S(2)}) collective-permute-start(bf16[1024,128]{1,0:T(8,128)(2,1)S(1)} %get-tuple-element.23), channel_id=1, source_target_pairs={{0,8},{4,12},{16,24},{20,28},{1,9},{5,13},{17,25},{21,29},{2,10},{... | collective-permute-start | bytes 786440 | tf_op jit(solution)/shard_map/ppermute | solution.py:452

commit v22 on v21

--- a/solution.py
+++ b/solution.py
@@ -104,17 +104,22 @@
         crossing = [p for p in far if p[0] // 2 % 2 == 1]
         touched = {b for p in crossing for b in p}
         targets = {p[1] for p in crossing}
-        first = crossing + [p for p in near if p[0] not in touched and p[1] not in targets]
-        second = [p for p in near if p not in first]
-        last = [p for p in far if p not in first]
-        self.pairs = [first, second, last]
+        first = [p for p in crossing if p[0] % 2 == 0]
+        first += [p for p in near if p[0] not in touched and p[1] not in targets]
+        after = [p for p in near if p not in first]
+        third = [p for p in crossing if p[0] % 2 == 1]
+        third += [p for p in after if p[0] in targets and p[0] % 2 == 1]
+        second = [p for p in after if p not in third]
+        last = [p for p in far if p not in first + third]
+        self.pairs = [first, second, third, last]
         self.senders = sorted({p[0] for p in first})
-        busy = {b for p in first for b in p} & {b for p in second for b in p}
+        busy = {b for p in second + third for b in p}
         self.early = [b for b in range(devices) if b not in busy]
-        self.late = sorted({p[1] for p in second})
+        self.late = sorted({p[1] for p in second + third})
+        self.latest = sorted({p[1] for p in third})
         received = {p[1] for pairs in self.pairs for p in pairs}
         self.alone = [b for b in range(devices) if b not in received]
-        self.memory_first = [p[1] for p in crossing if p[1] % 2 == 1]
+        self.memory_third = [p[1] for p in crossing if p[1] % 2 == 1]
 
 
 def among(members):
@@ -340,7 +345,7 @@
 
 
 def read_kernel(plan, turned_ref, own_ref, three_ref, gains_ref, read_ref):
-    @pl.when((lax.axis_index("kv") == 1) & jnp.logical_not(among(plan.memory_first)))
+    @pl.when((lax.axis_index("kv") == 1) & jnp.logical_not(among(plan.memory_third)))
     def _():
         read_into(read_ref, [three_ref], turned_ref, own_ref, gains_ref)
 
@@ -400,31 +405,54 @@
         for g, state in enumerate(memory_states([one_ref, three_ref], first)):
             state_ref[part_of(g, HEAD_DIM), :] = state
 
-    @pl.when((kv == 1) & among(plan.memory_first))
-    def _():
-        read_into(read_ref, [one_ref, three_ref], turned_ref, own_ref, gains_ref)
-
 
 def late_kernel(
-    plan, turned_ref, own_ref, two_ref, state_ref, summed_ref, stats_ref, gains_ref, read_ref, out_in,
+    plan, turned_ref, own_ref, two_ref, state_ref, stats_ref, gains_ref, read_ref, summed_in,
+    out_in, summed_ref, out_ref, held, sems,
+):
+    kv = lax.axis_index("kv")
+    latest = among(plan.latest)
+    late = among(plan.late) & jnp.logical_not(latest)
+
+    @pl.when((kv == 1) & late)
+    def _():
+        attend_and_store(
+            turned_ref, own_ref, two_ref, stats_ref, summed_ref, read_ref, out_ref, held, sems
+        )
+
+    @pl.when((kv == 0) & late)
+    def _():
+        first, same = first_document(block_docs(own_ref))
+        added = memory_states([two_ref], first)
+        states = [state_ref[part_of(g, HEAD_DIM), :] + added[g] for g in range(KV_HEADS)]
+        read_and_store(states, turned_ref, gains_ref, same, summed_ref, out_ref, held, sems)
+
+    @pl.when((kv == 1) & latest)
+    def _():
+        first, same = first_document(block_docs(own_ref))
+        attend = attend_before(turned_ref, two_ref, stats_ref, summed_ref, first, same)
+        for g in range(KV_HEADS):
+            summed_ref[part_of(g, HEAD_DIM), :] = attend(g)
+
+
+def latest_kernel(
+    plan, turned_ref, own_ref, three_ref, state_ref, gains_ref, summed_ref, out_in,
     out_ref, held, sems,
 ):
+    latest = among(plan.latest)
     kv = lax.axis_index("kv")
-    late = among(plan.late)
-
-    @pl.when((kv == 1) & late)
-    def _():
-        attend_and_store(
-            turned_ref, own_ref, two_ref, stats_ref, summed_ref, read_ref, out_ref, held, sems
-        )
-
-    @pl.when((kv == 0) & late)
+
+    @pl.when((kv == 1) & latest)
     def _():
         first, same = first_document(block_docs(own_ref))
-        states = [
-            state_ref[part_of(g, HEAD_DIM), :] + state
-            for g, state in enumerate(memory_states([two_ref], first))
-        ]
+        states = memory_states([three_ref], first)
+        read_and_store(states, turned_ref, gains_ref, same, summed_ref, out_ref, held, sems)
+
+    @pl.when((kv == 0) & latest)
+    def _():
+        first, same = first_document(block_docs(own_ref))
+        added = memory_states([three_ref], first)
+        states = [state_ref[part_of(g, HEAD_DIM), :] + added[g] for g in range(KV_HEADS)]
         read_and_store(states, turned_ref, gains_ref, same, summed_ref, out_ref, held, sems)
 
 
@@ -486,7 +514,8 @@
         cost_estimate=estimate(1.0),
     )(gain, packed, keys, values, docs, in_hbm(queries), beta)
     two = send(own, plan.pairs[1])
-    three = send(short, plan.pairs[2])
+    three = send(own, plan.pairs[2])
+    four = send(short, plan.pairs[3])
     out_shape = jax.ShapeDtypeStruct((rows, HEADS * HEAD_DIM), jnp.float32)
     store_scratch = [
         pltpu.VMEM((rows, HEADS * HEAD_DIM), jnp.float32),
@@ -509,7 +538,7 @@
         in_specs=[vmem] * 4,
         out_specs=vmem,
         compiler_params=params,
-    )(turned, own, three, gains)
+    )(turned, own, four, gains)
     read, state, out = pl.pallas_call(
         functools.partial(early_kernel, plan),
         out_shape=[gains_shape, state_shape, out_shape],
@@ -518,16 +547,25 @@
         scratch_shapes=store_scratch,
         input_output_aliases={7: 0, 8: 2},
         compiler_params=params,
-    )(turned, own, one, three, stats, gains, summed, read, out)
+    )(turned, own, one, four, stats, gains, summed, read, out)
+    summed, out = pl.pallas_call(
+        functools.partial(late_kernel, plan),
+        out_shape=[group_shape, out_shape],
+        in_specs=[vmem] * 8 + [hbm],
+        out_specs=[vmem, hbm],
+        scratch_shapes=store_scratch,
+        input_output_aliases={7: 0, 8: 1},
+        compiler_params=params,
+    )(turned, own, two, state, stats, gains, read, summed, out)
     return pl.pallas_call(
-        functools.partial(late_kernel, plan),
+        functools.partial(latest_kernel, plan),
         out_shape=out_shape,
-        in_specs=[vmem] * 8 + [hbm],
+        in_specs=[vmem] * 6 + [hbm],
         out_specs=hbm,
         scratch_shapes=store_scratch,
-        input_output_aliases={8: 0},
+        input_output_aliases={6: 0},
         compiler_params=params,
-    )(turned, own, two, state, summed, stats, gains, read, out)
+    )(turned, own, three, state, gains, summed, out)
 
 
 def carried_in(part, axis, combine, identity):

time: 14 us -> 14.6 us (1.043)
  the two profiles are of different devices: /device:TPU:27 before, /device:TPU:1 now
where the time goes in v22:
time: 14.6 us; the launch traced here: 14.4 us
  starting transfers between devices  7.15 us (49%)
  Pallas kernels  5.1 us (35%)
  waiting for transfers between devices  1.94 us (13%)
  between operations  0.15 us (1%)
    ppermute x4, starting transfers between devices, send(): return lax.ppermute(payload, ('seq', 'kv'), pairs)  7.15 us
    pallas_call x1, Pallas kernels, near_device(): pl.pallas_call(functools.partial(own_kernel, plan), out_shape=results + [...  2.09 us
    ppermute x4, waiting for transfers between devices, send(): return lax.ppermute(payload, ('seq', 'kv'), pairs)  1.94 us
    pallas_call x1, Pallas kernels, near_device(): pl.pallas_call(functools.partial(early_kernel, plan), out_shape=[gains_sh...  1.77 us
    pallas_call x1, Pallas kernels, near_device(): pl.pallas_call(functools.partial(pack_kernel, plan), out_shape=block_shap...  1.02 us
  transfers between devices with their start and end apart: 4, of which 1 were waited for; matrix products, arithmetic and copies ran while one was open for 0% of the time, Pallas kernels for 28%

profile of v22, /device:TPU:1, one launch (start us, length us, event | category | flops | bytes accessed | tf_op | source)
XLA Modules:
  0.0 14.4 jit_solution(16562253862998817382)
XLA Ops:
  0.0 0.0 copy-start.1
  0.0 0.0 copy-start.2
  0.0 0.0 copy-start.3
  0.0 1.0 %shard_map.64.packed_ref = bf16[1040,128]{1,0:T(8,128)(2,1)S(1)} custom-call(bf16[128,512]{1,0:T(8,128)(2,1)} %key_ref.3, bf16[128,512]{1,0:T(8,128)(2,1)} %value_ref.3, s32[1,128]{1,0:T(1,128)} %bitcast.4), custom_call_target="tpu_custom_call" | custom-call | flops 13421772 | bytes 419430 | tf_op jit(solution)/shard_map/pallas_call | solution.py:493
  1.0 0.0 copy-start.4
  1.1 3.7 %collective-permute-start.1 = (bf16[1040,128]{1,0:T(8,128)(2,1)S(1)}, bf16[1040,128]{1,0:T(8,128)(2,1)S(1)}, u32[]{:S(2)}, u32[]{:S(2)}) collective-permute-start(bf16[1040,128]{1,0:T(8,128)(2,1)S(1)} %shard_map.64.packed_ref), channel_id=1, source_target_pairs={{8,16},{0,4},{4,8},{24,28},{9,17},{1,5},{5,9},{25,29},{10,18},{2,6... | collective-permute-start | bytes 798728 | tf_op jit(solution)/shard_map/ppermute | solution.py:480
  4.8 0.0 copy-done.1
  4.8 0.0 copy-done.2
  4.8 0.0 copy-done.3
  4.8 0.0 copy-done.4
  4.8 0.0 copy-start
  4.9 0.1 shard_map.65
  4.9 1.4 %collective-permute-start.3 = (bf16[1040,128]{1,0:T(8,128)(2,1)S(1)}, bf16[1040,128]{1,0:T(8,128)(2,1)S(1)}, u32[]{:S(2)}, u32[]{:S(2)}) collective-permute-start(bf16[1040,128]{1,0:T(8,128)(2,1)S(1)} %get-tuple-element.20.own_ref), channel_id=1, source_target_pairs={{8,12},{12,16},{16,20},{9,13},{13,17},{17,21},{10,14},{14,18},{18,... | collective-permute-start | bytes 798728 | tf_op jit(solution)/shard_map/ppermute | solution.py:480
  6.4 0.7 %collective-permute-start = (bf16[1040,128]{1,0:T(8,128)(2,1)S(1)}, bf16[1040,128]{1,0:T(8,128)(2,1)S(1)}, u32[]{:S(2)}, u32[]{:S(2)}) collective-permute-start(bf16[1040,128]{1,0:T(8,128)(2,1)S(1)} %get-tuple-element.20.own_ref), channel_id=1, source_target_pairs={{12,20},{20,24},{13,21},{21,25},{14,22},{22,26},{15,23},{23,27}} | collective-permute-start | bytes 798728 | tf_op jit(solution)/shard_map/ppermute | solution.py:480
  7.1 1.3 %collective-permute-start.2 = (bf16[1024,128]{1,0:T(8,128)(2,1)S(1)}, bf16[1024,128]{1,0:T(8,128)(2,1)S(1)}, u32[]{:S(2)}, u32[]{:S(2)}) collective-permute-start(bf16[1024,128]{1,0:T(8,128)(2,1)S(1)} %get-tuple-element.25), channel_id=1, source_target_pairs={{0,8},{4,12},{16,24},{20,28},{1,9},{5,13},{17,25},{21,29},{2,10},{... | collective-permute-start | bytes 786440 | tf_op jit(solution)/shard_map/ppermute | solution.py:480
  8.4 0.0 copy-done
  8.4 2.1 %shard_map.66 = (f32[512,512]{1,0:T(8,128)S(1)}, f32[16,512]{1,0:T(8,128)S(1)}, f32[2048,128]{1,0:T(8,128)S(1)}, f32[128,2048]{1,0:T(8,128)}, bf16[512,512]{1,0:T(8,128)(2,1)S(1)}) custom-call(bf16[128,2048]{1,0:T(8,128)(2,1)S(1)} %copy-done, f32[16,128]{1,0:T(8,128)S(1)} %bitcast.3, ...), custom_call_target="tpu_custom_call", output_to_operand_aliasing={{0}: (4, {}), {1}: (5, {}), {2}: (6, {})} | custom-call | flops 134217728 | bytes 4194304 | tf_op jit(solution)/shard_map/pallas_call | solution.py:525
  10.5 1.9 %collective-permute-done.2.three_ref = bf16[1024,128]{1,0:T(8,128)(2,1)S(1)} collective-permute-done((bf16[1024,128]{1,0:T(8,128)(2,1)S(1)}, bf16[1024,128]{1,0:T(8,128)(2,1)S(1)}, u32[]{:S(2)}, u32[]{:S(2)}) %collective-permute-start.2) | collective-permute-done | bytes 262176 | tf_op jit(solution)/shard_map/ppermute | solution.py:480
  12.4 0.0 collective-permute-done.1.one_ref
  12.4 1.8 %shard_map.68 = (f32[2048,128]{1,0:T(8,128)S(1)}, f32[512,128]{1,0:T(8,128)S(1)}, f32[128,2048]{1,0:T(8,128)}) custom-call(bf16[512,512]{1,0:T(8,128)(2,1)S(1)} %get-tuple-element.24.turned_ref, bf16[1040,128]{1,0:T(8,128)(2,1)S(1)} %get-tuple-element.20.own_ref, ...), custom_call_target="tpu_custom_call", output_to_operand_aliasing={{0}: (7, {}), {2}: (8, {})} | custom-call | tf_op jit(solution)/shard_map/pallas_call | solution.py:542
  14.2 0.0 collective-permute-done.3.two_ref
  14.2 0.1 shard_map.69
  14.3 0.0 collective-permute-done.three_ref
  14.3 0.1 shard_map.70
  (1 shorter events, 0.0 us)
Async XLA Ops:
  0.0 4.8 %copy-start.1 = (bf16[128,512]{1,0:T(8,128)(2,1)S(1)}, bf16[128,512]{1,0:T(8,128)(2,1)}, u32[]{:S(2)}) copy-start(bf16[128,512]{1,0:T(8,128)(2,1)} %key_ref.3) | copy-start | bytes 393220
  0.0 4.8 %copy-start.2 = (bf16[128,512]{1,0:T(8,128)(2,1)S(1)}, bf16[128,512]{1,0:T(8,128)(2,1)}, u32[]{:S(2)}) copy-start(bf16[128,512]{1,0:T(8,128)(2,1)} %value_ref.3) | copy-start | bytes 393220
  0.0 4.8 %copy-start.3 = (f32[2048]{0:T(1024)S(1)}, f32[2048]{0:T(1024)}, u32[]{:S(2)}) copy-start(f32[2048]{0:T(1024)} %param.11) | copy-start | bytes 24580
  1.0 3.8 %copy-start.4 = (s32[128]{0:T(128)S(1)}, s32[128]{0:T(128)}, u32[]{:S(2)}) copy-start(s32[128]{0:T(128)} %param.9) | copy-start | bytes 1540
  1.1 11.4 %collective-permute-start.1 = (bf16[1040,128]{1,0:T(8,128)(2,1)S(1)}, bf16[1040,128]{1,0:T(8,128)(2,1)S(1)}, u32[]{:S(2)}, u32[]{:S(2)}) collective-permute-start(bf16[1040,128]{1,0:T(8,128)(2,1)S(1)} %shard_map.64.packed_ref), channel_id=1, source_target_pairs={{8,16},{0,4},{4,8},{24,28},{9,17},{1,5},{5,9},{25,29},{10,18},{2,6... | collective-permute-start | bytes 798728 | tf_op jit(solution)/shard_map/ppermute | solution.py:480
  4.8 3.5 %copy-start = (bf16[128,2048]{1,0:T(8,128)(2,1)S(1)}, bf16[128,2048]{1,0:T(8,128)(2,1)}, u32[]{:S(2)}) copy-start(bf16[128,2048]{1,0:T(8,128)(2,1)} %q_ref.1) | copy-start | bytes 1572868
  4.9 9.3 %collective-permute-start.3 = (bf16[1040,128]{1,0:T(8,128)(2,1)S(1)}, bf16[1040,128]{1,0:T(8,128)(2,1)S(1)}, u32[]{:S(2)}, u32[]{:S(2)}) collective-permute-start(bf16[1040,128]{1,0:T(8,128)(2,1)S(1)} %get-tuple-element.20.own_ref), channel_id=1, source_target_pairs={{8,12},{12,16},{16,20},{9,13},{13,17},{17,21},{10,14},{14,18},{18,... | collective-permute-start | bytes 798728 | tf_op jit(solution)/shard_map/ppermute | solution.py:480
  6.4 7.9 %collective-permute-start = (bf16[1040,128]{1,0:T(8,128)(2,1)S(1)}, bf16[1040,128]{1,0:T(8,128)(2,1)S(1)}, u32[]{:S(2)}, u32[]{:S(2)}) collective-permute-start(bf16[1040,128]{1,0:T(8,128)(2,1)S(1)} %get-tuple-element.20.own_ref), channel_id=1, source_target_pairs={{12,20},{20,24},{13,21},{21,25},{14,22},{22,26},{15,23},{23,27}} | collective-permute-start | bytes 798728 | tf_op jit(solution)/shard_map/ppermute | solution.py:480
  7.1 5.3 %collective-permute-start.2 = (bf16[1024,128]{1,0:T(8,128)(2,1)S(1)}, bf16[1024,128]{1,0:T(8,128)(2,1)S(1)}, u32[]{:S(2)}, u32[]{:S(2)}) collective-permute-start(bf16[1024,128]{1,0:T(8,128)(2,1)S(1)} %get-tuple-element.25), channel_id=1, source_target_pairs={{0,8},{4,12},{16,24},{20,28},{1,9},{5,13},{17,25},{21,29},{2,10},{... | collective-permute-start | bytes 786440 | tf_op jit(solution)/shard_map/ppermute | solution.py:480

commit v23 on v21

--- a/solution.py
+++ b/solution.py
@@ -60,27 +60,13 @@
     return first, docs == first
 
 
-def load_block(key_ref, value_ref, doc_ref, out_ref, doc_scratch, sems):
-    rows = key_ref.shape[0]
-    doc_copy = pltpu.make_async_copy(doc_ref, doc_scratch, sems.at[0])
-    doc_copy.start()
-    copies = []
-    for g in range(2 * KV_HEADS):
-        source = key_ref if g < KV_HEADS else value_ref
-        copy = pltpu.make_async_copy(
-            source.at[:, part_of(g % KV_HEADS, HEAD_DIM)],
-            out_ref.at[part_of(g, rows), :],
-            sems.at[1 + g],
-        )
-        copy.start()
-        copies.append(copy)
-    doc_copy.wait()
-    start = 2 * KV_HEADS * rows
-    docs = doc_scratch[...].astype(jnp.float32)
-    docs = jnp.broadcast_to(docs, (out_ref.shape[0] - start, rows))
-    out_ref[start:, :] = docs.astype(jnp.bfloat16)
-    for copy in copies:
-        copy.wait()
+def spread_heads(key_rows, value_rows, doc_row, out_ref):
+    for g in range(KV_HEADS):
+        out_ref[part_of(g, HEAD_DIM), :] = key_rows[:, part_of(g, HEAD_DIM)]
+    for g in range(KV_HEADS):
+        out_ref[part_of(KV_HEADS + g, HEAD_DIM), :] = value_rows[:, part_of(g, HEAD_DIM)]
+    docs = jnp.broadcast_to(doc_row[...].astype(jnp.float32), (EXTRA, HEAD_DIM))
+    out_ref[2 * KV_HEADS * HEAD_DIM :, :] = docs.astype(jnp.bfloat16)
 
 
 def block_keys(ref, g):
@@ -122,10 +108,18 @@
     return functools.reduce(jnp.logical_or, [block == b for b in members])
 
 
-def pack_kernel(plan, key_ref, value_ref, doc_ref, out_ref, doc_scratch, sems):
+def pack_kernel(
+    plan, key_ref, value_ref, doc_ref, out_ref, key_scratch, value_scratch, doc_scratch, sems
+):
     @pl.when(among(plan.senders))
     def _():
-        load_block(key_ref, value_ref, doc_ref, out_ref, doc_scratch, sems)
+        pairs = ((key_ref, key_scratch), (value_ref, value_scratch), (doc_ref, doc_scratch))
+        copies = [pltpu.make_async_copy(a, b, sems.at[i]) for i, (a, b) in enumerate(pairs)]
+        for copy in copies:
+            copy.start()
+        for copy in copies:
+            copy.wait()
+        spread_heads(key_scratch, value_scratch, doc_scratch, out_ref)
 
 
 def attend_own(q_ref, block_ref, g, bias):
@@ -187,13 +181,7 @@
 
     @pl.when(jnp.logical_not(sender))
     def _():
-        for g in range(KV_HEADS):
-            cols = part_of(g, HEAD_DIM)
-            own_ref[part_of(g, HEAD_DIM), :] = key_ref[:, cols]
-            own_ref[part_of(KV_HEADS + g, HEAD_DIM), :] = value_ref[:, cols]
-        start = 2 * KV_HEADS * HEAD_DIM
-        docs = jnp.broadcast_to(doc_ref[...].astype(jnp.float32), (EXTRA, HEAD_DIM))
-        own_ref[start:, :] = docs.astype(jnp.bfloat16)
+        spread_heads(key_ref, value_ref, doc_ref, own_ref)
 
     short_ref[...] = own_ref[0 : short_ref.shape[0], :]
     line = lax.broadcasted_iota(jnp.int32, (EXTRA, HEAD_DIM), 0)
@@ -457,9 +445,7 @@
     stats_shape = jax.ShapeDtypeStruct((4 * KV_HEADS, wide), jnp.float32)
     state_shape = jax.ShapeDtypeStruct((KV_HEADS * HEAD_DIM, HEAD_DIM), jnp.float32)
     results = [group_shape, stats_shape, gains_shape]
-    doc_scratch = pltpu.VMEM((1, rows), jnp.int32)
     beta_scratch = pltpu.SMEM((HEADS,), jnp.float32)
-    sems = pltpu.SemaphoreType.DMA((2 * KV_HEADS + 1,))
     block = (in_hbm(keys), in_hbm(values), in_hbm(docs))
     beta = in_hbm(beta)
     packed = pl.pallas_call(
@@ -467,7 +453,12 @@
         out_shape=block_shape,
         in_specs=[hbm] * 3,
         out_specs=vmem,
-        scratch_shapes=[doc_scratch, sems],
+        scratch_shapes=[
+            pltpu.VMEM(keys.shape, keys.dtype),
+            pltpu.VMEM(values.shape, values.dtype),
+            pltpu.VMEM((1, rows), jnp.int32),
+            pltpu.SemaphoreType.DMA((3,)),
+        ],
         compiler_params=params,
         cost_estimate=estimate(0.1),
     )(*block)

time: 14 us -> 14.1 us (level)
  no operation moved by 1% of the time
where the time goes in v23:
time: 14.1 us; the launch traced here: 13.9 us
  starting transfers between devices  6.14 us (44%)
  Pallas kernels  5.92 us (42%)
  waiting for transfers between devices  1.71 us (12%)
    ppermute x3, starting transfers between devices, send(): return lax.ppermute(payload, ('seq', 'kv'), pairs)  6.14 us
    pallas_call x1, Pallas kernels, near_device(): pl.pallas_call(functools.partial(own_kernel, plan), out_shape=results + [...  2.1 us
    ppermute x3, waiting for transfers between devices, send(): return lax.ppermute(payload, ('seq', 'kv'), pairs)  1.71 us
    pallas_call x1, Pallas kernels, near_device(): pl.pallas_call(functools.partial(late_kernel, plan), out_shape=out_shape,...  1.65 us
    pallas_call x1, Pallas kernels, near_device(): pl.pallas_call(functools.partial(pack_kernel, plan), out_shape=block_shap...  1.1 us
    pallas_call x1, Pallas kernels, near_device(): pl.pallas_call(functools.partial(read_kernel, plan), out_shape=gains_shap...  0.91 us
  transfers between devices with their start and end apart: 3, of which 1 were waited for; matrix products, arithmetic and copies ran while one was open for 0% of the time, Pallas kernels for 23%

profile of v23, /device:TPU:27, one launch (start us, length us, event | category | flops | bytes accessed | tf_op | source)
XLA Modules:
  0.0 13.9 jit_solution(580621025647672413)
XLA Ops:
  0.0 0.0 copy-start.1
  0.0 0.0 copy-start.2
  0.0 0.0 copy-start.3
  0.0 1.1 %shard_map.64.packed_ref = bf16[1040,128]{1,0:T(8,128)(2,1)S(1)} custom-call(bf16[128,512]{1,0:T(8,128)(2,1)} %key_ref.3, bf16[128,512]{1,0:T(8,128)(2,1)} %value_ref.3, s32[1,128]{1,0:T(1,128)} %bitcast.4), custom_call_target="tpu_custom_call" | custom-call | flops 13421772 | bytes 419430 | tf_op jit(solution)/shard_map/pallas_call | solution.py:451
  1.1 0.0 copy-start.4
  1.1 2.8 %collective-permute-start.1 = (bf16[1040,128]{1,0:T(8,128)(2,1)S(1)}, bf16[1040,128]{1,0:T(8,128)(2,1)S(1)}, u32[]{:S(2)}, u32[]{:S(2)}) collective-permute-start(bf16[1040,128]{1,0:T(8,128)(2,1)S(1)} %shard_map.64.packed_ref), channel_id=1, source_target_pairs={{8,16},{12,20},{0,4},{4,8},{24,28},{9,17},{13,21},{1,5},{5,9},{25,... | collective-permute-start | bytes 798728 | tf_op jit(solution)/shard_map/ppermute | solution.py:440
  3.9 0.0 copy-done.1
  3.9 0.0 copy-done.2
  4.0 0.0 copy-done.3
  4.0 0.0 copy-done.4
  4.0 0.0 copy-start
  4.0 0.1 shard_map.65
  4.1 2.1 %collective-permute-start = (bf16[1040,128]{1,0:T(8,128)(2,1)S(1)}, bf16[1040,128]{1,0:T(8,128)(2,1)S(1)}, u32[]{:S(2)}, u32[]{:S(2)}) collective-permute-start(bf16[1040,128]{1,0:T(8,128)(2,1)S(1)} %get-tuple-element.18.own_ref), channel_id=1, source_target_pairs={{8,12},{12,16},{16,20},{20,24},{9,13},{13,17},{17,21},{21,25},{10,... | collective-permute-start | bytes 798728 | tf_op jit(solution)/shard_map/ppermute | solution.py:440
  6.1 1.3 %collective-permute-start.2 = (bf16[1024,128]{1,0:T(8,128)(2,1)S(1)}, bf16[1024,128]{1,0:T(8,128)(2,1)S(1)}, u32[]{:S(2)}, u32[]{:S(2)}) collective-permute-start(bf16[1024,128]{1,0:T(8,128)(2,1)S(1)} %get-tuple-element.23), channel_id=1, source_target_pairs={{0,8},{4,12},{16,24},{20,28},{1,9},{5,13},{17,25},{21,29},{2,10},{... | collective-permute-start | bytes 786440 | tf_op jit(solution)/shard_map/ppermute | solution.py:440
  7.4 0.0 copy-done
  7.4 2.1 %shard_map.66 = (f32[512,512]{1,0:T(8,128)S(1)}, f32[16,512]{1,0:T(8,128)S(1)}, f32[2048,128]{1,0:T(8,128)S(1)}, f32[128,2048]{1,0:T(8,128)}, bf16[512,512]{1,0:T(8,128)(2,1)S(1)}) custom-call(bf16[128,2048]{1,0:T(8,128)(2,1)S(1)} %copy-done, f32[16,128]{1,0:T(8,128)S(1)} %bitcast.3, ...), custom_call_target="tpu_custom_call", output_to_operand_aliasing={{0}: (4, {}), {1}: (5, {}), {2}: (6, {})} | custom-call | flops 134217728 | bytes 4194304 | tf_op jit(solution)/shard_map/pallas_call | solution.py:487
  9.6 0.0 collective-permute-done.2.three_ref
  9.6 0.9 %shard_map.67.read_in = f32[2048,128]{1,0:T(8,128)S(1)} custom-call(bf16[512,512]{1,0:T(8,128)(2,1)S(1)} %get-tuple-element.22.turned_ref, bf16[1040,128]{1,0:T(8,128)(2,1)S(1)} %get-tuple-element.18.own_ref, bf16[1024,128]{1,0:T(8,128)(2,1)S(1)} %collective-permute-done.2.three_ref, f32[2048,128]{1,0:T(8,128)S(1)} %get-tuple-element.25.gains_ref), custom_call_target="tpu_custom_call" | custom-call | tf_op jit(solution)/shard_map/pallas_call | solution.py:497
  10.5 0.0 collective-permute-done.1.one_ref
  10.5 0.1 shard_map.68
  10.6 1.7 %collective-permute-done.two_ref = bf16[1040,128]{1,0:T(8,128)(2,1)S(1)} collective-permute-done((bf16[1040,128]{1,0:T(8,128)(2,1)S(1)}, bf16[1040,128]{1,0:T(8,128)(2,1)S(1)}, u32[]{:S(2)}, u32[]{:S(2)}) %collective-permute-start) | collective-permute-done | bytes 266272 | tf_op jit(solution)/shard_map/ppermute | solution.py:440
  12.3 1.7 %shard_map.69 = f32[128,2048]{1,0:T(8,128)} custom-call(bf16[512,512]{1,0:T(8,128)(2,1)S(1)} %get-tuple-element.22.turned_ref, bf16[1040,128]{1,0:T(8,128)(2,1)S(1)} %get-tuple-element.18.own_ref, bf16[1040,128]{1,0:T(8,128)(2,1)S(1)} %collective-permute-done.two_ref, f32[512,128]{1,0:T(8,128)S(1)} %get-tuple-element.28.state_ref, ...), custom_call_target="tpu_custom_call", output_to_operand_aliasing={{}: (8, {})} | custom-call | tf_op jit(solution)/shard_map/pallas_call | solution.py:513
Async XLA Ops:
  0.0 3.9 %copy-start.1 = (bf16[128,512]{1,0:T(8,128)(2,1)S(1)}, bf16[128,512]{1,0:T(8,128)(2,1)}, u32[]{:S(2)}) copy-start(bf16[128,512]{1,0:T(8,128)(2,1)} %key_ref.3) | copy-start | bytes 393220
  0.0 3.9 %copy-start.2 = (bf16[128,512]{1,0:T(8,128)(2,1)S(1)}, bf16[128,512]{1,0:T(8,128)(2,1)}, u32[]{:S(2)}) copy-start(bf16[128,512]{1,0:T(8,128)(2,1)} %value_ref.3) | copy-start | bytes 393220
  0.0 4.0 %copy-start.3 = (f32[2048]{0:T(1024)S(1)}, f32[2048]{0:T(1024)}, u32[]{:S(2)}) copy-start(f32[2048]{0:T(1024)} %param.11) | copy-start | bytes 24580
  1.1 2.9 %copy-start.4 = (s32[128]{0:T(128)S(1)}, s32[128]{0:T(128)}, u32[]{:S(2)}) copy-start(s32[128]{0:T(128)} %param.9) | copy-start | bytes 1540
  1.1 9.4 %collective-permute-start.1 = (bf16[1040,128]{1,0:T(8,128)(2,1)S(1)}, bf16[1040,128]{1,0:T(8,128)(2,1)S(1)}, u32[]{:S(2)}, u32[]{:S(2)}) collective-permute-start(bf16[1040,128]{1,0:T(8,128)(2,1)S(1)} %shard_map.64.packed_ref), channel_id=1, source_target_pairs={{8,16},{12,20},{0,4},{4,8},{24,28},{9,17},{13,21},{1,5},{5,9},{25,... | collective-permute-start | bytes 798728 | tf_op jit(solution)/shard_map/ppermute | solution.py:440
  4.0 3.5 %copy-start = (bf16[128,2048]{1,0:T(8,128)(2,1)S(1)}, bf16[128,2048]{1,0:T(8,128)(2,1)}, u32[]{:S(2)}) copy-start(bf16[128,2048]{1,0:T(8,128)(2,1)} %q_ref.1) | copy-start | bytes 1572868
  4.1 8.2 %collective-permute-start = (bf16[1040,128]{1,0:T(8,128)(2,1)S(1)}, bf16[1040,128]{1,0:T(8,128)(2,1)S(1)}, u32[]{:S(2)}, u32[]{:S(2)}) collective-permute-start(bf16[1040,128]{1,0:T(8,128)(2,1)S(1)} %get-tuple-element.18.own_ref), channel_id=1, source_target_pairs={{8,12},{12,16},{16,20},{20,24},{9,13},{13,17},{17,21},{21,25},{10,... | collective-permute-start | bytes 798728 | tf_op jit(solution)/shard_map/ppermute | solution.py:440
  6.1 3.4 %collective-permute-start.2 = (bf16[1024,128]{1,0:T(8,128)(2,1)S(1)}, bf16[1024,128]{1,0:T(8,128)(2,1)S(1)}, u32[]{:S(2)}, u32[]{:S(2)}) collective-permute-start(bf16[1024,128]{1,0:T(8,128)(2,1)S(1)} %get-tuple-element.23), channel_id=1, source_target_pairs={{0,8},{4,12},{16,24},{20,28},{1,9},{5,13},{17,25},{21,29},{2,10},{... | collective-permute-start | bytes 786440 | tf_op jit(solution)/shard_map/ppermute | solution.py:440

commit v24 on v21

--- a/solution.py
+++ b/solution.py
@@ -293,7 +293,7 @@
             ahead[g] = dot(block_keys(one_ref, g), turned_ref[part_of(g, HEAD_DIM), :], NN)
 
     def attend(g):
-        for later in range(3):
+        for later in range(KV_HEADS):
             score(g + later)
         weights, factors, scales = [], [], []
         for i in range(GROUPS):

time: 14 us -> 14.1 us (level)
  no operation moved by 1% of the time
where the time goes in v24:
time: 14.1 us; the launch traced here: 13.9 us
  starting transfers between devices  6.27 us (44%)
  Pallas kernels  5.89 us (42%)
  waiting for transfers between devices  1.61 us (11%)
    ppermute x3, starting transfers between devices, send(): return lax.ppermute(payload, ('seq', 'kv'), pairs)  6.27 us
    pallas_call x1, Pallas kernels, near_device(): pl.pallas_call(functools.partial(own_kernel, plan), out_shape=results + [...  2.09 us
    pallas_call x1, Pallas kernels, near_device(): pl.pallas_call(functools.partial(late_kernel, plan), out_shape=out_shape,...  1.72 us
    ppermute x3, waiting for transfers between devices, send(): return lax.ppermute(payload, ('seq', 'kv'), pairs)  1.61 us
    pallas_call x1, Pallas kernels, near_device(): pl.pallas_call(functools.partial(pack_kernel, plan), out_shape=block_shap...  1.02 us
    pallas_call x1, Pallas kernels, near_device(): pl.pallas_call(functools.partial(read_kernel, plan), out_shape=gains_shap...  0.9 us
  transfers between devices with their start and end apart: 3, of which 1 were waited for; matrix products, arithmetic and copies ran while one was open for 0% of the time, Pallas kernels for 23%

profile of v24, /device:TPU:27, one launch (start us, length us, event | category | flops | bytes accessed | tf_op | source)
XLA Modules:
  0.0 13.9 jit_solution(2493418943699550779)
XLA Ops:
  0.0 0.0 copy-start.1
  0.0 0.0 copy-start.2
  0.0 0.0 copy-start.3
  0.0 1.0 %shard_map.64.packed_ref = bf16[1040,128]{1,0:T(8,128)(2,1)S(1)} custom-call(bf16[128,512]{1,0:T(8,128)(2,1)} %key_ref.3, bf16[128,512]{1,0:T(8,128)(2,1)} %value_ref.3, s32[1,128]{1,0:T(1,128)} %bitcast.4), custom_call_target="tpu_custom_call" | custom-call | flops 13421772 | bytes 419430 | tf_op jit(solution)/shard_map/pallas_call | solution.py:465
  1.0 0.0 copy-start.4
  1.1 2.9 %collective-permute-start.1 = (bf16[1040,128]{1,0:T(8,128)(2,1)S(1)}, bf16[1040,128]{1,0:T(8,128)(2,1)S(1)}, u32[]{:S(2)}, u32[]{:S(2)}) collective-permute-start(bf16[1040,128]{1,0:T(8,128)(2,1)S(1)} %shard_map.64.packed_ref), channel_id=1, source_target_pairs={{8,16},{12,20},{0,4},{4,8},{24,28},{9,17},{13,21},{1,5},{5,9},{25,... | collective-permute-start | bytes 798728 | tf_op jit(solution)/shard_map/ppermute | solution.py:452
  4.0 0.0 copy-done.1
  4.0 0.0 copy-done.2
  4.0 0.0 copy-done.3
  4.0 0.0 copy-done.4
  4.0 0.0 copy-start
  4.0 0.1 shard_map.65
  4.1 2.1 %collective-permute-start = (bf16[1040,128]{1,0:T(8,128)(2,1)S(1)}, bf16[1040,128]{1,0:T(8,128)(2,1)S(1)}, u32[]{:S(2)}, u32[]{:S(2)}) collective-permute-start(bf16[1040,128]{1,0:T(8,128)(2,1)S(1)} %get-tuple-element.18.own_ref), channel_id=1, source_target_pairs={{8,12},{12,16},{16,20},{20,24},{9,13},{13,17},{17,21},{21,25},{10,... | collective-permute-start | bytes 798728 | tf_op jit(solution)/shard_map/ppermute | solution.py:452
  6.2 1.3 %collective-permute-start.2 = (bf16[1024,128]{1,0:T(8,128)(2,1)S(1)}, bf16[1024,128]{1,0:T(8,128)(2,1)S(1)}, u32[]{:S(2)}, u32[]{:S(2)}) collective-permute-start(bf16[1024,128]{1,0:T(8,128)(2,1)S(1)} %get-tuple-element.23), channel_id=1, source_target_pairs={{0,8},{4,12},{16,24},{20,28},{1,9},{5,13},{17,25},{21,29},{2,10},{... | collective-permute-start | bytes 786440 | tf_op jit(solution)/shard_map/ppermute | solution.py:452
  7.5 0.0 copy-done
  7.5 2.1 %shard_map.66 = (f32[512,512]{1,0:T(8,128)S(1)}, f32[16,512]{1,0:T(8,128)S(1)}, f32[2048,128]{1,0:T(8,128)S(1)}, f32[128,2048]{1,0:T(8,128)}, bf16[512,512]{1,0:T(8,128)(2,1)S(1)}) custom-call(bf16[128,2048]{1,0:T(8,128)(2,1)S(1)} %copy-done, f32[16,128]{1,0:T(8,128)S(1)} %bitcast.3, ...), custom_call_target="tpu_custom_call", output_to_operand_aliasing={{0}: (4, {}), {1}: (5, {}), {2}: (6, {})} | custom-call | flops 134217728 | bytes 4194304 | tf_op jit(solution)/shard_map/pallas_call | solution.py:496
  9.6 0.0 collective-permute-done.2.three_ref
  9.6 0.9 %shard_map.67.read_in = f32[2048,128]{1,0:T(8,128)S(1)} custom-call(bf16[512,512]{1,0:T(8,128)(2,1)S(1)} %get-tuple-element.22.turned_ref, bf16[1040,128]{1,0:T(8,128)(2,1)S(1)} %get-tuple-element.18.own_ref, bf16[1024,128]{1,0:T(8,128)(2,1)S(1)} %collective-permute-done.2.three_ref, f32[2048,128]{1,0:T(8,128)S(1)} %get-tuple-element.25.gains_ref), custom_call_target="tpu_custom_call" | custom-call | tf_op jit(solution)/shard_map/pallas_call | solution.py:506
  10.5 0.0 collective-permute-done.1.one_ref
  10.5 0.1 shard_map.68
  10.6 1.6 %collective-permute-done.two_ref = bf16[1040,128]{1,0:T(8,128)(2,1)S(1)} collective-permute-done((bf16[1040,128]{1,0:T(8,128)(2,1)S(1)}, bf16[1040,128]{1,0:T(8,128)(2,1)S(1)}, u32[]{:S(2)}, u32[]{:S(2)}) %collective-permute-start) | collective-permute-done | bytes 266272 | tf_op jit(solution)/shard_map/ppermute | solution.py:452
  12.2 1.7 %shard_map.69 = f32[128,2048]{1,0:T(8,128)} custom-call(bf16[512,512]{1,0:T(8,128)(2,1)S(1)} %get-tuple-element.22.turned_ref, bf16[1040,128]{1,0:T(8,128)(2,1)S(1)} %get-tuple-element.18.own_ref, bf16[1040,128]{1,0:T(8,128)(2,1)S(1)} %collective-permute-done.two_ref, f32[512,128]{1,0:T(8,128)S(1)} %get-tuple-element.28.state_ref, ...), custom_call_target="tpu_custom_call", output_to_operand_aliasing={{}: (8, {})} | custom-call | tf_op jit(solution)/shard_map/pallas_call | solution.py:522
Async XLA Ops:
  0.0 4.0 %copy-start.1 = (bf16[128,512]{1,0:T(8,128)(2,1)S(1)}, bf16[128,512]{1,0:T(8,128)(2,1)}, u32[]{:S(2)}) copy-start(bf16[128,512]{1,0:T(8,128)(2,1)} %key_ref.3) | copy-start | bytes 393220
  0.0 4.0 %copy-start.2 = (bf16[128,512]{1,0:T(8,128)(2,1)S(1)}, bf16[128,512]{1,0:T(8,128)(2,1)}, u32[]{:S(2)}) copy-start(bf16[128,512]{1,0:T(8,128)(2,1)} %value_ref.3) | copy-start | bytes 393220
  0.0 4.0 %copy-start.3 = (f32[2048]{0:T(1024)S(1)}, f32[2048]{0:T(1024)}, u32[]{:S(2)}) copy-start(f32[2048]{0:T(1024)} %param.11) | copy-start | bytes 24580
  1.0 3.0 %copy-start.4 = (s32[128]{0:T(128)S(1)}, s32[128]{0:T(128)}, u32[]{:S(2)}) copy-start(s32[128]{0:T(128)} %param.9) | copy-start | bytes 1540
  1.1 9.5 %collective-permute-start.1 = (bf16[1040,128]{1,0:T(8,128)(2,1)S(1)}, bf16[1040,128]{1,0:T(8,128)(2,1)S(1)}, u32[]{:S(2)}, u32[]{:S(2)}) collective-permute-start(bf16[1040,128]{1,0:T(8,128)(2,1)S(1)} %shard_map.64.packed_ref), channel_id=1, source_target_pairs={{8,16},{12,20},{0,4},{4,8},{24,28},{9,17},{13,21},{1,5},{5,9},{25,... | collective-permute-start | bytes 798728 | tf_op jit(solution)/shard_map/ppermute | solution.py:452
  4.0 3.5 %copy-start = (bf16[128,2048]{1,0:T(8,128)(2,1)S(1)}, bf16[128,2048]{1,0:T(8,128)(2,1)}, u32[]{:S(2)}) copy-start(bf16[128,2048]{1,0:T(8,128)(2,1)} %q_ref.1) | copy-start | bytes 1572868
  4.1 8.1 %collective-permute-start = (bf16[1040,128]{1,0:T(8,128)(2,1)S(1)}, bf16[1040,128]{1,0:T(8,128)(2,1)S(1)}, u32[]{:S(2)}, u32[]{:S(2)}) collective-permute-start(bf16[1040,128]{1,0:T(8,128)(2,1)S(1)} %get-tuple-element.18.own_ref), channel_id=1, source_target_pairs={{8,12},{12,16},{16,20},{20,24},{9,13},{13,17},{17,21},{21,25},{10,... | collective-permute-start | bytes 798728 | tf_op jit(solution)/shard_map/ppermute | solution.py:452
  6.2 3.4 %collective-permute-start.2 = (bf16[1024,128]{1,0:T(8,128)(2,1)S(1)}, bf16[1024,128]{1,0:T(8,128)(2,1)S(1)}, u32[]{:S(2)}, u32[]{:S(2)}) collective-permute-start(bf16[1024,128]{1,0:T(8,128)(2,1)S(1)} %get-tuple-element.23), channel_id=1, source_target_pairs={{0,8},{4,12},{16,24},{20,28},{1,9},{5,13},{17,25},{21,29},{2,10},{... | collective-permute-start | bytes 786440 | tf_op jit(solution)/shard_map/ppermute | solution.py:452

commit v25 on v19

--- a/solution.py
+++ b/solution.py
@@ -168,17 +168,15 @@
 
 
 def settle_kernel(
-    plan, gain_ref, packed_ref, query_ref, key_ref, value_ref, doc_ref, beta_ref,
+    plan, gain_ref, packed_ref, q_ref, key_ref, value_ref, doc_ref, beta_ref,
     own_ref, short_ref, summed_ref, stats_ref, gains_ref,
-    q_scratch, beta_scratch, doc_scratch, sems, early_sems,
+    beta_scratch, doc_scratch, sems, early_sem,
 ):
     sender, early = among(plan.senders), among(plan.early)
-    query_copy = pltpu.make_async_copy(query_ref, q_scratch, early_sems.at[0])
-    beta_copy = pltpu.make_async_copy(beta_ref, beta_scratch, early_sems.at[1])
+    beta_copy = pltpu.make_async_copy(beta_ref, beta_scratch, early_sem)
 
     @pl.when(early)
     def _():
-        query_copy.start()
         beta_copy.start()
 
     @pl.when(sender)
@@ -197,9 +195,8 @@
 
     @pl.when(early)
     def _():
-        query_copy.wait()
         attend_itself(
-            q_scratch, own_ref, gain_ref, beta_scratch, beta_copy,
+            q_ref, own_ref, gain_ref, beta_scratch, beta_copy,
             summed_ref, stats_ref, gains_ref,
         )
 
@@ -469,18 +466,12 @@
     own, short, summed, stats, gains = pl.pallas_call(
         functools.partial(settle_kernel, plan),
         out_shape=[block_shape, short_shape] + results,
-        in_specs=[vmem] * 2 + [hbm] * 5,
+        in_specs=[vmem] * 3 + [hbm] * 4,
         out_specs=[vmem] * 5,
-        scratch_shapes=[
-            pltpu.VMEM(queries.shape, queries.dtype),
-            beta_scratch,
-            doc_scratch,
-            sems,
-            pltpu.SemaphoreType.DMA((2,)),
-        ],
+        scratch_shapes=[beta_scratch, doc_scratch, sems, pltpu.SemaphoreType.DMA],
         compiler_params=params,
         cost_estimate=estimate(1.0),
-    )(gain, packed, in_hbm(queries), *block, beta)
+    )(gain, packed, queries, *block, beta)
     two = send(own, plan.pairs[1])
     three = send(short, plan.pairs[2])
     out_shape = jax.ShapeDtypeStruct((rows, HEADS * HEAD_DIM), jnp.float32)

time: 14 us -> 14.1 us (level)
  no operation moved by 1% of the time
where the time goes in v25:
time: 14.1 us; the launch traced here: 13.8 us
  starting transfers between devices  6.32 us (45%)
  Pallas kernels  5.9 us (42%)
  waiting for transfers between devices  1.52 us (11%)
    ppermute x3, starting transfers between devices, send(): return lax.ppermute(payload, ('seq', 'kv'), pairs)  6.32 us
    pallas_call x1, Pallas kernels, near_device(): pl.pallas_call(functools.partial(own_kernel, plan), out_shape=results + [...  2.1 us
    pallas_call x1, Pallas kernels, near_device(): pl.pallas_call(functools.partial(late_kernel, plan), out_shape=out_shape,...  1.65 us
    ppermute x3, waiting for transfers between devices, send(): return lax.ppermute(payload, ('seq', 'kv'), pairs)  1.52 us
    pallas_call x1, Pallas kernels, near_device(): pl.pallas_call(functools.partial(pack_kernel, plan), out_shape=block_shap...  1.03 us
    pallas_call x1, Pallas kernels, near_device(): pl.pallas_call(functools.partial(read_kernel, plan), out_shape=gains_shap...  0.9 us
  transfers between devices with their start and end apart: 3, of which 1 were waited for; matrix products, arithmetic and copies ran while one was open for 0% of the time, Pallas kernels for 23%

profile of v25, /device:TPU:27, one launch (start us, length us, event | category | flops | bytes accessed | tf_op | source)
XLA Modules:
  0.0 13.8 jit_solution(14646462203232995668)
XLA Ops:
  0.0 0.0 copy-start
  0.0 0.0 copy-start.1
  0.0 1.0 %shard_map.64.packed_ref = bf16[1040,128]{1,0:T(8,128)(2,1)S(1)} custom-call(bf16[128,512]{1,0:T(8,128)(2,1)} %key_ref.3, bf16[128,512]{1,0:T(8,128)(2,1)} %value_ref.3, s32[1,128]{1,0:T(1,128)} %bitcast.4), custom_call_target="tpu_custom_call" | custom-call | flops 13421772 | bytes 419430 | tf_op jit(solution)/shard_map/pallas_call | solution.py:456
  1.0 2.9 %collective-permute-start.1 = (bf16[1040,128]{1,0:T(8,128)(2,1)S(1)}, bf16[1040,128]{1,0:T(8,128)(2,1)S(1)}, u32[]{:S(2)}, u32[]{:S(2)}) collective-permute-start(bf16[1040,128]{1,0:T(8,128)(2,1)S(1)} %shard_map.64.packed_ref), channel_id=1, source_target_pairs={{8,16},{12,20},{0,4},{4,8},{24,28},{9,17},{13,21},{1,5},{5,9},{25,... | collective-permute-start | bytes 798728 | tf_op jit(solution)/shard_map/ppermute | solution.py:443
  4.0 0.0 copy-done
  4.0 0.0 copy-done.1
  4.0 0.2 %shard_map.65 = (bf16[1040,128]{1,0:T(8,128)(2,1)S(1)}, bf16[1024,128]{1,0:T(8,128)(2,1)S(1)}, f32[512,512]{1,0:T(8,128)S(1)}, f32[16,512]{1,0:T(8,128)S(1)}, f32[2048,128]{1,0:T(8,128)S(1)}) custom-call(f32[16,128]{1,0:T(8,128)S(1)} %bitcast.2, bf16[1040,128]{1,0:T(8,128)(2,1)S(1)} %shard_map.64.packed_ref, bf16[128,2048]{1,0:T(8,128)(2,1)S(1)} %copy-done, ...), custom_call_target="tpu_custom_call" | custom-call | flops 134217728 | bytes 4194304 | tf_op jit(solution)/shard_map/pallas_call | solution.py:466
  4.1 2.1 %collective-permute-start = (bf16[1040,128]{1,0:T(8,128)(2,1)S(1)}, bf16[1040,128]{1,0:T(8,128)(2,1)S(1)}, u32[]{:S(2)}, u32[]{:S(2)}) collective-permute-start(bf16[1040,128]{1,0:T(8,128)(2,1)S(1)} %get-tuple-element.18.own_ref), channel_id=1, source_target_pairs={{8,12},{12,16},{16,20},{20,24},{9,13},{13,17},{17,21},{21,25},{10,... | collective-permute-start | bytes 798728 | tf_op jit(solution)/shard_map/ppermute | solution.py:443
  6.3 1.3 %collective-permute-start.2 = (bf16[1024,128]{1,0:T(8,128)(2,1)S(1)}, bf16[1024,128]{1,0:T(8,128)(2,1)S(1)}, u32[]{:S(2)}, u32[]{:S(2)}) collective-permute-start(bf16[1024,128]{1,0:T(8,128)(2,1)S(1)} %get-tuple-element.23), channel_id=1, source_target_pairs={{0,8},{4,12},{16,24},{20,28},{1,9},{5,13},{17,25},{21,29},{2,10},{... | collective-permute-start | bytes 786440 | tf_op jit(solution)/shard_map/ppermute | solution.py:443
  7.6 2.1 %shard_map.66 = (f32[512,512]{1,0:T(8,128)S(1)}, f32[16,512]{1,0:T(8,128)S(1)}, f32[2048,128]{1,0:T(8,128)S(1)}, f32[128,2048]{1,0:T(8,128)}, bf16[512,512]{1,0:T(8,128)(2,1)S(1)}) custom-call(bf16[128,2048]{1,0:T(8,128)(2,1)S(1)} %copy-done, f32[16,128]{1,0:T(8,128)S(1)} %bitcast.3, ...), custom_call_target="tpu_custom_call", output_to_operand_aliasing={{0}: (4, {}), {1}: (5, {}), {2}: (6, {})} | custom-call | flops 134217728 | bytes 4194304 | tf_op jit(solution)/shard_map/pallas_call | solution.py:483
  9.7 0.0 collective-permute-done.2.three_ref
  9.7 0.9 %shard_map.67.read_in = f32[2048,128]{1,0:T(8,128)S(1)} custom-call(bf16[512,512]{1,0:T(8,128)(2,1)S(1)} %get-tuple-element.22.turned_ref, bf16[1040,128]{1,0:T(8,128)(2,1)S(1)} %get-tuple-element.18.own_ref, bf16[1024,128]{1,0:T(8,128)(2,1)S(1)} %collective-permute-done.2.three_ref, f32[2048,128]{1,0:T(8,128)S(1)} %get-tuple-element.25.gains_ref), custom_call_target="tpu_custom_call" | custom-call | tf_op jit(solution)/shard_map/pallas_call | solution.py:493
  10.6 0.0 collective-permute-done.1.one_ref
  10.6 0.1 shard_map.68
  10.7 1.5 %collective-permute-done.two_ref = bf16[1040,128]{1,0:T(8,128)(2,1)S(1)} collective-permute-done((bf16[1040,128]{1,0:T(8,128)(2,1)S(1)}, bf16[1040,128]{1,0:T(8,128)(2,1)S(1)}, u32[]{:S(2)}, u32[]{:S(2)}) %collective-permute-start) | collective-permute-done | bytes 266272 | tf_op jit(solution)/shard_map/ppermute | solution.py:443
  12.2 1.6 %shard_map.69 = f32[128,2048]{1,0:T(8,128)} custom-call(bf16[512,512]{1,0:T(8,128)(2,1)S(1)} %get-tuple-element.22.turned_ref, bf16[1040,128]{1,0:T(8,128)(2,1)S(1)} %get-tuple-element.18.own_ref, bf16[1040,128]{1,0:T(8,128)(2,1)S(1)} %collective-permute-done.two_ref, f32[512,128]{1,0:T(8,128)S(1)} %get-tuple-element.28.state_ref, ...), custom_call_target="tpu_custom_call", output_to_operand_aliasing={{}: (8, {})} | custom-call | tf_op jit(solution)/shard_map/pallas_call | solution.py:509
Async XLA Ops:
  0.0 4.0 %copy-start = (bf16[128,2048]{1,0:T(8,128)(2,1)S(1)}, bf16[128,2048]{1,0:T(8,128)(2,1)}, u32[]{:S(2)}) copy-start(bf16[128,2048]{1,0:T(8,128)(2,1)} %q_ref.3) | copy-start | bytes 1572868
  0.0 4.0 %copy-start.1 = (f32[2048]{0:T(1024)S(1)}, f32[2048]{0:T(1024)}, u32[]{:S(2)}) copy-start(f32[2048]{0:T(1024)} %param.11) | copy-start | bytes 24580
  1.0 9.6 %collective-permute-start.1 = (bf16[1040,128]{1,0:T(8,128)(2,1)S(1)}, bf16[1040,128]{1,0:T(8,128)(2,1)S(1)}, u32[]{:S(2)}, u32[]{:S(2)}) collective-permute-start(bf16[1040,128]{1,0:T(8,128)(2,1)S(1)} %shard_map.64.packed_ref), channel_id=1, source_target_pairs={{8,16},{12,20},{0,4},{4,8},{24,28},{9,17},{13,21},{1,5},{5,9},{25,... | collective-permute-start | bytes 798728 | tf_op jit(solution)/shard_map/ppermute | solution.py:443
  4.1 8.1 %collective-permute-start = (bf16[1040,128]{1,0:T(8,128)(2,1)S(1)}, bf16[1040,128]{1,0:T(8,128)(2,1)S(1)}, u32[]{:S(2)}, u32[]{:S(2)}) collective-permute-start(bf16[1040,128]{1,0:T(8,128)(2,1)S(1)} %get-tuple-element.18.own_ref), channel_id=1, source_target_pairs={{8,12},{12,16},{16,20},{20,24},{9,13},{13,17},{17,21},{21,25},{10,... | collective-permute-start | bytes 798728 | tf_op jit(solution)/shard_map/ppermute | solution.py:443
  6.3 3.4 %collective-permute-start.2 = (bf16[1024,128]{1,0:T(8,128)(2,1)S(1)}, bf16[1024,128]{1,0:T(8,128)(2,1)S(1)}, u32[]{:S(2)}, u32[]{:S(2)}) collective-permute-start(bf16[1024,128]{1,0:T(8,128)(2,1)S(1)} %get-tuple-element.23), channel_id=1, source_target_pairs={{0,8},{4,12},{16,24},{20,28},{1,9},{5,13},{17,25},{21,29},{2,10},{... | collective-permute-start | bytes 786440 | tf_op jit(solution)/shard_map/ppermute | solution.py:443

commit v26 on v25

--- a/solution.py
+++ b/solution.py
@@ -284,7 +284,7 @@
             ahead[g] = dot(block_keys(one_ref, g), turned_ref[part_of(g, HEAD_DIM), :], NN)
 
     def attend(g):
-        for later in range(3):
+        for later in range(2):
             score(g + later)
         weights, factors, scales = [], [], []
         for i in range(GROUPS):

time: 14.1 us -> 14.1 us (level)
  no operation moved by 1% of the time
where the time goes in v26:
time: 14.1 us; the launch traced here: 13.9 us
  starting transfers between devices  6.32 us (45%)
  Pallas kernels  5.95 us (42%)
  waiting for transfers between devices  1.52 us (11%)
    ppermute x3, starting transfers between devices, send(): return lax.ppermute(payload, ('seq', 'kv'), pairs)  6.32 us
    pallas_call x1, Pallas kernels, near_device(): pl.pallas_call(functools.partial(own_kernel, plan), out_shape=results + [...  2.1 us
    pallas_call x1, Pallas kernels, near_device(): pl.pallas_call(functools.partial(late_kernel, plan), out_shape=out_shape,...  1.7 us
    ppermute x3, waiting for transfers between devices, send(): return lax.ppermute(payload, ('seq', 'kv'), pairs)  1.52 us
    pallas_call x1, Pallas kernels, near_device(): pl.pallas_call(functools.partial(pack_kernel, plan), out_shape=block_shap...  1.03 us
    pallas_call x1, Pallas kernels, near_device(): pl.pallas_call(functools.partial(read_kernel, plan), out_shape=gains_shap...  0.9 us
  transfers between devices with their start and end apart: 3, of which 1 were waited for; matrix products, arithmetic and copies ran while one was open for 0% of the time, Pallas kernels for 23%

profile of v26, /device:TPU:27, one launch (start us, length us, event | category | flops | bytes accessed | tf_op | source)
XLA Modules:
  0.0 13.9 jit_solution(10092135529407026701)
XLA Ops:
  0.0 0.0 copy-start
  0.0 0.0 copy-start.1
  0.0 1.0 %shard_map.64.packed_ref = bf16[1040,128]{1,0:T(8,128)(2,1)S(1)} custom-call(bf16[128,512]{1,0:T(8,128)(2,1)} %key_ref.3, bf16[128,512]{1,0:T(8,128)(2,1)} %value_ref.3, s32[1,128]{1,0:T(1,128)} %bitcast.4), custom_call_target="tpu_custom_call" | custom-call | flops 13421772 | bytes 419430 | tf_op jit(solution)/shard_map/pallas_call | solution.py:456
  1.0 2.9 %collective-permute-start.1 = (bf16[1040,128]{1,0:T(8,128)(2,1)S(1)}, bf16[1040,128]{1,0:T(8,128)(2,1)S(1)}, u32[]{:S(2)}, u32[]{:S(2)}) collective-permute-start(bf16[1040,128]{1,0:T(8,128)(2,1)S(1)} %shard_map.64.packed_ref), channel_id=1, source_target_pairs={{8,16},{12,20},{0,4},{4,8},{24,28},{9,17},{13,21},{1,5},{5,9},{25,... | collective-permute-start | bytes 798728 | tf_op jit(solution)/shard_map/ppermute | solution.py:443
  4.0 0.0 copy-done
  4.0 0.0 copy-done.1
  4.0 0.2 %shard_map.65 = (bf16[1040,128]{1,0:T(8,128)(2,1)S(1)}, bf16[1024,128]{1,0:T(8,128)(2,1)S(1)}, f32[512,512]{1,0:T(8,128)S(1)}, f32[16,512]{1,0:T(8,128)S(1)}, f32[2048,128]{1,0:T(8,128)S(1)}) custom-call(f32[16,128]{1,0:T(8,128)S(1)} %bitcast.2, bf16[1040,128]{1,0:T(8,128)(2,1)S(1)} %shard_map.64.packed_ref, bf16[128,2048]{1,0:T(8,128)(2,1)S(1)} %copy-done, ...), custom_call_target="tpu_custom_call" | custom-call | flops 134217728 | bytes 4194304 | tf_op jit(solution)/shard_map/pallas_call | solution.py:466
  4.1 2.1 %collective-permute-start = (bf16[1040,128]{1,0:T(8,128)(2,1)S(1)}, bf16[1040,128]{1,0:T(8,128)(2,1)S(1)}, u32[]{:S(2)}, u32[]{:S(2)}) collective-permute-start(bf16[1040,128]{1,0:T(8,128)(2,1)S(1)} %get-tuple-element.18.own_ref), channel_id=1, source_target_pairs={{8,12},{12,16},{16,20},{20,24},{9,13},{13,17},{17,21},{21,25},{10,... | collective-permute-start | bytes 798728 | tf_op jit(solution)/shard_map/ppermute | solution.py:443
  6.3 1.3 %collective-permute-start.2 = (bf16[1024,128]{1,0:T(8,128)(2,1)S(1)}, bf16[1024,128]{1,0:T(8,128)(2,1)S(1)}, u32[]{:S(2)}, u32[]{:S(2)}) collective-permute-start(bf16[1024,128]{1,0:T(8,128)(2,1)S(1)} %get-tuple-element.23), channel_id=1, source_target_pairs={{0,8},{4,12},{16,24},{20,28},{1,9},{5,13},{17,25},{21,29},{2,10},{... | collective-permute-start | bytes 786440 | tf_op jit(solution)/shard_map/ppermute | solution.py:443
  7.6 2.1 %shard_map.66 = (f32[512,512]{1,0:T(8,128)S(1)}, f32[16,512]{1,0:T(8,128)S(1)}, f32[2048,128]{1,0:T(8,128)S(1)}, f32[128,2048]{1,0:T(8,128)}, bf16[512,512]{1,0:T(8,128)(2,1)S(1)}) custom-call(bf16[128,2048]{1,0:T(8,128)(2,1)S(1)} %copy-done, f32[16,128]{1,0:T(8,128)S(1)} %bitcast.3, ...), custom_call_target="tpu_custom_call", output_to_operand_aliasing={{0}: (4, {}), {1}: (5, {}), {2}: (6, {})} | custom-call | flops 134217728 | bytes 4194304 | tf_op jit(solution)/shard_map/pallas_call | solution.py:483
  9.7 0.0 collective-permute-done.2.three_ref
  9.7 0.9 %shard_map.67.read_in = f32[2048,128]{1,0:T(8,128)S(1)} custom-call(bf16[512,512]{1,0:T(8,128)(2,1)S(1)} %get-tuple-element.22.turned_ref, bf16[1040,128]{1,0:T(8,128)(2,1)S(1)} %get-tuple-element.18.own_ref, bf16[1024,128]{1,0:T(8,128)(2,1)S(1)} %collective-permute-done.2.three_ref, f32[2048,128]{1,0:T(8,128)S(1)} %get-tuple-element.25.gains_ref), custom_call_target="tpu_custom_call" | custom-call | tf_op jit(solution)/shard_map/pallas_call | solution.py:493
  10.6 0.0 collective-permute-done.1.one_ref
  10.6 0.1 shard_map.68
  10.7 1.5 %collective-permute-done.two_ref = bf16[1040,128]{1,0:T(8,128)(2,1)S(1)} collective-permute-done((bf16[1040,128]{1,0:T(8,128)(2,1)S(1)}, bf16[1040,128]{1,0:T(8,128)(2,1)S(1)}, u32[]{:S(2)}, u32[]{:S(2)}) %collective-permute-start) | collective-permute-done | bytes 266272 | tf_op jit(solution)/shard_map/ppermute | solution.py:443
  12.2 1.7 %shard_map.69 = f32[128,2048]{1,0:T(8,128)} custom-call(bf16[512,512]{1,0:T(8,128)(2,1)S(1)} %get-tuple-element.22.turned_ref, bf16[1040,128]{1,0:T(8,128)(2,1)S(1)} %get-tuple-element.18.own_ref, bf16[1040,128]{1,0:T(8,128)(2,1)S(1)} %collective-permute-done.two_ref, f32[512,128]{1,0:T(8,128)S(1)} %get-tuple-element.28.state_ref, ...), custom_call_target="tpu_custom_call", output_to_operand_aliasing={{}: (8, {})} | custom-call | tf_op jit(solution)/shard_map/pallas_call | solution.py:509
Async XLA Ops:
  0.0 4.0 %copy-start = (bf16[128,2048]{1,0:T(8,128)(2,1)S(1)}, bf16[128,2048]{1,0:T(8,128)(2,1)}, u32[]{:S(2)}) copy-start(bf16[128,2048]{1,0:T(8,128)(2,1)} %q_ref.3) | copy-start | bytes 1572868
  0.0 4.0 %copy-start.1 = (f32[2048]{0:T(1024)S(1)}, f32[2048]{0:T(1024)}, u32[]{:S(2)}) copy-start(f32[2048]{0:T(1024)} %param.11) | copy-start | bytes 24580
  1.0 9.6 %collective-permute-start.1 = (bf16[1040,128]{1,0:T(8,128)(2,1)S(1)}, bf16[1040,128]{1,0:T(8,128)(2,1)S(1)}, u32[]{:S(2)}, u32[]{:S(2)}) collective-permute-start(bf16[1040,128]{1,0:T(8,128)(2,1)S(1)} %shard_map.64.packed_ref), channel_id=1, source_target_pairs={{8,16},{12,20},{0,4},{4,8},{24,28},{9,17},{13,21},{1,5},{5,9},{25,... | collective-permute-start | bytes 798728 | tf_op jit(solution)/shard_map/ppermute | solution.py:443
  4.1 8.1 %collective-permute-start = (bf16[1040,128]{1,0:T(8,128)(2,1)S(1)}, bf16[1040,128]{1,0:T(8,128)(2,1)S(1)}, u32[]{:S(2)}, u32[]{:S(2)}) collective-permute-start(bf16[1040,128]{1,0:T(8,128)(2,1)S(1)} %get-tuple-element.18.own_ref), channel_id=1, source_target_pairs={{8,12},{12,16},{16,20},{20,24},{9,13},{13,17},{17,21},{21,25},{10,... | collective-permute-start | bytes 798728 | tf_op jit(solution)/shard_map/ppermute | solution.py:443
  6.3 3.4 %collective-permute-start.2 = (bf16[1024,128]{1,0:T(8,128)(2,1)S(1)}, bf16[1024,128]{1,0:T(8,128)(2,1)S(1)}, u32[]{:S(2)}, u32[]{:S(2)}) collective-permute-start(bf16[1024,128]{1,0:T(8,128)(2,1)S(1)} %get-tuple-element.23), channel_id=1, source_target_pairs={{0,8},{4,12},{16,24},{20,28},{1,9},{5,13},{17,25},{21,29},{2,10},{... | collective-permute-start | bytes 786440 | tf_op jit(solution)/shard_map/ppermute | solution.py:443
